TPU v7x, 256 devices: a whole 4x4x8 slice. The times are simulated.
256 devices in a mesh: clus: 4 (over x), trip: 32 (over y, z), mode: 2 (over core).
Axes of the slice: x: 4, y: 4, z: 8, core: 2. Of those that a mesh axis runs over, the one named last changes fastest.
Arguments:
- force_third: bfloat16 [8, 90, 8100], P('clus', 'mode'), may hold values from -0.0234375 to 0.0234375
- phase_angle: bfloat16 [8, 128], P('clus', 'trip'), may hold values from -3.140625 to 3.140625
- eigenvectors: bfloat16 [256, 90, 180], P('trip'), may hold values from -0.4375 to 0.4375
- frequencies: bfloat16 [256, 90], P('trip'), may hold values from 0.5 to 2
- deviation: bfloat16 [256, 90], P('trip'), may hold values from 0.5 to 2
- send_rows: int32 [32, 32], P('trip'), may hold values from 0 to 7
- trip_table: int32 [128, 3], P('trip'), may hold values from 0 to 31
- irreducible: int32 [128], P('trip'), may hold values from 0 to 31
- multiplicity: int32 [128], P('trip'), may hold values from 1 to 8
- drive_term: float32 [32, 90], P('trip', 'mode'), may hold values from -120 to 120
- boundary: float32 [32, 90], P('trip', 'mode'), may hold values from 5 to 40
Outputs:
- gamma_total: float32 [32, 90], P('trip', 'mode')
- new_deviation: float32 [32, 90], P('trip', 'mode')
All inputs are finite; a program needn't handle non-finite values.
Results may differ from a plain program's by a relative error of at most 0.00095.
Values may be sent and summed in bfloat16 or wider, within the bound.
No kernel may reach another device: no remote copies, remote signals or barrier semaphores. Data moves between devices by JAX's collectives and lax.ppermute only.
A program may use at most 64 MiB of HBM per device.

v0:
```python
import jax
import jax.numpy as jnp
from jax import lax
from jax.sharding import PartitionSpec as P

smearing = 0.3
highest = lax.Precision.HIGHEST


def gaussian_weights(freq_zero, freq_one, freq_two):
    decays = freq_zero - freq_one - freq_two
    merges = freq_zero + freq_one - freq_two
    scaled = 0.5 / (smearing * smearing)
    return (jnp.exp(-scaled * decays * decays) + jnp.exp(-scaled * merges * merges)) / (
        freq_zero * freq_one * freq_two
    )


def combine(by_real, by_imag, mode_count):
    return jnp.concatenate(
        [
            by_real[..., :mode_count] - by_imag[..., mode_count:],
            by_real[..., mode_count:] + by_imag[..., :mode_count],
        ],
        axis=-1,
    )


def trig_rows(angles):
    values = angles.astype(jnp.float32).T
    stacked = jnp.stack([jnp.cos(values), jnp.sin(values)], axis=1).astype(jnp.bfloat16)
    return stacked.reshape(2 * values.shape[0], values.shape[1])


def first_two(transform_rows, middle, last_vec, mode_count):
    row_count = transform_rows.shape[1]
    real_part = transform_rows[0].reshape(row_count * mode_count, mode_count)
    imag_part = transform_rows[1].reshape(row_count * mode_count, mode_count)
    flipped = jnp.concatenate([-last_vec[:, mode_count:], last_vec[:, :mode_count]], axis=1)
    section_one = jnp.dot(real_part, last_vec, preferred_element_type=jnp.float32) + jnp.dot(
        imag_part, flipped, preferred_element_type=jnp.float32
    )
    section_one = section_one.astype(jnp.bfloat16).reshape(row_count, mode_count, 2 * mode_count)
    by_real = jnp.einsum(
        "abk,bj->ajk", section_one, middle[:, :mode_count], preferred_element_type=jnp.float32
    )
    by_imag = jnp.einsum(
        "abk,bj->ajk", section_one, middle[:, mode_count:], preferred_element_type=jnp.float32
    )
    return combine(by_real, by_imag, mode_count).astype(jnp.bfloat16)


def leading_terms(section_two, lead_rows, column_start, column_count, mode_count):
    real_cols = lax.dynamic_slice_in_dim(lead_rows, column_start, column_count, 1)
    imag_cols = lax.dynamic_slice_in_dim(lead_rows, column_start + mode_count, column_count, 1)
    by_real = jnp.einsum("as,ajk->sjk", real_cols, section_two, preferred_element_type=jnp.float32)
    by_imag = jnp.einsum("as,ajk->sjk", imag_cols, section_two, preferred_element_type=jnp.float32)
    return combine(by_real, by_imag, mode_count)


def body(
    force_third,
    phase_angle,
    eigenvectors,
    frequencies,
    deviation,
    send_rows,
    trip_table,
    irreducible,
    multiplicity,
    drive_term,
    boundary,
):
    mode_count = eigenvectors.shape[1]
    half_rows = force_third.shape[1]
    mode_block = boundary.shape[1]
    cluster_local = force_third.shape[0]
    per_device = trip_table.shape[0] // lax.axis_size("clus")
    cluster_rank = lax.axis_index("clus")
    mode_rank = lax.axis_index("mode")
    chosen = cluster_rank * per_device
    picked = send_rows[0]
    outgoing = eigenvectors[picked]
    extras = jnp.stack([frequencies[picked], deviation[picked]], axis=1)
    arrived, arrived_extra = (
        lax.all_to_all(outgoing, "trip", split_axis=0, concat_axis=0, tiled=True),
        lax.all_to_all(extras, "trip", split_axis=0, concat_axis=0, tiled=True),
    )
    own_table = lax.dynamic_slice_in_dim(trip_table, chosen, per_device, 0)
    own_mult = lax.dynamic_slice_in_dim(multiplicity, chosen, per_device, 0)
    own_irreducible = lax.dynamic_slice_in_dim(irreducible, chosen, per_device, 0)
    vectors = arrived[own_table]
    extra_rows = arrived_extra[own_table]
    flat_tensor = force_third.reshape(cluster_local, -1)
    product = jnp.dot(trig_rows(phase_angle), flat_tensor, preferred_element_type=jnp.float32)
    summed = lax.psum_scatter(
        product.reshape(
            per_device * lax.axis_size("clus"), 2, half_rows, mode_count * mode_count
        ).astype(jnp.bfloat16),
        "clus",
        scatter_dimension=0,
        tiled=True,
    )
    leading = vectors[:, 0]
    middle = vectors[:, 1]
    last_vec = vectors[:, 2]
    column_start = mode_rank * mode_block
    terms = [
        leading_terms(
            first_two(
                lax.all_gather(summed, "mode", axis=2, tiled=True)[0],
                middle[0],
                last_vec[0],
                mode_count,
            ),
            leading[0],
            column_start,
            mode_block,
            mode_count,
        )
    ]
    amplitude = jnp.stack(terms, axis=1)
    freq_own = extra_rows[:, :, 0].astype(jnp.float32)
    occupied = extra_rows[:, :, 1].astype(jnp.float32)
    freq_zero = lax.dynamic_slice_in_dim(freq_own[:, 0], mode_rank * mode_block, mode_block, 1).T
    squared = amplitude[..., :mode_count] ** 2 + amplitude[..., mode_count:] ** 2
    weights = (
        squared
        * gaussian_weights(
            freq_zero[:, :, None, None],
            freq_own[None, :, 1, :, None],
            freq_own[None, :, 2, None, :],
        )
        * own_mult.astype(jnp.float32)[None, :, None, None]
    )
    totals = jnp.sum(weights, axis=(2, 3))
    couples = jnp.einsum("stjk,tj->st", weights, occupied[:, 1], precision=highest) + jnp.einsum(
        "stjk,tk->st", weights, occupied[:, 2], precision=highest
    )
    point_count = drive_term.shape[0] * lax.axis_size("trip")
    onehot = (own_irreducible[:, None] == jnp.arange(point_count, dtype=jnp.int32)[None, :]).astype(
        jnp.float32
    )
    rate_part = jnp.dot(onehot.T, totals.T, precision=highest)
    couple_part = jnp.dot(onehot.T, couples.T, precision=highest)
    rate_share, couple_share = (
        lax.psum_scatter(rate_part, "trip", scatter_dimension=0, tiled=True),
        lax.psum_scatter(couple_part, "trip", scatter_dimension=0, tiled=True),
    )
    rate_here, couple_here = lax.psum((rate_share, couple_share), "clus")
    gamma_total = rate_here + boundary
    return (gamma_total, (drive_term + couple_here) / gamma_total)


def solution(mesh):
    return jax.shard_map(
        body,
        mesh=mesh,
        in_specs=(
            P("clus", "mode", None),
            P("clus", "trip"),
            P("trip", None, None),
            P("trip", None),
            P("trip", None),
            P("trip", None),
            P("trip", None),
            P("trip"),
            P("trip"),
            P("trip", "mode"),
            P("trip", "mode"),
        ),
        out_specs=(P("trip", "mode"), P("trip", "mode")),
        check_vma=False,
    )
```

profile of v0, /device:TPU:2, one launch (start us, length us, event | category | flops | bytes accessed | tf_op | source)
XLA Modules:
  0.0 492.0 jit_solution(6455827065827384970)
XLA Ops:
  7.2 0.7 fusion.41
  8.0 2.2 copy.55
  10.2 2.0 reshape.323
  12.2 0.8 reshape.261
  13.0 0.9 reshape.325
  13.9 4.1 reshape.326
  18.1 5.0 %convolution_convert_fusion = bf16[4,2,45,8100]{3,0,2,1:T(4,128)(2,1)S(1)} fusion(bf16[45,8100,2]{1,0,2:T(8,128)(2,1)} %bitcast.105, bf16[4,1,2]{0,2,1:T(2,128)(2,1)S(1)} %get-tuple-element.33, bf16[4,1,2]{0,2,1:T(2,128)(2,1)S(1)} %get-tuple-element.32), kind=kOutput, calls=%fused_computation.5 | convolution fusion | flops 14580064 | bytes 7290032 | tf_op jit(solution)/shard_map/dot_general | solution.py:95
  23.1 10.7 %copy.57 = bf16[4,2,45,8100]{3,1,2,0:T(2,128)(2,1)} copy(bf16[4,2,45,8100]{3,0,2,1:T(4,128)(2,1)S(1)} %convolution_convert_fusion) | data formatting | bytes 11664000 | tf_op jit(solution)/shard_map/convert_element_type | solution.py:99
  33.9 0.6 copy-done.11
  34.5 0.6 dynamic-slice.3
  35.1 126.4 %all-reduce.7.cloned.1.call-done = bf16[4,2,45,8100]{3,1,2,0:T(2,128)(2,1)} async-done(((bf16[4,2,45,8100]{3,1,2,0:T(2,128)(2,1)}), bf16[4,2,45,8100]{3,1,2,0:T(2,128)(2,1)}) %all-reduce.7.cloned.1.call-update) | async-done | bytes 5832016
  161.5 5.2 %dynamic-slice_bitcast_fusion = bf16[1,2,45,8100]{3,1,0,2:T(2,128)(2,1)} fusion(bf16[4,2,45,8100]{3,1,2,0:T(2,128)(2,1)} %all-reduce.7.cloned.1.call-done, u32[]{:T(128)} %bitcast.44), kind=kLoop, calls=%fused_computation.35 | loop fusion | bytes 2916004 | tf_op jit(solution)/shard_map/reduce_scatter | solution.py:96
  166.8 0.6 gather_fusion.2
  167.4 0.6 gather_fusion.3
  168.0 0.6 copy.64
  168.6 20.5 %all-to-all-start.1 = ((bf16[32,2,90]{2,1,0:T(2,128)(2,1)}), bf16[32,2,90]{2,1,0:T(2,128)(2,1)S(1)}, u32[]{:S(2)}, u32[]{:S(2)}) async-start(bf16[32,2,90]{2,1,0:T(2,128)(2,1)} %copy.64), calls=%async_computation.1 | async-start | bytes 32768 | tf_op jit(solution)/shard_map/all_to_all | solution.py:87
  189.1 4.8 gather_fusion
  193.9 2.6 copy.52
  196.5 2.1 all-to-all-done.1
  198.6 7.6 %all-to-all-start = ((bf16[32,90,180]{1,2,0:T(8,128)(2,1)}), bf16[32,90,180]{1,2,0:T(8,128)(2,1)S(1)}, u32[]{:S(2)}, u32[]{:S(2)}) async-start(bf16[32,90,180]{1,2,0:T(8,128)(2,1)} %copy.52), calls=%async_computation | async-start | bytes 3014656 | tf_op jit(solution)/shard_map/all_to_all | solution.py:86
  206.3 0.6 dynamic_slice.29
  207.5 0.6 dynamic_slice.22
  208.1 0.6 dynamic-slice.5
  208.7 0.7 fusion.47
  209.4 0.6 compare_convert_fusion
  210.0 0.6 gather_fusion.4
  210.8 33.0 %all-to-all-done = bf16[32,90,180]{1,2,0:T(8,128)(2,1)S(1)} async-done(((bf16[32,90,180]{1,2,0:T(8,128)(2,1)}), bf16[32,90,180]{1,2,0:T(8,128)(2,1)S(1)}, u32[]{:S(2)}, u32[]{:S(2)}) %all-to-all-start) | async-done | bytes 1036832 | tf_op jit(solution)/shard_map/all_to_all | solution.py:86
  243.8 0.6 gather_fusion.1
  244.7 16.6 %slice_reduce_fusion = (bf16[90,8100]{1,0:T(8,128)(2,1)}, bf16[90,8100]{1,0:T(8,128)(2,1)}) fusion(bf16[1,2,90,8100]{3,1,0,2:T(2,128)(2,1)} %all-gather.2.cloned.1.call-done), kind=kLoop, calls=%fused_computation.22 | loop fusion | bytes 5832000 | tf_op jit(solution)/shard_map/slice | solution.py:38
  261.4 4.9 reshape_squeeze.6
  266.2 3.6 fusion.50
  269.8 6.1 %reshape_squeeze.7 = bf16[8100,90]{1,0:T(8,128)(2,1)} reshape(bf16[90,8100]{1,0:T(8,128)(2,1)} %get-tuple-element.2) | data formatting | bytes 2916000 | tf_op jit(solution)/shard_map/reshape;squeeze | solution.py:38
  275.9 4.4 fusion
  280.3 17.3 %reshape.262 = bf16[90,90,180]{1,0,2:T(8,128)(2,1)} reshape(bf16[8100,180]{0,1:T(8,128)(2,1)S(1)} %fusion) | data formatting | bytes 5832000 | tf_op jit(solution)/shard_map/reshape | solution.py:43
  297.7 4.3 fusion.7
  301.9 2.1 fusion.10
  304.0 2.0 fusion.2
  306.0 3.3 pad_maximum_fusion
  309.3 10.6 %copy.61 = bf16[90,90,180]{0,2,1:T(8,128)(2,1)} copy(bf16[90,90,180]{1,2,0:T(8,128)(2,1)} %pad_maximum_fusion) | data formatting | bytes 5832000 | tf_op jit(solution)/shard_map/concatenate | solution.py:20
  319.9 5.1 %fusion.28 = f32[45,90,180]{2,0,1:T(8,128)S(1)} fusion(bf16[90,90,180]{0,2,1:T(8,128)(2,1)} %copy.61, bf16[1,1,90,180]{3,2,1,0:T(8,128)(2,1)S(1)} %get-tuple-element.17, s32[]{:T(128)S(6)} %select_n.33), kind=kOutput, calls=%fused_computation.51 | convolution fusion | flops 131220000 | bytes 5856580 | tf_op jit(solution)/shard_map/as,ajk->sjk/dot_general | solution.py:56
  325.1 2.8 fusion.26
  327.9 1.2 slice_subtract_fusion.1
  329.2 1.2 maximum_bitcast_fusion
  330.4 3.8 fusion.51
  334.5 140.0 %all-reduce.3 = (f32[32,45]{1,0:T(8,128)S(1)}, f32[32,45]{1,0:T(8,128)S(1)}) all-reduce(f32[32,45]{1,0:T(8,128)S(1)} %get-tuple-element.31, f32[32,45]{1,0:T(8,128)S(1)} %get-tuple-element.30), channel_id=3, replica_groups=mesh['clus'=4,'trip'=32,'mode'=2] {'trip'}, use_global_device_ids=true, to_apply=%region_2.0.clone | all-reduce | flops 2880 | bytes 23040
  474.6 0.6 constant_dynamic-slice_fusion
  475.1 9.3 %all-reduce.4 = (f32[1,45]{1,0:T(1,128)S(1)}, f32[1,45]{1,0:T(1,128)S(1)}) all-reduce(f32[1,45]{1,0:T(1,128)S(1)} %get-tuple-element.35, f32[1,45]{1,0:T(1,128)S(1)} %get-tuple-element.34), channel_id=1, replica_groups=mesh['clus'=4,'trip'=32,'mode'=2] {'clus'}, use_global_device_ids=true, to_apply=%region_3.0 | all-reduce | flops 90 | bytes 720 | tf_op jit(solution)/shard_map/psum | solution.py:150
  484.5 0.5 add_divide_fusion
  (48 shorter events, 1.0 us)
Async XLA Ops:
  7.2 181.9 %copy-start = (bf16[8,90,180]{2,0,1:T(8,128)(2,1)S(1)}, bf16[8,90,180]{2,0,1:T(8,128)(2,1)}, u32[]{:S(2)}) copy-start(bf16[8,90,180]{2,0,1:T(8,128)(2,1)} %param.13) | copy-start | bytes 777604
  7.2 154.3 %all-reduce.7.cloned.1.call-start = ((), (), s32[]{:S(2)}) async-start(), calls=%async_computation.3 | async-start | bytes 11796480
  33.8 0.7 copy-start.11
  33.9 210.9 %all-gather.2.cloned.1.call-start = ((), (), s32[]{:S(2)}) async-start(), calls=%async_computation.2 | async-start | bytes 4423680 | tf_op jit(solution)/shard_map/all_gather | solution.py:111
  161.5 5.2 %copy-start.7 = (s32[1,32]{1,0:T(1,128)S(1)}, s32[1,32]{1,0:T(1,128)}, u32[]{:S(2)}) copy-start(s32[1,32]{1,0:T(1,128)} %param.16) | copy-start | bytes 388
  161.5 5.3 %copy-start.3 = (bf16[8,90]{1,0:T(8,128)(2,1)S(1)}, bf16[8,90]{1,0:T(8,128)(2,1)}, u32[]{:S(2)}) copy-start(bf16[8,90]{1,0:T(8,128)(2,1)} %param.14) | copy-start | bytes 4324
  161.5 5.9 %copy-start.4 = (bf16[8,90]{1,0:T(8,128)(2,1)S(1)}, bf16[8,90]{1,0:T(8,128)(2,1)}, u32[]{:S(2)}) copy-start(bf16[8,90]{1,0:T(8,128)(2,1)} %param.15) | copy-start | bytes 4324
  168.6 30.0 %all-to-all-start.1 = ((bf16[32,2,90]{2,1,0:T(2,128)(2,1)}), bf16[32,2,90]{2,1,0:T(2,128)(2,1)S(1)}, u32[]{:S(2)}, u32[]{:S(2)}) async-start(bf16[32,2,90]{2,1,0:T(2,128)(2,1)} %copy.64), calls=%async_computation.1 | async-start | bytes 32768 | tf_op jit(solution)/shard_map/all_to_all | solution.py:87
  196.4 9.8 %copy-start.8 = (s32[4]{0:T(128)S(1)}, s32[4]{0:T(128)}, u32[]{:S(2)}) copy-start(s32[4]{0:T(128)} %param.19) | copy-start | bytes 52
  196.4 11.0 %copy-start.9 = (s32[4]{0:T(128)S(1)}, s32[4]{0:T(128)}, u32[]{:S(2)}) copy-start(s32[4]{0:T(128)} %param.18) | copy-start | bytes 52
  196.4 11.6 %copy-start.10 = (u32[256]{0:T(256)S(1)}, u32[256]{0:T(256)}, u32[]{:S(2)}) copy-start(u32[256]{0:T(256)} %constant.52) | copy-start | bytes 3076
  198.6 45.2 %all-to-all-start = ((bf16[32,90,180]{1,2,0:T(8,128)(2,1)}), bf16[32,90,180]{1,2,0:T(8,128)(2,1)S(1)}, u32[]{:S(2)}, u32[]{:S(2)}) async-start(bf16[32,90,180]{1,2,0:T(8,128)(2,1)} %copy.52), calls=%async_computation | async-start | bytes 3014656 | tf_op jit(solution)/shard_map/all_to_all | solution.py:86
  297.7 4.3 copy-start.2
  319.9 5.2 %slice-start = ((s8[4239360]{0:T(1024)(128)(4,1)}), s8[4194304]{0:T(1024)(128)(4,1)S(1)}, s32[]{:S(2)}) async-start(s8[4239360]{0:T(1024)(128)(4,1)} %bitcast.103), calls=%async_computation.4 | async-start | bytes 8388608
  319.9 5.2 %slice-start.1 = ((s8[4239360]{0:T(1024)(128)(4,1)}), s8[45056]{0:T(1024)(128)(4,1)S(1)}, s32[]{:S(2)}) async-start(s8[4239360]{0:T(1024)(128)(4,1)} %bitcast.103), calls=%async_computation.5 | async-start | bytes 90112
  330.4 154.6 %copy-start.1 = (bf16[8,90,180]{2,0,1:T(8,128)(2,1)S(1)}, bf16[8,90,180]{2,0,1:T(8,128)(2,1)}, u32[]{:S(2)}) copy-start(bf16[8,90,180]{2,0,1:T(8,128)(2,1)} %param.13) | copy-start | bytes 777604
  330.4 154.1 %copy-start.5 = (f32[1,45]{1,0:T(1,128)S(1)}, f32[1,45]{1,0:T(1,128)}, u32[]{:S(2)}) copy-start(f32[1,45]{1,0:T(1,128)} %param.20) | copy-start | bytes 544
  330.4 154.1 %copy-start.6 = (f32[1,45]{1,0:T(1,128)S(1)}, f32[1,45]{1,0:T(1,128)}, u32[]{:S(2)}) copy-start(f32[1,45]{1,0:T(1,128)} %param.21) | copy-start | bytes 544
Sparse Core Ops, SparseCore 0:
  34.0 127.4 all-reduce.6
  166.9 18.1 all-gather.1
where the time goes:
time: 495 us; the launch traced here: 492 us
  waiting for transfers between devices  162 us (33%)
  blocking collectives  149 us (30%)
  local copies, waits for them, and re-layouts  95.8 us (19%)
  starting transfers between devices  28.2 us (6%)
  matrix products  27.5 us (6%)
  between operations  15.2 us (3%)
  other arithmetic  14.4 us (3%)
    unnamed x1, blocking collectives  140 us
    unnamed x3, waiting for transfers between devices  126 us
    all_to_all x1, waiting for transfers between devices, body(): lax.all_to_all(outgoing, 'trip', split_axis=0, concat_axis=0, tiled=True)  33 us
    all_to_all x1, starting transfers between devices, body(): lax.all_to_all(extras, 'trip', split_axis=0, concat_axis=0, tiled=True)  20.5 us
    reshape x1, local copies, waits for them, and re-layouts, first_two(): section_one.astype(jnp.bfloat16)  17.3 us
    slice x1, local copies, waits for them, and re-layouts, first_two(): imag_part = transform_rows[1].reshape(row_count * mode_count, mode_count)  16.6 us
    unnamed x36, local copies, waits for them, and re-layouts  11.7 us
    convert_element_type x1, local copies, waits for them, and re-layouts, body(): summed = lax.psum_scatter(product.reshape(per_device * lax.axis_size('clu...  10.7 us
  transfers between devices with their start and end apart: 4, of which 3 were waited for; matrix products, arithmetic and copies ran while one was open for 3% of the time, Pallas kernels for 0%

commit v1 on v0

v1 whole, which is shorter than its diff:
```python
import jax
import jax.numpy as jnp
from jax import lax
from jax.experimental import pallas as pl
from jax.experimental.pallas import tpu as pltpu
from jax.sharding import PartitionSpec as P

smearing = 0.3
SPLIT = 4096
LANES = 256
RING_Y = 4
RING_Z = 8
PAD = 48
WIDE = 96


def send_kernel(rows_ref, share_ref, out_ref):
    for target in range(out_ref.shape[0]):
        out_ref[target] = share_ref[rows_ref[0, target]]


def pick_kernel(table_ref, arrived_ref, phase_ref, out_ref):
    for triplet in range(4):
        for member in range(3):
            block = arrived_ref[table_ref[triplet, member]]
            out_ref[2 * triplet, member] = block
            out_ref[2 * triplet + 1, member] = block
        out_ref[2 * triplet, 3] = phase_ref[triplet]
        out_ref[2 * triplet + 1, 3] = phase_ref[triplet]


def transform_kernel(where_ref, trig_ref, own_ref, *refs):
    out_ref = refs[-1]
    rank = where_ref[0]
    color = where_ref[1]
    pieces = [
        (3, True, refs[0], refs[1]),
        (1, True, refs[2], refs[3]),
        (3, False, refs[4], refs[5]),
        (1, False, refs[6], refs[7]),
        (2, True, refs[8], refs[9]),
        (2, False, refs[10], refs[11]),
    ]
    factors = []
    for offset, same, _, _ in pieces:
        which = color if same else 1 - color
        at = 2 * (2 * ((rank + offset) & 3) + which)
        factors.append((trig_ref[at], trig_ref[at + 1]))
    own = [(trig_ref[4 * rank + 2 * r], trig_ref[4 * rank + 2 * r + 1]) for r in range(2)]
    out_ref[:, 45:PAD, :] = jnp.zeros((2, PAD - 45, out_ref.shape[2]), out_ref.dtype)

    def chunk(half, start, width):
        whole = start + half * SPLIT
        if not isinstance(start, int):
            whole = pl.multiple_of(whole, LANES)
            start = pl.multiple_of(start, LANES)
        real = imag = None
        for r in range(2):
            values = own_ref[r, :, pl.ds(whole, width)].astype(jnp.float32)
            real = own[r][0] * values if real is None else real + own[r][0] * values
            imag = own[r][1] * values if imag is None else imag + own[r][1] * values
        for (cosine, sine), piece in zip(factors, pieces):
            values = piece[2 + half][:, pl.ds(start, width)].astype(jnp.float32)
            real = real + cosine * values
            imag = imag + sine * values
        out_ref[0, 0:45, pl.ds(whole, width)] = real.astype(out_ref.dtype)
        out_ref[1, 0:45, pl.ds(whole, width)] = imag.astype(out_ref.dtype)

    total = own_ref.shape[2]
    for half, length in ((0, SPLIT), (1, total - SPLIT)):
        count = length // LANES

        @pl.loop(0, count)
        def _(i, half=half):
            chunk(half, i * LANES, LANES)

        if length % LANES:
            chunk(half, count * LANES, length % LANES)


def interaction_kernel(
    scalars_ref,
    lead_ref,
    middle_ref,
    last_ref,
    tables_ref,
    mine_ref,
    other_ref,
    out_ref,
    flat,
    windows,
    mid_real,
    mid_imag,
    rate_acc,
    couple_acc,
):
    total = mine_ref.shape[2]
    flat[:, 8064:8320] = jnp.zeros((2 * PAD, 256), flat.dtype)
    for start in range(0, total, 1024):
        width = min(1024, total - start)
        cols = pl.ds(start, width)
        stacked = jnp.concatenate(
            [mine_ref[0, :, cols], mine_ref[1, :, cols], other_ref[0, :, cols], other_ref[1, :, cols]],
            axis=0,
        )
        flat[:, cols] = jnp.dot(
            lead_ref[...], stacked, preferred_element_type=jnp.float32
        ).astype(flat.dtype)
    for b in range(90):
        tile, shift = divmod(90 * b, 128)
        pair = flat[:, tile * 128 : tile * 128 + 256]
        window = pair[:, shift : shift + 128]
        windows[b * PAD : (b + 1) * PAD, 0:128] = window[0:PAD]
        windows[b * PAD : (b + 1) * PAD, 128:256] = window[PAD:]
    zeros = jnp.zeros((PAD, 128), jnp.float32)
    for b in range(90, WIDE):
        mid_real[pl.ds(b, PAD, stride=WIDE), :] = zeros
        mid_imag[pl.ds(b, PAD, stride=WIDE), :] = zeros
    for group in range(9):
        product = jnp.dot(
            windows[group * 480 : (group + 1) * 480, :],
            last_ref[...],
            preferred_element_type=jnp.float32,
        )
        for i in range(10):
            rows = pl.ds(group * 10 + i, PAD, stride=WIDE)
            mid_real[rows, :] = product[i * PAD : (i + 1) * PAD, 0:128]
            mid_imag[rows, :] = product[i * PAD : (i + 1) * PAD, 128:256]

    scaled = 0.5 / (smearing * smearing)
    tail = jnp.zeros((8 * (PAD - 45), 128), jnp.float32)
    rate_acc[8 * 45 :, :] = tail
    couple_acc[8 * 45 :, :] = tail

    def one_mode(s):
        rows = pl.ds(pl.multiple_of(s * WIDE, WIDE), WIDE)
        operand = jnp.concatenate([mid_real[rows, :], mid_imag[rows, :]], axis=0)
        value = jnp.dot(
            middle_ref[...], operand.astype(jnp.bfloat16), preferred_element_type=jnp.float32
        )
        real = value[0:WIDE]
        imag = value[WIDE:]
        freq = scalars_ref[0, s]
        decays = freq - tables_ref[0]
        merges = freq + tables_ref[1]
        weight = (real * real + imag * imag) * (
            jnp.exp(-scaled * decays * decays) + jnp.exp(-scaled * merges * merges)
        )
        weight = weight * tables_ref[2] * scalars_ref[1, s]
        at = pl.ds(pl.multiple_of(s * 8, 8), 8)
        rate_acc[at, :] = jnp.sum(weight.reshape(WIDE // 8, 8, 128), axis=0)
        couple_acc[at, :] = jnp.sum((weight * tables_ref[3]).reshape(WIDE // 8, 8, 128), axis=0)

    @pl.loop(0, 15)
    def _(i):
        for j in range(3):
            one_mode(3 * i + j)

    sums = jnp.concatenate(
        [
            jnp.sum(rate_acc[...].reshape(PAD, 8, 128), axis=1),
            jnp.sum(couple_acc[...].reshape(PAD, 8, 128), axis=1),
        ],
        axis=0,
    )
    out_ref[:, 0:WIDE] = lax.dot_general(
        jnp.ones((8, 128), jnp.float32),
        sums,
        (((1,), (1,)), ((), ())),
        precision=lax.Precision.HIGHEST,
        preferred_element_type=jnp.float32,
    )
    out_ref[:, WIDE:128] = jnp.zeros((8, 128 - WIDE), jnp.float32)


VMEM = pl.BlockSpec(memory_space=pltpu.VMEM)
SMEM = pl.BlockSpec(memory_space=pltpu.SMEM)


def ring(count, step):
    return [(i, (i + step) % count) for i in range(count)]


def grid_shift(step_y, step_z):
    return [
        (y * RING_Z + z, (y + step_y) % RING_Y * RING_Z + (z + step_z) % RING_Z)
        for y in range(RING_Y)
        for z in range(RING_Z)
    ]


def pad_to(array, rows, cols):
    return jnp.pad(array, ((0, rows - array.shape[0]), (0, cols - array.shape[1])))


def body(
    force_third,
    phase_angle,
    eigenvectors,
    frequencies,
    deviation,
    send_rows,
    trip_table,
    irreducible,
    multiplicity,
    drive_term,
    boundary,
):
    f32, b16 = jnp.float32, jnp.bfloat16
    clus = lax.axis_index("clus")
    mode = lax.axis_index("mode")
    trip = lax.axis_index("trip")
    color = (trip // RING_Z + trip % RING_Z) % 2

    picked_force = lax.dynamic_index_in_dim(force_third, color, 0, keepdims=False)
    half0, half1 = picked_force[:, :SPLIT], picked_force[:, SPLIT:]
    up, down = ring(4, 1), ring(4, 3)
    with jax.named_scope("force_neighbours"):
        low0 = lax.ppermute(half0, "clus", up)
        high0 = lax.ppermute(half0, "clus", down)
        low1 = lax.ppermute(half1, "clus", up)
        high1 = lax.ppermute(half1, "clus", down)
    with jax.named_scope("force_second"):
        opp0 = lax.ppermute(low0, "clus", up)
        opp1 = lax.ppermute(high1, "clus", down)
        low_other0 = lax.ppermute(low0, "trip", grid_shift(1, 0))
        high_other0 = lax.ppermute(high0, "trip", grid_shift(0, 1))
        low_other1 = lax.ppermute(low1, "trip", grid_shift(-1, 0))
        high_other1 = lax.ppermute(high1, "trip", grid_shift(0, -1))
    with jax.named_scope("force_third_step"):
        opp_other0 = lax.ppermute(opp0, "trip", grid_shift(1, 0))
        opp_other1 = lax.ppermute(opp1, "trip", grid_shift(0, 1))

    with jax.named_scope("records"):
        extra = jnp.concatenate([frequencies, deviation], axis=1)[:, None, :]
        record = jnp.concatenate(
            [eigenvectors, extra, jnp.zeros((extra.shape[0], 5, 180), b16)], axis=1
        )
        share = lax.dynamic_slice_in_dim(record, 12 * (2 * clus + mode), 12, 1)
        chosen = pl.pallas_call(
            send_kernel,
            out_shape=jax.ShapeDtypeStruct((send_rows.shape[1],) + share.shape[1:], b16),
            in_specs=[SMEM, VMEM],
            out_specs=VMEM,
        )(send_rows, share)
        arrived = lax.all_to_all(chosen, "trip", 0, 0, tiled=True)
        angles = phase_angle.astype(f32)
        trig = jnp.stack([jnp.cos(angles), jnp.sin(angles)], axis=1).astype(b16)
        trig = trig.reshape(4, 4).T
        phases = jnp.pad(trig[:, None, :], ((0, 0), (0, 11), (0, 176)))
        outgoing = pl.pallas_call(
            pick_kernel,
            out_shape=jax.ShapeDtypeStruct((8, 4, 12, 180), b16),
            in_specs=[SMEM, VMEM, VMEM],
            out_specs=VMEM,
        )(trip_table, arrived, phases)
        members = lax.all_to_all(outgoing, ("clus", "mode"), 0, 0, tiled=True)
        factors = members[0::2, 3, 0, 0:4].astype(f32).reshape(16)
        blocks = jnp.transpose(members[:, :3], (1, 0, 2, 3)).reshape(3, 96, 180)
    with jax.named_scope("operands"):
        leading, middle, last = blocks[0, :90], blocks[1, :90], blocks[2, :90]
        freq = blocks[:, 90, :90].astype(f32)
        occupied = blocks[:, 90, 90:].astype(f32)

        def lead_part(row_rank):
            real = lax.dynamic_slice(leading, (45 * row_rank, 45 * mode), (45, 45)).T
            imag = lax.dynamic_slice(leading, (45 * row_rank, 90 + 45 * mode), (45, 45)).T
            real, imag = pad_to(real, PAD, PAD), pad_to(imag, PAD, PAD)
            return jnp.block([[real, -imag], [imag, real]])

        lead = jnp.concatenate([lead_part(mode), lead_part(1 - mode)], axis=1)
        mid_r, mid_i = pad_to(middle[:, :90].T, WIDE, WIDE), pad_to(middle[:, 90:].T, WIDE, WIDE)
        mid = jnp.block([[mid_r, -mid_i], [mid_i, mid_r]])
        last_r, last_i = pad_to(last[:, :90], 128, 128), pad_to(last[:, 90:], 128, 128)
        last_all = jnp.block([[last_r, last_i], [-last_i, last_r]])
        one = jnp.pad(freq[1], (0, 6), constant_values=1.0)[:, None]
        two = jnp.pad(freq[2], (0, 38), constant_values=1.0)[None, :]
        tables = jnp.stack(
            [
                one + two,
                one - two,
                1.0 / (one * two),
                jnp.pad(occupied[1], (0, 6))[:, None] + jnp.pad(occupied[2], (0, 38))[None, :],
            ]
        )
        zero = lax.dynamic_slice_in_dim(freq[0], 45 * mode, 45, 0)
        mult = lax.dynamic_index_in_dim(multiplicity, clus, 0, keepdims=False).astype(f32)
        scalars = jnp.stack([zero, mult / zero])
        where = jnp.stack([clus, color]).astype(jnp.int32)

    with jax.named_scope("transform"):
        mine = pl.pallas_call(
            transform_kernel,
            out_shape=jax.ShapeDtypeStruct((2, PAD, force_third.shape[2]), b16),
            in_specs=[SMEM, SMEM] + [VMEM] * 13,
            out_specs=VMEM,
            compiler_params=pltpu.CompilerParams(vmem_limit_bytes=48 << 20),
        )(
            where,
            factors,
            force_third,
            low0,
            low1,
            high0,
            high1,
            low_other0,
            low_other1,
            high_other0,
            high_other1,
            opp0,
            opp1,
            opp_other0,
            opp_other1,
        )
        other = lax.ppermute(mine, "mode", [(0, 1), (1, 0)])
    with jax.named_scope("interaction"):
        sums = pl.pallas_call(
            interaction_kernel,
            out_shape=jax.ShapeDtypeStruct((8, 128), f32),
            in_specs=[SMEM] + [VMEM] * 6,
            out_specs=VMEM,
            scratch_shapes=[
                pltpu.VMEM((2 * PAD, 8320), b16),
                pltpu.VMEM((90 * PAD, 256), b16),
                pltpu.VMEM((PAD * WIDE, 128), f32),
                pltpu.VMEM((PAD * WIDE, 128), f32),
                pltpu.VMEM((8 * PAD, 128), f32),
                pltpu.VMEM((8 * PAD, 128), f32),
            ],
            compiler_params=pltpu.CompilerParams(vmem_limit_bytes=48 << 20),
        )(scalars, lead, mid, last_all, tables, mine, other)
    with jax.named_scope("collect"):
        own_row = sums[0:1]
        rows = [own_row] + [lax.ppermute(own_row, "clus", ring(4, step)) for step in (1, 2, 3)]
        points = jnp.arange(32, dtype=jnp.int32)
        partial = jnp.zeros((32, 128), f32)
        for step in range(4):
            point = lax.dynamic_index_in_dim(irreducible, (clus - step) % 4, 0, keepdims=False)
            partial = partial + jnp.where((points == point)[:, None], rows[step], 0.0)
        received = lax.all_to_all(partial[:, None, :], "trip", 0, 0, tiled=True)
        final = jnp.sum(received[:, 0, :], axis=0)[None, :]
        gamma_total = final[:, 0:45] + boundary
        return gamma_total, (drive_term + final[:, PAD : PAD + 45]) / gamma_total


def solution(mesh):
    return jax.shard_map(
        body,
        mesh=mesh,
        in_specs=(
            P("clus", "mode", None),
            P("clus", "trip"),
            P("trip", None, None),
            P("trip", None),
            P("trip", None),
            P("trip", None),
            P("trip", None),
            P("trip"),
            P("trip"),
            P("trip", "mode"),
            P("trip", "mode"),
        ),
        out_specs=(P("trip", "mode"), P("trip", "mode")),
        check_vma=False,
    )
```

time: 495 us -> 125 us (0.25)
  waiting for transfers between devices: 162 us -> 25.6 us
  blocking collectives: 149 us -> 14 us
  local copies, waits for them, and re-layouts: 95.8 us -> 18.1 us
  matrix products: 27.5 us -> 0 us
  Pallas kernels: 0 us -> 18.5 us
  between operations: 15.2 us -> 1.71 us
  starting transfers between devices: 28.2 us -> 35 us
    unnamed x1 -> x0, blocking collectives: 140 us -> none
    unnamed x3 -> x0, waiting for transfers between devices: 126 us -> none
    dot_general x9 -> x0, matrix products: 27.5 us -> none  [the longest x1 5.15 us: leading_terms(): jnp.einsum('as,ajk->sjk', real_cols, section_two, preferred_element_type=...]
    all_to_all x2, waiting for transfers between devices: 35.2 us -> 10.5 us  [the longest x1 10.5 us: body(): arrived = lax.all_to_all(chosen, 'trip', 0, 0, tiled=True)]
    pallas_call x0 -> x4, Pallas kernels: none -> 18.5 us  [the longest x1 9.63 us: body(): pl.pallas_call(interaction_kernel, out_shape=jax.ShapeDtypeStruct((8, 128...]
    reshape x2 -> x0, local copies, waits for them, and re-layouts: 18.1 us -> none  [the longest x1 17.3 us: first_two(): section_one.astype(jnp.bfloat16)]
    ppermute x0 -> x16, starting transfers between devices: none -> 17.8 us  [the longest x3 5.96 us: body(): lax.ppermute(own_row, 'clus', ring(4, step))]
    ppermute x0 -> x16, waiting for transfers between devices: none -> 15.2 us  [the longest x1 6.71 us: body(): opp_other1 = lax.ppermute(opp1, 'trip', grid_shift(0, 1))]
  transfers between devices with their start and end apart: 4 -> 18, of which waited for: 3 -> 6; matrix products, arithmetic and copies ran while one was open for 3% -> 19% of each run, Pallas kernels for 0% -> 3%
where the time goes in v1:
time: 125 us; the launch traced here: 123 us
  starting transfers between devices  35 us (28%)
  waiting for transfers between devices  25.6 us (20%)
  Pallas kernels  18.5 us (15%)
  local copies, waits for them, and re-layouts  18.1 us (14%)
  blocking collectives  14 us (11%)
  other arithmetic  9.95 us (8%)
  between operations  1.71 us (1%)
    all_to_all x1, blocking collectives, body(): received = lax.all_to_all(partial[:, None, :], 'trip', 0, 0, tiled=True)  14 us
    all_to_all x1, starting transfers between devices, body(): arrived = lax.all_to_all(chosen, 'trip', 0, 0, tiled=True)  11.2 us
    all_to_all x1, waiting for transfers between devices, body(): arrived = lax.all_to_all(chosen, 'trip', 0, 0, tiled=True)  10.5 us
    pallas_call x1, Pallas kernels, body(): pl.pallas_call(interaction_kernel, out_shape=jax.ShapeDtypeStruct((8, 128...  9.63 us
    ppermute x1, waiting for transfers between devices, body(): opp_other1 = lax.ppermute(opp1, 'trip', grid_shift(0, 1))  6.71 us
    all_to_all x1, starting transfers between devices, body(): members = lax.all_to_all(outgoing, ('clus', 'mode'), 0, 0, tiled=True)  5.99 us
    ppermute x3, starting transfers between devices, body(): lax.ppermute(own_row, 'clus', ring(4, step))  5.96 us
    unnamed x28, local copies, waits for them, and re-layouts  5.72 us
  transfers between devices with their start and end apart: 18, of which 6 were waited for; matrix products, arithmetic and copies ran while one was open for 19% of the time, Pallas kernels for 3%

profile of v1, /device:TPU:2, one launch (start us, length us, event | category | flops | bytes accessed | tf_op | source)
XLA Modules:
  0.0 122.9 jit_solution(5532945323465927360)
XLA Ops:
  0.7 2.2 %copy.74.own_ref = bf16[2,45,8100]{2,1,0:T(8,128)(2,1)S(1)} copy(bf16[2,45,8100]{2,0,1:T(2,128)(2,1)} %param.11) | data formatting | bytes 2916000 | tf_op args[0]
  3.0 1.1 copy-done.1
  4.1 2.3 %collective-permute-start.3 = (bf16[45,4004]{1,0:T(8,128)(2,1)S(1)}, bf16[45,4004]{1,0:T(8,128)(2,1)S(1)}, u32[]{:S(2)}, u32[]{:S(2)}) collective-permute-start(bf16[45,4004]{1,0:T(8,128)(2,1)S(1)} %slice.108), channel_id=1, source_target_pairs={{0,192},{64,0},{128,64},{192,128},{1,193},{65,1},{129,65},{193,129... | collective-permute-start | bytes 1081088 | tf_op jit(solution)/shard_map/force_neighbours/ppermute | solution.py:222
  6.4 0.8 slice.107
  7.2 1.2 %collective-permute-start = (bf16[45,4096]{1,0:T(8,128)(2,1)}, bf16[45,4096]{1,0:T(8,128)(2,1)S(1)}, u32[]{:S(2)}, u32[]{:S(2)}) collective-permute-start(bf16[45,4096]{1,0:T(8,128)(2,1)} %slice.107), channel_id=1, source_target_pairs={{0,64},{64,128},{128,192},{192,0},{1,65},{65,129},{129,193},{193,1... | collective-permute-start | bytes 1105928 | tf_op jit(solution)/shard_map/force_neighbours/ppermute | solution.py:219
  8.5 0.8 collective-permute-start.2
  9.5 0.7 fusion.1.share_ref
  10.2 1.6 %records.2 = bf16[32,12,180]{2,1,0:T(8,128)(2,1)} custom-call(s32[1,32]{1,0:T(1,128)} %rows_ref.1, bf16[8,12,180]{2,1,0:T(8,128)(2,1)} %fusion.1.share_ref), custom_call_target="tpu_custom_call" | custom-call | tf_op jit(solution)/shard_map/records/pallas_call | solution.py:240
  11.8 11.2 %all-to-all-start = ((bf16[32,12,180]{2,1,0:T(8,128)(2,1)}), bf16[32,12,180]{2,1,0:T(8,128)(2,1)S(1)}, u32[]{:S(2)}, u32[]{:S(2)}) async-start(bf16[32,12,180]{2,1,0:T(8,128)(2,1)} %records.2), calls=%async_computation | async-start | bytes 524288 | tf_op jit(solution)/shard_map/records/all_to_all | solution.py:246
  23.3 0.6 pad.47.phase_ref
  23.9 10.5 %all-to-all-done.arrived_ref = bf16[32,12,180]{2,1,0:T(8,128)(2,1)S(1)} async-done(((bf16[32,12,180]{2,1,0:T(8,128)(2,1)}), bf16[32,12,180]{2,1,0:T(8,128)(2,1)S(1)}, u32[]{:S(2)}, u32[]{:S(2)}) %all-to-all-start) | async-done | bytes 138272 | tf_op jit(solution)/shard_map/records/all_to_all | solution.py:246
  34.3 0.7 copy-done.2
  35.1 1.7 %records.3 = bf16[8,4,12,180]{3,2,1,0:T(8,128)(2,1)} custom-call(s32[4,3]{1,0:T(4,128)} %table_ref.1, bf16[32,12,180]{2,1,0:T(8,128)(2,1)} %copy-done.2, bf16[4,12,180]{2,1,0:T(8,128)(2,1)} %pad.47.phase_ref), custom_call_target="tpu_custom_call" | custom-call | tf_op jit(solution)/shard_map/records/pallas_call | solution.py:251
  36.7 1.7 %copy.66 = bf16[8,4,12,180]{3,1,2,0:T(4,128)(2,1)} copy(bf16[8,4,12,180]{3,2,1,0:T(8,128)(2,1)} %records.3) | data formatting | bytes 276480 | tf_op jit(solution)/shard_map/records/pallas_call | solution.py:251
  38.5 6.0 %all-to-all-start.1 = ((bf16[8,4,12,180]{3,1,2,0:T(4,128)(2,1)}), bf16[8,4,12,180]{3,1,2,0:T(4,128)(2,1)S(1)}, u32[]{:S(2)}, u32[]{:S(2)}) async-start(bf16[8,4,12,180]{3,1,2,0:T(4,128)(2,1)} %copy.66), calls=%async_computation.1 | async-start | bytes 393216 | tf_op jit(solution)/shard_map/records/all_to_all | solution.py:257
  44.6 0.6 dynamic_slice.52
  45.8 0.6 fusion.15
  46.5 1.3 %iota_compare_fusion.2 = (pred[32]{0:T(512)(128)(4,1)S(1)}, pred[32]{0:T(512)(128)(4,1)S(1)}) fusion(s32[]{:T(128)} %bitcast.32, s32[]{:T(128)} %bitcast), kind=kLoop, calls=%fused_computation.51 | loop fusion | flops 64 | bytes 72 | tf_op jit(solution)/shard_map/collect/eq | solution.py:339
  48.4 2.0 %collective-permute-start.5 = (bf16[45,4004]{1,0:T(8,128)(2,1)S(1)}, bf16[45,4004]{1,0:T(8,128)(2,1)S(1)}, u32[]{:S(2)}, u32[]{:S(2)}) collective-permute-start(bf16[45,4004]{1,0:T(8,128)(2,1)S(1)} %collective-permute-done.1.refs_1_), channel_id=1, source_target_pairs={{0,48},{2,50},{4,52},{6,54},{8,56},{10,58},{12,60},{14,62},{16,0},... | collective-permute-start | bytes 1081088 | tf_op jit(solution)/shard_map/force_second/ppermute | solution.py:228
  50.4 1.9 %collective-permute-start.8 = (bf16[45,4096]{1,0:T(8,128)(2,1)S(1)}, bf16[45,4096]{1,0:T(8,128)(2,1)S(1)}, u32[]{:S(2)}, u32[]{:S(2)}) collective-permute-start(bf16[45,4096]{1,0:T(8,128)(2,1)S(1)} %collective-permute-done.refs_0_), channel_id=1, source_target_pairs={{0,64},{64,128},{128,192},{192,0},{1,65},{65,129},{129,193},{193,1... | collective-permute-start | bytes 1105928 | tf_op jit(solution)/shard_map/force_second/ppermute | solution.py:224
  53.0 0.6 pad.56
  54.1 0.6 pad.58
  55.2 0.9 fusion.12
  56.3 2.8 %collective-permute-done.9.refs_9_ = bf16[45,4004]{1,0:T(8,128)(2,1)S(1)} collective-permute-done((bf16[45,4004]{1,0:T(8,128)(2,1)S(1)}, bf16[45,4004]{1,0:T(8,128)(2,1)S(1)}, u32[]{:S(2)}, u32[]{:S(2)}) %collective-permute-start.9) | collective-permute-done | bytes 360392 | tf_op jit(solution)/shard_map/force_second/ppermute | solution.py:225
  59.0 1.8 %collective-permute-start.6 = (bf16[45,4096]{1,0:T(8,128)(2,1)S(1)}, bf16[45,4096]{1,0:T(8,128)(2,1)}, u32[]{:S(2)}, u32[]{:S(2)}) collective-permute-start(bf16[45,4096]{1,0:T(8,128)(2,1)S(1)} %collective-permute-done.2.refs_2_), channel_id=1, source_target_pairs={{0,2},{2,4},{4,6},{6,8},{8,10},{10,12},{12,14},{14,0},{16,18},{18,... | collective-permute-start | bytes 1105928 | tf_op jit(solution)/shard_map/force_second/ppermute | solution.py:227
  60.8 0.9 collective-permute-start.11
  62.3 0.7 fusion.13
  63.0 0.6 pad.54
  63.6 1.6 %copy.86 = bf16[1,90,180]{1,2,0:T(8,128)(2,1)} copy(bf16[1,90,180]{2,0,1:T(2,128)(2,1)} %get-tuple-element.9) | data formatting | bytes 64800
  65.2 1.4 %slice_bitcast_fusion = (bf16[90,90]{1,0:T(8,128)(2,1)}, bf16[90,90]{1,0:T(8,128)(2,1)S(1)}) fusion(bf16[90,180]{0,1:T(8,128)(2,1)} %bitcast.68), kind=kLoop, calls=%fused_computation.15 | loop fusion | bytes 64800 | tf_op jit(solution)/shard_map/operands/transpose | solution.py:272
  66.6 0.6 pad.52
  67.2 2.2 %collective-permute-done.4.refs_4_ = bf16[45,4096]{1,0:T(8,128)(2,1)S(1)} collective-permute-done((bf16[45,4096]{1,0:T(8,128)(2,1)S(1)}, bf16[45,4096]{1,0:T(8,128)(2,1)S(1)}, u32[]{:S(2)}, u32[]{:S(2)}) %collective-permute-start.4) | collective-permute-done | bytes 368672 | tf_op jit(solution)/shard_map/force_second/ppermute | solution.py:226
  69.5 2.9 %collective-permute-done.6.refs_6_ = bf16[45,4096]{1,0:T(8,128)(2,1)} collective-permute-done((bf16[45,4096]{1,0:T(8,128)(2,1)S(1)}, bf16[45,4096]{1,0:T(8,128)(2,1)}, u32[]{:S(2)}, u32[]{:S(2)}) %collective-permute-start.6) | collective-permute-done | bytes 368672 | tf_op jit(solution)/shard_map/force_second/ppermute | solution.py:227
  72.4 6.7 %collective-permute-done.11.refs_11_ = bf16[45,4004]{1,0:T(8,128)(2,1)} collective-permute-done((bf16[45,4004]{1,0:T(8,128)(2,1)S(1)}, bf16[45,4004]{1,0:T(8,128)(2,1)}, u32[]{:S(2)}, u32[]{:S(2)}) %collective-permute-start.11) | collective-permute-done | bytes 360392 | tf_op jit(solution)/shard_map/force_third_step/ppermute | solution.py:232
  79.1 5.6 %transform.1.mine_ref = bf16[2,48,8100]{2,1,0:T(8,128)(2,1)} custom-call(s32[2]{0:T(128)S(1)} %pad_add_fusion.where_ref, f32[16]{0:T(128)S(1)} %reshape.406.trig_ref, bf16[2,45,8100]{2,1,0:T(8,128)(2,1)} %copy-done.1, bf16[45,4096]{1,0:T(8,128)(2,1)S(1)} %collective-permute-done.refs_0_, bf16[45,4004]{1,0:T(8,128)(2,1)S(1)} %collective-permute-done.1.refs_1_, ...), custom_call_target="tpu_custom_call" | custom-call | tf_op jit(solution)/shard_map/transform/pallas_call | solution.py:292
  85.3 0.7 broadcast_divide_fusion
  86.1 0.8 pad_negate_fusion.3
  87.0 0.8 fusion.14
  87.7 0.9 maximum_maximum_fusion.1.middle_ref
  88.7 0.8 maximum_maximum_fusion.last_ref
  89.5 0.8 broadcast_add_fusion
  90.3 0.8 broadcast_add_fusion.1
  91.1 9.6 %interaction.1 = f32[8,128]{1,0:T(8,128)S(1)} custom-call(f32[2,45]{1,0:T(2,128)S(1)} %pad_maximum_fusion.2.scalars_ref, bf16[96,192]{1,0:T(8,128)(2,1)S(1)} %maximum_maximum_fusion.2.lead_ref, bf16[192,192]{1,0:T(8,128)(2,1)S(1)} %maximum_maximum_fusion.1.middle_ref, bf16[256,256]{1,0:T(8,128)(2,1)S(1)} %maximum_maximum_fusion.last_ref, ...), custom_call_target="tpu_custom_call" | custom-call | tf_op jit(solution)/shard_map/interaction/pallas_call | solution.py:317
  100.8 1.5 %collective-permute-start.13 = (f32[1,128]{1,0:T(1,128)S(1)}, f32[1,128]{1,0:T(1,128)S(1)}, u32[]{:S(2)}, u32[]{:S(2)}) collective-permute-start(f32[1,128]{1,0:T(1,128)S(1)} %get-tuple-element.28), channel_id=1, source_target_pairs={{0,64},{64,128},{128,192},{192,0},{1,65},{65,129},{129,193},{193,1... | collective-permute-start | bytes 1544 | tf_op jit(solution)/shard_map/collect/ppermute | solution.py:334
  102.3 1.9 %collective-permute-start.14 = (f32[1,128]{1,0:T(1,128)S(1)}, f32[1,128]{1,0:T(1,128)S(1)}, u32[]{:S(2)}, u32[]{:S(2)}) collective-permute-start(f32[1,128]{1,0:T(1,128)S(1)} %get-tuple-element.28), channel_id=1, source_target_pairs={{0,128},{64,192},{128,0},{192,64},{1,129},{65,193},{129,1},{193,65... | collective-permute-start | bytes 1544 | tf_op jit(solution)/shard_map/collect/ppermute | solution.py:334
  104.2 2.6 %collective-permute-start.15 = (f32[1,128]{1,0:T(1,128)S(1)}, f32[1,128]{1,0:T(1,128)S(1)}, u32[]{:S(2)}, u32[]{:S(2)}) collective-permute-start(f32[1,128]{1,0:T(1,128)S(1)} %get-tuple-element.28), channel_id=1, source_target_pairs={{0,192},{64,0},{128,64},{192,128},{1,193},{65,1},{129,65},{193,129... | collective-permute-start | bytes 1544 | tf_op jit(solution)/shard_map/collect/ppermute | solution.py:334
  106.7 1.2 iota_compare_fusion
  108.2 14.0 %all_to_all.15 = f32[32,1,128]{2,1,0:T(1,128)S(1)} all-to-all(f32[32,1,128]{2,1,0:T(1,128)S(1)} %fusion.4), channel_id=1, replica_groups=mesh['clus'=4,'trip'=32,'mode'=2] {'trip'}, dimensions={0} | all-to-all | bytes 32768 | tf_op jit(solution)/shard_map/collect/all_to_all | solution.py:340
  (77 shorter events, 5.4 us)
Async XLA Ops:
  2.9 1.2 copy-start.1
  2.9 6.4 %copy-start.3 = (bf16[8,90,180]{2,0,1:T(8,128)(2,1)S(1)}, bf16[8,90,180]{2,0,1:T(8,128)(2,1)}, u32[]{:S(2)}) copy-start(bf16[8,90,180]{2,0,1:T(8,128)(2,1)} %param.13) | copy-start | bytes 777604
  2.9 6.4 %copy-start.6 = (bf16[8,90]{1,0:T(8,128)(2,1)S(1)}, bf16[8,90]{1,0:T(8,128)(2,1)}, u32[]{:S(2)}) copy-start(bf16[8,90]{1,0:T(8,128)(2,1)} %param.15) | copy-start | bytes 4324
  2.9 6.4 %copy-start.7 = (bf16[8,90]{1,0:T(8,128)(2,1)S(1)}, bf16[8,90]{1,0:T(8,128)(2,1)}, u32[]{:S(2)}) copy-start(bf16[8,90]{1,0:T(8,128)(2,1)} %param.14) | copy-start | bytes 4324
  4.1 19.0 %copy-start.10 = (bf16[2,4]{1,0:T(2,128)(2,1)S(1)}, bf16[2,4]{1,0:T(2,128)(2,1)}, u32[]{:S(2)}) copy-start(bf16[2,4]{1,0:T(2,128)(2,1)} %param.12) | copy-start | bytes 52
  4.1 43.7 %collective-permute-start.3 = (bf16[45,4004]{1,0:T(8,128)(2,1)S(1)}, bf16[45,4004]{1,0:T(8,128)(2,1)S(1)}, u32[]{:S(2)}, u32[]{:S(2)}) collective-permute-start(bf16[45,4004]{1,0:T(8,128)(2,1)S(1)} %slice.108), channel_id=1, source_target_pairs={{0,192},{64,0},{128,64},{192,128},{1,193},{65,1},{129,65},{193,129... | collective-permute-start | bytes 1081088 | tf_op jit(solution)/shard_map/force_neighbours/ppermute | solution.py:222
  6.4 42.0 %collective-permute-start.1 = (bf16[45,4004]{1,0:T(8,128)(2,1)S(1)}, bf16[45,4004]{1,0:T(8,128)(2,1)S(1)}, u32[]{:S(2)}, u32[]{:S(2)}) collective-permute-start(bf16[45,4004]{1,0:T(8,128)(2,1)S(1)} %slice.108), channel_id=1, source_target_pairs={{0,64},{64,128},{128,192},{192,0},{1,65},{65,129},{129,193},{193,1... | collective-permute-start | bytes 1081088 | tf_op jit(solution)/shard_map/force_neighbours/ppermute | solution.py:221
  7.2 43.2 %collective-permute-start = (bf16[45,4096]{1,0:T(8,128)(2,1)}, bf16[45,4096]{1,0:T(8,128)(2,1)S(1)}, u32[]{:S(2)}, u32[]{:S(2)}) collective-permute-start(bf16[45,4096]{1,0:T(8,128)(2,1)} %slice.107), channel_id=1, source_target_pairs={{0,64},{64,128},{128,192},{192,0},{1,65},{65,129},{129,193},{193,1... | collective-permute-start | bytes 1105928 | tf_op jit(solution)/shard_map/force_neighbours/ppermute | solution.py:219
  8.5 47.7 %collective-permute-start.2 = (bf16[45,4096]{1,0:T(8,128)(2,1)}, bf16[45,4096]{1,0:T(8,128)(2,1)S(1)}, u32[]{:S(2)}, u32[]{:S(2)}) collective-permute-start(bf16[45,4096]{1,0:T(8,128)(2,1)} %slice.107), channel_id=1, source_target_pairs={{0,192},{64,0},{128,64},{192,128},{1,193},{65,1},{129,65},{193,129... | collective-permute-start | bytes 1105928 | tf_op jit(solution)/shard_map/force_neighbours/ppermute | solution.py:220
  9.3 35.2 %copy-start.11 = (s32[4]{0:T(128)S(1)}, s32[4]{0:T(128)}, u32[]{:S(2)}) copy-start(s32[4]{0:T(128)} %param.19) | copy-start | bytes 52
  9.3 36.5 %copy-start.5 = (s32[4]{0:T(128)S(1)}, s32[4]{0:T(128)}, u32[]{:S(2)}) copy-start(s32[4]{0:T(128)} %param.18) | copy-start | bytes 52
  11.8 22.5 %all-to-all-start = ((bf16[32,12,180]{2,1,0:T(8,128)(2,1)}), bf16[32,12,180]{2,1,0:T(8,128)(2,1)S(1)}, u32[]{:S(2)}, u32[]{:S(2)}) async-start(bf16[32,12,180]{2,1,0:T(8,128)(2,1)} %records.2), calls=%async_computation | async-start | bytes 524288 | tf_op jit(solution)/shard_map/records/all_to_all | solution.py:246
  34.3 0.7 copy-start.2
  38.5 13.8 %all-to-all-start.1 = ((bf16[8,4,12,180]{3,1,2,0:T(4,128)(2,1)}), bf16[8,4,12,180]{3,1,2,0:T(4,128)(2,1)S(1)}, u32[]{:S(2)}, u32[]{:S(2)}) async-start(bf16[8,4,12,180]{3,1,2,0:T(4,128)(2,1)} %copy.66), calls=%async_computation.1 | async-start | bytes 393216 | tf_op jit(solution)/shard_map/records/all_to_all | solution.py:257
  47.8 11.2 %collective-permute-start.9 = (bf16[45,4004]{1,0:T(8,128)(2,1)S(1)}, bf16[45,4004]{1,0:T(8,128)(2,1)S(1)}, u32[]{:S(2)}, u32[]{:S(2)}) collective-permute-start(bf16[45,4004]{1,0:T(8,128)(2,1)S(1)} %collective-permute-done.3.refs_3_), channel_id=1, source_target_pairs={{0,192},{64,0},{128,64},{192,128},{1,193},{65,1},{129,65},{193,129... | collective-permute-start | bytes 1081088 | tf_op jit(solution)/shard_map/force_second/ppermute | solution.py:225
  48.0 19.3 %collective-permute-start.7 = (bf16[45,4004]{1,0:T(8,128)(2,1)S(1)}, bf16[45,4004]{1,0:T(8,128)(2,1)S(1)}, u32[]{:S(2)}, u32[]{:S(2)}) collective-permute-start(bf16[45,4004]{1,0:T(8,128)(2,1)S(1)} %collective-permute-done.3.refs_3_), channel_id=1, source_target_pairs={{0,14},{2,0},{4,2},{6,4},{8,6},{10,8},{12,10},{14,12},{16,30},{18,... | collective-permute-start | bytes 1081088 | tf_op jit(solution)/shard_map/force_second/ppermute | solution.py:229
  48.4 12.4 %collective-permute-start.5 = (bf16[45,4004]{1,0:T(8,128)(2,1)S(1)}, bf16[45,4004]{1,0:T(8,128)(2,1)S(1)}, u32[]{:S(2)}, u32[]{:S(2)}) collective-permute-start(bf16[45,4004]{1,0:T(8,128)(2,1)S(1)} %collective-permute-done.1.refs_1_), channel_id=1, source_target_pairs={{0,48},{2,50},{4,52},{6,54},{8,56},{10,58},{12,60},{14,62},{16,0},... | collective-permute-start | bytes 1081088 | tf_op jit(solution)/shard_map/force_second/ppermute | solution.py:228
  50.4 11.7 %collective-permute-start.8 = (bf16[45,4096]{1,0:T(8,128)(2,1)S(1)}, bf16[45,4096]{1,0:T(8,128)(2,1)S(1)}, u32[]{:S(2)}, u32[]{:S(2)}) collective-permute-start(bf16[45,4096]{1,0:T(8,128)(2,1)S(1)} %collective-permute-done.refs_0_), channel_id=1, source_target_pairs={{0,64},{64,128},{128,192},{192,0},{1,65},{65,129},{129,193},{193,1... | collective-permute-start | bytes 1105928 | tf_op jit(solution)/shard_map/force_second/ppermute | solution.py:224
  56.1 13.3 %collective-permute-start.4 = (bf16[45,4096]{1,0:T(8,128)(2,1)S(1)}, bf16[45,4096]{1,0:T(8,128)(2,1)S(1)}, u32[]{:S(2)}, u32[]{:S(2)}) collective-permute-start(bf16[45,4096]{1,0:T(8,128)(2,1)S(1)} %collective-permute-done.refs_0_), channel_id=1, source_target_pairs={{0,16},{2,18},{4,20},{6,22},{8,24},{10,26},{12,28},{14,30},{16,32}... | collective-permute-start | bytes 1105928 | tf_op jit(solution)/shard_map/force_second/ppermute | solution.py:226
  59.0 13.4 %collective-permute-start.6 = (bf16[45,4096]{1,0:T(8,128)(2,1)S(1)}, bf16[45,4096]{1,0:T(8,128)(2,1)}, u32[]{:S(2)}, u32[]{:S(2)}) collective-permute-start(bf16[45,4096]{1,0:T(8,128)(2,1)S(1)} %collective-permute-done.2.refs_2_), channel_id=1, source_target_pairs={{0,2},{2,4},{4,6},{6,8},{8,10},{10,12},{12,14},{14,0},{16,18},{18,... | collective-permute-start | bytes 1105928 | tf_op jit(solution)/shard_map/force_second/ppermute | solution.py:227
  60.8 18.3 %collective-permute-start.11 = (bf16[45,4004]{1,0:T(8,128)(2,1)S(1)}, bf16[45,4004]{1,0:T(8,128)(2,1)}, u32[]{:S(2)}, u32[]{:S(2)}) collective-permute-start(bf16[45,4004]{1,0:T(8,128)(2,1)S(1)} %collective-permute-done.9.refs_9_), channel_id=1, source_target_pairs={{0,2},{2,4},{4,6},{6,8},{8,10},{10,12},{12,14},{14,0},{16,18},{18,... | collective-permute-start | bytes 1081088 | tf_op jit(solution)/shard_map/force_third_step/ppermute | solution.py:232
  62.1 17.0 %collective-permute-start.10 = (bf16[45,4096]{1,0:T(8,128)(2,1)S(1)}, bf16[45,4096]{1,0:T(8,128)(2,1)}, u32[]{:S(2)}, u32[]{:S(2)}) collective-permute-start(bf16[45,4096]{1,0:T(8,128)(2,1)S(1)} %collective-permute-done.8.refs_8_), channel_id=1, source_target_pairs={{0,16},{2,18},{4,20},{6,22},{8,24},{10,26},{12,28},{14,30},{16,32}... | collective-permute-start | bytes 1105928 | tf_op jit(solution)/shard_map/force_third_step/ppermute | solution.py:231
  67.2 17.5 %copy-start.4 = (bf16[1,90,180]{2,0,1:T(2,128)(2,1)S(1)}, bf16[1,90,180]{2,0,1:T(2,128)(2,1)}, u32[]{:S(2)}) copy-start(bf16[1,90,180]{2,0,1:T(2,128)(2,1)} %get-tuple-element.10) | copy-start | bytes 97204
  84.7 6.4 %copy-start = (bf16[2,48,8100]{2,1,0:T(8,128)(2,1)S(1)}, bf16[2,48,8100]{2,1,0:T(8,128)(2,1)}, u32[]{:S(2)}) copy-start(bf16[2,48,8100]{2,1,0:T(8,128)(2,1)} %transform.1.mine_ref) | copy-start | bytes 4665604
  84.7 6.4 %collective-permute-start.12 = (bf16[2,48,8100]{2,1,0:T(8,128)(2,1)}, bf16[2,48,8100]{2,1,0:T(8,128)(2,1)S(1)}, u32[]{:S(2)}, u32[]{:S(2)}) collective-permute-start(bf16[2,48,8100]{2,1,0:T(8,128)(2,1)} %transform.1.mine_ref), channel_id=1, source_target_pairs={{0,1},{1,0},{2,3},{3,2},{4,5},{5,4},{6,7},{7,6},{8,9},{9,8},{10,11... | collective-permute-start | bytes 4665608 | tf_op jit(solution)/shard_map/transform/ppermute | solution.py:315
  91.1 31.2 %copy-start.8 = (f32[1,45]{1,0:T(1,128)S(1)}, f32[1,45]{1,0:T(1,128)}, u32[]{:S(2)}) copy-start(f32[1,45]{1,0:T(1,128)} %param.20) | copy-start | bytes 544
  91.1 31.2 %copy-start.9 = (f32[1,45]{1,0:T(1,128)S(1)}, f32[1,45]{1,0:T(1,128)}, u32[]{:S(2)}) copy-start(f32[1,45]{1,0:T(1,128)} %param.21) | copy-start | bytes 544
  100.8 7.2 %collective-permute-start.13 = (f32[1,128]{1,0:T(1,128)S(1)}, f32[1,128]{1,0:T(1,128)S(1)}, u32[]{:S(2)}, u32[]{:S(2)}) collective-permute-start(f32[1,128]{1,0:T(1,128)S(1)} %get-tuple-element.28), channel_id=1, source_target_pairs={{0,64},{64,128},{128,192},{192,0},{1,65},{65,129},{129,193},{193,1... | collective-permute-start | bytes 1544 | tf_op jit(solution)/shard_map/collect/ppermute | solution.py:334
  102.3 5.7 %collective-permute-start.14 = (f32[1,128]{1,0:T(1,128)S(1)}, f32[1,128]{1,0:T(1,128)S(1)}, u32[]{:S(2)}, u32[]{:S(2)}) collective-permute-start(f32[1,128]{1,0:T(1,128)S(1)} %get-tuple-element.28), channel_id=1, source_target_pairs={{0,128},{64,192},{128,0},{192,64},{1,129},{65,193},{129,1},{193,65... | collective-permute-start | bytes 1544 | tf_op jit(solution)/shard_map/collect/ppermute | solution.py:334
  104.2 3.9 %collective-permute-start.15 = (f32[1,128]{1,0:T(1,128)S(1)}, f32[1,128]{1,0:T(1,128)S(1)}, u32[]{:S(2)}, u32[]{:S(2)}) collective-permute-start(f32[1,128]{1,0:T(1,128)S(1)} %get-tuple-element.28), channel_id=1, source_target_pairs={{0,192},{64,0},{128,64},{192,128},{1,193},{65,1},{129,65},{193,129... | collective-permute-start | bytes 1544 | tf_op jit(solution)/shard_map/collect/ppermute | solution.py:334

commit v2 on v1

v2 whole, which is shorter than its diff:
```python
import jax
import jax.numpy as jnp
from jax import lax
from jax.experimental import pallas as pl
from jax.experimental.pallas import tpu as pltpu
from jax.sharding import PartitionSpec as P

smearing = 0.3
SPLIT = 4096
LANES = 512
RING_Y = 4
RING_Z = 8
PAD = 48
WIDE = 96
PIECES = ((0, 0), (0, 1), (3, 0), (1, 0), (3, 1), (1, 1), (2, 0), (2, 1))


def send_kernel(rows_ref, share_ref, out_ref):
    for target in range(out_ref.shape[0]):
        out_ref[target] = share_ref[rows_ref[0, target]]


def pick_kernel(rank_ref, table_ref, arrived_ref, phase_ref, *out_refs):
    for offset, out_ref in enumerate(out_refs):
        triplet = (rank_ref[0] + offset) & 3
        for member in range(3):
            out_ref[member] = arrived_ref[table_ref[triplet, member]]
        out_ref[3] = phase_ref[triplet]


def operand_kernel(where_ref, *refs):
    members, refs = refs[:8], refs[8:]
    lead_ref, middle_ref, last_ref, tables_ref, scalars_ref, record = refs
    rank, mode, color, mult = where_ref[0], where_ref[1], where_ref[2], where_ref[3]
    f32 = jnp.float32
    record[...] = jnp.zeros(record.shape, f32)
    for source in range(8):
        block = 2 * ((rank - source // 2) & 3) + (mode if source % 2 == 0 else 1 - mode)
        rows = pl.ds(pl.multiple_of(16 * block, 16), 12)
        for member in range(3):
            values = members[source][member].astype(f32)
            record[member, rows, 0:90] = values[:, 0:90]
            record[member, rows, 128:218] = values[:, 90:180]
    records = [
        jnp.concatenate([record[member, 16 * j : 16 * j + 12, :] for j in range(8)], axis=0)
        for member in range(3)
    ]
    first = mode == 0

    def transposed(member):
        return records[member][:, 0:128].T, records[member][:, 128:256].T

    def halves(array):
        low, high = array[0:PAD], array[45 : 45 + PAD]
        return jnp.where(first, low, high), jnp.where(first, high, low)

    def own_columns(array):
        picked = jnp.where(first, array[:, 0:PAD], array[:, 45 : 45 + PAD])
        column = lax.broadcasted_iota(jnp.int32, picked.shape, 1)
        return jnp.where(column < 45, picked, 0.0)

    lead_r, lead_i = transposed(0)
    real_own, real_far = halves(own_columns(lead_r))
    imag_own, imag_far = halves(own_columns(lead_i))
    columns = []
    for offset, which in PIECES:
        trig = members[2 * ((4 - offset) % 4)][3].astype(f32)[0:1]
        pair = [trig[:, 0:1], trig[:, 1:2], trig[:, 2:3], trig[:, 3:4]]
        if offset == 0:
            cosine, sine = pair[2 * which], pair[2 * which + 1]
        else:
            early = color == which
            cosine = jnp.where(early, pair[0], pair[2])
            sine = jnp.where(early, pair[1], pair[3])
        columns.append(
            jnp.concatenate(
                [
                    cosine * real_own - sine * imag_own,
                    cosine * imag_own + sine * real_own,
                    cosine * real_far - sine * imag_far,
                    cosine * imag_far + sine * real_far,
                ],
                axis=0,
            )
        )
    lead_ref[...] = jnp.concatenate(columns, axis=1).astype(lead_ref.dtype)

    mid_r, mid_i = transposed(1)
    within = lax.broadcasted_iota(jnp.int32, (WIDE, WIDE), 1) < 90
    real = jnp.where(within, mid_r[0:WIDE], 0.0)
    imag = jnp.where(within, mid_i[0:WIDE], 0.0)
    middle_ref[...] = jnp.concatenate(
        [jnp.concatenate([real, -imag], axis=1), jnp.concatenate([imag, real], axis=1)], axis=0
    ).astype(middle_ref.dtype)

    last_r, last_i = records[2][:, 0:128], records[2][:, 128:256]
    within = lax.broadcasted_iota(jnp.int32, (WIDE, 128), 0) < 90
    real = jnp.where(within, last_r, 0.0)
    imag = jnp.where(within, last_i, 0.0)
    zeros = jnp.zeros((32, 256), f32)
    last_ref[...] = jnp.concatenate(
        [
            jnp.concatenate([real, imag], axis=1),
            zeros,
            jnp.concatenate([-imag, real], axis=1),
            zeros,
        ],
        axis=0,
    ).astype(last_ref.dtype)

    row = lax.broadcasted_iota(jnp.int32, (WIDE, 128), 0)
    column = lax.broadcasted_iota(jnp.int32, (WIDE, 128), 1)
    one = jnp.where(row < 90, jnp.broadcast_to(mid_r[0:WIDE, 90:91], (WIDE, 128)), 1.0)
    two = jnp.where(column < 90, jnp.broadcast_to(last_r[90:91, :], (WIDE, 128)), 1.0)
    tables_ref[0] = one + two
    tables_ref[1] = one - two
    tables_ref[2] = 1.0 / (one * two)
    tables_ref[3] = jnp.broadcast_to(mid_i[0:WIDE, 90:91], (WIDE, 128)) + jnp.broadcast_to(
        last_i[90:91, :], (WIDE, 128)
    )
    zero = halves(lead_r[:, 90:91])[0]
    zero = jnp.where(lax.broadcasted_iota(jnp.int32, (PAD, 1), 0) < 45, zero, 1.0)
    scalars_ref[0] = jnp.broadcast_to(zero, (PAD, 128))
    scalars_ref[1] = jnp.broadcast_to(mult.astype(f32) / zero, (PAD, 128))


def contract_kernel(lead_ref, own_ref, *refs):
    pieces, mine_ref, far_ref = refs[:-2], refs[-2], refs[-1]
    length = mine_ref.shape[1]
    begin = 0 if length == SPLIT else SPLIT

    def chunk(start, width):
        whole = start + begin
        if not isinstance(start, int):
            whole = pl.multiple_of(whole, LANES)
            start = pl.multiple_of(start, LANES)
        values = [own_ref[r, :, pl.ds(whole, width)] for r in range(2)]
        values += [piece[:, pl.ds(whole, width)] for piece in pieces[:2]]
        values += [piece[:, pl.ds(start, width)] for piece in pieces[2:]]
        rows = [jnp.pad(v, ((0, PAD - 45), (0, 0))) for v in values]
        product = jnp.dot(
            lead_ref[...], jnp.concatenate(rows, axis=0), preferred_element_type=jnp.float32
        ).astype(mine_ref.dtype)
        mine_ref[:, pl.ds(start, width)] = product[0 : 2 * PAD]
        far_ref[:, pl.ds(start, width)] = product[2 * PAD :]

    count = length // LANES

    @pl.loop(0, count)
    def _(i):
        chunk(i * LANES, LANES)

    if length % LANES:
        chunk(count * LANES, length % LANES)


def interaction_kernel(
    scalars_ref,
    middle_ref,
    last_ref,
    tables_ref,
    mine0_ref,
    other0_ref,
    mine1_ref,
    other1_ref,
    out_ref,
    flat,
    windows,
    mid_real,
    mid_imag,
    rate_acc,
    couple_acc,
):
    flat[:, 8064:8320] = jnp.zeros((2 * PAD, 256), flat.dtype)
    for begin, mine, other in ((0, mine0_ref, other0_ref), (SPLIT, mine1_ref, other1_ref)):
        for start in range(0, mine.shape[1], LANES):
            width = min(LANES, mine.shape[1] - start)
            cols = pl.ds(start, width)
            both = mine[:, cols].astype(jnp.float32) + other[:, cols].astype(jnp.float32)
            flat[:, begin + start : begin + start + width] = both.astype(flat.dtype)
    for b in range(90):
        tile, shift = divmod(90 * b, 128)
        pair = flat[:, tile * 128 : tile * 128 + 256]
        window = pair[:, shift : shift + 128]
        windows[b * PAD : (b + 1) * PAD, 0:128] = window[0:PAD]
        windows[b * PAD : (b + 1) * PAD, 128:256] = window[PAD:]
    zeros = jnp.zeros((PAD, 128), jnp.float32)
    for b in range(90, WIDE):
        mid_real[pl.ds(b, PAD, stride=WIDE), :] = zeros
        mid_imag[pl.ds(b, PAD, stride=WIDE), :] = zeros
    for group in range(9):
        product = jnp.dot(
            windows[group * 480 : (group + 1) * 480, :],
            last_ref[...],
            preferred_element_type=jnp.float32,
        )
        for i in range(10):
            rows = pl.ds(group * 10 + i, PAD, stride=WIDE)
            mid_real[rows, :] = product[i * PAD : (i + 1) * PAD, 0:128]
            mid_imag[rows, :] = product[i * PAD : (i + 1) * PAD, 128:256]

    scaled = 0.5 / (smearing * smearing)
    tail = jnp.zeros((8 * (PAD - 45), 128), jnp.float32)
    rate_acc[8 * 45 :, :] = tail
    couple_acc[8 * 45 :, :] = tail

    def one_mode(s):
        rows = pl.ds(pl.multiple_of(s * WIDE, WIDE), WIDE)
        operand = jnp.concatenate([mid_real[rows, :], mid_imag[rows, :]], axis=0)
        value = jnp.dot(
            middle_ref[...], operand.astype(jnp.bfloat16), preferred_element_type=jnp.float32
        )
        real = value[0:WIDE]
        imag = value[WIDE:]
        freq = scalars_ref[0, pl.ds(s, 1), :]
        decays = freq - tables_ref[0]
        merges = freq + tables_ref[1]
        weight = (real * real + imag * imag) * (
            jnp.exp(-scaled * decays * decays) + jnp.exp(-scaled * merges * merges)
        )
        weight = weight * tables_ref[2] * scalars_ref[1, pl.ds(s, 1), :]
        at = pl.ds(pl.multiple_of(s * 8, 8), 8)
        rate_acc[at, :] = jnp.sum(weight.reshape(WIDE // 8, 8, 128), axis=0)
        couple_acc[at, :] = jnp.sum((weight * tables_ref[3]).reshape(WIDE // 8, 8, 128), axis=0)

    @pl.loop(0, 15)
    def _(i):
        for j in range(3):
            one_mode(3 * i + j)

    sums = jnp.concatenate(
        [
            jnp.sum(rate_acc[...].reshape(PAD, 8, 128), axis=1),
            jnp.sum(couple_acc[...].reshape(PAD, 8, 128), axis=1),
        ],
        axis=0,
    )
    out_ref[:, 0:WIDE] = lax.dot_general(
        jnp.ones((8, 128), jnp.float32),
        sums,
        (((1,), (1,)), ((), ())),
        precision=lax.Precision.HIGHEST,
        preferred_element_type=jnp.float32,
    )
    out_ref[:, WIDE:128] = jnp.zeros((8, 128 - WIDE), jnp.float32)


VMEM = pl.BlockSpec(memory_space=pltpu.VMEM)
SMEM = pl.BlockSpec(memory_space=pltpu.SMEM)


def ring(count, step):
    return [(i, (i + step) % count) for i in range(count)]


def grid_shift(step_y, step_z):
    return [
        (y * RING_Z + z, (y + step_y) % RING_Y * RING_Z + (z + step_z) % RING_Z)
        for y in range(RING_Y)
        for z in range(RING_Z)
    ]


def body(
    force_third,
    phase_angle,
    eigenvectors,
    frequencies,
    deviation,
    send_rows,
    trip_table,
    irreducible,
    multiplicity,
    drive_term,
    boundary,
):
    f32, b16 = jnp.float32, jnp.bfloat16
    clus = lax.axis_index("clus")
    mode = lax.axis_index("mode")
    trip = lax.axis_index("trip")
    color = (trip // RING_Z + trip % RING_Z) % 2

    picked_force = lax.dynamic_index_in_dim(force_third, color, 0, keepdims=False)
    up, down = ring(4, 1), ring(4, 3)
    with jax.named_scope("force_neighbours"):
        low = lax.ppermute(picked_force, "clus", up)
        high = lax.ppermute(picked_force, "clus", down)

    with jax.named_scope("records"):
        extra = jnp.concatenate([frequencies, deviation], axis=1)[:, None, :]
        record = jnp.concatenate(
            [eigenvectors, extra, jnp.zeros((extra.shape[0], 5, 180), b16)], axis=1
        )
        share = lax.dynamic_slice_in_dim(record, 12 * (2 * clus + mode), 12, 1)
        chosen = pl.pallas_call(
            send_kernel,
            out_shape=jax.ShapeDtypeStruct((send_rows.shape[1],) + share.shape[1:], b16),
            in_specs=[SMEM, VMEM],
            out_specs=VMEM,
        )(send_rows, share)
        arrived = lax.all_to_all(chosen, "trip", 0, 0, tiled=True)
        angles = phase_angle.astype(f32)
        trig = jnp.stack([jnp.cos(angles), jnp.sin(angles)], axis=1).astype(b16)
        trig = trig.reshape(4, 4).T
        phases = jnp.pad(trig[:, None, :], ((0, 0), (0, 11), (0, 176)))
        picks = pl.pallas_call(
            pick_kernel,
            out_shape=(jax.ShapeDtypeStruct((4, 12, 180), b16),) * 4,
            in_specs=[SMEM, SMEM, VMEM, VMEM],
            out_specs=(VMEM,) * 4,
        )(clus.reshape(1).astype(jnp.int32), trip_table, arrived, phases)

    with jax.named_scope("force_second"):
        low, high, _ = lax.optimization_barrier((low, high, arrived))
        low0, low1 = low[:, :SPLIT], low[:, SPLIT:]
        high0, high1 = high[:, :SPLIT], high[:, SPLIT:]
        opp0 = lax.ppermute(low0, "clus", up)
        opp1 = lax.ppermute(high1, "clus", down)
        low_other0 = lax.ppermute(low0, "trip", grid_shift(1, 0))
        low_other1 = lax.ppermute(low1, "trip", grid_shift(-1, 0))
        high_other0 = lax.ppermute(high0, "trip", grid_shift(0, 1))
        high_other1 = lax.ppermute(high1, "trip", grid_shift(0, -1))
    with jax.named_scope("force_third_step"):
        opp_other0 = lax.ppermute(opp0, "trip", grid_shift(1, 0))
        opp_other1 = lax.ppermute(opp1, "trip", grid_shift(0, 1))

    with jax.named_scope("members"):
        swap = [(0, 1), (1, 0)]
        picks = lax.optimization_barrier(
            (*picks, opp0, opp1, low_other0, low_other1, high_other0, high_other1)
        )[:4]
        members = [picks[0]]
        for k in range(4):
            for far in (0, 1):
                if k or far:
                    step = [
                        (2 * c + m, (2 * c + 2 * k) % 8 + (m + far) % 2)
                        for c in range(4)
                        for m in range(2)
                    ]
                    members.append(lax.ppermute(picks[k], ("clus", "mode"), step))
    with jax.named_scope("operands"):
        mult = lax.dynamic_index_in_dim(multiplicity, clus, 0, keepdims=False)
        where = jnp.stack([clus, mode, color, mult]).astype(jnp.int32)
        lead, mid, last_all, tables, scalars = pl.pallas_call(
            operand_kernel,
            out_shape=(
                jax.ShapeDtypeStruct((4 * PAD, 8 * PAD), b16),
                jax.ShapeDtypeStruct((2 * WIDE, 2 * WIDE), b16),
                jax.ShapeDtypeStruct((256, 256), b16),
                jax.ShapeDtypeStruct((4, WIDE, 128), f32),
                jax.ShapeDtypeStruct((2, PAD, 128), f32),
            ),
            in_specs=[SMEM] + [VMEM] * 8,
            out_specs=(VMEM,) * 5,
            scratch_shapes=[pltpu.VMEM((3, 128, 256), f32)],
        )(where, *members)

    with jax.named_scope("contract"):
        own = lax.optimization_barrier((force_third, low))[0]
        products = []
        for parts in (
            (low_other0, high_other0, opp0, opp_other0),
            (low_other1, high_other1, opp1, opp_other1),
        ):
            length = parts[0].shape[1]
            mine, far = pl.pallas_call(
                contract_kernel,
                out_shape=(jax.ShapeDtypeStruct((2 * PAD, length), b16),) * 2,
                in_specs=[VMEM] * 8,
                out_specs=(VMEM, VMEM),
                compiler_params=pltpu.CompilerParams(vmem_limit_bytes=16 << 20),
                cost_estimate=pl.CostEstimate(
                    flops=2 * 192 * 384 * length, bytes_accessed=1000 * length, transcendentals=0
                ),
            )(lead, own, low, high, *parts)
            products += [mine, lax.ppermute(far, "mode", swap)]
    with jax.named_scope("interaction"):
        sums = pl.pallas_call(
            interaction_kernel,
            out_shape=jax.ShapeDtypeStruct((8, 128), f32),
            in_specs=[VMEM] * 8,
            out_specs=VMEM,
            scratch_shapes=[
                pltpu.VMEM((2 * PAD, 8320), b16),
                pltpu.VMEM((90 * PAD, 256), b16),
                pltpu.VMEM((PAD * WIDE, 128), f32),
                pltpu.VMEM((PAD * WIDE, 128), f32),
                pltpu.VMEM((8 * PAD, 128), f32),
                pltpu.VMEM((8 * PAD, 128), f32),
            ],
            compiler_params=pltpu.CompilerParams(vmem_limit_bytes=24 << 20),
        )(scalars, mid, last_all, tables, *products)
    with jax.named_scope("collect"):
        own_row = sums[0:1]
        rows = [own_row] + [lax.ppermute(own_row, "clus", ring(4, step)) for step in (1, 2, 3)]
        points = jnp.arange(32, dtype=jnp.int32)
        partial = jnp.zeros((32, 128), f32)
        for step in range(4):
            point = lax.dynamic_index_in_dim(irreducible, (clus - step) % 4, 0, keepdims=False)
            partial = partial + jnp.where((points == point)[:, None], rows[step], 0.0)
        received = lax.all_to_all(partial[:, None, :], "trip", 0, 0, tiled=True)
        final = jnp.sum(received[:, 0, :], axis=0)[None, :]
        gamma_total = final[:, 0:45] + boundary
        return gamma_total, (drive_term + final[:, PAD : PAD + 45]) / gamma_total


def solution(mesh):
    return jax.shard_map(
        body,
        mesh=mesh,
        in_specs=(
            P("clus", "mode", None),
            P("clus", "trip"),
            P("trip", None, None),
            P("trip", None),
            P("trip", None),
            P("trip", None),
            P("trip", None),
            P("trip"),
            P("trip"),
            P("trip", "mode"),
            P("trip", "mode"),
        ),
        out_specs=(P("trip", "mode"), P("trip", "mode")),
        check_vma=False,
    )
```

time: 125 us -> 126 us (level)
  blocking collectives: 14 us -> 38.6 us
  waiting for transfers between devices: 25.6 us -> 3.94 us
  starting transfers between devices: 35 us -> 26.9 us
  local copies, waits for them, and re-layouts: 18.1 us -> 24.6 us
  Pallas kernels: 18.5 us -> 24.3 us
  other arithmetic: 9.95 us -> 5.51 us
    all_to_all x0 -> x1, blocking collectives: none -> 23 us  [body(): arrived = lax.all_to_all(chosen, 'trip', 0, 0, tiled=True)]
    all_to_all x2 -> x0, starting transfers between devices: 17.2 us -> none  [the longest x1 11.2 us: body(): arrived = lax.all_to_all(chosen, 'trip', 0, 0, tiled=True)]
    all_to_all x2 -> x0, waiting for transfers between devices: 10.5 us -> none  [the longest x1 10.5 us: body(): arrived = lax.all_to_all(chosen, 'trip', 0, 0, tiled=True)]
    unnamed x28 -> x58, local copies, waits for them, and re-layouts: 5.72 us -> 14.9 us
    ppermute x5 -> x11, starting transfers between devices: 4.38 us -> 11.3 us  [the longest x7 8.31 us: body(): members.append(lax.ppermute(picks[k], ('clus', 'mode'), step))]
    ppermute x1, waiting for transfers between devices: 6.71 us -> 0.01 us  [body(): opp_other1 = lax.ppermute(opp1, 'trip', grid_shift(0, 1))]
    pallas_call x2 -> x4, Pallas kernels: 7.25 us -> 12.2 us  [the longest x2 8.25 us: body(): pl.pallas_call(contract_kernel, out_shape=(jax.ShapeDtypeStruct((2 * PAD,...]
    pad x8 -> x0, local copies, waits for them, and re-layouts: 3.47 us -> none  [the longest x4 1.24 us: pad_to(): jnp.pad(array, ((0, rows - array.shape[0]), (0, cols - array.shape[1])))]
  transfers between devices with their start and end apart: 18 -> 22, of which waited for: 6 -> 7; matrix products, arithmetic and copies ran while one was open for 19% -> 9% of each run, Pallas kernels for 3% -> 11%
where the time goes in v2:
time: 126 us; the launch traced here: 125 us
  blocking collectives  38.6 us (31%)
  starting transfers between devices  26.9 us (21%)
  local copies, waits for them, and re-layouts  24.6 us (20%)
  Pallas kernels  24.3 us (19%)
  other arithmetic  5.51 us (4%)
  waiting for transfers between devices  3.94 us (3%)
    all_to_all x1, blocking collectives, body(): arrived = lax.all_to_all(chosen, 'trip', 0, 0, tiled=True)  23 us
    all_to_all x1, blocking collectives, body(): received = lax.all_to_all(partial[:, None, :], 'trip', 0, 0, tiled=True)  15.6 us
    unnamed x58, local copies, waits for them, and re-layouts  14.9 us
    pallas_call x1, Pallas kernels, body(): pl.pallas_call(interaction_kernel, out_shape=jax.ShapeDtypeStruct((8, 128...  10.5 us
    ppermute x7, starting transfers between devices, body(): members.append(lax.ppermute(picks[k], ('clus', 'mode'), step))  8.31 us
    pallas_call x2, Pallas kernels, body(): pl.pallas_call(contract_kernel, out_shape=(jax.ShapeDtypeStruct((2 * PAD,...  8.25 us
    ppermute x3, starting transfers between devices, body(): lax.ppermute(own_row, 'clus', ring(4, step))  6 us
    dynamic_slice x1, local copies, waits for them, and re-layouts, body(): lax.dynamic_index_in_dim(force_third, color, 0, keepdims=False)  3.84 us
  transfers between devices with their start and end apart: 22, of which 7 were waited for; matrix products, arithmetic and copies ran while one was open for 9% of the time, Pallas kernels for 11%

profile of v2, /device:TPU:2, one launch (start us, length us, event | category | flops | bytes accessed | tf_op | source)
XLA Modules:
  0.0 124.8 jit_solution(11478226422109476458)
XLA Ops:
  0.7 3.8 %constant_dynamic-slice_fusion = bf16[1,45,8100]{2,0,1:T(2,128)(2,1)S(1)} fusion(bf16[2,45,8100]{2,0,1:T(2,128)(2,1)} %param.11, s32[]{:T(128)S(6)} %select_n.102), kind=kLoop, calls=%fused_computation.18 | loop fusion | bytes 1458004 | tf_op jit(solution)/shard_map/jit(dynamic_index_in_dim)/dynamic_slice | solution.py:283
  4.6 0.8 copy.48
  5.4 1.6 %collective-permute-start = (bf16[45,8100]{1,0:T(8,128)(2,1)S(1)}, bf16[45,8100]{1,0:T(8,128)(2,1)S(1)}, u32[]{:S(2)}, u32[]{:S(2)}) collective-permute-start(bf16[45,8100]{1,0:T(8,128)(2,1)S(1)} %bitcast.28), channel_id=1, source_target_pairs={{0,64},{64,128},{128,192},{192,0},{1,65},{65,129},{129,193},{193,1... | collective-permute-start | bytes 2187008 | tf_op jit(solution)/shard_map/force_neighbours/ppermute | solution.py:286
  6.9 0.9 collective-permute-start.1
  8.8 1.6 %records.2 = bf16[32,12,180]{2,1,0:T(8,128)(2,1)} custom-call(s32[1,32]{1,0:T(1,128)} %rows_ref.1, bf16[8,12,180]{2,1,0:T(8,128)(2,1)} %fusion.1.share_ref), custom_call_target="tpu_custom_call" | custom-call | tf_op jit(solution)/shard_map/records/pallas_call | solution.py:295
  10.4 23.0 %all_to_all.10.arrived_ref = bf16[32,12,180]{2,1,0:T(8,128)(2,1)} all-to-all(bf16[32,12,180]{2,1,0:T(8,128)(2,1)} %records.2), channel_id=1, replica_groups=mesh['clus'=4,'trip'=32,'mode'=2] {'trip'}, dimensions={0} | all-to-all | bytes 276480 | tf_op jit(solution)/shard_map/records/all_to_all | solution.py:301
  33.5 1.8 %collective-permute-start.3 = (bf16[45,4004]{1,0:T(8,128)(2,1)S(1)}, bf16[45,4004]{1,0:T(8,128)(2,1)S(1)}, u32[]{:S(2)}, u32[]{:S(2)}) collective-permute-start(bf16[45,4004]{1,0:T(8,128)(2,1)S(1)} %slice.24), channel_id=1, source_target_pairs={{0,192},{64,0},{128,64},{192,128},{1,193},{65,1},{129,65},{193,129... | collective-permute-start | bytes 1081088 | tf_op jit(solution)/shard_map/force_second/ppermute | solution.py:318
  35.3 0.8 slice.23
  36.4 1.3 %collective-permute-start.5 = (bf16[45,4004]{1,0:T(8,128)(2,1)S(1)}, bf16[45,4004]{1,0:T(8,128)(2,1)S(1)}, u32[]{:S(2)}, u32[]{:S(2)}) collective-permute-start(bf16[45,4004]{1,0:T(8,128)(2,1)S(1)} %slice.25), channel_id=1, source_target_pairs={{0,48},{2,50},{4,52},{6,54},{8,56},{10,58},{12,60},{14,62},{16,0},... | collective-permute-start | bytes 1081088 | tf_op jit(solution)/shard_map/force_second/ppermute | solution.py:320
  37.6 0.8 collective-permute-start.4
  38.5 0.8 slice.26
  39.3 1.7 %collective-permute-start.6 = (bf16[45,4096]{1,0:T(8,128)(2,1)}, bf16[45,4096]{1,0:T(8,128)(2,1)S(1)}, u32[]{:S(2)}, u32[]{:S(2)}) collective-permute-start(bf16[45,4096]{1,0:T(8,128)(2,1)} %slice.26), channel_id=1, source_target_pairs={{0,2},{2,4},{4,6},{6,8},{8,10},{10,12},{12,14},{14,0},{16,18},{18,... | collective-permute-start | bytes 1105928 | tf_op jit(solution)/shard_map/force_second/ppermute | solution.py:321
  41.4 1.1 collective-permute-start.7
  42.5 1.7 %collective-permute-done.5.refs_2_ = bf16[45,4004]{1,0:T(8,128)(2,1)S(1)} collective-permute-done((bf16[45,4004]{1,0:T(8,128)(2,1)S(1)}, bf16[45,4004]{1,0:T(8,128)(2,1)S(1)}, u32[]{:S(2)}, u32[]{:S(2)}) %collective-permute-start.5) | collective-permute-done | bytes 360392 | tf_op jit(solution)/shard_map/force_second/ppermute | solution.py:320
  44.2 0.7 copy-done.5
  45.0 2.1 %collective-permute-start.17 = (bf16[45,4004]{1,0:T(8,128)(2,1)S(1)}, bf16[45,4004]{1,0:T(8,128)(2,1)}, u32[]{:S(2)}, u32[]{:S(2)}) collective-permute-start(bf16[45,4004]{1,0:T(8,128)(2,1)S(1)} %collective-permute-done.3.refs_4_), channel_id=1, source_target_pairs={{0,2},{2,4},{4,6},{6,8},{8,10},{10,12},{12,14},{14,0},{16,18},{18,... | collective-permute-start | bytes 1081088 | tf_op jit(solution)/shard_map/force_third_step/ppermute | solution.py:325
  48.4 1.6 %records.3 = (bf16[4,12,180]{2,1,0:T(8,128)(2,1)}, bf16[4,12,180]{2,1,0:T(8,128)(2,1)}, bf16[4,12,180]{2,1,0:T(8,128)(2,1)}, bf16[4,12,180]{2,1,0:T(8,128)(2,1)}) custom-call(s32[1]{0:T(128)} %bitcast.1.rank_ref, s32[4,3]{1,0:T(4,128)} %table_ref.1, bf16[32,12,180]{2,1,0:T(8,128)(2,1)} %all_to_all.10.arrived_ref, bf16[4,12,180]{2,1,0:T(8,128)(2,1)} %pad.4.phase_ref), custom_call_target="tpu_custom_call" | custom-call | tf_op jit(solution)/shard_map/records/pallas_call | solution.py:306
  50.1 0.7 copy-done.7
  50.8 0.7 copy-done.9
  51.6 1.0 collective-permute-done.6.refs_3_
  52.6 0.8 copy-done.11
  53.4 3.3 %collective-permute-start.11 = (bf16[4,12,180]{2,1,0:T(8,128)(2,1)}, bf16[4,12,180]{2,1,0:T(8,128)(2,1)S(1)}, u32[]{:S(2)}, u32[]{:S(2)}) collective-permute-start(bf16[4,12,180]{2,1,0:T(8,128)(2,1)} %get-tuple-element.30), channel_id=1, source_target_pairs={{0,128},{1,129},{64,192},{65,193},{128,0},{129,1},{192,64},{193,65... | collective-permute-start | bytes 51848 | tf_op jit(solution)/shard_map/members/ppermute | solution.py:341
  56.7 1.1 collective-permute-start.12
  57.8 2.4 %collective-permute-start.13 = (bf16[4,12,180]{2,1,0:T(8,128)(2,1)}, bf16[4,12,180]{2,1,0:T(8,128)(2,1)S(1)}, u32[]{:S(2)}, u32[]{:S(2)}) collective-permute-start(bf16[4,12,180]{2,1,0:T(8,128)(2,1)} %get-tuple-element.31), channel_id=1, source_target_pairs={{0,192},{1,193},{64,0},{65,1},{128,64},{129,65},{192,128},{193,129... | collective-permute-start | bytes 51848 | tf_op jit(solution)/shard_map/members/ppermute | solution.py:341
  61.7 0.8 collective-permute-start.9
  63.2 1.3 %pad_add_fusion.where_ref = s32[4]{0:T(128)} fusion(s32[1]{0:T(128)} %dynamic_slice.24, s32[1]{0:T(128)} %bitcast.3, s32[1]{0:T(128)} %bitcast.2, s32[1]{0:T(128)} %bitcast.1.rank_ref), kind=kLoop, calls=%fused_computation.22 | loop fusion | flops 12 | bytes 32 | tf_op jit(solution)/shard_map/operands/stack | solution.py:344
  64.5 2.2 %copy.41.own_ref = bf16[2,45,8100]{2,1,0:T(8,128)(2,1)S(1)} copy(bf16[2,45,8100]{2,0,1:T(2,128)(2,1)} %param.11) | data formatting | bytes 2916000 | tf_op jit(solution)/shard_map/contract/optimization_barrier | solution.py:360
  66.8 2.3 %operands.1 = (bf16[192,384]{1,0:T(8,128)(2,1)}, bf16[192,192]{1,0:T(8,128)(2,1)}, bf16[256,256]{1,0:T(8,128)(2,1)}, f32[4,96,128]{2,1,0:T(8,128)}, f32[2,48,128]{2,1,0:T(8,128)}) custom-call(s32[4]{0:T(128)} %pad_add_fusion.where_ref, bf16[4,12,180]{2,1,0:T(8,128)(2,1)} %get-tuple-element.28.refs_0_, bf16[4,12,180]{2,1,0:T(8,128)(2,1)} %collective-permute-done.8.refs_1_, ...), custom_call_target="tpu_custom_call" | custom-call | tf_op jit(solution)/shard_map/operands/pallas_call | solution.py:345
  69.1 0.9 copy-done.4
  70.0 1.0 copy-done.10
  71.0 1.0 copy-done.12
  72.0 4.2 %contract.2 = (bf16[96,4096]{1,0:T(8,128)(2,1)S(1)}, bf16[96,4096]{1,0:T(8,128)(2,1)}) custom-call(bf16[192,384]{1,0:T(8,128)(2,1)S(1)} %copy-done.4, bf16[2,45,8100]{2,1,0:T(8,128)(2,1)S(1)} %copy.41.own_ref, bf16[45,8100]{1,0:T(8,128)(2,1)S(1)} %collective-permute-done.refs_0_, bf16[45,8100]{1,0:T(8,128)(2,1)S(1)} %collective-permute-done.1.refs_1_, ...), custom_call_target="tpu_custom_call" | custom-call | flops 603979776 | bytes 4096000 | tf_op jit(solution)/shard_map/contract/pallas_call | solution.py:367
  76.2 0.9 copy-done
  77.2 4.0 %contract.3 = (bf16[96,4004]{1,0:T(8,128)(2,1)S(1)}, bf16[96,4004]{1,0:T(8,128)(2,1)}) custom-call(bf16[192,384]{1,0:T(8,128)(2,1)S(1)} %copy-done.4, bf16[2,45,8100]{2,1,0:T(8,128)(2,1)S(1)} %copy.41.own_ref, bf16[45,8100]{1,0:T(8,128)(2,1)S(1)} %collective-permute-done.refs_0_, bf16[45,8100]{1,0:T(8,128)(2,1)S(1)} %collective-permute-done.1.refs_1_, ...), custom_call_target="tpu_custom_call" | custom-call | flops 590413824 | bytes 4004000 | tf_op jit(solution)/shard_map/contract/pallas_call | solution.py:367
  81.2 0.9 copy-done.2
  83.2 1.3 %iota_compare_fusion.2 = (pred[32]{0:T(512)(128)(4,1)S(1)}, pred[32]{0:T(512)(128)(4,1)S(1)}) fusion(s32[]{:T(128)} %bitcast.12, s32[]{:T(128)} %bitcast), kind=kLoop, calls=%fused_computation.27 | loop fusion | flops 64 | bytes 72 | tf_op jit(solution)/shard_map/collect/eq | solution.py:401
  84.7 1.1 copy-done.1
  85.8 1.1 copy-done.3
  86.9 0.9 copy-done.13
  87.8 0.9 copy-done.14
  88.8 0.9 copy-done.15
  89.6 0.8 copy-done.16
  90.4 10.5 %interaction.1 = f32[8,128]{1,0:T(8,128)S(1)} custom-call(f32[2,48,128]{2,1,0:T(8,128)S(1)} %copy-done.16, bf16[192,192]{1,0:T(8,128)(2,1)S(1)} %copy-done.15, bf16[256,256]{1,0:T(8,128)(2,1)S(1)} %copy-done.14, f32[4,96,128]{2,1,0:T(8,128)S(1)} %copy-done.13, bf16[96,4096]{1,0:T(8,128)(2,1)S(1)} %copy-done.1, ...), custom_call_target="tpu_custom_call" | custom-call | tf_op jit(solution)/shard_map/interaction/pallas_call | solution.py:379
  101.0 2.1 %collective-permute-start.19 = (f32[1,128]{1,0:T(1,128)S(1)}, f32[1,128]{1,0:T(1,128)S(1)}, u32[]{:S(2)}, u32[]{:S(2)}) collective-permute-start(f32[1,128]{1,0:T(1,128)S(1)} %get-tuple-element.45), channel_id=1, source_target_pairs={{0,64},{64,128},{128,192},{192,0},{1,65},{65,129},{129,193},{193,1... | collective-permute-start | bytes 1544 | tf_op jit(solution)/shard_map/collect/ppermute | solution.py:396
  103.0 1.8 %collective-permute-start.20 = (f32[1,128]{1,0:T(1,128)S(1)}, f32[1,128]{1,0:T(1,128)S(1)}, u32[]{:S(2)}, u32[]{:S(2)}) collective-permute-start(f32[1,128]{1,0:T(1,128)S(1)} %get-tuple-element.45), channel_id=1, source_target_pairs={{0,128},{64,192},{128,0},{192,64},{1,129},{65,193},{129,1},{193,65... | collective-permute-start | bytes 1544 | tf_op jit(solution)/shard_map/collect/ppermute | solution.py:396
  104.8 2.1 %collective-permute-start.21 = (f32[1,128]{1,0:T(1,128)S(1)}, f32[1,128]{1,0:T(1,128)S(1)}, u32[]{:S(2)}, u32[]{:S(2)}) collective-permute-start(f32[1,128]{1,0:T(1,128)S(1)} %get-tuple-element.45), channel_id=1, source_target_pairs={{0,192},{64,0},{128,64},{192,128},{1,193},{65,1},{129,65},{193,129... | collective-permute-start | bytes 1544 | tf_op jit(solution)/shard_map/collect/ppermute | solution.py:396
  107.0 1.3 %iota_compare_fusion = (pred[32]{0:T(512)(128)(4,1)S(1)}, pred[32]{0:T(512)(128)(4,1)S(1)}) fusion(s32[]{:T(128)} %bitcast.16, s32[]{:T(128)} %bitcast.14), kind=kLoop, calls=%fused_computation.25 | loop fusion | flops 64 | bytes 72 | tf_op jit(solution)/shard_map/collect/eq | solution.py:401
  108.6 15.6 %all_to_all.11 = f32[32,1,128]{2,1,0:T(1,128)S(1)} all-to-all(f32[32,1,128]{2,1,0:T(1,128)S(1)} %fusion.4), channel_id=1, replica_groups=mesh['clus'=4,'trip'=32,'mode'=2] {'trip'}, dimensions={0} | all-to-all | bytes 32768 | tf_op jit(solution)/shard_map/collect/all_to_all | solution.py:402
  (87 shorter events, 7.7 us)
Async XLA Ops:
  4.5 3.3 %copy-start.17 = (bf16[8,90,180]{2,0,1:T(8,128)(2,1)S(1)}, bf16[8,90,180]{2,0,1:T(8,128)(2,1)}, u32[]{:S(2)}) copy-start(bf16[8,90,180]{2,0,1:T(8,128)(2,1)} %param.13) | copy-start | bytes 777604
  4.5 3.4 %copy-start.22 = (bf16[8,90]{1,0:T(8,128)(2,1)S(1)}, bf16[8,90]{1,0:T(8,128)(2,1)}, u32[]{:S(2)}) copy-start(bf16[8,90]{1,0:T(8,128)(2,1)} %param.15) | copy-start | bytes 4324
  4.5 3.4 %copy-start.23 = (bf16[8,90]{1,0:T(8,128)(2,1)S(1)}, bf16[8,90]{1,0:T(8,128)(2,1)}, u32[]{:S(2)}) copy-start(bf16[8,90]{1,0:T(8,128)(2,1)} %param.14) | copy-start | bytes 4324
  5.4 28.0 %collective-permute-start = (bf16[45,8100]{1,0:T(8,128)(2,1)S(1)}, bf16[45,8100]{1,0:T(8,128)(2,1)S(1)}, u32[]{:S(2)}, u32[]{:S(2)}) collective-permute-start(bf16[45,8100]{1,0:T(8,128)(2,1)S(1)} %bitcast.28), channel_id=1, source_target_pairs={{0,64},{64,128},{128,192},{192,0},{1,65},{65,129},{129,193},{193,1... | collective-permute-start | bytes 2187008 | tf_op jit(solution)/shard_map/force_neighbours/ppermute | solution.py:286
  6.9 26.5 %collective-permute-start.1 = (bf16[45,8100]{1,0:T(8,128)(2,1)S(1)}, bf16[45,8100]{1,0:T(8,128)(2,1)S(1)}, u32[]{:S(2)}, u32[]{:S(2)}) collective-permute-start(bf16[45,8100]{1,0:T(8,128)(2,1)S(1)} %bitcast.29), channel_id=1, source_target_pairs={{0,192},{64,0},{128,64},{192,128},{1,193},{65,1},{129,65},{193,129... | collective-permute-start | bytes 2187008 | tf_op jit(solution)/shard_map/force_neighbours/ppermute | solution.py:287
  33.4 14.2 %copy-start.26 = (bf16[2,4]{1,0:T(2,128)(2,1)S(1)}, bf16[2,4]{1,0:T(2,128)(2,1)}, u32[]{:S(2)}) copy-start(bf16[2,4]{1,0:T(2,128)(2,1)} %param.12) | copy-start | bytes 52
  33.5 26.8 %copy-start.27 = (s32[4]{0:T(128)S(1)}, s32[4]{0:T(128)}, u32[]{:S(2)}) copy-start(s32[4]{0:T(128)} %param.19) | copy-start | bytes 52
  33.5 8.0 %collective-permute-start.3 = (bf16[45,4004]{1,0:T(8,128)(2,1)S(1)}, bf16[45,4004]{1,0:T(8,128)(2,1)S(1)}, u32[]{:S(2)}, u32[]{:S(2)}) collective-permute-start(bf16[45,4004]{1,0:T(8,128)(2,1)S(1)} %slice.24), channel_id=1, source_target_pairs={{0,192},{64,0},{128,64},{192,128},{1,193},{65,1},{129,65},{193,129... | collective-permute-start | bytes 1081088 | tf_op jit(solution)/shard_map/force_second/ppermute | solution.py:318
  36.1 11.0 %collective-permute-start.2 = (bf16[45,4096]{1,0:T(8,128)(2,1)}, bf16[45,4096]{1,0:T(8,128)(2,1)}, u32[]{:S(2)}, u32[]{:S(2)}) collective-permute-start(bf16[45,4096]{1,0:T(8,128)(2,1)} %slice.23), channel_id=1, source_target_pairs={{0,64},{64,128},{128,192},{192,0},{1,65},{65,129},{129,193},{193,1... | collective-permute-start | bytes 1105928 | tf_op jit(solution)/shard_map/force_second/ppermute | solution.py:317
  36.4 7.9 %collective-permute-start.5 = (bf16[45,4004]{1,0:T(8,128)(2,1)S(1)}, bf16[45,4004]{1,0:T(8,128)(2,1)S(1)}, u32[]{:S(2)}, u32[]{:S(2)}) collective-permute-start(bf16[45,4004]{1,0:T(8,128)(2,1)S(1)} %slice.25), channel_id=1, source_target_pairs={{0,48},{2,50},{4,52},{6,54},{8,56},{10,58},{12,60},{14,62},{16,0},... | collective-permute-start | bytes 1081088 | tf_op jit(solution)/shard_map/force_second/ppermute | solution.py:320
  37.6 13.2 %collective-permute-start.4 = (bf16[45,4096]{1,0:T(8,128)(2,1)}, bf16[45,4096]{1,0:T(8,128)(2,1)S(1)}, u32[]{:S(2)}, u32[]{:S(2)}) collective-permute-start(bf16[45,4096]{1,0:T(8,128)(2,1)} %slice.23), channel_id=1, source_target_pairs={{0,16},{2,18},{4,20},{6,22},{8,24},{10,26},{12,28},{14,30},{16,32}... | collective-permute-start | bytes 1105928 | tf_op jit(solution)/shard_map/force_second/ppermute | solution.py:319
  39.3 13.3 %collective-permute-start.6 = (bf16[45,4096]{1,0:T(8,128)(2,1)}, bf16[45,4096]{1,0:T(8,128)(2,1)S(1)}, u32[]{:S(2)}, u32[]{:S(2)}) collective-permute-start(bf16[45,4096]{1,0:T(8,128)(2,1)} %slice.26), channel_id=1, source_target_pairs={{0,2},{2,4},{4,6},{6,8},{8,10},{10,12},{12,14},{14,0},{16,18},{18,... | collective-permute-start | bytes 1105928 | tf_op jit(solution)/shard_map/force_second/ppermute | solution.py:321
  41.4 8.6 %collective-permute-start.7 = (bf16[45,4004]{1,0:T(8,128)(2,1)S(1)}, bf16[45,4004]{1,0:T(8,128)(2,1)S(1)}, u32[]{:S(2)}, u32[]{:S(2)}) collective-permute-start(bf16[45,4004]{1,0:T(8,128)(2,1)S(1)} %slice.24), channel_id=1, source_target_pairs={{0,14},{2,0},{4,2},{6,4},{8,6},{10,8},{12,10},{14,12},{16,30},{18,... | collective-permute-start | bytes 1081088 | tf_op jit(solution)/shard_map/force_second/ppermute | solution.py:322
  44.2 0.7 copy-start.5
  45.0 32.2 %collective-permute-start.17 = (bf16[45,4004]{1,0:T(8,128)(2,1)S(1)}, bf16[45,4004]{1,0:T(8,128)(2,1)}, u32[]{:S(2)}, u32[]{:S(2)}) collective-permute-start(bf16[45,4004]{1,0:T(8,128)(2,1)S(1)} %collective-permute-done.3.refs_4_), channel_id=1, source_target_pairs={{0,2},{2,4},{4,6},{6,8},{8,10},{10,12},{12,14},{14,0},{16,18},{18,... | collective-permute-start | bytes 1081088 | tf_op jit(solution)/shard_map/force_third_step/ppermute | solution.py:325
  47.0 22.0 %collective-permute-start.15 = (bf16[45,4096]{1,0:T(8,128)(2,1)}, bf16[45,4096]{1,0:T(8,128)(2,1)}, u32[]{:S(2)}, u32[]{:S(2)}) collective-permute-start(bf16[45,4096]{1,0:T(8,128)(2,1)} %collective-permute-done.2.refs_4_), channel_id=1, source_target_pairs={{0,16},{2,18},{4,20},{6,22},{8,24},{10,26},{12,28},{14,30},{16,32}... | collective-permute-start | bytes 1105928 | tf_op jit(solution)/shard_map/force_third_step/ppermute | solution.py:324
  50.8 0.7 copy-start.9
  52.6 0.8 copy-start.11
  53.3 4.4 %collective-permute-start.10 = (bf16[4,12,180]{2,1,0:T(8,128)(2,1)}, bf16[4,12,180]{2,1,0:T(8,128)(2,1)}, u32[]{:S(2)}, u32[]{:S(2)}) collective-permute-start(bf16[4,12,180]{2,1,0:T(8,128)(2,1)} %get-tuple-element.29), channel_id=1, source_target_pairs={{0,65},{1,64},{64,129},{65,128},{128,193},{129,192},{192,1},{193,0... | collective-permute-start | bytes 51848 | tf_op jit(solution)/shard_map/members/ppermute | solution.py:341
  53.4 7.5 %collective-permute-start.11 = (bf16[4,12,180]{2,1,0:T(8,128)(2,1)}, bf16[4,12,180]{2,1,0:T(8,128)(2,1)S(1)}, u32[]{:S(2)}, u32[]{:S(2)}) collective-permute-start(bf16[4,12,180]{2,1,0:T(8,128)(2,1)} %get-tuple-element.30), channel_id=1, source_target_pairs={{0,128},{1,129},{64,192},{65,193},{128,0},{129,1},{192,64},{193,65... | collective-permute-start | bytes 51848 | tf_op jit(solution)/shard_map/members/ppermute | solution.py:341
  56.7 5.1 %collective-permute-start.12 = (bf16[4,12,180]{2,1,0:T(8,128)(2,1)}, bf16[4,12,180]{2,1,0:T(8,128)(2,1)S(1)}, u32[]{:S(2)}, u32[]{:S(2)}) collective-permute-start(bf16[4,12,180]{2,1,0:T(8,128)(2,1)} %get-tuple-element.30), channel_id=1, source_target_pairs={{0,129},{1,128},{64,193},{65,192},{128,1},{129,0},{192,65},{193,64... | collective-permute-start | bytes 51848 | tf_op jit(solution)/shard_map/members/ppermute | solution.py:341
  57.8 4.8 %collective-permute-start.13 = (bf16[4,12,180]{2,1,0:T(8,128)(2,1)}, bf16[4,12,180]{2,1,0:T(8,128)(2,1)S(1)}, u32[]{:S(2)}, u32[]{:S(2)}) collective-permute-start(bf16[4,12,180]{2,1,0:T(8,128)(2,1)} %get-tuple-element.31), channel_id=1, source_target_pairs={{0,192},{1,193},{64,0},{65,1},{128,64},{129,65},{192,128},{193,129... | collective-permute-start | bytes 51848 | tf_op jit(solution)/shard_map/members/ppermute | solution.py:341
  60.8 1.9 %copy-start.18 = (bf16[4,12,180]{2,1,0:T(8,128)(2,1)}, bf16[4,12,180]{2,1,0:T(8,128)(2,1)S(1)}, u32[]{:S(2)}) copy-start(bf16[4,12,180]{2,1,0:T(8,128)(2,1)S(1)} %collective-permute-done.11.refs_4_) | copy-start | bytes 51844
  60.8 5.9 %collective-permute-start.14 = (bf16[4,12,180]{2,1,0:T(8,128)(2,1)}, bf16[4,12,180]{2,1,0:T(8,128)(2,1)}, u32[]{:S(2)}, u32[]{:S(2)}) collective-permute-start(bf16[4,12,180]{2,1,0:T(8,128)(2,1)} %get-tuple-element.31), channel_id=1, source_target_pairs={{0,193},{1,192},{64,1},{65,0},{128,65},{129,64},{192,129},{193,128... | collective-permute-start | bytes 51848 | tf_op jit(solution)/shard_map/members/ppermute | solution.py:341
  61.7 1.0 copy-start.19
  61.7 5.0 %collective-permute-start.9 = (bf16[4,12,180]{2,1,0:T(8,128)(2,1)}, bf16[4,12,180]{2,1,0:T(8,128)(2,1)}, u32[]{:S(2)}, u32[]{:S(2)}) collective-permute-start(bf16[4,12,180]{2,1,0:T(8,128)(2,1)} %get-tuple-element.29), channel_id=1, source_target_pairs={{0,64},{1,65},{64,128},{65,129},{128,192},{129,193},{192,0},{193,1... | collective-permute-start | bytes 51848 | tf_op jit(solution)/shard_map/members/ppermute | solution.py:341
  62.6 4.1 %collective-permute-start.8 = (bf16[4,12,180]{2,1,0:T(8,128)(2,1)}, bf16[4,12,180]{2,1,0:T(8,128)(2,1)}, u32[]{:S(2)}, u32[]{:S(2)}) collective-permute-start(bf16[4,12,180]{2,1,0:T(8,128)(2,1)} %get-tuple-element.28.refs_0_), channel_id=1, source_target_pairs={{0,1},{1,0},{64,65},{65,64},{128,129},{129,128},{192,193},{193,192... | collective-permute-start | bytes 51848 | tf_op jit(solution)/shard_map/members/ppermute | solution.py:341
  69.1 0.9 copy-start.4
  70.0 1.0 copy-start.10
  71.0 1.0 copy-start.12
  72.0 5.2 %copy-start.6 = (bf16[45,4004]{1,0:T(8,128)(2,1)S(1)}, bf16[45,4004]{1,0:T(8,128)(2,1)}, u32[]{:S(2)}) copy-start(bf16[45,4004]{1,0:T(8,128)(2,1)} %copy-done.5) | copy-start | bytes 1081084
  72.0 5.2 %copy-start.8 = (bf16[45,4004]{1,0:T(8,128)(2,1)S(1)}, bf16[45,4004]{1,0:T(8,128)(2,1)}, u32[]{:S(2)}) copy-start(bf16[45,4004]{1,0:T(8,128)(2,1)} %copy-done.7) | copy-start | bytes 1081084
  76.2 0.9 copy-start
  77.1 5.4 %copy-start.21 = (s32[4]{0:T(128)S(1)}, s32[4]{0:T(128)}, u32[]{:S(2)}) copy-start(s32[4]{0:T(128)} %param.18) | copy-start | bytes 52
  77.1 7.6 %collective-permute-start.16 = (bf16[96,4096]{1,0:T(8,128)(2,1)}, bf16[96,4096]{1,0:T(8,128)(2,1)}, u32[]{:S(2)}, u32[]{:S(2)}) collective-permute-start(bf16[96,4096]{1,0:T(8,128)(2,1)} %get-tuple-element.39), channel_id=1, source_target_pairs={{0,1},{1,0},{2,3},{3,2},{4,5},{5,4},{6,7},{7,6},{8,9},{9,8},{10,11... | collective-permute-start | bytes 2359304 | tf_op jit(solution)/shard_map/contract/ppermute | solution.py:377
  81.2 0.9 copy-start.2
  82.1 2.5 %collective-permute-start.18 = (bf16[96,4004]{1,0:T(8,128)(2,1)}, bf16[96,4004]{1,0:T(8,128)(2,1)S(1)}, u32[]{:S(2)}, u32[]{:S(2)}) collective-permute-start(bf16[96,4004]{1,0:T(8,128)(2,1)} %get-tuple-element.41), channel_id=1, source_target_pairs={{0,1},{1,0},{2,3},{3,2},{4,5},{5,4},{6,7},{7,6},{8,9},{9,8},{10,11... | collective-permute-start | bytes 2306312 | tf_op jit(solution)/shard_map/contract/ppermute | solution.py:377
  84.7 1.1 copy-start.1
  85.8 1.1 copy-start.3
  86.9 0.9 copy-start.13
  87.8 0.9 copy-start.14
  88.8 0.9 copy-start.15
  89.6 0.8 copy-start.16
  90.4 33.8 %copy-start.24 = (f32[1,45]{1,0:T(1,128)S(1)}, f32[1,45]{1,0:T(1,128)}, u32[]{:S(2)}) copy-start(f32[1,45]{1,0:T(1,128)} %param.20) | copy-start | bytes 544
  90.4 33.8 %copy-start.25 = (f32[1,45]{1,0:T(1,128)S(1)}, f32[1,45]{1,0:T(1,128)}, u32[]{:S(2)}) copy-start(f32[1,45]{1,0:T(1,128)} %param.21) | copy-start | bytes 544
  101.0 7.3 %collective-permute-start.19 = (f32[1,128]{1,0:T(1,128)S(1)}, f32[1,128]{1,0:T(1,128)S(1)}, u32[]{:S(2)}, u32[]{:S(2)}) collective-permute-start(f32[1,128]{1,0:T(1,128)S(1)} %get-tuple-element.45), channel_id=1, source_target_pairs={{0,64},{64,128},{128,192},{192,0},{1,65},{65,129},{129,193},{193,1... | collective-permute-start | bytes 1544 | tf_op jit(solution)/shard_map/collect/ppermute | solution.py:396
  103.0 5.2 %collective-permute-start.20 = (f32[1,128]{1,0:T(1,128)S(1)}, f32[1,128]{1,0:T(1,128)S(1)}, u32[]{:S(2)}, u32[]{:S(2)}) collective-permute-start(f32[1,128]{1,0:T(1,128)S(1)} %get-tuple-element.45), channel_id=1, source_target_pairs={{0,128},{64,192},{128,0},{192,64},{1,129},{65,193},{129,1},{193,65... | collective-permute-start | bytes 1544 | tf_op jit(solution)/shard_map/collect/ppermute | solution.py:396
  104.8 3.5 %collective-permute-start.21 = (f32[1,128]{1,0:T(1,128)S(1)}, f32[1,128]{1,0:T(1,128)S(1)}, u32[]{:S(2)}, u32[]{:S(2)}) collective-permute-start(f32[1,128]{1,0:T(1,128)S(1)} %get-tuple-element.45), channel_id=1, source_target_pairs={{0,192},{64,0},{128,64},{192,128},{1,193},{65,1},{129,65},{193,129... | collective-permute-start | bytes 1544 | tf_op jit(solution)/shard_map/collect/ppermute | solution.py:396
  (2 other events, 1.3 us)

commit v3 on v2

v3 whole, which is shorter than its diff:
```python
import jax
import jax.numpy as jnp
from jax import lax
from jax.experimental import pallas as pl
from jax.experimental.pallas import tpu as pltpu
from jax.sharding import PartitionSpec as P

smearing = 0.3
PAD = 48
WIDE = 96
CHUNK = 2048
TOP = 23


def send_kernel(rows_ref, share_ref, out_ref):
    for target in range(out_ref.shape[0]):
        out_ref[target] = share_ref[rows_ref[0, target]]


def pick_kernel(table_ref, arrived_ref, phase_ref, out_ref):
    for triplet in range(4):
        for member in range(3):
            block = arrived_ref[table_ref[triplet, member]]
            out_ref[2 * triplet, member] = block
            out_ref[2 * triplet + 1, member] = block
        out_ref[2 * triplet, 3] = phase_ref[triplet]
        out_ref[2 * triplet + 1, 3] = phase_ref[triplet]


def whole_record(members_ref, slot):
    parts = [members_ref[j, slot].astype(jnp.float32) for j in range(8)]
    rows = jnp.concatenate(parts, axis=0)
    fill = jnp.zeros((WIDE, 38), jnp.float32)
    return jnp.concatenate([rows[:, 0:90], fill, rows[:, 90:180], fill], axis=1)


def operand_kernel(
    where_ref, members_ref, early_ref, late_ref, middle_ref, last_ref, tables_ref, scalars_ref
):
    rank, first, mult = where_ref[0], where_ref[1] == 0, where_ref[2]
    f32 = jnp.float32
    records = [whole_record(members_ref, member) for member in range(3)]
    lead_r, lead_i = records[0][:, 0:128].T, records[0][:, 128:256].T

    def halves(array):
        low, high = array[0:PAD], array[45 : 45 + PAD]
        return jnp.where(first, low, high), jnp.where(first, high, low)

    def sides(array):
        low, high = array[:, 0:PAD], array[:, 45 : 45 + PAD]
        return jnp.where(first, low, high), jnp.where(first, high, low)

    row = lax.broadcasted_iota(jnp.int32, (PAD, WIDE), 0)
    column = lax.broadcasted_iota(jnp.int32, (PAD, WIDE), 1)

    def spread(array, start, count):
        taken = (column // 2 + start == row) & (column < 2 * count)
        return jnp.dot(array, taken.astype(f32), preferred_element_type=f32)

    def turned(real, imag, offset):
        trig = members_ref[2 * ((rank + offset) & 3), 3].astype(f32)
        even = lax.broadcasted_iota(jnp.int32, (1, real.shape[1]), 1) % 2 == 0
        cosine = jnp.where(even, trig[0:1, 0:1], trig[0:1, 2:3])
        sine = jnp.where(even, trig[0:1, 1:2], trig[0:1, 3:4])
        return jnp.concatenate([cosine * real - sine * imag, cosine * imag + sine * real], axis=0)

    columns = []
    for array in (lead_r, lead_i):
        columns.append([halves(side) for side in sides(array)])
    whole = [[spread(columns[i][0][h], 0, 45) for i in range(2)] for h in range(2)]
    early_ref[...] = jnp.concatenate(
        [
            jnp.concatenate([turned(*whole[h], offset) for h in range(2)], axis=0)
            for offset in (0, 3, 1)
        ],
        axis=1,
    ).astype(early_ref.dtype)
    parts = []
    for side in range(2):
        for start, count in ((0, TOP), (TOP, 45 - TOP)):
            real, imag = (spread(columns[i][side][0], start, count)[:, 0:PAD] for i in range(2))
            parts.append(turned(real, imag, 2))
    late_ref[...] = jnp.concatenate(parts, axis=1).astype(late_ref.dtype)

    mid_r, mid_i = records[1][:, 0:128].T, records[1][:, 128:256].T
    within = lax.broadcasted_iota(jnp.int32, (WIDE, WIDE), 1) < 90
    real = jnp.where(within, mid_r[0:WIDE], 0.0)
    imag = jnp.where(within, mid_i[0:WIDE], 0.0)
    middle_ref[...] = jnp.concatenate(
        [jnp.concatenate([real, -imag], axis=1), jnp.concatenate([imag, real], axis=1)], axis=0
    ).astype(middle_ref.dtype)

    last_r, last_i = records[2][:, 0:128], records[2][:, 128:256]
    within = lax.broadcasted_iota(jnp.int32, (WIDE, 128), 0) < 90
    real = jnp.where(within, last_r, 0.0)
    imag = jnp.where(within, last_i, 0.0)
    zeros = jnp.zeros((32, 256), f32)
    last_ref[...] = jnp.concatenate(
        [
            jnp.concatenate([real, imag], axis=1),
            zeros,
            jnp.concatenate([-imag, real], axis=1),
            zeros,
        ],
        axis=0,
    ).astype(last_ref.dtype)

    row = lax.broadcasted_iota(jnp.int32, (WIDE, 128), 0)
    column = lax.broadcasted_iota(jnp.int32, (WIDE, 128), 1)
    one = jnp.where(row < 90, jnp.broadcast_to(mid_r[0:WIDE, 90:91], (WIDE, 128)), 1.0)
    two = jnp.where(column < 90, jnp.broadcast_to(last_r[90:91, :], (WIDE, 128)), 1.0)
    tables_ref[0] = one + two
    tables_ref[1] = one - two
    tables_ref[2] = 1.0 / (one * two)
    tables_ref[3] = jnp.broadcast_to(mid_i[0:WIDE, 90:91], (WIDE, 128)) + jnp.broadcast_to(
        last_i[90:91, :], (WIDE, 128)
    )
    zero = halves(lead_r[:, 90:91])[0]
    zero = jnp.where(lax.broadcasted_iota(jnp.int32, (PAD, 1), 0) < 45, zero, 1.0)
    scalars_ref[0] = jnp.broadcast_to(zero, (PAD, 128))
    scalars_ref[1] = jnp.broadcast_to(mult.astype(f32) / zero, (PAD, 128))


def rows_of(ref, cols, count):
    values = ref[:, :, cols]
    rows = values.shape[0] * values.shape[1]
    return jnp.pad(values.reshape(rows, values.shape[2]), ((0, count - rows), (0, 0)))


def early_kernel(lead_ref, own_ref, low_ref, high_ref, mine_ref, far_ref):
    total = own_ref.shape[2]
    for start in range(0, total, CHUNK):
        cols = slice(start, min(start + CHUNK, total))
        product = jnp.dot(
            lead_ref[...],
            jnp.concatenate([rows_of(ref, cols, WIDE) for ref in (own_ref, low_ref, high_ref)], axis=0),
            preferred_element_type=jnp.float32,
        )
        mine_ref[:, cols] = product[0:WIDE].astype(mine_ref.dtype)
        far_ref[:, cols] = product[WIDE:].astype(far_ref.dtype)


def interaction_kernel(
    scalars_ref,
    middle_ref,
    last_ref,
    tables_ref,
    late_ref,
    top_ref,
    bottom_ref,
    far_top_ref,
    far_bottom_ref,
    mine_ref,
    other_ref,
    out_ref,
    flat,
    windows,
    mid_real,
    mid_imag,
    rate_acc,
    couple_acc,
):
    total = mine_ref.shape[1]
    flat[:, 8064:8320] = jnp.zeros((WIDE, 256), flat.dtype)
    for start in range(0, total, 1024):
        cols = slice(start, min(start + 1024, total))
        late = (top_ref, bottom_ref, far_top_ref, far_bottom_ref)
        both = mine_ref[:, cols].astype(jnp.float32) + other_ref[:, cols].astype(jnp.float32)
        both = both + jnp.dot(
            late_ref[...],
            jnp.concatenate([rows_of(ref, cols, PAD) for ref in late], axis=0),
            preferred_element_type=jnp.float32,
        )
        flat[:, cols] = both.astype(flat.dtype)
    for b in range(90):
        tile, shift = divmod(90 * b, 128)
        pair = flat[:, tile * 128 : tile * 128 + 256]
        window = pair[:, shift : shift + 128]
        windows[b * PAD : (b + 1) * PAD, 0:128] = window[0:PAD]
        windows[b * PAD : (b + 1) * PAD, 128:256] = window[PAD:]
    zeros = jnp.zeros((PAD, 128), jnp.float32)
    for b in range(90, WIDE):
        mid_real[pl.ds(b, PAD, stride=WIDE), :] = zeros
        mid_imag[pl.ds(b, PAD, stride=WIDE), :] = zeros
    for group in range(9):
        product = jnp.dot(
            windows[group * 480 : (group + 1) * 480, :],
            last_ref[...],
            preferred_element_type=jnp.float32,
        )
        for i in range(10):
            rows = pl.ds(group * 10 + i, PAD, stride=WIDE)
            mid_real[rows, :] = product[i * PAD : (i + 1) * PAD, 0:128]
            mid_imag[rows, :] = product[i * PAD : (i + 1) * PAD, 128:256]

    scaled = 0.5 / (smearing * smearing)
    def two_modes(s):
        low = pl.ds(pl.multiple_of(s * WIDE, WIDE), WIDE)
        high = pl.ds(pl.multiple_of(s * WIDE + WIDE, WIDE), WIDE)
        operand = jnp.concatenate(
            [
                jnp.concatenate([ref[low, :], ref[high, :]], axis=1).astype(jnp.bfloat16)
                for ref in (mid_real, mid_imag)
            ],
            axis=0,
        )
        value = jnp.dot(middle_ref[...], operand, preferred_element_type=jnp.float32)
        for i in range(2):
            real = value[0:WIDE, 128 * i : 128 * i + 128]
            imag = value[WIDE:, 128 * i : 128 * i + 128]
            freq = scalars_ref[0, pl.ds(s + i, 1), :]
            decays = freq - tables_ref[0]
            merges = freq + tables_ref[1]
            weight = (real * real + imag * imag) * (
                jnp.exp(-scaled * decays * decays) + jnp.exp(-scaled * merges * merges)
            )
            weight = weight * tables_ref[2] * scalars_ref[1, pl.ds(s + i, 1), :]
            at = pl.ds(pl.multiple_of((s + i) * 8, 8), 8)
            rate_acc[at, :] = jnp.sum(weight.reshape(WIDE // 8, 8, 128), axis=0)
            weight = weight * tables_ref[3]
            couple_acc[at, :] = jnp.sum(weight.reshape(WIDE // 8, 8, 128), axis=0)

    @pl.loop(0, 12)
    def _(i):
        two_modes(4 * i)
        two_modes(4 * i + 2)

    sums = jnp.concatenate(
        [
            jnp.sum(rate_acc[...].reshape(PAD, 8, 128), axis=1),
            jnp.sum(couple_acc[...].reshape(PAD, 8, 128), axis=1),
        ],
        axis=0,
    )
    out_ref[:, 0:WIDE] = lax.dot_general(
        jnp.ones((8, 128), jnp.float32),
        sums,
        (((1,), (1,)), ((), ())),
        precision=lax.Precision.HIGHEST,
        preferred_element_type=jnp.float32,
    )
    out_ref[:, WIDE:128] = jnp.zeros((8, 128 - WIDE), jnp.float32)


VMEM = pl.BlockSpec(memory_space=pltpu.VMEM)
SMEM = pl.BlockSpec(memory_space=pltpu.SMEM)
PARAMS = pltpu.CompilerParams(vmem_limit_bytes=56 << 20)


def ring(count, step):
    return [(i, (i + step) % count) for i in range(count)]


def body(
    force_third,
    phase_angle,
    eigenvectors,
    frequencies,
    deviation,
    send_rows,
    trip_table,
    irreducible,
    multiplicity,
    drive_term,
    boundary,
):
    f32, b16 = jnp.float32, jnp.bfloat16
    clus = lax.axis_index("clus")
    mode = lax.axis_index("mode")
    group = ("clus", "mode")

    with jax.named_scope("records"):
        extra = jnp.concatenate([frequencies, deviation], axis=1)[:, None, :]
        record = jnp.concatenate(
            [eigenvectors, extra, jnp.zeros((extra.shape[0], 5, 180), b16)], axis=1
        )
        share = lax.dynamic_slice_in_dim(record, 12 * (2 * clus + mode), 12, 1)
        chosen = pl.pallas_call(
            send_kernel,
            out_shape=jax.ShapeDtypeStruct((send_rows.shape[1],) + share.shape[1:], b16),
            in_specs=[SMEM, VMEM],
            out_specs=VMEM,
            compiler_params=PARAMS,
        )(send_rows, share)
        arrived = lax.all_to_all(chosen, "trip", 0, 0, tiled=True)
        angles = phase_angle.astype(f32)
        trig = jnp.stack([jnp.cos(angles), jnp.sin(angles)], axis=1).astype(b16)
        phases = jnp.pad(trig.reshape(4, 4).T[:, None, :], ((0, 0), (0, 11), (0, 176)))

    with jax.named_scope("force"):
        own = jnp.transpose(force_third, (1, 0, 2))
        low = lax.ppermute(own, "clus", ring(4, 1))
        high = lax.ppermute(own, "clus", ring(4, 3))
        low, high, _ = lax.optimization_barrier((low, high, arrived))
        top = lax.ppermute(low[:TOP], "clus", ring(4, 1))
        bottom = lax.ppermute(high[TOP:], "clus", ring(4, 3))

    with jax.named_scope("members"):
        picks = pl.pallas_call(
            pick_kernel,
            out_shape=jax.ShapeDtypeStruct((8, 4, 12, 180), b16),
            in_specs=[SMEM, VMEM, VMEM],
            out_specs=VMEM,
            compiler_params=PARAMS,
        )(trip_table, arrived, phases)
        members = lax.all_to_all(picks, group, 0, 0, tiled=True)

    with jax.named_scope("operands"):
        mult = lax.dynamic_index_in_dim(multiplicity, clus, 0, keepdims=False)
        where = jnp.stack([clus, mode, mult]).astype(jnp.int32)
        early, late, mid, last_all, tables, scalars = pl.pallas_call(
            operand_kernel,
            out_shape=(
                jax.ShapeDtypeStruct((2 * WIDE, 3 * WIDE), b16),
                jax.ShapeDtypeStruct((WIDE, 4 * PAD), b16),
                jax.ShapeDtypeStruct((2 * WIDE, 2 * WIDE), b16),
                jax.ShapeDtypeStruct((256, 256), b16),
                jax.ShapeDtypeStruct((4, WIDE, 128), f32),
                jax.ShapeDtypeStruct((2, PAD, 128), f32),
            ),
            in_specs=[SMEM, VMEM],
            out_specs=(VMEM,) * 6,
            compiler_params=PARAMS,
        )(where, members)

    with jax.named_scope("contract"):
        total = force_third.shape[2]
        swap = [(0, 1), (1, 0)]
        mine, far = pl.pallas_call(
            early_kernel,
            out_shape=(jax.ShapeDtypeStruct((WIDE, total), b16),) * 2,
            in_specs=[VMEM] * 4,
            out_specs=(VMEM,) * 2,
            compiler_params=PARAMS,
            cost_estimate=pl.CostEstimate(
                flops=2 * 192 * 288 * total, bytes_accessed=1200 * total, transcendentals=0
            ),
        )(early, own, low, high)
        other = lax.ppermute(far, "mode", swap)
        far_top = lax.ppermute(top, "mode", swap)
        far_bottom = lax.ppermute(bottom, "mode", swap)

    with jax.named_scope("interaction"):
        sums = pl.pallas_call(
            interaction_kernel,
            out_shape=jax.ShapeDtypeStruct((8, 128), f32),
            in_specs=[VMEM] * 11,
            out_specs=VMEM,
            scratch_shapes=[
                pltpu.VMEM((WIDE, 8320), b16),
                pltpu.VMEM((90 * PAD, 256), b16),
                pltpu.VMEM((PAD * WIDE, 128), f32),
                pltpu.VMEM((PAD * WIDE, 128), f32),
                pltpu.VMEM((8 * PAD, 128), f32),
                pltpu.VMEM((8 * PAD, 128), f32),
            ],
            compiler_params=PARAMS,
        )(scalars, mid, last_all, tables, late, top, bottom, far_top, far_bottom, mine, other)
    with jax.named_scope("collect"):
        own_row = sums[0:1]
        rows = [own_row] + [lax.ppermute(own_row, "clus", ring(4, step)) for step in (1, 2, 3)]
        points = jnp.arange(32, dtype=jnp.int32)
        partial = jnp.zeros((32, 128), f32)
        for step in range(4):
            point = lax.dynamic_index_in_dim(irreducible, (clus - step) % 4, 0, keepdims=False)
            partial = partial + jnp.where((points == point)[:, None], rows[step], 0.0)
        received = lax.all_to_all(partial[:, None, :], "trip", 0, 0, tiled=True)
        final = jnp.sum(received[:, 0, :], axis=0)[None, :]
        gamma_total = final[:, 0:45] + boundary
        return gamma_total, (drive_term + final[:, PAD : PAD + 45]) / gamma_total


def solution(mesh):
    return jax.shard_map(
        body,
        mesh=mesh,
        in_specs=(
            P("clus", "mode", None),
            P("clus", "trip"),
            P("trip", None, None),
            P("trip", None),
            P("trip", None),
            P("trip", None),
            P("trip", None),
            P("trip"),
            P("trip"),
            P("trip", "mode"),
            P("trip", "mode"),
        ),
        out_specs=(P("trip", "mode"), P("trip", "mode")),
        check_vma=False,
    )
```

time: 126 us -> 120 us (0.952)
  waiting for transfers between devices: 3.94 us -> 31.7 us
  blocking collectives: 38.6 us -> 14.6 us
  local copies, waits for them, and re-layouts: 24.6 us -> 13.5 us
    all_to_all x1 -> x0, blocking collectives: 23 us -> none  [body(): arrived = lax.all_to_all(chosen, 'trip', 0, 0, tiled=True)]
    ppermute x19 -> x7, starting transfers between devices: 20.9 us -> 4.62 us  [the longest x1 2.09 us: body(): bottom = lax.ppermute(high[TOP:], 'clus', ring(4, 3))]
    all_to_all x0 -> x2, starting transfers between devices: none -> 16.2 us  [the longest x1 11.1 us: body(): arrived = lax.all_to_all(chosen, 'trip', 0, 0, tiled=True)]
    all_to_all x0 -> x2, waiting for transfers between devices: none -> 14.5 us  [the longest x1 11 us: body(): arrived = lax.all_to_all(chosen, 'trip', 0, 0, tiled=True)]
    ppermute x19 -> x7, waiting for transfers between devices: 3.83 us -> 17.2 us  [the longest x1 15.4 us: body(): top = lax.ppermute(low[:TOP], 'clus', ring(4, 1))]
    unnamed x58 -> x23, local copies, waits for them, and re-layouts: 14.9 us -> 4.76 us
    dynamic_slice x1 -> x0, local copies, waits for them, and re-layouts: 3.84 us -> none  [body(): lax.dynamic_index_in_dim(force_third, color, 0, keepdims=False)]
    pallas_call x4 -> x3, Pallas kernels: 12.2 us -> 9.8 us  [the longest x1 5.79 us: body(): pl.pallas_call(early_kernel, out_shape=(jax.ShapeDtypeStruct((WIDE, total...]
  transfers between devices with their start and end apart: 22 -> 12, of which waited for: 7 -> 5; matrix products, arithmetic and copies ran while one was open for 9% -> 12% of each run, Pallas kernels for 11% -> 5%
where the time goes in v3:
time: 120 us; the launch traced here: 119 us
  waiting for transfers between devices  31.7 us (26%)
  starting transfers between devices  27.9 us (23%)
  Pallas kernels  24.2 us (20%)
  blocking collectives  14.6 us (12%)
  local copies, waits for them, and re-layouts  13.5 us (11%)
  other arithmetic  6.15 us (5%)
    ppermute x1, waiting for transfers between devices, body(): top = lax.ppermute(low[:TOP], 'clus', ring(4, 1))  15.4 us
    all_to_all x1, blocking collectives, body(): received = lax.all_to_all(partial[:, None, :], 'trip', 0, 0, tiled=True)  14.6 us
    pallas_call x1, Pallas kernels, body(): pl.pallas_call(interaction_kernel, out_shape=jax.ShapeDtypeStruct((8, 128...  12.8 us
    all_to_all x1, starting transfers between devices, body(): arrived = lax.all_to_all(chosen, 'trip', 0, 0, tiled=True)  11.1 us
    all_to_all x1, waiting for transfers between devices, body(): arrived = lax.all_to_all(chosen, 'trip', 0, 0, tiled=True)  11 us
    ppermute x3, starting transfers between devices, body(): lax.ppermute(own_row, 'clus', ring(4, step))  7.05 us
    pallas_call x1, Pallas kernels, body(): pl.pallas_call(early_kernel, out_shape=(jax.ShapeDtypeStruct((WIDE, total...  5.79 us
    all_to_all x1, starting transfers between devices, body(): members = lax.all_to_all(picks, group, 0, 0, tiled=True)  5.04 us
  transfers between devices with their start and end apart: 12, of which 5 were waited for; matrix products, arithmetic and copies ran while one was open for 12% of the time, Pallas kernels for 5%

profile of v3, /device:TPU:2, one launch (start us, length us, event | category | flops | bytes accessed | tf_op | source)
XLA Modules:
  0.0 118.8 jit_solution(14328344985682668322)
XLA Ops:
  0.6 1.6 %collective-permute-start = (bf16[45,2,8100]{2,1,0:T(2,128)(2,1)}, bf16[45,2,8100]{2,1,0:T(2,128)(2,1)S(1)}, u32[]{:S(2)}, u32[]{:S(2)}) collective-permute-start(bf16[45,2,8100]{2,1,0:T(2,128)(2,1)} %bitcast.25), channel_id=1, source_target_pairs={{0,64},{64,128},{128,192},{192,0},{1,65},{65,129},{129,193},{193,1... | collective-permute-start | bytes 4374008 | tf_op jit(solution)/shard_map/force/ppermute | solution.py:292
  2.2 0.9 collective-permute-start.1
  3.1 1.1 copy.36
  4.1 0.0 copy-start.10
  4.2 0.8 maximum_bitcast_fusion
  5.0 0.1 pad_dynamic-slice_fusion.2
  5.0 0.7 fusion.1.share_ref
  5.7 1.6 %records.1 = bf16[32,12,180]{2,1,0:T(8,128)(2,1)} custom-call(s32[1,32]{1,0:T(1,128)} %rows_ref.1, bf16[8,12,180]{2,1,0:T(8,128)(2,1)} %fusion.1.share_ref), custom_call_target="tpu_custom_call" | custom-call | tf_op jit(solution)/shard_map/records/pallas_call | solution.py:278
  7.3 11.1 %all-to-all-start = ((bf16[32,12,180]{2,1,0:T(8,128)(2,1)}), bf16[32,12,180]{2,1,0:T(8,128)(2,1)S(1)}, u32[]{:S(2)}, u32[]{:S(2)}) async-start(bf16[32,12,180]{2,1,0:T(8,128)(2,1)} %records.1), calls=%async_computation | async-start | bytes 524288 | tf_op jit(solution)/shard_map/records/all_to_all | solution.py:285
  18.6 0.1 copy.40
  18.7 0.6 pad.4.phase_ref
  19.3 11.0 %all-to-all-done.arrived_ref = bf16[32,12,180]{2,1,0:T(8,128)(2,1)S(1)} async-done(((bf16[32,12,180]{2,1,0:T(8,128)(2,1)}), bf16[32,12,180]{2,1,0:T(8,128)(2,1)S(1)}, u32[]{:S(2)}, u32[]{:S(2)}) %all-to-all-start) | async-done | bytes 138272 | tf_op jit(solution)/shard_map/records/all_to_all | solution.py:285
  30.3 0.7 copy-done.3
  31.0 1.7 %members.1 = bf16[8,4,12,180]{3,2,1,0:T(8,128)(2,1)} custom-call(s32[4,3]{1,0:T(4,128)} %table_ref.1, bf16[32,12,180]{2,1,0:T(8,128)(2,1)} %copy-done.3, bf16[4,12,180]{2,1,0:T(8,128)(2,1)} %pad.4.phase_ref), custom_call_target="tpu_custom_call" | custom-call | tf_op jit(solution)/shard_map/members/pallas_call | solution.py:299
  32.7 1.7 %copy.41 = bf16[8,4,12,180]{3,1,2,0:T(4,128)(2,1)} copy(bf16[8,4,12,180]{3,2,1,0:T(8,128)(2,1)} %members.1) | data formatting | bytes 276480 | tf_op jit(solution)/shard_map/members/pallas_call | solution.py:299
  34.4 5.0 %all-to-all-start.1 = ((bf16[8,4,12,180]{3,1,2,0:T(4,128)(2,1)}), bf16[8,4,12,180]{3,1,2,0:T(4,128)(2,1)S(1)}, u32[]{:S(2)}, u32[]{:S(2)}) async-start(bf16[8,4,12,180]{3,1,2,0:T(4,128)(2,1)} %copy.41), calls=%async_computation.1 | async-start | bytes 393216 | tf_op jit(solution)/shard_map/members/all_to_all | solution.py:306
  39.4 0.6 dynamic_slice.20
  40.0 1.3 %pad_add_fusion.where_ref = s32[3]{0:T(128)} fusion(s32[1]{0:T(128)} %dynamic_slice.20, s32[1]{0:T(128)} %bitcast.2, s32[1]{0:T(128)} %bitcast.1), kind=kLoop, calls=%fused_computation.20 | loop fusion | flops 6 | bytes 24 | tf_op jit(solution)/shard_map/operands/stack | solution.py:310
  41.3 3.6 %all-to-all-done.1 = bf16[8,4,12,180]{3,1,2,0:T(4,128)(2,1)S(1)} async-done(((bf16[8,4,12,180]{3,1,2,0:T(4,128)(2,1)}), bf16[8,4,12,180]{3,1,2,0:T(4,128)(2,1)S(1)}, u32[]{:S(2)}, u32[]{:S(2)}) %all-to-all-start.1) | async-done | bytes 138272 | tf_op jit(solution)/shard_map/members/all_to_all | solution.py:306
  44.8 0.7 copy.42.members_ref
  45.6 2.3 %operands.1 = (bf16[192,288]{1,0:T(8,128)(2,1)}, bf16[96,192]{1,0:T(8,128)(2,1)}, bf16[192,192]{1,0:T(8,128)(2,1)}, bf16[256,256]{1,0:T(8,128)(2,1)}, f32[4,96,128]{2,1,0:T(8,128)}, /*index=5*/f32[2,48,128]{2,1,0:T(8,128)}) custom-call(s32[3]{0:T(128)} %pad_add_fusion.where_ref, bf16[8,4,12,180]{3,2,1,0:T(8,128)(2,1)} %copy.42.members_ref), custom_call_target="tpu_custom_call" | custom-call | tf_op jit(solution)/shard_map/operands/pallas_call | solution.py:311
  47.9 0.0 collective-permute-done.low_ref
  47.9 0.0 collective-permute-done.1.high_ref
  47.9 1.1 copy-done
  49.0 0.5 copy-done.1
  49.5 5.8 %contract.1 = (bf16[96,8100]{1,0:T(8,128)(2,1)}, bf16[96,8100]{1,0:T(8,128)(2,1)}) custom-call(bf16[192,288]{1,0:T(8,128)(2,1)} %get-tuple-element.19.lead_ref, bf16[45,2,8100]{2,1,0:T(2,128)(2,1)} %bitcast.27, bf16[45,2,8100]{2,1,0:T(2,128)(2,1)} %copy-done, bf16[45,2,8100]{2,1,0:T(2,128)(2,1)} %copy-done.1), custom_call_target="tpu_custom_call" | custom-call | flops 895795200 | bytes 9720000 | tf_op jit(solution)/shard_map/contract/pallas_call | solution.py:329
  55.3 1.8 %slice.17 = bf16[23,2,8100]{2,1,0:T(2,128)(2,1)S(1)} slice(bf16[45,2,8100]{2,1,0:T(2,128)(2,1)} %copy-done), slice={[0:23], [0:2], [0:8100]} | slice | bytes 1490400 | tf_op jit(solution)/shard_map/force/slice | solution.py:295
  57.1 0.1 collective-permute-start.2
  57.2 1.7 %slice.18 = bf16[22,2,8100]{2,1,0:T(2,128)(2,1)S(1)} slice(bf16[45,2,8100]{2,1,0:T(2,128)(2,1)} %copy-done.1), slice={[23:45], [0:2], [0:8100]} | slice | bytes 1425600 | tf_op jit(solution)/shard_map/force/slice | solution.py:296
  58.9 2.1 %collective-permute-start.3 = (bf16[22,2,8100]{2,1,0:T(2,128)(2,1)S(1)}, bf16[22,2,8100]{2,1,0:T(2,128)(2,1)}, u32[]{:S(2)}, u32[]{:S(2)}) collective-permute-start(bf16[22,2,8100]{2,1,0:T(2,128)(2,1)S(1)} %slice.18), channel_id=1, source_target_pairs={{0,192},{64,0},{128,64},{192,128},{1,193},{65,1},{129,65},{193,129... | collective-permute-start | bytes 2138408 | tf_op jit(solution)/shard_map/force/ppermute | solution.py:296
  61.0 15.4 %collective-permute-done.2.top_ref = bf16[23,2,8100]{2,1,0:T(2,128)(2,1)S(1)} collective-permute-done((bf16[23,2,8100]{2,1,0:T(2,128)(2,1)S(1)}, bf16[23,2,8100]{2,1,0:T(2,128)(2,1)S(1)}, u32[]{:S(2)}, u32[]{:S(2)}) %collective-permute-start.2) | collective-permute-done | bytes 745232 | tf_op jit(solution)/shard_map/force/ppermute | solution.py:295
  76.4 1.2 %collective-permute-done.3.bottom_ref = bf16[22,2,8100]{2,1,0:T(2,128)(2,1)} collective-permute-done((bf16[22,2,8100]{2,1,0:T(2,128)(2,1)S(1)}, bf16[22,2,8100]{2,1,0:T(2,128)(2,1)}, u32[]{:S(2)}, u32[]{:S(2)}) %collective-permute-start.3) | collective-permute-done | bytes 712832 | tf_op jit(solution)/shard_map/force/ppermute | solution.py:296
  77.6 0.0 collective-permute-start.5
  77.7 0.7 fusion.9
  78.3 1.3 %iota_compare_fusion.2 = (pred[32]{0:T(512)(128)(4,1)S(1)}, pred[32]{0:T(512)(128)(4,1)S(1)}) fusion(s32[]{:T(128)} %bitcast.11, s32[]{:T(128)} %bitcast), kind=kLoop, calls=%fused_computation.25 | loop fusion | flops 64 | bytes 72 | tf_op jit(solution)/shard_map/collect/eq | solution.py:366
  79.6 0.6 collective-permute-done.5.far_bottom_ref
  80.2 0.8 copy-done.5
  81.1 0.5 copy-done.2
  81.6 12.8 %interaction.1 = f32[8,128]{1,0:T(8,128)} custom-call(f32[2,48,128]{2,1,0:T(8,128)} %get-tuple-element.12.scalars_ref, bf16[192,192]{1,0:T(8,128)(2,1)} %get-tuple-element.13.middle_ref, bf16[256,256]{1,0:T(8,128)(2,1)} %get-tuple-element.14.last_ref, f32[4,96,128]{2,1,0:T(8,128)} %get-tuple-element.15.tables_ref, ...), custom_call_target="tpu_custom_call" | custom-call | tf_op jit(solution)/shard_map/interaction/pallas_call | solution.py:344
  94.4 0.7 slice_bitcast_fusion
  95.1 2.0 %collective-permute-start.7 = (f32[1,128]{1,0:T(1,128)S(1)}, f32[1,128]{1,0:T(1,128)S(1)}, u32[]{:S(2)}, u32[]{:S(2)}) collective-permute-start(f32[1,128]{1,0:T(1,128)S(1)} %get-tuple-element.25), channel_id=1, source_target_pairs={{0,64},{64,128},{128,192},{192,0},{1,65},{65,129},{129,193},{193,1... | collective-permute-start | bytes 1544 | tf_op jit(solution)/shard_map/collect/ppermute | solution.py:361
  97.1 2.5 %collective-permute-start.8 = (f32[1,128]{1,0:T(1,128)S(1)}, f32[1,128]{1,0:T(1,128)S(1)}, u32[]{:S(2)}, u32[]{:S(2)}) collective-permute-start(f32[1,128]{1,0:T(1,128)S(1)} %get-tuple-element.25), channel_id=1, source_target_pairs={{0,128},{64,192},{128,0},{192,64},{1,129},{65,193},{129,1},{193,65... | collective-permute-start | bytes 1544 | tf_op jit(solution)/shard_map/collect/ppermute | solution.py:361
  99.7 2.5 %collective-permute-start.9 = (f32[1,128]{1,0:T(1,128)S(1)}, f32[1,128]{1,0:T(1,128)S(1)}, u32[]{:S(2)}, u32[]{:S(2)}) collective-permute-start(f32[1,128]{1,0:T(1,128)S(1)} %get-tuple-element.25), channel_id=1, source_target_pairs={{0,192},{64,0},{128,64},{192,128},{1,193},{65,1},{129,65},{193,129... | collective-permute-start | bytes 1544 | tf_op jit(solution)/shard_map/collect/ppermute | solution.py:361
  102.1 1.3 %iota_compare_fusion = (pred[32]{0:T(512)(128)(4,1)S(1)}, pred[32]{0:T(512)(128)(4,1)S(1)}) fusion(s32[]{:T(128)} %bitcast.15, s32[]{:T(128)} %bitcast.13), kind=kLoop, calls=%fused_computation.23 | loop fusion | flops 64 | bytes 72 | tf_op jit(solution)/shard_map/collect/eq | solution.py:366
  103.4 0.0 collective-permute-done.9
  103.4 0.2 fusion.4
  103.6 14.6 %all_to_all.15 = f32[32,1,128]{2,1,0:T(1,128)S(1)} all-to-all(f32[32,1,128]{2,1,0:T(1,128)S(1)} %fusion.4), channel_id=1, replica_groups=mesh['clus'=4,'trip'=32,'mode'=2] {'trip'}, dimensions={0} | all-to-all | bytes 32768 | tf_op jit(solution)/shard_map/collect/all_to_all | solution.py:367
  118.3 0.6 add_divide_fusion
  (28 shorter events, 0.1 us)
Async XLA Ops:
  0.6 17.9 %copy-start.9 = (bf16[2,4]{1,0:T(2,128)(2,1)S(1)}, bf16[2,4]{1,0:T(2,128)(2,1)}, u32[]{:S(2)}) copy-start(bf16[2,4]{1,0:T(2,128)(2,1)} %param.12) | copy-start | bytes 52
  0.6 47.3 %collective-permute-start = (bf16[45,2,8100]{2,1,0:T(2,128)(2,1)}, bf16[45,2,8100]{2,1,0:T(2,128)(2,1)S(1)}, u32[]{:S(2)}, u32[]{:S(2)}) collective-permute-start(bf16[45,2,8100]{2,1,0:T(2,128)(2,1)} %bitcast.25), channel_id=1, source_target_pairs={{0,64},{64,128},{128,192},{192,0},{1,65},{65,129},{129,193},{193,1... | collective-permute-start | bytes 4374008 | tf_op jit(solution)/shard_map/force/ppermute | solution.py:292
  2.2 45.7 %collective-permute-start.1 = (bf16[45,2,8100]{2,1,0:T(2,128)(2,1)}, bf16[45,2,8100]{2,1,0:T(2,128)(2,1)S(1)}, u32[]{:S(2)}, u32[]{:S(2)}) collective-permute-start(bf16[45,2,8100]{2,1,0:T(2,128)(2,1)} %bitcast.26), channel_id=1, source_target_pairs={{0,192},{64,0},{128,64},{192,128},{1,193},{65,1},{129,65},{193,129... | collective-permute-start | bytes 4374008 | tf_op jit(solution)/shard_map/force/ppermute | solution.py:293
  4.1 35.3 %copy-start.10 = (s32[4]{0:T(128)S(1)}, s32[4]{0:T(128)}, u32[]{:S(2)}) copy-start(s32[4]{0:T(128)} %param.19) | copy-start | bytes 52
  7.3 22.9 %all-to-all-start = ((bf16[32,12,180]{2,1,0:T(8,128)(2,1)}), bf16[32,12,180]{2,1,0:T(8,128)(2,1)S(1)}, u32[]{:S(2)}, u32[]{:S(2)}) async-start(bf16[32,12,180]{2,1,0:T(8,128)(2,1)} %records.1), calls=%async_computation | async-start | bytes 524288 | tf_op jit(solution)/shard_map/records/all_to_all | solution.py:285
  30.3 0.7 copy-start.3
  34.4 10.5 %all-to-all-start.1 = ((bf16[8,4,12,180]{3,1,2,0:T(4,128)(2,1)}), bf16[8,4,12,180]{3,1,2,0:T(4,128)(2,1)S(1)}, u32[]{:S(2)}, u32[]{:S(2)}) async-start(bf16[8,4,12,180]{3,1,2,0:T(4,128)(2,1)} %copy.41), calls=%async_computation.1 | async-start | bytes 393216 | tf_op jit(solution)/shard_map/members/all_to_all | solution.py:306
  47.9 1.1 copy-start
  47.9 1.6 %copy-start.1 = (bf16[45,2,8100]{2,1,0:T(2,128)(2,1)}, bf16[45,2,8100]{2,1,0:T(2,128)(2,1)S(1)}, u32[]{:S(2)}) copy-start(bf16[45,2,8100]{2,1,0:T(2,128)(2,1)S(1)} %collective-permute-done.1.high_ref) | copy-start | bytes 4374004
  55.3 22.3 %copy-start.6 = (s32[4]{0:T(128)S(1)}, s32[4]{0:T(128)}, u32[]{:S(2)}) copy-start(s32[4]{0:T(128)} %param.18) | copy-start | bytes 52
  55.3 24.9 %collective-permute-start.6 = (bf16[96,8100]{1,0:T(8,128)(2,1)}, bf16[96,8100]{1,0:T(8,128)(2,1)S(1)}, u32[]{:S(2)}, u32[]{:S(2)}) collective-permute-start(bf16[96,8100]{1,0:T(8,128)(2,1)} %get-tuple-element.21), channel_id=1, source_target_pairs={{0,1},{1,0},{2,3},{3,2},{4,5},{5,4},{6,7},{7,6},{8,9},{9,8},{10,11... | collective-permute-start | bytes 4665608 | tf_op jit(solution)/shard_map/contract/ppermute | solution.py:339
  57.1 19.3 %collective-permute-start.2 = (bf16[23,2,8100]{2,1,0:T(2,128)(2,1)S(1)}, bf16[23,2,8100]{2,1,0:T(2,128)(2,1)S(1)}, u32[]{:S(2)}, u32[]{:S(2)}) collective-permute-start(bf16[23,2,8100]{2,1,0:T(2,128)(2,1)S(1)} %slice.17), channel_id=1, source_target_pairs={{0,64},{64,128},{128,192},{192,0},{1,65},{65,129},{129,193},{193,1... | collective-permute-start | bytes 2235608 | tf_op jit(solution)/shard_map/force/ppermute | solution.py:295
  58.9 18.7 %collective-permute-start.3 = (bf16[22,2,8100]{2,1,0:T(2,128)(2,1)S(1)}, bf16[22,2,8100]{2,1,0:T(2,128)(2,1)}, u32[]{:S(2)}, u32[]{:S(2)}) collective-permute-start(bf16[22,2,8100]{2,1,0:T(2,128)(2,1)S(1)} %slice.18), channel_id=1, source_target_pairs={{0,192},{64,0},{128,64},{192,128},{1,193},{65,1},{129,65},{193,129... | collective-permute-start | bytes 2138408 | tf_op jit(solution)/shard_map/force/ppermute | solution.py:296
  76.4 3.8 %copy-start.4 = (bf16[23,2,8100]{2,1,0:T(2,128)(2,1)}, bf16[23,2,8100]{2,1,0:T(2,128)(2,1)S(1)}, u32[]{:S(2)}) copy-start(bf16[23,2,8100]{2,1,0:T(2,128)(2,1)S(1)} %collective-permute-done.2.top_ref) | copy-start | bytes 2235604
  76.4 3.8 %collective-permute-start.4 = (bf16[23,2,8100]{2,1,0:T(2,128)(2,1)S(1)}, bf16[23,2,8100]{2,1,0:T(2,128)(2,1)S(1)}, u32[]{:S(2)}, u32[]{:S(2)}) collective-permute-start(bf16[23,2,8100]{2,1,0:T(2,128)(2,1)S(1)} %collective-permute-done.2.top_ref), channel_id=1, source_target_pairs={{0,1},{1,0},{2,3},{3,2},{4,5},{5,4},{6,7},{7,6},{8,9},{9,8},{10,11... | collective-permute-start | bytes 2235608 | tf_op jit(solution)/shard_map/contract/ppermute | solution.py:340
  77.6 2.5 %collective-permute-start.5 = (bf16[22,2,8100]{2,1,0:T(2,128)(2,1)}, bf16[22,2,8100]{2,1,0:T(2,128)(2,1)}, u32[]{:S(2)}, u32[]{:S(2)}) collective-permute-start(bf16[22,2,8100]{2,1,0:T(2,128)(2,1)} %collective-permute-done.3.bottom_ref), channel_id=1, source_target_pairs={{0,1},{1,0},{2,3},{3,2},{4,5},{5,4},{6,7},{7,6},{8,9},{9,8},{10,11... | collective-permute-start | bytes 2138408 | tf_op jit(solution)/shard_map/contract/ppermute | solution.py:341
  80.2 0.9 copy-start.5
  80.2 1.4 %copy-start.2 = (bf16[96,8100]{1,0:T(8,128)(2,1)}, bf16[96,8100]{1,0:T(8,128)(2,1)S(1)}, u32[]{:S(2)}) copy-start(bf16[96,8100]{1,0:T(8,128)(2,1)S(1)} %collective-permute-done.6.other_ref) | copy-start | bytes 4665604
  81.6 36.7 %copy-start.7 = (f32[1,45]{1,0:T(1,128)S(1)}, f32[1,45]{1,0:T(1,128)}, u32[]{:S(2)}) copy-start(f32[1,45]{1,0:T(1,128)} %param.20) | copy-start | bytes 544
  81.6 36.7 %copy-start.8 = (f32[1,45]{1,0:T(1,128)S(1)}, f32[1,45]{1,0:T(1,128)}, u32[]{:S(2)}) copy-start(f32[1,45]{1,0:T(1,128)} %param.21) | copy-start | bytes 544
  95.1 8.3 %collective-permute-start.7 = (f32[1,128]{1,0:T(1,128)S(1)}, f32[1,128]{1,0:T(1,128)S(1)}, u32[]{:S(2)}, u32[]{:S(2)}) collective-permute-start(f32[1,128]{1,0:T(1,128)S(1)} %get-tuple-element.25), channel_id=1, source_target_pairs={{0,64},{64,128},{128,192},{192,0},{1,65},{65,129},{129,193},{193,1... | collective-permute-start | bytes 1544 | tf_op jit(solution)/shard_map/collect/ppermute | solution.py:361
  97.1 6.3 %collective-permute-start.8 = (f32[1,128]{1,0:T(1,128)S(1)}, f32[1,128]{1,0:T(1,128)S(1)}, u32[]{:S(2)}, u32[]{:S(2)}) collective-permute-start(f32[1,128]{1,0:T(1,128)S(1)} %get-tuple-element.25), channel_id=1, source_target_pairs={{0,128},{64,192},{128,0},{192,64},{1,129},{65,193},{129,1},{193,65... | collective-permute-start | bytes 1544 | tf_op jit(solution)/shard_map/collect/ppermute | solution.py:361
  99.7 3.8 %collective-permute-start.9 = (f32[1,128]{1,0:T(1,128)S(1)}, f32[1,128]{1,0:T(1,128)S(1)}, u32[]{:S(2)}, u32[]{:S(2)}) collective-permute-start(f32[1,128]{1,0:T(1,128)S(1)} %get-tuple-element.25), channel_id=1, source_target_pairs={{0,192},{64,0},{128,64},{192,128},{1,193},{65,1},{129,65},{193,129... | collective-permute-start | bytes 1544 | tf_op jit(solution)/shard_map/collect/ppermute | solution.py:361

commit v4 on v3

--- a/solution.py
+++ b/solution.py
@@ -127,7 +127,7 @@
     return jnp.pad(values.reshape(rows, values.shape[2]), ((0, count - rows), (0, 0)))
 
 
-def early_kernel(lead_ref, own_ref, low_ref, high_ref, mine_ref, far_ref):
+def early_kernel(lead_ref, own_ref, low_ref, high_ref, mine_ref, *far_refs):
     total = own_ref.shape[2]
     for start in range(0, total, CHUNK):
         cols = slice(start, min(start + CHUNK, total))
@@ -137,7 +137,9 @@
             preferred_element_type=jnp.float32,
         )
         mine_ref[:, cols] = product[0:WIDE].astype(mine_ref.dtype)
-        far_ref[:, cols] = product[WIDE:].astype(far_ref.dtype)
+        for i, far_ref in enumerate(far_refs):
+            rows = product[WIDE + 24 * i : WIDE + 24 * i + 24]
+            far_ref[:, cols] = rows.astype(far_ref.dtype)
 
 
 def interaction_kernel(
@@ -151,7 +153,10 @@
     far_top_ref,
     far_bottom_ref,
     mine_ref,
-    other_ref,
+    other0_ref,
+    other1_ref,
+    other2_ref,
+    other3_ref,
     out_ref,
     flat,
     windows,
@@ -165,7 +170,9 @@
     for start in range(0, total, 1024):
         cols = slice(start, min(start + 1024, total))
         late = (top_ref, bottom_ref, far_top_ref, far_bottom_ref)
-        both = mine_ref[:, cols].astype(jnp.float32) + other_ref[:, cols].astype(jnp.float32)
+        others = (other0_ref, other1_ref, other2_ref, other3_ref)
+        other = jnp.concatenate([ref[:, cols].astype(jnp.float32) for ref in others], axis=0)
+        both = mine_ref[:, cols].astype(jnp.float32) + other
         both = both + jnp.dot(
             late_ref[...],
             jnp.concatenate([rows_of(ref, cols, PAD) for ref in late], axis=0),
@@ -326,17 +333,18 @@
     with jax.named_scope("contract"):
         total = force_third.shape[2]
         swap = [(0, 1), (1, 0)]
-        mine, far = pl.pallas_call(
+        mine, *far = pl.pallas_call(
             early_kernel,
-            out_shape=(jax.ShapeDtypeStruct((WIDE, total), b16),) * 2,
+            out_shape=(jax.ShapeDtypeStruct((WIDE, total), b16),)
+            + (jax.ShapeDtypeStruct((WIDE // 4, total), b16),) * 4,
             in_specs=[VMEM] * 4,
-            out_specs=(VMEM,) * 2,
+            out_specs=(VMEM,) * 5,
             compiler_params=PARAMS,
             cost_estimate=pl.CostEstimate(
                 flops=2 * 192 * 288 * total, bytes_accessed=1200 * total, transcendentals=0
             ),
         )(early, own, low, high)
-        other = lax.ppermute(far, "mode", swap)
+        other = [lax.ppermute(rows, "mode", swap) for rows in far]
         far_top = lax.ppermute(top, "mode", swap)
         far_bottom = lax.ppermute(bottom, "mode", swap)
 
@@ -344,7 +352,7 @@
         sums = pl.pallas_call(
             interaction_kernel,
             out_shape=jax.ShapeDtypeStruct((8, 128), f32),
-            in_specs=[VMEM] * 11,
+            in_specs=[VMEM] * 14,
             out_specs=VMEM,
             scratch_shapes=[
                 pltpu.VMEM((WIDE, 8320), b16),
@@ -355,7 +363,7 @@
                 pltpu.VMEM((8 * PAD, 128), f32),
             ],
             compiler_params=PARAMS,
-        )(scalars, mid, last_all, tables, late, top, bottom, far_top, far_bottom, mine, other)
+        )(scalars, mid, last_all, tables, late, top, bottom, far_top, far_bottom, mine, *other)
     with jax.named_scope("collect"):
         own_row = sums[0:1]
         rows = [own_row] + [lax.ppermute(own_row, "clus", ring(4, step)) for step in (1, 2, 3)]

time: 120 us -> 119 us (level)
  blocking collectives: 14.6 us -> 45 us
  waiting for transfers between devices: 31.7 us -> 15.4 us
  starting transfers between devices: 27.9 us -> 15.5 us
  local copies, waits for them, and re-layouts: 13.5 us -> 10.5 us
    all_to_all x0 -> x1, blocking collectives: none -> 23 us  [body(): arrived = lax.all_to_all(chosen, 'trip', 0, 0, tiled=True)]
    ppermute x1, waiting for transfers between devices: 15.4 us -> 0.01 us  [body(): top = lax.ppermute(low[:TOP], 'clus', ring(4, 1))]
    all_to_all x1 -> x0, starting transfers between devices: 11.1 us -> none  [body(): arrived = lax.all_to_all(chosen, 'trip', 0, 0, tiled=True)]
    all_to_all x1 -> x0, waiting for transfers between devices: 11 us -> none  [body(): arrived = lax.all_to_all(chosen, 'trip', 0, 0, tiled=True)]
    all_to_all x1, blocking collectives: 14.6 us -> 22 us  [body(): received = lax.all_to_all(partial[:, None, :], 'trip', 0, 0, tiled=True)]
    ppermute x1, waiting for transfers between devices: 0.01 us -> 4.61 us  [body(): low = lax.ppermute(own, 'clus', ring(4, 1))]
    all_to_all x1, waiting for transfers between devices: 3.56 us -> 7.03 us  [body(): members = lax.all_to_all(picks, group, 0, 0, tiled=True)]
    ppermute x1 -> x4, waiting for transfers between devices: 0.01 us -> 2.51 us  [body(): other = [lax.ppermute(rows, 'mode', swap) for rows in far]]
  transfers between devices with their start and end apart: 12 -> 14, of which waited for: 5 -> 7; matrix products, arithmetic and copies ran while one was open for 12% -> 11% of each run, Pallas kernels for 5% -> 10%
where the time goes in v4:
time: 119 us; the launch traced here: 118 us
  blocking collectives  45 us (38%)
  Pallas kernels  24.2 us (20%)
  starting transfers between devices  15.5 us (13%)
  waiting for transfers between devices  15.4 us (13%)
  local copies, waits for them, and re-layouts  10.5 us (9%)
  other arithmetic  6.12 us (5%)
    all_to_all x1, blocking collectives, body(): arrived = lax.all_to_all(chosen, 'trip', 0, 0, tiled=True)  23 us
    all_to_all x1, blocking collectives, body(): received = lax.all_to_all(partial[:, None, :], 'trip', 0, 0, tiled=True)  22 us
    pallas_call x1, Pallas kernels, body(): pl.pallas_call(interaction_kernel, out_shape=jax.ShapeDtypeStruct((8, 128...  12.8 us
    all_to_all x1, waiting for transfers between devices, body(): members = lax.all_to_all(picks, group, 0, 0, tiled=True)  7.03 us
    pallas_call x1, Pallas kernels, body(): pl.pallas_call(early_kernel, out_shape=(jax.ShapeDtypeStruct((WIDE, total...  5.88 us
    all_to_all x1, starting transfers between devices, body(): members = lax.all_to_all(picks, group, 0, 0, tiled=True)  5.19 us
    ppermute x1, waiting for transfers between devices, body(): low = lax.ppermute(own, 'clus', ring(4, 1))  4.61 us
    ppermute x3, starting transfers between devices, body(): lax.ppermute(own_row, 'clus', ring(4, step))  4.59 us
  transfers between devices with their start and end apart: 14, of which 7 were waited for; matrix products, arithmetic and copies ran while one was open for 11% of the time, Pallas kernels for 10%

profile of v4, /device:TPU:2, one launch (start us, length us, event | category | flops | bytes accessed | tf_op | source)
XLA Modules:
  0.0 117.5 jit_solution(16154811529766791060)
XLA Ops:
  0.6 1.6 %collective-permute-start = (bf16[45,2,8100]{2,1,0:T(2,128)(2,1)}, bf16[45,2,8100]{2,1,0:T(2,128)(2,1)S(1)}, u32[]{:S(2)}, u32[]{:S(2)}) collective-permute-start(bf16[45,2,8100]{2,1,0:T(2,128)(2,1)} %bitcast.25), channel_id=1, source_target_pairs={{0,64},{64,128},{128,192},{192,0},{1,65},{65,129},{129,193},{193,1... | collective-permute-start | bytes 4374008 | tf_op jit(solution)/shard_map/force/ppermute | solution.py:299
  2.2 0.9 collective-permute-start.1
  3.1 1.1 copy.36
  4.1 0.8 maximum_bitcast_fusion
  4.9 0.1 pad_dynamic-slice_fusion.2
  5.0 0.7 fusion.1.share_ref
  5.7 1.6 %records.1 = bf16[32,12,180]{2,1,0:T(8,128)(2,1)} custom-call(s32[1,32]{1,0:T(1,128)} %rows_ref.1, bf16[8,12,180]{2,1,0:T(8,128)(2,1)} %fusion.1.share_ref), custom_call_target="tpu_custom_call" | custom-call | tf_op jit(solution)/shard_map/records/pallas_call | solution.py:285
  7.3 23.0 %all_to_all.15.arrived_ref = bf16[32,12,180]{2,1,0:T(8,128)(2,1)} all-to-all(bf16[32,12,180]{2,1,0:T(8,128)(2,1)} %records.1), channel_id=1, replica_groups=mesh['clus'=4,'trip'=32,'mode'=2] {'trip'}, dimensions={0} | all-to-all | bytes 276480 | tf_op jit(solution)/shard_map/records/all_to_all | solution.py:292
  30.3 4.6 %collective-permute-done.low_ref = bf16[45,2,8100]{2,1,0:T(2,128)(2,1)S(1)} collective-permute-done((bf16[45,2,8100]{2,1,0:T(2,128)(2,1)}, bf16[45,2,8100]{2,1,0:T(2,128)(2,1)S(1)}, u32[]{:S(2)}, u32[]{:S(2)}) %collective-permute-start) | collective-permute-done | bytes 1458032 | tf_op jit(solution)/shard_map/force/ppermute | solution.py:299
  34.9 1.2 %collective-permute-done.1.high_ref = bf16[45,2,8100]{2,1,0:T(2,128)(2,1)S(1)} collective-permute-done((bf16[45,2,8100]{2,1,0:T(2,128)(2,1)}, bf16[45,2,8100]{2,1,0:T(2,128)(2,1)S(1)}, u32[]{:S(2)}, u32[]{:S(2)}) %collective-permute-start.1) | collective-permute-done | bytes 1458032 | tf_op jit(solution)/shard_map/force/ppermute | solution.py:300
  36.2 1.5 %slice.17 = bf16[23,2,8100]{2,1,0:T(2,128)(2,1)} slice(bf16[45,2,8100]{2,1,0:T(2,128)(2,1)S(1)} %collective-permute-done.low_ref), slice={[0:23], [0:2], [0:8100]} | slice | bytes 1490400 | tf_op jit(solution)/shard_map/force/slice | solution.py:302
  37.7 1.2 %collective-permute-start.2 = (bf16[23,2,8100]{2,1,0:T(2,128)(2,1)}, bf16[23,2,8100]{2,1,0:T(2,128)(2,1)}, u32[]{:S(2)}, u32[]{:S(2)}) collective-permute-start(bf16[23,2,8100]{2,1,0:T(2,128)(2,1)} %slice.17), channel_id=1, source_target_pairs={{0,64},{64,128},{128,192},{192,0},{1,65},{65,129},{129,193},{193,1... | collective-permute-start | bytes 2235608 | tf_op jit(solution)/shard_map/force/ppermute | solution.py:302
  38.9 1.5 %slice.18 = bf16[22,2,8100]{2,1,0:T(2,128)(2,1)} slice(bf16[45,2,8100]{2,1,0:T(2,128)(2,1)S(1)} %collective-permute-done.1.high_ref), slice={[23:45], [0:2], [0:8100]} | slice | bytes 1425600 | tf_op jit(solution)/shard_map/force/slice | solution.py:303
  40.4 0.8 collective-permute-start.3
  41.3 0.1 copy.40
  41.4 0.6 pad.4.phase_ref
  42.0 1.7 %members.1 = bf16[8,4,12,180]{3,2,1,0:T(8,128)(2,1)} custom-call(s32[4,3]{1,0:T(4,128)} %table_ref.1, bf16[32,12,180]{2,1,0:T(8,128)(2,1)} %all_to_all.15.arrived_ref, bf16[4,12,180]{2,1,0:T(8,128)(2,1)} %pad.4.phase_ref), custom_call_target="tpu_custom_call" | custom-call | tf_op jit(solution)/shard_map/members/pallas_call | solution.py:306
  43.7 1.7 %copy.41 = bf16[8,4,12,180]{3,1,2,0:T(4,128)(2,1)} copy(bf16[8,4,12,180]{3,2,1,0:T(8,128)(2,1)} %members.1) | data formatting | bytes 276480 | tf_op jit(solution)/shard_map/members/pallas_call | solution.py:306
  45.4 5.2 %all-to-all-start.1 = ((bf16[8,4,12,180]{3,1,2,0:T(4,128)(2,1)}), bf16[8,4,12,180]{3,1,2,0:T(4,128)(2,1)S(1)}, u32[]{:S(2)}, u32[]{:S(2)}) async-start(bf16[8,4,12,180]{3,1,2,0:T(4,128)(2,1)} %copy.41), calls=%async_computation.1 | async-start | bytes 393216 | tf_op jit(solution)/shard_map/members/all_to_all | solution.py:313
  50.6 0.6 dynamic_slice.20
  51.2 1.3 %pad_add_fusion.where_ref = s32[3]{0:T(128)} fusion(s32[1]{0:T(128)} %dynamic_slice.20, s32[1]{0:T(128)} %bitcast.2, s32[1]{0:T(128)} %bitcast.1), kind=kLoop, calls=%fused_computation.20 | loop fusion | flops 6 | bytes 24 | tf_op jit(solution)/shard_map/operands/stack | solution.py:317
  52.4 7.0 %all-to-all-done.1 = bf16[8,4,12,180]{3,1,2,0:T(4,128)(2,1)S(1)} async-done(((bf16[8,4,12,180]{3,1,2,0:T(4,128)(2,1)}), bf16[8,4,12,180]{3,1,2,0:T(4,128)(2,1)S(1)}, u32[]{:S(2)}, u32[]{:S(2)}) %all-to-all-start.1) | async-done | bytes 138272 | tf_op jit(solution)/shard_map/members/all_to_all | solution.py:313
  59.5 0.7 copy.42.members_ref
  60.2 2.3 %operands.1 = (bf16[192,288]{1,0:T(8,128)(2,1)}, bf16[96,192]{1,0:T(8,128)(2,1)}, bf16[192,192]{1,0:T(8,128)(2,1)}, bf16[256,256]{1,0:T(8,128)(2,1)}, f32[4,96,128]{2,1,0:T(8,128)}, /*index=5*/f32[2,48,128]{2,1,0:T(8,128)}) custom-call(s32[3]{0:T(128)} %pad_add_fusion.where_ref, bf16[8,4,12,180]{3,2,1,0:T(8,128)(2,1)} %copy.42.members_ref), custom_call_target="tpu_custom_call" | custom-call | tf_op jit(solution)/shard_map/operands/pallas_call | solution.py:318
  62.5 5.9 %contract.1 = (bf16[96,8100]{1,0:T(8,128)(2,1)}, bf16[24,8100]{1,0:T(8,128)(2,1)}, bf16[24,8100]{1,0:T(8,128)(2,1)}, bf16[24,8100]{1,0:T(8,128)(2,1)}, bf16[24,8100]{1,0:T(8,128)(2,1)}) custom-call(bf16[192,288]{1,0:T(8,128)(2,1)} %get-tuple-element.22.lead_ref, bf16[45,2,8100]{2,1,0:T(2,128)(2,1)} %bitcast.27, bf16[45,2,8100]{2,1,0:T(2,128)(2,1)} %copy-done, ...), custom_call_target="tpu_custom_call" | custom-call | flops 895795200 | bytes 9720000 | tf_op jit(solution)/shard_map/contract/pallas_call | solution.py:336
  68.4 0.5 collective-permute-start.4
  68.9 0.1 collective-permute-start.5
  69.0 0.4 collective-permute-start.7
  69.4 0.1 collective-permute-start.8
  69.5 0.8 collective-permute-done.6.other0_ref
  70.3 0.1 collective-permute-start.9
  70.5 0.7 fusion.9
  71.1 1.3 %iota_compare_fusion.2 = (pred[32]{0:T(512)(128)(4,1)S(1)}, pred[32]{0:T(512)(128)(4,1)S(1)}) fusion(s32[]{:T(128)} %bitcast.11, s32[]{:T(128)} %bitcast), kind=kLoop, calls=%fused_computation.25 | loop fusion | flops 64 | bytes 72 | tf_op jit(solution)/shard_map/collect/eq | solution.py:374
  72.4 0.6 collective-permute-done.7.other1_ref
  73.0 0.6 collective-permute-done.8.other2_ref
  73.6 0.6 collective-permute-done.9.other3_ref
  74.2 0.1 copy-done.6
  74.3 0.6 copy-done.7
  74.9 0.3 copy-done.3
  75.1 0.3 copy-done.2
  75.4 12.8 %interaction.1 = f32[8,128]{1,0:T(8,128)} custom-call(f32[2,48,128]{2,1,0:T(8,128)} %get-tuple-element.15.scalars_ref, bf16[192,192]{1,0:T(8,128)(2,1)} %get-tuple-element.16.middle_ref, bf16[256,256]{1,0:T(8,128)(2,1)} %get-tuple-element.17.last_ref, f32[4,96,128]{2,1,0:T(8,128)} %get-tuple-element.18.tables_ref, ...), custom_call_target="tpu_custom_call" | custom-call | tf_op jit(solution)/shard_map/interaction/pallas_call | solution.py:352
  88.1 0.7 slice_bitcast_fusion
  88.8 2.2 %collective-permute-start.11 = (f32[1,128]{1,0:T(1,128)S(1)}, f32[1,128]{1,0:T(1,128)S(1)}, u32[]{:S(2)}, u32[]{:S(2)}) collective-permute-start(f32[1,128]{1,0:T(1,128)S(1)} %get-tuple-element.31), channel_id=1, source_target_pairs={{0,128},{64,192},{128,0},{192,64},{1,129},{65,193},{129,1},{193,65... | collective-permute-start | bytes 1544 | tf_op jit(solution)/shard_map/collect/ppermute | solution.py:369
  91.0 2.4 %collective-permute-start.12 = (f32[1,128]{1,0:T(1,128)S(1)}, f32[1,128]{1,0:T(1,128)S(1)}, u32[]{:S(2)}, u32[]{:S(2)}) collective-permute-start(f32[1,128]{1,0:T(1,128)S(1)} %get-tuple-element.31), channel_id=1, source_target_pairs={{0,192},{64,0},{128,64},{192,128},{1,193},{65,1},{129,65},{193,129... | collective-permute-start | bytes 1544 | tf_op jit(solution)/shard_map/collect/ppermute | solution.py:369
  93.4 1.2 %iota_compare_fusion = (pred[32]{0:T(512)(128)(4,1)S(1)}, pred[32]{0:T(512)(128)(4,1)S(1)}) fusion(s32[]{:T(128)} %bitcast.15, s32[]{:T(128)} %bitcast.13), kind=kLoop, calls=%fused_computation.23 | loop fusion | flops 64 | bytes 72 | tf_op jit(solution)/shard_map/collect/eq | solution.py:374
  94.7 0.2 fusion.4
  94.9 22.0 %all_to_all.16 = f32[32,1,128]{2,1,0:T(1,128)S(1)} all-to-all(f32[32,1,128]{2,1,0:T(1,128)S(1)} %fusion.4), channel_id=1, replica_groups=mesh['clus'=4,'trip'=32,'mode'=2] {'trip'}, dimensions={0} | all-to-all | bytes 32768 | tf_op jit(solution)/shard_map/collect/all_to_all | solution.py:375
  117.0 0.6 add_divide_fusion
  (37 shorter events, 0.2 us)
Async XLA Ops:
  0.6 34.3 %collective-permute-start = (bf16[45,2,8100]{2,1,0:T(2,128)(2,1)}, bf16[45,2,8100]{2,1,0:T(2,128)(2,1)S(1)}, u32[]{:S(2)}, u32[]{:S(2)}) collective-permute-start(bf16[45,2,8100]{2,1,0:T(2,128)(2,1)} %bitcast.25), channel_id=1, source_target_pairs={{0,64},{64,128},{128,192},{192,0},{1,65},{65,129},{129,193},{193,1... | collective-permute-start | bytes 4374008 | tf_op jit(solution)/shard_map/force/ppermute | solution.py:299
  2.2 34.0 %collective-permute-start.1 = (bf16[45,2,8100]{2,1,0:T(2,128)(2,1)}, bf16[45,2,8100]{2,1,0:T(2,128)(2,1)S(1)}, u32[]{:S(2)}, u32[]{:S(2)}) collective-permute-start(bf16[45,2,8100]{2,1,0:T(2,128)(2,1)} %bitcast.26), channel_id=1, source_target_pairs={{0,192},{64,0},{128,64},{192,128},{1,193},{65,1},{129,65},{193,129... | collective-permute-start | bytes 4374008 | tf_op jit(solution)/shard_map/force/ppermute | solution.py:300
  30.3 10.9 %copy-start.11 = (bf16[2,4]{1,0:T(2,128)(2,1)S(1)}, bf16[2,4]{1,0:T(2,128)(2,1)}, u32[]{:S(2)}) copy-start(bf16[2,4]{1,0:T(2,128)(2,1)} %param.12) | copy-start | bytes 52
  34.9 5.4 %copy-start = (bf16[45,2,8100]{2,1,0:T(2,128)(2,1)}, bf16[45,2,8100]{2,1,0:T(2,128)(2,1)S(1)}, u32[]{:S(2)}) copy-start(bf16[45,2,8100]{2,1,0:T(2,128)(2,1)S(1)} %collective-permute-done.low_ref) | copy-start | bytes 4374004
  36.2 26.3 %copy-start.1 = (bf16[45,2,8100]{2,1,0:T(2,128)(2,1)}, bf16[45,2,8100]{2,1,0:T(2,128)(2,1)S(1)}, u32[]{:S(2)}) copy-start(bf16[45,2,8100]{2,1,0:T(2,128)(2,1)S(1)} %collective-permute-done.1.high_ref) | copy-start | bytes 4374004
  37.7 12.9 %copy-start.12 = (s32[4]{0:T(128)S(1)}, s32[4]{0:T(128)}, u32[]{:S(2)}) copy-start(s32[4]{0:T(128)} %param.19) | copy-start | bytes 52
  37.7 30.7 %collective-permute-start.2 = (bf16[23,2,8100]{2,1,0:T(2,128)(2,1)}, bf16[23,2,8100]{2,1,0:T(2,128)(2,1)}, u32[]{:S(2)}, u32[]{:S(2)}) collective-permute-start(bf16[23,2,8100]{2,1,0:T(2,128)(2,1)} %slice.17), channel_id=1, source_target_pairs={{0,64},{64,128},{128,192},{192,0},{1,65},{65,129},{129,193},{193,1... | collective-permute-start | bytes 2235608 | tf_op jit(solution)/shard_map/force/ppermute | solution.py:302
  40.4 28.5 %collective-permute-start.3 = (bf16[22,2,8100]{2,1,0:T(2,128)(2,1)}, bf16[22,2,8100]{2,1,0:T(2,128)(2,1)}, u32[]{:S(2)}, u32[]{:S(2)}) collective-permute-start(bf16[22,2,8100]{2,1,0:T(2,128)(2,1)} %slice.18), channel_id=1, source_target_pairs={{0,192},{64,0},{128,64},{192,128},{1,193},{65,1},{129,65},{193,129... | collective-permute-start | bytes 2138408 | tf_op jit(solution)/shard_map/force/ppermute | solution.py:303
  45.4 14.1 %all-to-all-start.1 = ((bf16[8,4,12,180]{3,1,2,0:T(4,128)(2,1)}), bf16[8,4,12,180]{3,1,2,0:T(4,128)(2,1)S(1)}, u32[]{:S(2)}, u32[]{:S(2)}) async-start(bf16[8,4,12,180]{3,1,2,0:T(4,128)(2,1)} %copy.41), calls=%async_computation.1 | async-start | bytes 393216 | tf_op jit(solution)/shard_map/members/all_to_all | solution.py:313
  62.5 8.0 %copy-start.8 = (s32[4]{0:T(128)S(1)}, s32[4]{0:T(128)}, u32[]{:S(2)}) copy-start(s32[4]{0:T(128)} %param.18) | copy-start | bytes 52
  68.4 1.9 %collective-permute-start.6 = (bf16[24,8100]{1,0:T(8,128)(2,1)}, bf16[24,8100]{1,0:T(8,128)(2,1)S(1)}, u32[]{:S(2)}, u32[]{:S(2)}) collective-permute-start(bf16[24,8100]{1,0:T(8,128)(2,1)} %get-tuple-element.24), channel_id=1, source_target_pairs={{0,1},{1,0},{2,3},{3,2},{4,5},{5,4},{6,7},{7,6},{8,9},{9,8},{10,11... | collective-permute-start | bytes 1166408 | tf_op jit(solution)/shard_map/contract/ppermute | solution.py:347
  68.4 5.7 %collective-permute-start.4 = (bf16[23,2,8100]{2,1,0:T(2,128)(2,1)}, bf16[23,2,8100]{2,1,0:T(2,128)(2,1)S(1)}, u32[]{:S(2)}, u32[]{:S(2)}) collective-permute-start(bf16[23,2,8100]{2,1,0:T(2,128)(2,1)} %collective-permute-done.2.top_ref), channel_id=1, source_target_pairs={{0,1},{1,0},{2,3},{3,2},{4,5},{5,4},{6,7},{7,6},{8,9},{9,8},{10,11... | collective-permute-start | bytes 2235608 | tf_op jit(solution)/shard_map/contract/ppermute | solution.py:348
  68.9 5.2 %collective-permute-start.5 = (bf16[22,2,8100]{2,1,0:T(2,128)(2,1)}, bf16[22,2,8100]{2,1,0:T(2,128)(2,1)S(1)}, u32[]{:S(2)}, u32[]{:S(2)}) collective-permute-start(bf16[22,2,8100]{2,1,0:T(2,128)(2,1)} %collective-permute-done.3.bottom_ref), channel_id=1, source_target_pairs={{0,1},{1,0},{2,3},{3,2},{4,5},{5,4},{6,7},{7,6},{8,9},{9,8},{10,11... | collective-permute-start | bytes 2138408 | tf_op jit(solution)/shard_map/contract/ppermute | solution.py:349
  69.0 4.0 %collective-permute-start.7 = (bf16[24,8100]{1,0:T(8,128)(2,1)}, bf16[24,8100]{1,0:T(8,128)(2,1)S(1)}, u32[]{:S(2)}, u32[]{:S(2)}) collective-permute-start(bf16[24,8100]{1,0:T(8,128)(2,1)} %get-tuple-element.25), channel_id=1, source_target_pairs={{0,1},{1,0},{2,3},{3,2},{4,5},{5,4},{6,7},{7,6},{8,9},{9,8},{10,11... | collective-permute-start | bytes 1166408 | tf_op jit(solution)/shard_map/contract/ppermute | solution.py:347
  69.4 4.1 %collective-permute-start.8 = (bf16[24,8100]{1,0:T(8,128)(2,1)}, bf16[24,8100]{1,0:T(8,128)(2,1)S(1)}, u32[]{:S(2)}, u32[]{:S(2)}) collective-permute-start(bf16[24,8100]{1,0:T(8,128)(2,1)} %get-tuple-element.26), channel_id=1, source_target_pairs={{0,1},{1,0},{2,3},{3,2},{4,5},{5,4},{6,7},{7,6},{8,9},{9,8},{10,11... | collective-permute-start | bytes 1166408 | tf_op jit(solution)/shard_map/contract/ppermute | solution.py:347
  70.3 3.8 %copy-start.4 = (bf16[24,8100]{1,0:T(8,128)(2,1)}, bf16[24,8100]{1,0:T(8,128)(2,1)S(1)}, u32[]{:S(2)}) copy-start(bf16[24,8100]{1,0:T(8,128)(2,1)S(1)} %collective-permute-done.6.other0_ref) | copy-start | bytes 1166404
  70.3 3.8 %collective-permute-start.9 = (bf16[24,8100]{1,0:T(8,128)(2,1)}, bf16[24,8100]{1,0:T(8,128)(2,1)S(1)}, u32[]{:S(2)}, u32[]{:S(2)}) collective-permute-start(bf16[24,8100]{1,0:T(8,128)(2,1)} %get-tuple-element.27), channel_id=1, source_target_pairs={{0,1},{1,0},{2,3},{3,2},{4,5},{5,4},{6,7},{7,6},{8,9},{9,8},{10,11... | collective-permute-start | bytes 1166408 | tf_op jit(solution)/shard_map/contract/ppermute | solution.py:347
  73.0 1.2 copy-start.5
  73.6 0.7 copy-start.6
  74.1 0.7 copy-start.7
  74.1 1.0 copy-start.3
  74.1 1.2 %copy-start.2 = (bf16[23,2,8100]{2,1,0:T(2,128)(2,1)}, bf16[23,2,8100]{2,1,0:T(2,128)(2,1)S(1)}, u32[]{:S(2)}) copy-start(bf16[23,2,8100]{2,1,0:T(2,128)(2,1)S(1)} %collective-permute-done.4.far_top_ref) | copy-start | bytes 2235604
  75.4 41.6 %copy-start.9 = (f32[1,45]{1,0:T(1,128)S(1)}, f32[1,45]{1,0:T(1,128)}, u32[]{:S(2)}) copy-start(f32[1,45]{1,0:T(1,128)} %param.20) | copy-start | bytes 544
  75.4 41.6 %copy-start.10 = (f32[1,45]{1,0:T(1,128)S(1)}, f32[1,45]{1,0:T(1,128)}, u32[]{:S(2)}) copy-start(f32[1,45]{1,0:T(1,128)} %param.21) | copy-start | bytes 544
  88.8 5.8 %collective-permute-start.10 = (f32[1,128]{1,0:T(1,128)S(1)}, f32[1,128]{1,0:T(1,128)S(1)}, u32[]{:S(2)}, u32[]{:S(2)}) collective-permute-start(f32[1,128]{1,0:T(1,128)S(1)} %get-tuple-element.31), channel_id=1, source_target_pairs={{0,64},{64,128},{128,192},{192,0},{1,65},{65,129},{129,193},{193,1... | collective-permute-start | bytes 1544 | tf_op jit(solution)/shard_map/collect/ppermute | solution.py:369
  88.8 5.8 %collective-permute-start.11 = (f32[1,128]{1,0:T(1,128)S(1)}, f32[1,128]{1,0:T(1,128)S(1)}, u32[]{:S(2)}, u32[]{:S(2)}) collective-permute-start(f32[1,128]{1,0:T(1,128)S(1)} %get-tuple-element.31), channel_id=1, source_target_pairs={{0,128},{64,192},{128,0},{192,64},{1,129},{65,193},{129,1},{193,65... | collective-permute-start | bytes 1544 | tf_op jit(solution)/shard_map/collect/ppermute | solution.py:369
  91.0 3.7 %collective-permute-start.12 = (f32[1,128]{1,0:T(1,128)S(1)}, f32[1,128]{1,0:T(1,128)S(1)}, u32[]{:S(2)}, u32[]{:S(2)}) collective-permute-start(f32[1,128]{1,0:T(1,128)S(1)} %get-tuple-element.31), channel_id=1, source_target_pairs={{0,192},{64,0},{128,64},{192,128},{1,193},{65,1},{129,65},{193,129... | collective-permute-start | bytes 1544 | tf_op jit(solution)/shard_map/collect/ppermute | solution.py:369

commit v5 on v4

--- a/solution.py
+++ b/solution.py
@@ -21,14 +21,17 @@
     for triplet in range(4):
         for member in range(3):
             block = arrived_ref[table_ref[triplet, member]]
-            out_ref[2 * triplet, member] = block
-            out_ref[2 * triplet + 1, member] = block
+            out_ref[2 * triplet, member, 0:12] = block
+            out_ref[2 * triplet + 1, member, 0:12] = block
+            fill = jnp.zeros((4, block.shape[1]), block.dtype)
+            out_ref[2 * triplet, member, 12:16] = fill
+            out_ref[2 * triplet + 1, member, 12:16] = fill
         out_ref[2 * triplet, 3] = phase_ref[triplet]
         out_ref[2 * triplet + 1, 3] = phase_ref[triplet]
 
 
 def whole_record(members_ref, slot):
-    parts = [members_ref[j, slot].astype(jnp.float32) for j in range(8)]
+    parts = [members_ref[j, slot].astype(jnp.float32)[0:12] for j in range(8)]
     rows = jnp.concatenate(parts, axis=0)
     fill = jnp.zeros((WIDE, 38), jnp.float32)
     return jnp.concatenate([rows[:, 0:90], fill, rows[:, 90:180], fill], axis=1)
@@ -292,25 +295,27 @@
         arrived = lax.all_to_all(chosen, "trip", 0, 0, tiled=True)
         angles = phase_angle.astype(f32)
         trig = jnp.stack([jnp.cos(angles), jnp.sin(angles)], axis=1).astype(b16)
-        phases = jnp.pad(trig.reshape(4, 4).T[:, None, :], ((0, 0), (0, 11), (0, 176)))
+        phases = jnp.pad(trig.reshape(4, 4).T[:, None, :], ((0, 0), (0, 15), (0, 176)))
 
     with jax.named_scope("force"):
         own = jnp.transpose(force_third, (1, 0, 2))
         low = lax.ppermute(own, "clus", ring(4, 1))
         high = lax.ppermute(own, "clus", ring(4, 3))
-        low, high, _ = lax.optimization_barrier((low, high, arrived))
-        top = lax.ppermute(low[:TOP], "clus", ring(4, 1))
-        bottom = lax.ppermute(high[TOP:], "clus", ring(4, 3))
 
     with jax.named_scope("members"):
         picks = pl.pallas_call(
             pick_kernel,
-            out_shape=jax.ShapeDtypeStruct((8, 4, 12, 180), b16),
+            out_shape=jax.ShapeDtypeStruct((8, 4, 16, 180), b16),
             in_specs=[SMEM, VMEM, VMEM],
             out_specs=VMEM,
             compiler_params=PARAMS,
         )(trip_table, arrived, phases)
         members = lax.all_to_all(picks, group, 0, 0, tiled=True)
+
+    with jax.named_scope("force_second"):
+        low, high, _ = lax.optimization_barrier((low, high, members))
+        top = lax.ppermute(low[:TOP], "clus", ring(4, 1))
+        bottom = lax.ppermute(high[TOP:], "clus", ring(4, 3))
 
     with jax.named_scope("operands"):
         mult = lax.dynamic_index_in_dim(multiplicity, clus, 0, keepdims=False)

time: 119 us -> 111 us (0.933)
  blocking collectives: 45 us -> 27.6 us
  starting transfers between devices: 15.5 us -> 23.4 us
  waiting for transfers between devices: 15.4 us -> 18.4 us
  local copies, waits for them, and re-layouts: 10.5 us -> 9.05 us
    all_to_all x1, blocking collectives: 23 us -> 11.9 us  [body(): members = lax.all_to_all(picks, group, 0, 0, tiled=True)]
    all_to_all x1, blocking collectives: 22 us -> 15.7 us  [body(): received = lax.all_to_all(partial[:, None, :], 'trip', 0, 0, tiled=True)]
    all_to_all x1, starting transfers between devices: 5.19 us -> 11.1 us  [body(): arrived = lax.all_to_all(chosen, 'trip', 0, 0, tiled=True)]
    ppermute x1, waiting for transfers between devices: 0.01 us -> 4.9 us  [body(): top = lax.ppermute(low[:TOP], 'clus', ring(4, 1))]
    ppermute x1, waiting for transfers between devices: 4.61 us -> 0.01 us  [body(): low = lax.ppermute(own, 'clus', ring(4, 1))]
    all_to_all x1, waiting for transfers between devices: 7.03 us -> 11 us  [body(): arrived = lax.all_to_all(chosen, 'trip', 0, 0, tiled=True)]
    ppermute x3, starting transfers between devices: 4.59 us -> 6.8 us  [body(): lax.ppermute(own_row, 'clus', ring(4, step))]
    pallas_call x1 -> x0, local copies, waits for them, and re-layouts: 1.72 us -> none  [body(): pl.pallas_call(pick_kernel, out_shape=jax.ShapeDtypeStruct((8, 4, 12, 180...]
  transfers between devices with their start and end apart: 14 -> 14, of which waited for: 7 -> 7; matrix products, arithmetic and copies ran while one was open for 11% -> 9% of each run, Pallas kernels for 10% -> 10%
where the time goes in v5:
time: 111 us; the launch traced here: 110 us
  blocking collectives  27.6 us (25%)
  Pallas kernels  24.2 us (22%)
  starting transfers between devices  23.4 us (21%)
  waiting for transfers between devices  18.4 us (17%)
  local copies, waits for them, and re-layouts  9.05 us (8%)
  other arithmetic  6.14 us (6%)
    all_to_all x1, blocking collectives, body(): received = lax.all_to_all(partial[:, None, :], 'trip', 0, 0, tiled=True)  15.7 us
    pallas_call x1, Pallas kernels, body(): pl.pallas_call(interaction_kernel, out_shape=jax.ShapeDtypeStruct((8, 128...  12.7 us
    all_to_all x1, blocking collectives, body(): members = lax.all_to_all(picks, group, 0, 0, tiled=True)  11.9 us
    all_to_all x1, starting transfers between devices, body(): arrived = lax.all_to_all(chosen, 'trip', 0, 0, tiled=True)  11.1 us
    all_to_all x1, waiting for transfers between devices, body(): arrived = lax.all_to_all(chosen, 'trip', 0, 0, tiled=True)  11 us
    ppermute x3, starting transfers between devices, body(): lax.ppermute(own_row, 'clus', ring(4, step))  6.8 us
    pallas_call x1, Pallas kernels, body(): pl.pallas_call(early_kernel, out_shape=(jax.ShapeDtypeStruct((WIDE, total...  5.91 us
    ppermute x1, waiting for transfers between devices, body(): top = lax.ppermute(low[:TOP], 'clus', ring(4, 1))  4.9 us
  transfers between devices with their start and end apart: 14, of which 7 were waited for; matrix products, arithmetic and copies ran while one was open for 9% of the time, Pallas kernels for 10%

profile of v5, /device:TPU:2, one launch (start us, length us, event | category | flops | bytes accessed | tf_op | source)
XLA Modules:
  0.0 109.6 jit_solution(9324136844467074130)
XLA Ops:
  0.6 1.6 %collective-permute-start = (bf16[45,2,8100]{2,1,0:T(2,128)(2,1)}, bf16[45,2,8100]{2,1,0:T(2,128)(2,1)S(1)}, u32[]{:S(2)}, u32[]{:S(2)}) collective-permute-start(bf16[45,2,8100]{2,1,0:T(2,128)(2,1)} %bitcast.25), channel_id=1, source_target_pairs={{0,64},{64,128},{128,192},{192,0},{1,65},{65,129},{129,193},{193,1... | collective-permute-start | bytes 4374008 | tf_op jit(solution)/shard_map/force/ppermute | solution.py:302
  2.2 0.9 collective-permute-start.1
  3.1 1.1 copy.27
  4.1 0.8 maximum_bitcast_fusion
  4.9 0.1 pad_dynamic-slice_fusion.2
  5.0 0.7 fusion.1.share_ref
  5.7 1.6 %records.1 = bf16[32,12,180]{2,1,0:T(8,128)(2,1)} custom-call(s32[1,32]{1,0:T(1,128)} %rows_ref.1, bf16[8,12,180]{2,1,0:T(8,128)(2,1)} %fusion.1.share_ref), custom_call_target="tpu_custom_call" | custom-call | tf_op jit(solution)/shard_map/records/pallas_call | solution.py:288
  7.3 11.1 %all-to-all-start = ((bf16[32,12,180]{2,1,0:T(8,128)(2,1)}), bf16[32,12,180]{2,1,0:T(8,128)(2,1)S(1)}, u32[]{:S(2)}, u32[]{:S(2)}) async-start(bf16[32,12,180]{2,1,0:T(8,128)(2,1)} %records.1), calls=%async_computation | async-start | bytes 524288 | tf_op jit(solution)/shard_map/records/all_to_all | solution.py:295
  18.6 0.1 copy.31
  18.7 0.6 pad.4.phase_ref
  19.3 11.0 %all-to-all-done.arrived_ref = bf16[32,12,180]{2,1,0:T(8,128)(2,1)S(1)} async-done(((bf16[32,12,180]{2,1,0:T(8,128)(2,1)}), bf16[32,12,180]{2,1,0:T(8,128)(2,1)S(1)}, u32[]{:S(2)}, u32[]{:S(2)}) %all-to-all-start) | async-done | bytes 138272 | tf_op jit(solution)/shard_map/records/all_to_all | solution.py:295
  30.3 0.7 copy-done.2
  30.9 1.7 %members.1 = bf16[8,4,16,180]{3,2,1,0:T(8,128)(2,1)} custom-call(s32[4,3]{1,0:T(4,128)} %table_ref.1, bf16[32,12,180]{2,1,0:T(8,128)(2,1)} %copy-done.2, bf16[4,16,180]{2,1,0:T(8,128)(2,1)} %pad.4.phase_ref), custom_call_target="tpu_custom_call" | custom-call | tf_op jit(solution)/shard_map/members/pallas_call | solution.py:306
  32.6 11.9 %all_to_all.15.members_ref = bf16[8,4,16,180]{3,2,1,0:T(8,128)(2,1)} all-to-all(bf16[8,4,16,180]{3,2,1,0:T(8,128)(2,1)} %members.1), channel_id=1, replica_groups=mesh['clus'=4,'trip'=32,'mode'=2] {'clus','mode'}, dimensions={0} | all-to-all | bytes 368640 | tf_op jit(solution)/shard_map/members/all_to_all | solution.py:313
  44.5 0.0 collective-permute-done.low_ref
  44.5 0.0 collective-permute-done.1.high_ref
  44.5 1.9 %slice.17 = bf16[23,2,8100]{2,1,0:T(2,128)(2,1)} slice(bf16[45,2,8100]{2,1,0:T(2,128)(2,1)S(1)} %collective-permute-done.low_ref), slice={[0:23], [0:2], [0:8100]} | slice | bytes 1490400 | tf_op jit(solution)/shard_map/force_second/slice | solution.py:317
  46.4 0.0 collective-permute-start.2
  46.4 1.5 %slice.18 = bf16[22,2,8100]{2,1,0:T(2,128)(2,1)} slice(bf16[45,2,8100]{2,1,0:T(2,128)(2,1)S(1)} %collective-permute-done.1.high_ref), slice={[23:45], [0:2], [0:8100]} | slice | bytes 1425600 | tf_op jit(solution)/shard_map/force_second/slice | solution.py:318
  47.9 2.0 %collective-permute-start.3 = (bf16[22,2,8100]{2,1,0:T(2,128)(2,1)}, bf16[22,2,8100]{2,1,0:T(2,128)(2,1)}, u32[]{:S(2)}, u32[]{:S(2)}) collective-permute-start(bf16[22,2,8100]{2,1,0:T(2,128)(2,1)} %slice.18), channel_id=1, source_target_pairs={{0,192},{64,0},{128,64},{192,128},{1,193},{65,1},{129,65},{193,129... | collective-permute-start | bytes 2138408 | tf_op jit(solution)/shard_map/force_second/ppermute | solution.py:318
  49.9 0.6 dynamic_slice.20
  50.5 1.3 %pad_add_fusion.where_ref = s32[3]{0:T(128)} fusion(s32[1]{0:T(128)} %dynamic_slice.20, s32[1]{0:T(128)} %bitcast.2, s32[1]{0:T(128)} %bitcast.1), kind=kLoop, calls=%fused_computation.20 | loop fusion | flops 6 | bytes 24 | tf_op jit(solution)/shard_map/operands/stack | solution.py:322
  51.8 2.3 %operands.1 = (bf16[192,288]{1,0:T(8,128)(2,1)}, bf16[96,192]{1,0:T(8,128)(2,1)}, bf16[192,192]{1,0:T(8,128)(2,1)}, bf16[256,256]{1,0:T(8,128)(2,1)}, f32[4,96,128]{2,1,0:T(8,128)}, /*index=5*/f32[2,48,128]{2,1,0:T(8,128)}) custom-call(s32[3]{0:T(128)} %pad_add_fusion.where_ref, bf16[8,4,16,180]{3,2,1,0:T(8,128)(2,1)} %all_to_all.15.members_ref), custom_call_target="tpu_custom_call" | custom-call | tf_op jit(solution)/shard_map/operands/pallas_call | solution.py:323
  54.1 5.9 %contract.1 = (bf16[96,8100]{1,0:T(8,128)(2,1)}, bf16[24,8100]{1,0:T(8,128)(2,1)}, bf16[24,8100]{1,0:T(8,128)(2,1)}, bf16[24,8100]{1,0:T(8,128)(2,1)}, bf16[24,8100]{1,0:T(8,128)(2,1)}) custom-call(bf16[192,288]{1,0:T(8,128)(2,1)} %get-tuple-element.22.lead_ref, bf16[45,2,8100]{2,1,0:T(2,128)(2,1)} %bitcast.27, bf16[45,2,8100]{2,1,0:T(2,128)(2,1)} %copy-done, ...), custom_call_target="tpu_custom_call" | custom-call | flops 895795200 | bytes 9720000 | tf_op jit(solution)/shard_map/contract/pallas_call | solution.py:341
  60.0 4.9 %collective-permute-done.2.top_ref = bf16[23,2,8100]{2,1,0:T(2,128)(2,1)} collective-permute-done((bf16[23,2,8100]{2,1,0:T(2,128)(2,1)}, bf16[23,2,8100]{2,1,0:T(2,128)(2,1)}, u32[]{:S(2)}, u32[]{:S(2)}) %collective-permute-start.2) | collective-permute-done | bytes 745232 | tf_op jit(solution)/shard_map/force_second/ppermute | solution.py:317
  64.9 0.8 collective-permute-done.3.bottom_ref
  65.7 0.5 collective-permute-start.7
  66.2 0.0 collective-permute-start.8
  66.2 0.5 collective-permute-start.9
  66.7 0.6 fusion.9
  67.3 1.3 %iota_compare_fusion.2 = (pred[32]{0:T(512)(128)(4,1)S(1)}, pred[32]{0:T(512)(128)(4,1)S(1)}) fusion(s32[]{:T(128)} %bitcast.11, s32[]{:T(128)} %bitcast), kind=kLoop, calls=%fused_computation.25 | loop fusion | flops 64 | bytes 72 | tf_op jit(solution)/shard_map/collect/eq | solution.py:379
  68.6 0.3 collective-permute-done.7.other1_ref
  69.0 0.6 collective-permute-done.8.other2_ref
  69.5 0.6 collective-permute-done.9.other3_ref
  70.1 0.1 copy-done.7
  70.3 0.6 copy-done.8
  70.8 0.3 copy-done.4
  71.1 0.2 copy-done.3
  71.3 12.7 %interaction.1 = f32[8,128]{1,0:T(8,128)} custom-call(f32[2,48,128]{2,1,0:T(8,128)} %get-tuple-element.15.scalars_ref, bf16[192,192]{1,0:T(8,128)(2,1)} %get-tuple-element.16.middle_ref, bf16[256,256]{1,0:T(8,128)(2,1)} %get-tuple-element.17.last_ref, f32[4,96,128]{2,1,0:T(8,128)} %get-tuple-element.18.tables_ref, ...), custom_call_target="tpu_custom_call" | custom-call | tf_op jit(solution)/shard_map/interaction/pallas_call | solution.py:357
  84.1 0.7 slice_bitcast_fusion
  84.8 1.8 %collective-permute-start.10 = (f32[1,128]{1,0:T(1,128)S(1)}, f32[1,128]{1,0:T(1,128)S(1)}, u32[]{:S(2)}, u32[]{:S(2)}) collective-permute-start(f32[1,128]{1,0:T(1,128)S(1)} %get-tuple-element.31), channel_id=1, source_target_pairs={{0,64},{64,128},{128,192},{192,0},{1,65},{65,129},{129,193},{193,1... | collective-permute-start | bytes 1544 | tf_op jit(solution)/shard_map/collect/ppermute | solution.py:374
  86.5 3.0 %collective-permute-start.11 = (f32[1,128]{1,0:T(1,128)S(1)}, f32[1,128]{1,0:T(1,128)S(1)}, u32[]{:S(2)}, u32[]{:S(2)}) collective-permute-start(f32[1,128]{1,0:T(1,128)S(1)} %get-tuple-element.31), channel_id=1, source_target_pairs={{0,128},{64,192},{128,0},{192,64},{1,129},{65,193},{129,1},{193,65... | collective-permute-start | bytes 1544 | tf_op jit(solution)/shard_map/collect/ppermute | solution.py:374
  89.5 2.1 %collective-permute-start.12 = (f32[1,128]{1,0:T(1,128)S(1)}, f32[1,128]{1,0:T(1,128)S(1)}, u32[]{:S(2)}, u32[]{:S(2)}) collective-permute-start(f32[1,128]{1,0:T(1,128)S(1)} %get-tuple-element.31), channel_id=1, source_target_pairs={{0,192},{64,0},{128,64},{192,128},{1,193},{65,1},{129,65},{193,129... | collective-permute-start | bytes 1544 | tf_op jit(solution)/shard_map/collect/ppermute | solution.py:374
  91.6 1.2 %iota_compare_fusion = (pred[32]{0:T(512)(128)(4,1)S(1)}, pred[32]{0:T(512)(128)(4,1)S(1)}) fusion(s32[]{:T(128)} %bitcast.15, s32[]{:T(128)} %bitcast.13), kind=kLoop, calls=%fused_computation.23 | loop fusion | flops 64 | bytes 72 | tf_op jit(solution)/shard_map/collect/eq | solution.py:379
  92.8 0.3 collective-permute-done.12
  93.0 0.2 fusion.4
  93.2 15.7 %all_to_all.16 = f32[32,1,128]{2,1,0:T(1,128)S(1)} all-to-all(f32[32,1,128]{2,1,0:T(1,128)S(1)} %fusion.4), channel_id=1, replica_groups=mesh['clus'=4,'trip'=32,'mode'=2] {'trip'}, dimensions={0} | all-to-all | bytes 32768 | tf_op jit(solution)/shard_map/collect/all_to_all | solution.py:380
  109.0 0.6 add_divide_fusion
  (37 shorter events, 0.2 us)
Async XLA Ops:
  0.6 17.8 %copy-start.12 = (bf16[2,4]{1,0:T(2,128)(2,1)S(1)}, bf16[2,4]{1,0:T(2,128)(2,1)}, u32[]{:S(2)}) copy-start(bf16[2,4]{1,0:T(2,128)(2,1)} %param.12) | copy-start | bytes 52
  0.6 43.9 %collective-permute-start = (bf16[45,2,8100]{2,1,0:T(2,128)(2,1)}, bf16[45,2,8100]{2,1,0:T(2,128)(2,1)S(1)}, u32[]{:S(2)}, u32[]{:S(2)}) collective-permute-start(bf16[45,2,8100]{2,1,0:T(2,128)(2,1)} %bitcast.25), channel_id=1, source_target_pairs={{0,64},{64,128},{128,192},{192,0},{1,65},{65,129},{129,193},{193,1... | collective-permute-start | bytes 4374008 | tf_op jit(solution)/shard_map/force/ppermute | solution.py:302
  2.2 42.3 %collective-permute-start.1 = (bf16[45,2,8100]{2,1,0:T(2,128)(2,1)}, bf16[45,2,8100]{2,1,0:T(2,128)(2,1)S(1)}, u32[]{:S(2)}, u32[]{:S(2)}) collective-permute-start(bf16[45,2,8100]{2,1,0:T(2,128)(2,1)} %bitcast.26), channel_id=1, source_target_pairs={{0,192},{64,0},{128,64},{192,128},{1,193},{65,1},{129,65},{193,129... | collective-permute-start | bytes 4374008 | tf_op jit(solution)/shard_map/force/ppermute | solution.py:303
  7.3 22.9 %all-to-all-start = ((bf16[32,12,180]{2,1,0:T(8,128)(2,1)}), bf16[32,12,180]{2,1,0:T(8,128)(2,1)S(1)}, u32[]{:S(2)}, u32[]{:S(2)}) async-start(bf16[32,12,180]{2,1,0:T(8,128)(2,1)} %records.1), calls=%async_computation | async-start | bytes 524288 | tf_op jit(solution)/shard_map/records/all_to_all | solution.py:295
  30.3 0.7 copy-start.2
  44.5 5.4 %copy-start.13 = (s32[4]{0:T(128)S(1)}, s32[4]{0:T(128)}, u32[]{:S(2)}) copy-start(s32[4]{0:T(128)} %param.19) | copy-start | bytes 52
  44.5 3.4 %copy-start = (bf16[45,2,8100]{2,1,0:T(2,128)(2,1)}, bf16[45,2,8100]{2,1,0:T(2,128)(2,1)S(1)}, u32[]{:S(2)}) copy-start(bf16[45,2,8100]{2,1,0:T(2,128)(2,1)S(1)} %collective-permute-done.low_ref) | copy-start | bytes 4374004
  44.5 9.6 %copy-start.1 = (bf16[45,2,8100]{2,1,0:T(2,128)(2,1)}, bf16[45,2,8100]{2,1,0:T(2,128)(2,1)S(1)}, u32[]{:S(2)}) copy-start(bf16[45,2,8100]{2,1,0:T(2,128)(2,1)S(1)} %collective-permute-done.1.high_ref) | copy-start | bytes 4374004
  46.4 18.5 %collective-permute-start.2 = (bf16[23,2,8100]{2,1,0:T(2,128)(2,1)}, bf16[23,2,8100]{2,1,0:T(2,128)(2,1)}, u32[]{:S(2)}, u32[]{:S(2)}) collective-permute-start(bf16[23,2,8100]{2,1,0:T(2,128)(2,1)} %slice.17), channel_id=1, source_target_pairs={{0,64},{64,128},{128,192},{192,0},{1,65},{65,129},{129,193},{193,1... | collective-permute-start | bytes 2235608 | tf_op jit(solution)/shard_map/force_second/ppermute | solution.py:317
  47.9 17.8 %collective-permute-start.3 = (bf16[22,2,8100]{2,1,0:T(2,128)(2,1)}, bf16[22,2,8100]{2,1,0:T(2,128)(2,1)}, u32[]{:S(2)}, u32[]{:S(2)}) collective-permute-start(bf16[22,2,8100]{2,1,0:T(2,128)(2,1)} %slice.18), channel_id=1, source_target_pairs={{0,192},{64,0},{128,64},{192,128},{1,193},{65,1},{129,65},{193,129... | collective-permute-start | bytes 2138408 | tf_op jit(solution)/shard_map/force_second/ppermute | solution.py:318
  54.1 12.6 %copy-start.9 = (s32[4]{0:T(128)S(1)}, s32[4]{0:T(128)}, u32[]{:S(2)}) copy-start(s32[4]{0:T(128)} %param.18) | copy-start | bytes 52
  60.0 6.2 %collective-permute-start.6 = (bf16[24,8100]{1,0:T(8,128)(2,1)}, bf16[24,8100]{1,0:T(8,128)(2,1)S(1)}, u32[]{:S(2)}, u32[]{:S(2)}) collective-permute-start(bf16[24,8100]{1,0:T(8,128)(2,1)} %get-tuple-element.24), channel_id=1, source_target_pairs={{0,1},{1,0},{2,3},{3,2},{4,5},{5,4},{6,7},{7,6},{8,9},{9,8},{10,11... | collective-permute-start | bytes 1166408 | tf_op jit(solution)/shard_map/contract/ppermute | solution.py:352
  64.9 5.2 %collective-permute-start.4 = (bf16[23,2,8100]{2,1,0:T(2,128)(2,1)}, bf16[23,2,8100]{2,1,0:T(2,128)(2,1)S(1)}, u32[]{:S(2)}, u32[]{:S(2)}) collective-permute-start(bf16[23,2,8100]{2,1,0:T(2,128)(2,1)} %collective-permute-done.2.top_ref), channel_id=1, source_target_pairs={{0,1},{1,0},{2,3},{3,2},{4,5},{5,4},{6,7},{7,6},{8,9},{9,8},{10,11... | collective-permute-start | bytes 2235608 | tf_op jit(solution)/shard_map/contract/ppermute | solution.py:353
  65.7 4.4 %collective-permute-start.5 = (bf16[22,2,8100]{2,1,0:T(2,128)(2,1)}, bf16[22,2,8100]{2,1,0:T(2,128)(2,1)S(1)}, u32[]{:S(2)}, u32[]{:S(2)}) collective-permute-start(bf16[22,2,8100]{2,1,0:T(2,128)(2,1)} %collective-permute-done.3.bottom_ref), channel_id=1, source_target_pairs={{0,1},{1,0},{2,3},{3,2},{4,5},{5,4},{6,7},{7,6},{8,9},{9,8},{10,11... | collective-permute-start | bytes 2138408 | tf_op jit(solution)/shard_map/contract/ppermute | solution.py:354
  65.7 3.2 %collective-permute-start.7 = (bf16[24,8100]{1,0:T(8,128)(2,1)}, bf16[24,8100]{1,0:T(8,128)(2,1)S(1)}, u32[]{:S(2)}, u32[]{:S(2)}) collective-permute-start(bf16[24,8100]{1,0:T(8,128)(2,1)} %get-tuple-element.25), channel_id=1, source_target_pairs={{0,1},{1,0},{2,3},{3,2},{4,5},{5,4},{6,7},{7,6},{8,9},{9,8},{10,11... | collective-permute-start | bytes 1166408 | tf_op jit(solution)/shard_map/contract/ppermute | solution.py:352
  66.2 3.3 %collective-permute-start.8 = (bf16[24,8100]{1,0:T(8,128)(2,1)}, bf16[24,8100]{1,0:T(8,128)(2,1)S(1)}, u32[]{:S(2)}, u32[]{:S(2)}) collective-permute-start(bf16[24,8100]{1,0:T(8,128)(2,1)} %get-tuple-element.26), channel_id=1, source_target_pairs={{0,1},{1,0},{2,3},{3,2},{4,5},{5,4},{6,7},{7,6},{8,9},{9,8},{10,11... | collective-permute-start | bytes 1166408 | tf_op jit(solution)/shard_map/contract/ppermute | solution.py:352
  66.2 3.9 %copy-start.5 = (bf16[24,8100]{1,0:T(8,128)(2,1)}, bf16[24,8100]{1,0:T(8,128)(2,1)S(1)}, u32[]{:S(2)}) copy-start(bf16[24,8100]{1,0:T(8,128)(2,1)S(1)} %collective-permute-done.6.other0_ref) | copy-start | bytes 1166404
  66.2 3.9 %collective-permute-start.9 = (bf16[24,8100]{1,0:T(8,128)(2,1)}, bf16[24,8100]{1,0:T(8,128)(2,1)S(1)}, u32[]{:S(2)}, u32[]{:S(2)}) collective-permute-start(bf16[24,8100]{1,0:T(8,128)(2,1)} %get-tuple-element.27), channel_id=1, source_target_pairs={{0,1},{1,0},{2,3},{3,2},{4,5},{5,4},{6,7},{7,6},{8,9},{9,8},{10,11... | collective-permute-start | bytes 1166408 | tf_op jit(solution)/shard_map/contract/ppermute | solution.py:352
  69.0 1.2 %copy-start.6 = (bf16[24,8100]{1,0:T(8,128)(2,1)}, bf16[24,8100]{1,0:T(8,128)(2,1)S(1)}, u32[]{:S(2)}) copy-start(bf16[24,8100]{1,0:T(8,128)(2,1)S(1)} %collective-permute-done.7.other1_ref) | copy-start | bytes 1166404
  69.5 0.7 copy-start.7
  70.1 0.7 copy-start.8
  70.1 1.0 copy-start.4
  70.1 1.2 %copy-start.3 = (bf16[23,2,8100]{2,1,0:T(2,128)(2,1)}, bf16[23,2,8100]{2,1,0:T(2,128)(2,1)S(1)}, u32[]{:S(2)}) copy-start(bf16[23,2,8100]{2,1,0:T(2,128)(2,1)S(1)} %collective-permute-done.4.far_top_ref) | copy-start | bytes 2235604
  71.3 37.6 %copy-start.10 = (f32[1,45]{1,0:T(1,128)S(1)}, f32[1,45]{1,0:T(1,128)}, u32[]{:S(2)}) copy-start(f32[1,45]{1,0:T(1,128)} %param.20) | copy-start | bytes 544
  71.3 37.6 %copy-start.11 = (f32[1,45]{1,0:T(1,128)S(1)}, f32[1,45]{1,0:T(1,128)}, u32[]{:S(2)}) copy-start(f32[1,45]{1,0:T(1,128)} %param.21) | copy-start | bytes 544
  84.8 8.0 %collective-permute-start.10 = (f32[1,128]{1,0:T(1,128)S(1)}, f32[1,128]{1,0:T(1,128)S(1)}, u32[]{:S(2)}, u32[]{:S(2)}) collective-permute-start(f32[1,128]{1,0:T(1,128)S(1)} %get-tuple-element.31), channel_id=1, source_target_pairs={{0,64},{64,128},{128,192},{192,0},{1,65},{65,129},{129,193},{193,1... | collective-permute-start | bytes 1544 | tf_op jit(solution)/shard_map/collect/ppermute | solution.py:374
  86.5 6.2 %collective-permute-start.11 = (f32[1,128]{1,0:T(1,128)S(1)}, f32[1,128]{1,0:T(1,128)S(1)}, u32[]{:S(2)}, u32[]{:S(2)}) collective-permute-start(f32[1,128]{1,0:T(1,128)S(1)} %get-tuple-element.31), channel_id=1, source_target_pairs={{0,128},{64,192},{128,0},{192,64},{1,129},{65,193},{129,1},{193,65... | collective-permute-start | bytes 1544 | tf_op jit(solution)/shard_map/collect/ppermute | solution.py:374
  89.5 3.5 %collective-permute-start.12 = (f32[1,128]{1,0:T(1,128)S(1)}, f32[1,128]{1,0:T(1,128)S(1)}, u32[]{:S(2)}, u32[]{:S(2)}) collective-permute-start(f32[1,128]{1,0:T(1,128)S(1)} %get-tuple-element.31), channel_id=1, source_target_pairs={{0,192},{64,0},{128,64},{192,128},{1,193},{65,1},{129,65},{193,129... | collective-permute-start | bytes 1544 | tf_op jit(solution)/shard_map/collect/ppermute | solution.py:374

commit v6 on v5

--- a/solution.py
+++ b/solution.py
@@ -145,54 +145,49 @@
             far_ref[:, cols] = rows.astype(far_ref.dtype)
 
 
-def interaction_kernel(
-    scalars_ref,
-    middle_ref,
-    last_ref,
-    tables_ref,
-    late_ref,
-    top_ref,
-    bottom_ref,
-    far_top_ref,
-    far_bottom_ref,
-    mine_ref,
-    other0_ref,
-    other1_ref,
-    other2_ref,
-    other3_ref,
-    out_ref,
-    flat,
-    windows,
-    mid_real,
-    mid_imag,
-    rate_acc,
-    couple_acc,
-):
+def interaction_kernel(*refs):
+    count = 14
+    operands, out_ref, buffers = refs[:count], refs[count], refs[count + 1 : 2 * count + 1]
+    flat, windows, mid_real, mid_imag, rate_acc, couple_acc, done = refs[2 * count + 1 :]
+    scalars_ref, middle_ref, last_ref, tables_ref, late_ref = buffers[:5]
+    top_ref, bottom_ref, far_top_ref, far_bottom_ref, mine_ref = buffers[5:10]
+    late, others = buffers[5:9], buffers[10:]
     total = mine_ref.shape[1]
+    pieces = [slice(at, min(at + CHUNK, total)) for at in range(0, total, CHUNK)]
+    whole = {}
+    for i in range(5):
+        whole[i] = pltpu.make_async_copy(operands[i], buffers[i], done.at[i, 0])
+    parts = {}
+    for k, cols in enumerate(pieces):
+        for i in range(5, count):
+            where = (slice(None),) * (len(operands[i].shape) - 1) + (cols,)
+            parts[i, k] = pltpu.make_async_copy(
+                operands[i].at[where], buffers[i].at[where], done.at[i, k]
+            )
+    whole[4].start()
+    for i in range(5, count):
+        parts[i, 0].start()
+    whole[2].start()
+    for k in range(1, len(pieces)):
+        for i in range(5, count):
+            parts[i, k].start()
+    for i in (0, 1, 3):
+        whole[i].start()
+
     flat[:, 8064:8320] = jnp.zeros((WIDE, 256), flat.dtype)
-    for start in range(0, total, 1024):
-        cols = slice(start, min(start + 1024, total))
-        late = (top_ref, bottom_ref, far_top_ref, far_bottom_ref)
-        others = (other0_ref, other1_ref, other2_ref, other3_ref)
-        other = jnp.concatenate([ref[:, cols].astype(jnp.float32) for ref in others], axis=0)
-        both = mine_ref[:, cols].astype(jnp.float32) + other
-        both = both + jnp.dot(
-            late_ref[...],
-            jnp.concatenate([rows_of(ref, cols, PAD) for ref in late], axis=0),
-            preferred_element_type=jnp.float32,
-        )
-        flat[:, cols] = both.astype(flat.dtype)
-    for b in range(90):
+    zeros = jnp.zeros((PAD, 128), jnp.float32)
+    for b in range(90, WIDE):
+        mid_real[pl.ds(b, PAD, stride=WIDE), :] = zeros
+        mid_imag[pl.ds(b, PAD, stride=WIDE), :] = zeros
+
+    def window_of(b):
         tile, shift = divmod(90 * b, 128)
         pair = flat[:, tile * 128 : tile * 128 + 256]
         window = pair[:, shift : shift + 128]
         windows[b * PAD : (b + 1) * PAD, 0:128] = window[0:PAD]
         windows[b * PAD : (b + 1) * PAD, 128:256] = window[PAD:]
-    zeros = jnp.zeros((PAD, 128), jnp.float32)
-    for b in range(90, WIDE):
-        mid_real[pl.ds(b, PAD, stride=WIDE), :] = zeros
-        mid_imag[pl.ds(b, PAD, stride=WIDE), :] = zeros
-    for group in range(9):
+
+    def product_of(group):
         product = jnp.dot(
             windows[group * 480 : (group + 1) * 480, :],
             last_ref[...],
@@ -202,6 +197,30 @@
             rows = pl.ds(group * 10 + i, PAD, stride=WIDE)
             mid_real[rows, :] = product[i * PAD : (i + 1) * PAD, 0:128]
             mid_imag[rows, :] = product[i * PAD : (i + 1) * PAD, 128:256]
+
+    whole[4].wait()
+    b = 0
+    for k, cols in enumerate(pieces):
+        for i in range(5, count):
+            parts[i, k].wait()
+        if k == 0:
+            whole[2].wait()
+        other = jnp.concatenate([ref[:, cols].astype(jnp.float32) for ref in others], axis=0)
+        both = mine_ref[:, cols].astype(jnp.float32) + other
+        both = both + jnp.dot(
+            late_ref[...],
+            jnp.concatenate([rows_of(ref, cols, PAD) for ref in late], axis=0),
+            preferred_element_type=jnp.float32,
+        )
+        flat[:, cols] = both.astype(flat.dtype)
+        ready = 8320 if cols.stop == total else cols.stop
+        while b < 90 and 90 * b // 128 * 128 + 256 <= ready:
+            window_of(b)
+            b += 1
+            if b % 10 == 0:
+                product_of(b // 10 - 1)
+    for i in (0, 1, 3):
+        whole[i].wait()
 
     scaled = 0.5 / (smearing * smearing)
     def two_modes(s):
@@ -248,8 +267,8 @@
         (((1,), (1,)), ((), ())),
         precision=lax.Precision.HIGHEST,
         preferred_element_type=jnp.float32,
-    )
-    out_ref[:, WIDE:128] = jnp.zeros((8, 128 - WIDE), jnp.float32)
+    )[0:1]
+    out_ref[:, WIDE:128] = jnp.zeros((1, 128 - WIDE), jnp.float32)
 
 
 VMEM = pl.BlockSpec(memory_space=pltpu.VMEM)
@@ -313,9 +332,9 @@
         members = lax.all_to_all(picks, group, 0, 0, tiled=True)
 
     with jax.named_scope("force_second"):
-        low, high, _ = lax.optimization_barrier((low, high, members))
-        top = lax.ppermute(low[:TOP], "clus", ring(4, 1))
-        bottom = lax.ppermute(high[TOP:], "clus", ring(4, 3))
+        low_top, high_bottom, _ = lax.optimization_barrier((low[:TOP], high[TOP:], members))
+        top = lax.ppermute(low_top, "clus", ring(4, 1))
+        bottom = lax.ppermute(high_bottom, "clus", ring(4, 3))
 
     with jax.named_scope("operands"):
         mult = lax.dynamic_index_in_dim(multiplicity, clus, 0, keepdims=False)
@@ -354,23 +373,26 @@
         far_bottom = lax.ppermute(bottom, "mode", swap)
 
     with jax.named_scope("interaction"):
+        inputs = (scalars, mid, last_all, tables, late, top, bottom, far_top, far_bottom, mine, *other)
         sums = pl.pallas_call(
             interaction_kernel,
-            out_shape=jax.ShapeDtypeStruct((8, 128), f32),
-            in_specs=[VMEM] * 14,
+            out_shape=jax.ShapeDtypeStruct((1, 128), f32),
+            in_specs=[pl.BlockSpec(memory_space=pl.ANY)] * len(inputs),
             out_specs=VMEM,
-            scratch_shapes=[
+            scratch_shapes=[pltpu.VMEM(x.shape, x.dtype) for x in inputs]
+            + [
                 pltpu.VMEM((WIDE, 8320), b16),
                 pltpu.VMEM((90 * PAD, 256), b16),
                 pltpu.VMEM((PAD * WIDE, 128), f32),
                 pltpu.VMEM((PAD * WIDE, 128), f32),
                 pltpu.VMEM((8 * PAD, 128), f32),
                 pltpu.VMEM((8 * PAD, 128), f32),
+                pltpu.SemaphoreType.DMA((len(inputs), 4)),
             ],
             compiler_params=PARAMS,
-        )(scalars, mid, last_all, tables, late, top, bottom, far_top, far_bottom, mine, *other)
+        )(*inputs)
     with jax.named_scope("collect"):
-        own_row = sums[0:1]
+        own_row = sums
         rows = [own_row] + [lax.ppermute(own_row, "clus", ring(4, step)) for step in (1, 2, 3)]
         points = jnp.arange(32, dtype=jnp.int32)
         partial = jnp.zeros((32, 128), f32)

time: 111 us -> 107 us (0.964); the launches traced: 110 us -> 107 us
  blocking collectives: 27.6 us -> 16.3 us
  waiting for transfers between devices: 18.4 us -> 24.1 us
  starting transfers between devices: 23.4 us -> 27.3 us
    all_to_all x1 -> x0, blocking collectives: 11.9 us -> none  [body(): members = lax.all_to_all(picks, group, 0, 0, tiled=True)]
    all_to_all x0 -> x1, starting transfers between devices: none -> 5.06 us  [body(): members = lax.all_to_all(picks, group, 0, 0, tiled=True)]
    all_to_all x0 -> x1, waiting for transfers between devices: none -> 3.04 us  [body(): members = lax.all_to_all(picks, group, 0, 0, tiled=True)]
    ppermute x3, waiting for transfers between devices: 0.26 us -> 1.75 us  [body(): lax.ppermute(own_row, 'clus', ring(4, step))]
    ppermute x3, starting transfers between devices: 6.8 us -> 5.38 us  [body(): lax.ppermute(own_row, 'clus', ring(4, step))]
    slice x3 -> x2, local copies, waits for them, and re-layouts: 4.04 us -> 3.04 us  [the longest x1 1.53 us: body(): low[:TOP]]
  transfers between devices with their start and end apart: 14 -> 15, of which waited for: 7 -> 7; matrix products, arithmetic and copies ran while one was open for 9% -> 11% of each run, Pallas kernels for 10% -> 11%
where the time goes in v6:
time: 107 us
  starting transfers between devices  27.3 us (26%)
  waiting for transfers between devices  24.1 us (23%)
  Pallas kernels  23.3 us (22%)
  blocking collectives  16.3 us (15%)
  local copies, waits for them, and re-layouts  8.01 us (7%)
  other arithmetic  6.89 us (6%)
    all_to_all x1, blocking collectives, body(): received = lax.all_to_all(partial[:, None, :], 'trip', 0, 0, tiled=True)  16.3 us
    pallas_call x1, Pallas kernels, body(): pl.pallas_call(interaction_kernel, out_shape=jax.ShapeDtypeStruct((1, 128...  11.9 us
    all_to_all x1, starting transfers between devices, body(): arrived = lax.all_to_all(chosen, 'trip', 0, 0, tiled=True)  11.1 us
    all_to_all x1, waiting for transfers between devices, body(): arrived = lax.all_to_all(chosen, 'trip', 0, 0, tiled=True)  11 us
    ppermute x1, waiting for transfers between devices, body(): top = lax.ppermute(low_top, 'clus', ring(4, 1))  6.36 us
    pallas_call x1, Pallas kernels, body(): pl.pallas_call(early_kernel, out_shape=(jax.ShapeDtypeStruct((WIDE, total...  5.83 us
    ppermute x3, starting transfers between devices, body(): lax.ppermute(own_row, 'clus', ring(4, step))  5.38 us
    all_to_all x1, starting transfers between devices, body(): members = lax.all_to_all(picks, group, 0, 0, tiled=True)  5.06 us
  transfers between devices with their start and end apart: 15, of which 7 were waited for; matrix products, arithmetic and copies ran while one was open for 11% of the time, Pallas kernels for 11%

profile of v6, /device:TPU:2, one launch (start us, length us, event | category | flops | bytes accessed | tf_op | source)
XLA Modules:
  0.0 106.8 jit_solution(11035087829239510206)
XLA Ops:
  0.6 1.6 %collective-permute-start = (bf16[45,2,8100]{2,1,0:T(2,128)(2,1)}, bf16[45,2,8100]{2,1,0:T(2,128)(2,1)S(1)}, u32[]{:S(2)}, u32[]{:S(2)}) collective-permute-start(bf16[45,2,8100]{2,1,0:T(2,128)(2,1)} %bitcast.24), channel_id=1, source_target_pairs={{0,64},{64,128},{128,192},{192,0},{1,65},{65,129},{129,193},{193,1... | collective-permute-start | bytes 4374008 | tf_op jit(solution)/shard_map/force/ppermute | solution.py:321
  2.2 0.9 collective-permute-start.1
  3.1 1.1 copy.27
  4.1 0.8 maximum_bitcast_fusion
  4.9 0.1 pad_dynamic-slice_fusion.2
  5.0 0.7 fusion.1.share_ref
  5.7 1.6 %records.1 = bf16[32,12,180]{2,1,0:T(8,128)(2,1)} custom-call(s32[1,32]{1,0:T(1,128)} %rows_ref.1, bf16[8,12,180]{2,1,0:T(8,128)(2,1)} %fusion.1.share_ref), custom_call_target="tpu_custom_call" | custom-call | tf_op jit(solution)/shard_map/records/pallas_call | solution.py:307
  7.3 11.1 %all-to-all-start = ((bf16[32,12,180]{2,1,0:T(8,128)(2,1)}), bf16[32,12,180]{2,1,0:T(8,128)(2,1)S(1)}, u32[]{:S(2)}, u32[]{:S(2)}) async-start(bf16[32,12,180]{2,1,0:T(8,128)(2,1)} %records.1), calls=%async_computation | async-start | bytes 524288 | tf_op jit(solution)/shard_map/records/all_to_all | solution.py:314
  18.5 0.1 copy.31
  18.7 0.6 pad.4.phase_ref
  19.3 11.0 %all-to-all-done.arrived_ref = bf16[32,12,180]{2,1,0:T(8,128)(2,1)S(1)} async-done(((bf16[32,12,180]{2,1,0:T(8,128)(2,1)}), bf16[32,12,180]{2,1,0:T(8,128)(2,1)S(1)}, u32[]{:S(2)}, u32[]{:S(2)}) %all-to-all-start) | async-done | bytes 138272 | tf_op jit(solution)/shard_map/records/all_to_all | solution.py:314
  30.2 0.7 copy-done.3
  30.9 1.7 %members.1 = bf16[8,4,16,180]{3,2,1,0:T(8,128)(2,1)} custom-call(s32[4,3]{1,0:T(4,128)} %table_ref.1, bf16[32,12,180]{2,1,0:T(8,128)(2,1)} %copy-done.3, bf16[4,16,180]{2,1,0:T(8,128)(2,1)} %pad.4.phase_ref), custom_call_target="tpu_custom_call" | custom-call | tf_op jit(solution)/shard_map/members/pallas_call | solution.py:325
  32.6 5.1 %all-to-all-start.1 = ((bf16[8,4,16,180]{3,2,1,0:T(8,128)(2,1)}), bf16[8,4,16,180]{3,2,1,0:T(8,128)(2,1)S(1)}, u32[]{:S(2)}, u32[]{:S(2)}) async-start(bf16[8,4,16,180]{3,2,1,0:T(8,128)(2,1)} %members.1), calls=%async_computation.1 | async-start | bytes 524288 | tf_op jit(solution)/shard_map/members/all_to_all | solution.py:332
  37.7 1.5 %slice.16 = bf16[23,2,8100]{2,1,0:T(2,128)(2,1)} slice(bf16[45,2,8100]{2,1,0:T(2,128)(2,1)S(1)} %collective-permute-done.low_ref), slice={[0:23], [0:2], [0:8100]} | slice | bytes 1490400 | tf_op jit(solution)/shard_map/force_second/slice | solution.py:335
  39.2 1.5 %slice.17 = bf16[22,2,8100]{2,1,0:T(2,128)(2,1)} slice(bf16[45,2,8100]{2,1,0:T(2,128)(2,1)S(1)} %collective-permute-done.1.high_ref), slice={[23:45], [0:2], [0:8100]} | slice | bytes 1425600 | tf_op jit(solution)/shard_map/force_second/slice | solution.py:335
  40.8 3.0 %all-to-all-done.1.members_ref = bf16[8,4,16,180]{3,2,1,0:T(8,128)(2,1)S(1)} async-done(((bf16[8,4,16,180]{3,2,1,0:T(8,128)(2,1)}), bf16[8,4,16,180]{3,2,1,0:T(8,128)(2,1)S(1)}, u32[]{:S(2)}, u32[]{:S(2)}) %all-to-all-start.1) | async-done | bytes 184352 | tf_op jit(solution)/shard_map/members/all_to_all | solution.py:332
  43.8 0.0 collective-permute-start.2
  43.8 2.0 %collective-permute-start.3 = (bf16[22,2,8100]{2,1,0:T(2,128)(2,1)}, bf16[22,2,8100]{2,1,0:T(2,128)(2,1)S(1)}, u32[]{:S(2)}, u32[]{:S(2)}) collective-permute-start(bf16[22,2,8100]{2,1,0:T(2,128)(2,1)} %slice.17), channel_id=1, source_target_pairs={{0,192},{64,0},{128,64},{192,128},{1,193},{65,1},{129,65},{193,129... | collective-permute-start | bytes 2138408 | tf_op jit(solution)/shard_map/force_second/ppermute | solution.py:337
  45.8 0.6 dynamic_slice.20
  46.4 1.3 %pad_add_fusion.where_ref = s32[3]{0:T(128)} fusion(s32[1]{0:T(128)} %dynamic_slice.20, s32[1]{0:T(128)} %bitcast.2, s32[1]{0:T(128)} %bitcast.1), kind=kLoop, calls=%fused_computation.20 | loop fusion | flops 6 | bytes 24 | tf_op jit(solution)/shard_map/operands/stack | solution.py:341
  47.7 2.3 %operands.1 = (bf16[192,288]{1,0:T(8,128)(2,1)}, bf16[96,192]{1,0:T(8,128)(2,1)}, bf16[192,192]{1,0:T(8,128)(2,1)}, bf16[256,256]{1,0:T(8,128)(2,1)}, f32[4,96,128]{2,1,0:T(8,128)}, /*index=5*/f32[2,48,128]{2,1,0:T(8,128)}) custom-call(s32[3]{0:T(128)} %pad_add_fusion.where_ref, bf16[8,4,16,180]{3,2,1,0:T(8,128)(2,1)} %copy-done.2), custom_call_target="tpu_custom_call" | custom-call | tf_op jit(solution)/shard_map/operands/pallas_call | solution.py:342
  50.0 5.8 %contract.1 = (bf16[96,8100]{1,0:T(8,128)(2,1)}, bf16[24,8100]{1,0:T(8,128)(2,1)}, bf16[24,8100]{1,0:T(8,128)(2,1)}, bf16[24,8100]{1,0:T(8,128)(2,1)}, bf16[24,8100]{1,0:T(8,128)(2,1)}) custom-call(bf16[192,288]{1,0:T(8,128)(2,1)} %get-tuple-element.22.lead_ref, bf16[45,2,8100]{2,1,0:T(2,128)(2,1)} %bitcast.26, bf16[45,2,8100]{2,1,0:T(2,128)(2,1)} %copy-done, ...), custom_call_target="tpu_custom_call" | custom-call | flops 895795200 | bytes 9720000 | tf_op jit(solution)/shard_map/contract/pallas_call | solution.py:360
  55.9 0.0 collective-permute-start.6
  55.9 6.4 %collective-permute-done.2.refs_5_ = bf16[23,2,8100]{2,1,0:T(2,128)(2,1)S(1)} collective-permute-done((bf16[23,2,8100]{2,1,0:T(2,128)(2,1)}, bf16[23,2,8100]{2,1,0:T(2,128)(2,1)S(1)}, u32[]{:S(2)}, u32[]{:S(2)}) %collective-permute-start.2) | collective-permute-done | bytes 745232 | tf_op jit(solution)/shard_map/force_second/ppermute | solution.py:336
  62.2 0.0 collective-permute-start.4
  62.2 0.0 collective-permute-done.3.refs_6_
  62.2 0.5 collective-permute-start.5
  62.7 0.1 collective-permute-start.7
  62.8 0.4 collective-permute-start.8
  63.3 0.3 collective-permute-start.9
  63.5 0.7 fusion.9
  64.2 1.3 %iota_compare_fusion.2 = (pred[32]{0:T(512)(128)(4,1)S(1)}, pred[32]{0:T(512)(128)(4,1)S(1)}) fusion(s32[]{:T(128)} %bitcast.11, s32[]{:T(128)} %bitcast), kind=kLoop, calls=%fused_computation.25 | loop fusion | flops 64 | bytes 72 | tf_op jit(solution)/shard_map/collect/eq | solution.py:401
  65.5 0.4 collective-permute-done.7.refs_11_
  65.9 1.0 collective-permute-done.8.refs_12_
  67.0 0.6 collective-permute-done.9.refs_13_
  67.6 0.8 copy-done.7
  68.4 0.3 copy-done.5
  68.7 11.9 %interaction.1 = f32[1,128]{1,0:T(1,128)} custom-call(f32[2,48,128]{2,1,0:T(8,128)} %get-tuple-element.15.refs_0_, bf16[192,192]{1,0:T(8,128)(2,1)} %get-tuple-element.16.refs_1_, bf16[256,256]{1,0:T(8,128)(2,1)} %get-tuple-element.17.refs_2_, f32[4,96,128]{2,1,0:T(8,128)} %get-tuple-element.18.refs_3_, bf16[96,192]{1,0:T(8,128)(2,1)} %get-tuple-element.19.refs_4_, ...), custom_call_target="tpu_custom_call" | custom-call | tf_op jit(solution)/shard_map/interaction/pallas_call | solution.py:377
  80.5 0.4 collective-permute-start.10
  80.9 4.4 %collective-permute-start.11 = (f32[1,128]{1,0:T(1,128)}, f32[1,128]{1,0:T(1,128)S(1)}, u32[]{:S(2)}, u32[]{:S(2)}) collective-permute-start(f32[1,128]{1,0:T(1,128)} %interaction.1), channel_id=1, source_target_pairs={{0,128},{64,192},{128,0},{192,64},{1,129},{65,193},{129,1},{193,65... | collective-permute-start | bytes 1544 | tf_op jit(solution)/shard_map/collect/ppermute | solution.py:396
  85.3 0.6 collective-permute-start.12
  85.9 1.3 %iota_compare_fusion = (pred[32]{0:T(512)(128)(4,1)S(1)}, pred[32]{0:T(512)(128)(4,1)S(1)}) fusion(s32[]{:T(128)} %bitcast.15, s32[]{:T(128)} %bitcast.13), kind=kLoop, calls=%fused_computation.23 | loop fusion | flops 64 | bytes 72 | tf_op jit(solution)/shard_map/collect/eq | solution.py:401
  87.3 0.0 collective-permute-done.11
  87.3 1.7 %collective-permute-done.12 = f32[1,128]{1,0:T(1,128)S(1)} collective-permute-done((f32[1,128]{1,0:T(1,128)}, f32[1,128]{1,0:T(1,128)S(1)}, u32[]{:S(2)}, u32[]{:S(2)}) %collective-permute-start.12) | collective-permute-done | bytes 544 | tf_op jit(solution)/shard_map/collect/ppermute | solution.py:396
  89.0 0.9 fusion.4
  89.9 16.3 %all_to_all.15 = f32[32,1,128]{2,1,0:T(1,128)S(1)} all-to-all(f32[32,1,128]{2,1,0:T(1,128)S(1)} %fusion.4), channel_id=1, replica_groups=mesh['clus'=4,'trip'=32,'mode'=2] {'trip'}, dimensions={0} | all-to-all | bytes 32768 | tf_op jit(solution)/shard_map/collect/all_to_all | solution.py:402
  106.2 0.6 add_divide_fusion
  (37 shorter events, 0.2 us)
Async XLA Ops:
  0.6 17.8 %copy-start.12 = (bf16[2,4]{1,0:T(2,128)(2,1)S(1)}, bf16[2,4]{1,0:T(2,128)(2,1)}, u32[]{:S(2)}) copy-start(bf16[2,4]{1,0:T(2,128)(2,1)} %param.12) | copy-start | bytes 52
  0.6 37.1 %collective-permute-start = (bf16[45,2,8100]{2,1,0:T(2,128)(2,1)}, bf16[45,2,8100]{2,1,0:T(2,128)(2,1)S(1)}, u32[]{:S(2)}, u32[]{:S(2)}) collective-permute-start(bf16[45,2,8100]{2,1,0:T(2,128)(2,1)} %bitcast.24), channel_id=1, source_target_pairs={{0,64},{64,128},{128,192},{192,0},{1,65},{65,129},{129,193},{193,1... | collective-permute-start | bytes 4374008 | tf_op jit(solution)/shard_map/force/ppermute | solution.py:321
  2.2 37.0 %collective-permute-start.1 = (bf16[45,2,8100]{2,1,0:T(2,128)(2,1)}, bf16[45,2,8100]{2,1,0:T(2,128)(2,1)S(1)}, u32[]{:S(2)}, u32[]{:S(2)}) collective-permute-start(bf16[45,2,8100]{2,1,0:T(2,128)(2,1)} %bitcast.25), channel_id=1, source_target_pairs={{0,192},{64,0},{128,64},{192,128},{1,193},{65,1},{129,65},{193,129... | collective-permute-start | bytes 4374008 | tf_op jit(solution)/shard_map/force/ppermute | solution.py:322
  7.3 22.9 %all-to-all-start = ((bf16[32,12,180]{2,1,0:T(8,128)(2,1)}), bf16[32,12,180]{2,1,0:T(8,128)(2,1)S(1)}, u32[]{:S(2)}, u32[]{:S(2)}) async-start(bf16[32,12,180]{2,1,0:T(8,128)(2,1)} %records.1), calls=%async_computation | async-start | bytes 524288 | tf_op jit(solution)/shard_map/records/all_to_all | solution.py:314
  30.2 0.7 copy-start.3
  32.6 11.2 %all-to-all-start.1 = ((bf16[8,4,16,180]{3,2,1,0:T(8,128)(2,1)}), bf16[8,4,16,180]{3,2,1,0:T(8,128)(2,1)S(1)}, u32[]{:S(2)}, u32[]{:S(2)}) async-start(bf16[8,4,16,180]{3,2,1,0:T(8,128)(2,1)} %members.1), calls=%async_computation.1 | async-start | bytes 524288 | tf_op jit(solution)/shard_map/members/all_to_all | solution.py:332
  37.7 8.1 %copy-start.13 = (s32[4]{0:T(128)S(1)}, s32[4]{0:T(128)}, u32[]{:S(2)}) copy-start(s32[4]{0:T(128)} %param.19) | copy-start | bytes 52
  37.7 3.1 %copy-start = (bf16[45,2,8100]{2,1,0:T(2,128)(2,1)}, bf16[45,2,8100]{2,1,0:T(2,128)(2,1)S(1)}, u32[]{:S(2)}) copy-start(bf16[45,2,8100]{2,1,0:T(2,128)(2,1)S(1)} %collective-permute-done.low_ref) | copy-start | bytes 4374004
  39.2 10.8 %copy-start.1 = (bf16[45,2,8100]{2,1,0:T(2,128)(2,1)}, bf16[45,2,8100]{2,1,0:T(2,128)(2,1)S(1)}, u32[]{:S(2)}) copy-start(bf16[45,2,8100]{2,1,0:T(2,128)(2,1)S(1)} %collective-permute-done.1.high_ref) | copy-start | bytes 4374004
  43.8 3.9 %copy-start.2 = (bf16[8,4,16,180]{3,2,1,0:T(8,128)(2,1)}, bf16[8,4,16,180]{3,2,1,0:T(8,128)(2,1)S(1)}, u32[]{:S(2)}) copy-start(bf16[8,4,16,180]{3,2,1,0:T(8,128)(2,1)S(1)} %all-to-all-done.1.members_ref) | copy-start | bytes 552964
  43.8 18.4 %collective-permute-start.2 = (bf16[23,2,8100]{2,1,0:T(2,128)(2,1)}, bf16[23,2,8100]{2,1,0:T(2,128)(2,1)S(1)}, u32[]{:S(2)}, u32[]{:S(2)}) collective-permute-start(bf16[23,2,8100]{2,1,0:T(2,128)(2,1)} %slice.16), channel_id=1, source_target_pairs={{0,64},{64,128},{128,192},{192,0},{1,65},{65,129},{129,193},{193,1... | collective-permute-start | bytes 2235608 | tf_op jit(solution)/shard_map/force_second/ppermute | solution.py:336
  43.8 18.4 %collective-permute-start.3 = (bf16[22,2,8100]{2,1,0:T(2,128)(2,1)}, bf16[22,2,8100]{2,1,0:T(2,128)(2,1)S(1)}, u32[]{:S(2)}, u32[]{:S(2)}) collective-permute-start(bf16[22,2,8100]{2,1,0:T(2,128)(2,1)} %slice.17), channel_id=1, source_target_pairs={{0,192},{64,0},{128,64},{192,128},{1,193},{65,1},{129,65},{193,129... | collective-permute-start | bytes 2138408 | tf_op jit(solution)/shard_map/force_second/ppermute | solution.py:337
  50.0 13.5 %copy-start.9 = (s32[4]{0:T(128)S(1)}, s32[4]{0:T(128)}, u32[]{:S(2)}) copy-start(s32[4]{0:T(128)} %param.18) | copy-start | bytes 52
  55.9 7.4 %collective-permute-start.6 = (bf16[24,8100]{1,0:T(8,128)(2,1)}, bf16[24,8100]{1,0:T(8,128)(2,1)S(1)}, u32[]{:S(2)}, u32[]{:S(2)}) collective-permute-start(bf16[24,8100]{1,0:T(8,128)(2,1)} %get-tuple-element.24), channel_id=1, source_target_pairs={{0,1},{1,0},{2,3},{3,2},{4,5},{5,4},{6,7},{7,6},{8,9},{9,8},{10,11... | collective-permute-start | bytes 1166408 | tf_op jit(solution)/shard_map/contract/ppermute | solution.py:371
  62.2 5.3 %copy-start.4 = (bf16[23,2,8100]{2,1,0:T(2,128)(2,1)}, bf16[23,2,8100]{2,1,0:T(2,128)(2,1)S(1)}, u32[]{:S(2)}) copy-start(bf16[23,2,8100]{2,1,0:T(2,128)(2,1)S(1)} %collective-permute-done.2.refs_5_) | copy-start | bytes 2235604
  62.2 5.3 %collective-permute-start.4 = (bf16[23,2,8100]{2,1,0:T(2,128)(2,1)S(1)}, bf16[23,2,8100]{2,1,0:T(2,128)(2,1)S(1)}, u32[]{:S(2)}, u32[]{:S(2)}) collective-permute-start(bf16[23,2,8100]{2,1,0:T(2,128)(2,1)S(1)} %collective-permute-done.2.refs_5_), channel_id=1, source_target_pairs={{0,1},{1,0},{2,3},{3,2},{4,5},{5,4},{6,7},{7,6},{8,9},{9,8},{10,11... | collective-permute-start | bytes 2235608 | tf_op jit(solution)/shard_map/contract/ppermute | solution.py:372
  62.2 5.3 %copy-start.6 = (bf16[22,2,8100]{2,1,0:T(2,128)(2,1)}, bf16[22,2,8100]{2,1,0:T(2,128)(2,1)S(1)}, u32[]{:S(2)}) copy-start(bf16[22,2,8100]{2,1,0:T(2,128)(2,1)S(1)} %collective-permute-done.3.refs_6_) | copy-start | bytes 2138404
  62.2 5.3 %collective-permute-start.5 = (bf16[22,2,8100]{2,1,0:T(2,128)(2,1)S(1)}, bf16[22,2,8100]{2,1,0:T(2,128)(2,1)S(1)}, u32[]{:S(2)}, u32[]{:S(2)}) collective-permute-start(bf16[22,2,8100]{2,1,0:T(2,128)(2,1)S(1)} %collective-permute-done.3.refs_6_), channel_id=1, source_target_pairs={{0,1},{1,0},{2,3},{3,2},{4,5},{5,4},{6,7},{7,6},{8,9},{9,8},{10,11... | collective-permute-start | bytes 2138408 | tf_op jit(solution)/shard_map/contract/ppermute | solution.py:373
  62.7 3.2 %collective-permute-start.7 = (bf16[24,8100]{1,0:T(8,128)(2,1)}, bf16[24,8100]{1,0:T(8,128)(2,1)}, u32[]{:S(2)}, u32[]{:S(2)}) collective-permute-start(bf16[24,8100]{1,0:T(8,128)(2,1)} %get-tuple-element.25), channel_id=1, source_target_pairs={{0,1},{1,0},{2,3},{3,2},{4,5},{5,4},{6,7},{7,6},{8,9},{9,8},{10,11... | collective-permute-start | bytes 1166408 | tf_op jit(solution)/shard_map/contract/ppermute | solution.py:371
  62.8 4.1 %collective-permute-start.8 = (bf16[24,8100]{1,0:T(8,128)(2,1)}, bf16[24,8100]{1,0:T(8,128)(2,1)}, u32[]{:S(2)}, u32[]{:S(2)}) collective-permute-start(bf16[24,8100]{1,0:T(8,128)(2,1)} %get-tuple-element.26), channel_id=1, source_target_pairs={{0,1},{1,0},{2,3},{3,2},{4,5},{5,4},{6,7},{7,6},{8,9},{9,8},{10,11... | collective-permute-start | bytes 1166408 | tf_op jit(solution)/shard_map/contract/ppermute | solution.py:371
  63.3 4.3 %copy-start.8 = (bf16[24,8100]{1,0:T(8,128)(2,1)}, bf16[24,8100]{1,0:T(8,128)(2,1)S(1)}, u32[]{:S(2)}) copy-start(bf16[24,8100]{1,0:T(8,128)(2,1)S(1)} %collective-permute-done.6.refs_10_) | copy-start | bytes 1166404
  63.3 4.3 %collective-permute-start.9 = (bf16[24,8100]{1,0:T(8,128)(2,1)}, bf16[24,8100]{1,0:T(8,128)(2,1)}, u32[]{:S(2)}, u32[]{:S(2)}) collective-permute-start(bf16[24,8100]{1,0:T(8,128)(2,1)} %get-tuple-element.27), channel_id=1, source_target_pairs={{0,1},{1,0},{2,3},{3,2},{4,5},{5,4},{6,7},{7,6},{8,9},{9,8},{10,11... | collective-permute-start | bytes 1166408 | tf_op jit(solution)/shard_map/contract/ppermute | solution.py:371
  67.5 0.9 copy-start.7
  67.5 1.1 %copy-start.5 = (bf16[23,2,8100]{2,1,0:T(2,128)(2,1)}, bf16[23,2,8100]{2,1,0:T(2,128)(2,1)S(1)}, u32[]{:S(2)}) copy-start(bf16[23,2,8100]{2,1,0:T(2,128)(2,1)S(1)} %collective-permute-done.4.refs_7_) | copy-start | bytes 2235604
  68.7 37.6 %copy-start.10 = (f32[1,45]{1,0:T(1,128)S(1)}, f32[1,45]{1,0:T(1,128)}, u32[]{:S(2)}) copy-start(f32[1,45]{1,0:T(1,128)} %param.20) | copy-start | bytes 544
  68.7 37.6 %copy-start.11 = (f32[1,45]{1,0:T(1,128)S(1)}, f32[1,45]{1,0:T(1,128)}, u32[]{:S(2)}) copy-start(f32[1,45]{1,0:T(1,128)} %param.21) | copy-start | bytes 544
  80.5 6.7 %collective-permute-start.10 = (f32[1,128]{1,0:T(1,128)}, f32[1,128]{1,0:T(1,128)S(1)}, u32[]{:S(2)}, u32[]{:S(2)}) collective-permute-start(f32[1,128]{1,0:T(1,128)} %interaction.1), channel_id=1, source_target_pairs={{0,64},{64,128},{128,192},{192,0},{1,65},{65,129},{129,193},{193,1... | collective-permute-start | bytes 1544 | tf_op jit(solution)/shard_map/collect/ppermute | solution.py:396
  80.9 6.4 %collective-permute-start.11 = (f32[1,128]{1,0:T(1,128)}, f32[1,128]{1,0:T(1,128)S(1)}, u32[]{:S(2)}, u32[]{:S(2)}) collective-permute-start(f32[1,128]{1,0:T(1,128)} %interaction.1), channel_id=1, source_target_pairs={{0,128},{64,192},{128,0},{192,64},{1,129},{65,193},{129,1},{193,65... | collective-permute-start | bytes 1544 | tf_op jit(solution)/shard_map/collect/ppermute | solution.py:396
  85.3 3.7 %collective-permute-start.12 = (f32[1,128]{1,0:T(1,128)}, f32[1,128]{1,0:T(1,128)S(1)}, u32[]{:S(2)}, u32[]{:S(2)}) collective-permute-start(f32[1,128]{1,0:T(1,128)} %interaction.1), channel_id=1, source_target_pairs={{0,192},{64,0},{128,64},{192,128},{1,193},{65,1},{129,65},{193,129... | collective-permute-start | bytes 1544 | tf_op jit(solution)/shard_map/collect/ppermute | solution.py:396

commit v7 on v6

--- a/solution.py
+++ b/solution.py
@@ -9,7 +9,12 @@
 PAD = 48
 WIDE = 96
 CHUNK = 2048
-TOP = 23
+HALF = 23
+SHARED = 22
+TOP = 12
+SLOT = 32
+RING_Y = 4
+RING_Z = 8
 
 
 def send_kernel(rows_ref, share_ref, out_ref):
@@ -40,7 +45,7 @@
 def operand_kernel(
     where_ref, members_ref, early_ref, late_ref, middle_ref, last_ref, tables_ref, scalars_ref
 ):
-    rank, first, mult = where_ref[0], where_ref[1] == 0, where_ref[2]
+    rank, first, mult, color = where_ref[0], where_ref[1] == 0, where_ref[2], where_ref[3]
     f32 = jnp.float32
     records = [whole_record(members_ref, member) for member in range(3)]
     lead_r, lead_i = records[0][:, 0:128].T, records[0][:, 128:256].T
@@ -56,8 +61,10 @@
     row = lax.broadcasted_iota(jnp.int32, (PAD, WIDE), 0)
     column = lax.broadcasted_iota(jnp.int32, (PAD, WIDE), 1)
 
-    def spread(array, start, count):
+    def spread(array, start, count, again=False):
         taken = (column // 2 + start == row) & (column < 2 * count)
+        if again:
+            taken = taken & (row != SHARED)
         return jnp.dot(array, taken.astype(f32), preferred_element_type=f32)
 
     def turned(real, imag, offset):
@@ -70,19 +77,32 @@
     columns = []
     for array in (lead_r, lead_i):
         columns.append([halves(side) for side in sides(array)])
-    whole = [[spread(columns[i][0][h], 0, 45) for i in range(2)] for h in range(2)]
-    early_ref[...] = jnp.concatenate(
-        [
-            jnp.concatenate([turned(*whole[h], offset) for h in range(2)], axis=0)
-            for offset in (0, 3, 1)
-        ],
-        axis=1,
-    ).astype(early_ref.dtype)
+    same, differ = SHARED * color, SHARED * (1 - color)
+    blocks = []
+    for offset, start, count, width, again in (
+        (0, 0, 45, WIDE, False),
+        (3, same, HALF, PAD, False),
+        (3, differ, HALF, PAD, True),
+        (1, same, HALF, PAD, False),
+        (1, differ, HALF, PAD, True),
+    ):
+        rows = []
+        for h in range(2):
+            real, imag = (
+                spread(columns[i][0][h], start, count, again)[:, 0:width] for i in range(2)
+            )
+            rows.append(turned(real, imag, offset))
+        blocks.append(jnp.concatenate(rows, axis=0))
+    early_ref[...] = jnp.concatenate(blocks, axis=1).astype(early_ref.dtype)
     parts = []
     for side in range(2):
-        for start, count in ((0, TOP), (TOP, 45 - TOP)):
-            real, imag = (spread(columns[i][side][0], start, count)[:, 0:PAD] for i in range(2))
-            parts.append(turned(real, imag, 2))
+        for start, again in ((same, False), (differ, True)):
+            for skip, count in ((0, TOP), (TOP, HALF - TOP)):
+                real, imag = (
+                    spread(columns[i][side][0], start + skip, count, again)[:, 0:SLOT]
+                    for i in range(2)
+                )
+                parts.append(turned(real, imag, 2))
     late_ref[...] = jnp.concatenate(parts, axis=1).astype(late_ref.dtype)
 
     mid_r, mid_i = records[1][:, 0:128].T, records[1][:, 128:256].T
@@ -130,28 +150,30 @@
     return jnp.pad(values.reshape(rows, values.shape[2]), ((0, count - rows), (0, 0)))
 
 
-def early_kernel(lead_ref, own_ref, low_ref, high_ref, mine_ref, *far_refs):
+def early_kernel(lead_ref, own_ref, *refs):
+    halves, mine_ref, far_refs = refs[:4], refs[4], refs[5:]
     total = own_ref.shape[2]
     for start in range(0, total, CHUNK):
         cols = slice(start, min(start + CHUNK, total))
         product = jnp.dot(
             lead_ref[...],
-            jnp.concatenate([rows_of(ref, cols, WIDE) for ref in (own_ref, low_ref, high_ref)], axis=0),
+            jnp.concatenate(
+                [rows_of(own_ref, cols, WIDE)] + [rows_of(ref, cols, PAD) for ref in halves], axis=0
+            ),
             preferred_element_type=jnp.float32,
         )
         mine_ref[:, cols] = product[0:WIDE].astype(mine_ref.dtype)
         for i, far_ref in enumerate(far_refs):
-            rows = product[WIDE + 24 * i : WIDE + 24 * i + 24]
+            rows = product[WIDE + 48 * i : WIDE + 48 * i + 48]
             far_ref[:, cols] = rows.astype(far_ref.dtype)
 
 
 def interaction_kernel(*refs):
-    count = 14
+    count = 16
     operands, out_ref, buffers = refs[:count], refs[count], refs[count + 1 : 2 * count + 1]
     flat, windows, mid_real, mid_imag, rate_acc, couple_acc, done = refs[2 * count + 1 :]
     scalars_ref, middle_ref, last_ref, tables_ref, late_ref = buffers[:5]
-    top_ref, bottom_ref, far_top_ref, far_bottom_ref, mine_ref = buffers[5:10]
-    late, others = buffers[5:9], buffers[10:]
+    late, mine_ref, others = buffers[5:13], buffers[13], buffers[14:]
     total = mine_ref.shape[1]
     pieces = [slice(at, min(at + CHUNK, total)) for at in range(0, total, CHUNK)]
     whole = {}
@@ -209,7 +231,7 @@
         both = mine_ref[:, cols].astype(jnp.float32) + other
         both = both + jnp.dot(
             late_ref[...],
-            jnp.concatenate([rows_of(ref, cols, PAD) for ref in late], axis=0),
+            jnp.concatenate([rows_of(ref, cols, SLOT) for ref in late], axis=0),
             preferred_element_type=jnp.float32,
         )
         flat[:, cols] = both.astype(flat.dtype)
@@ -224,8 +246,8 @@
 
     scaled = 0.5 / (smearing * smearing)
     def two_modes(s):
-        low = pl.ds(pl.multiple_of(s * WIDE, WIDE), WIDE)
-        high = pl.ds(pl.multiple_of(s * WIDE + WIDE, WIDE), WIDE)
+        low = pl.ds(s * WIDE, WIDE)
+        high = pl.ds(s * WIDE + WIDE, WIDE)
         operand = jnp.concatenate(
             [
                 jnp.concatenate([ref[low, :], ref[high, :]], axis=1).astype(jnp.bfloat16)
@@ -244,15 +266,13 @@
                 jnp.exp(-scaled * decays * decays) + jnp.exp(-scaled * merges * merges)
             )
             weight = weight * tables_ref[2] * scalars_ref[1, pl.ds(s + i, 1), :]
-            at = pl.ds(pl.multiple_of((s + i) * 8, 8), 8)
+            at = pl.ds((s + i) * 8, 8)
             rate_acc[at, :] = jnp.sum(weight.reshape(WIDE // 8, 8, 128), axis=0)
             weight = weight * tables_ref[3]
             couple_acc[at, :] = jnp.sum(weight.reshape(WIDE // 8, 8, 128), axis=0)
 
-    @pl.loop(0, 12)
-    def _(i):
-        two_modes(4 * i)
-        two_modes(4 * i + 2)
+    for i in range(24):
+        two_modes(2 * i)
 
     sums = jnp.concatenate(
         [
@@ -274,6 +294,14 @@
 VMEM = pl.BlockSpec(memory_space=pltpu.VMEM)
 SMEM = pl.BlockSpec(memory_space=pltpu.SMEM)
 PARAMS = pltpu.CompilerParams(vmem_limit_bytes=56 << 20)
+
+
+def grid_shift(step_y, step_z):
+    return [
+        (y * RING_Z + z, (y + step_y) % RING_Y * RING_Z + (z + step_z) % RING_Z)
+        for y in range(RING_Y)
+        for z in range(RING_Z)
+    ]
 
 
 def ring(count, step):
@@ -296,6 +324,8 @@
     f32, b16 = jnp.float32, jnp.bfloat16
     clus = lax.axis_index("clus")
     mode = lax.axis_index("mode")
+    trip = lax.axis_index("trip")
+    color = (trip // RING_Z + trip % RING_Z) % 2
     group = ("clus", "mode")
 
     with jax.named_scope("records"):
@@ -318,8 +348,16 @@
 
     with jax.named_scope("force"):
         own = jnp.transpose(force_third, (1, 0, 2))
-        low = lax.ppermute(own, "clus", ring(4, 1))
-        high = lax.ppermute(own, "clus", ring(4, 3))
+        half = lax.dynamic_slice_in_dim(own, SHARED * color, HALF, 0)
+        low = lax.ppermute(half, "clus", ring(4, 1))
+        high = lax.ppermute(half, "clus", ring(4, 3))
+
+    with jax.named_scope("force_second"):
+        low, high, _ = lax.optimization_barrier((low, high, arrived))
+        low_other = lax.ppermute(low, "trip", grid_shift(1, 0))
+        high_other = lax.ppermute(high, "trip", grid_shift(0, 1))
+        top = lax.ppermute(low[:TOP], "clus", ring(4, 1))
+        bottom = lax.ppermute(high[TOP:], "clus", ring(4, 3))
 
     with jax.named_scope("members"):
         picks = pl.pallas_call(
@@ -331,19 +369,19 @@
         )(trip_table, arrived, phases)
         members = lax.all_to_all(picks, group, 0, 0, tiled=True)
 
-    with jax.named_scope("force_second"):
-        low_top, high_bottom, _ = lax.optimization_barrier((low[:TOP], high[TOP:], members))
-        top = lax.ppermute(low_top, "clus", ring(4, 1))
-        bottom = lax.ppermute(high_bottom, "clus", ring(4, 3))
+    with jax.named_scope("force_shared"):
+        sent_top, sent_bottom, _ = lax.optimization_barrier((top, bottom, members))
+        top_other = lax.ppermute(sent_top, "trip", grid_shift(-1, 0))
+        bottom_other = lax.ppermute(sent_bottom, "trip", grid_shift(0, -1))
 
     with jax.named_scope("operands"):
         mult = lax.dynamic_index_in_dim(multiplicity, clus, 0, keepdims=False)
-        where = jnp.stack([clus, mode, mult]).astype(jnp.int32)
+        where = jnp.stack([clus, mode, mult, color]).astype(jnp.int32)
         early, late, mid, last_all, tables, scalars = pl.pallas_call(
             operand_kernel,
             out_shape=(
                 jax.ShapeDtypeStruct((2 * WIDE, 3 * WIDE), b16),
-                jax.ShapeDtypeStruct((WIDE, 4 * PAD), b16),
+                jax.ShapeDtypeStruct((WIDE, 8 * SLOT), b16),
                 jax.ShapeDtypeStruct((2 * WIDE, 2 * WIDE), b16),
                 jax.ShapeDtypeStruct((256, 256), b16),
                 jax.ShapeDtypeStruct((4, WIDE, 128), f32),
@@ -360,20 +398,20 @@
         mine, *far = pl.pallas_call(
             early_kernel,
             out_shape=(jax.ShapeDtypeStruct((WIDE, total), b16),)
-            + (jax.ShapeDtypeStruct((WIDE // 4, total), b16),) * 4,
-            in_specs=[VMEM] * 4,
-            out_specs=(VMEM,) * 5,
+            + (jax.ShapeDtypeStruct((WIDE // 2, total), b16),) * 2,
+            in_specs=[VMEM] * 6,
+            out_specs=(VMEM,) * 3,
             compiler_params=PARAMS,
             cost_estimate=pl.CostEstimate(
                 flops=2 * 192 * 288 * total, bytes_accessed=1200 * total, transcendentals=0
             ),
-        )(early, own, low, high)
+        )(early, own, low, low_other, high, high_other)
         other = [lax.ppermute(rows, "mode", swap) for rows in far]
-        far_top = lax.ppermute(top, "mode", swap)
-        far_bottom = lax.ppermute(bottom, "mode", swap)
+        late_rows = [top, bottom, top_other, bottom_other]
+        late_rows += [lax.ppermute(rows, "mode", swap) for rows in late_rows]
 
     with jax.named_scope("interaction"):
-        inputs = (scalars, mid, last_all, tables, late, top, bottom, far_top, far_bottom, mine, *other)
+        inputs = (scalars, mid, last_all, tables, late, *late_rows, mine, *other)
         sums = pl.pallas_call(
             interaction_kernel,
             out_shape=jax.ShapeDtypeStruct((1, 128), f32),

time: 107 us -> 114 us (1.065)
  blocking collectives: 16.3 us -> 37.1 us
  waiting for transfers between devices: 24.1 us -> 15.3 us
  starting transfers between devices: 27.3 us -> 22.5 us
  local copies, waits for them, and re-layouts: 8.01 us -> 9.53 us
    all_to_all x0 -> x1, blocking collectives: none -> 23.2 us  [body(): arrived = lax.all_to_all(chosen, 'trip', 0, 0, tiled=True)]
    all_to_all x1 -> x0, starting transfers between devices: 11.1 us -> none  [body(): arrived = lax.all_to_all(chosen, 'trip', 0, 0, tiled=True)]
    all_to_all x1 -> x0, waiting for transfers between devices: 11 us -> none  [body(): arrived = lax.all_to_all(chosen, 'trip', 0, 0, tiled=True)]
    ppermute x6 -> x12, starting transfers between devices: 4.97 us -> 11.6 us  [the longest x1 2.7 us: body(): top_other = lax.ppermute(sent_top, 'trip', grid_shift(-1, 0))]
    ppermute x6 -> x12, waiting for transfers between devices: 6.37 us -> 9.05 us  [the longest x1 6.9 us: body(): bottom_other = lax.ppermute(sent_bottom, 'trip', grid_shift(0, -1))]
    all_to_all x1, blocking collectives: 16.3 us -> 14 us  [body(): received = lax.all_to_all(partial[:, None, :], 'trip', 0, 0, tiled=True)]
    ppermute x4 -> x2, waiting for transfers between devices: 2.02 us -> 0.01 us  [body(): other = [lax.ppermute(rows, 'mode', swap) for rows in far]]
    dynamic_slice x0 -> x1, local copies, waits for them, and re-layouts: none -> 1.95 us  [body(): half = lax.dynamic_slice_in_dim(own, SHARED * color, HALF, 0)]
  transfers between devices with their start and end apart: 15 -> 18, of which waited for: 7 -> 5; matrix products, arithmetic and copies ran while one was open for 11% -> 8% of each run, Pallas kernels for 11% -> 10%
where the time goes in v7:
time: 114 us
  blocking collectives  37.1 us (33%)
  starting transfers between devices  22.5 us (20%)
  Pallas kernels  22.4 us (20%)
  waiting for transfers between devices  15.3 us (13%)
  local copies, waits for them, and re-layouts  9.53 us (8%)
  other arithmetic  5.95 us (5%)
    all_to_all x1, blocking collectives, body(): arrived = lax.all_to_all(chosen, 'trip', 0, 0, tiled=True)  23.2 us
    all_to_all x1, blocking collectives, body(): received = lax.all_to_all(partial[:, None, :], 'trip', 0, 0, tiled=True)  14 us
    pallas_call x1, Pallas kernels, body(): pl.pallas_call(interaction_kernel, out_shape=jax.ShapeDtypeStruct((1, 128...  10.9 us
    ppermute x1, waiting for transfers between devices, body(): bottom_other = lax.ppermute(sent_bottom, 'trip', grid_shift(0, -1))  6.9 us
    all_to_all x1, starting transfers between devices, body(): members = lax.all_to_all(picks, group, 0, 0, tiled=True)  6.27 us
    pallas_call x1, Pallas kernels, body(): pl.pallas_call(early_kernel, out_shape=(jax.ShapeDtypeStruct((WIDE, total...  5.8 us
    all_to_all x1, waiting for transfers between devices, body(): members = lax.all_to_all(picks, group, 0, 0, tiled=True)  4.29 us
    ppermute x3, starting transfers between devices, body(): lax.ppermute(own_row, 'clus', ring(4, step))  4.13 us
  transfers between devices with their start and end apart: 18, of which 5 were waited for; matrix products, arithmetic and copies ran while one was open for 8% of the time, Pallas kernels for 10%

profile of v7, /device:TPU:2, one launch (start us, length us, event | category | flops | bytes accessed | tf_op | source)
XLA Modules:
  0.0 113.8 jit_solution(126701772725612572)
XLA Ops:
  0.7 2.0 %dynamic-slice_bitcast_fusion = bf16[23,2,8100]{2,1,0:T(2,128)(2,1)S(1)} fusion(bf16[2,45,8100]{2,0,1:T(2,128)(2,1)} %param.11, s32[]{:T(128)S(6)} %select_n.101), kind=kLoop, calls=%fused_computation | loop fusion | bytes 1490404 | tf_op jit(solution)/shard_map/force/dynamic_slice | solution.py:351
  2.7 1.6 %collective-permute-start = (bf16[23,2,8100]{2,1,0:T(2,128)(2,1)S(1)}, bf16[23,2,8100]{2,1,0:T(2,128)(2,1)S(1)}, u32[]{:S(2)}, u32[]{:S(2)}) collective-permute-start(bf16[23,2,8100]{2,1,0:T(2,128)(2,1)S(1)} %dynamic-slice_bitcast_fusion), channel_id=1, source_target_pairs={{0,64},{64,128},{128,192},{192,0},{1,65},{65,129},{129,193},{193,1... | collective-permute-start | bytes 2235608 | tf_op jit(solution)/shard_map/force/ppermute | solution.py:352
  4.2 0.9 collective-permute-start.1
  5.3 0.1 pad_dynamic-slice_fusion.2
  5.4 0.7 fusion.1.share_ref
  6.1 1.6 %records.1 = bf16[32,12,180]{2,1,0:T(8,128)(2,1)} custom-call(s32[1,32]{1,0:T(1,128)} %rows_ref.1, bf16[8,12,180]{2,1,0:T(8,128)(2,1)} %fusion.1.share_ref), custom_call_target="tpu_custom_call" | custom-call | tf_op jit(solution)/shard_map/records/pallas_call | solution.py:337
  7.7 23.2 %all_to_all.15.arrived_ref = bf16[32,12,180]{2,1,0:T(8,128)(2,1)} all-to-all(bf16[32,12,180]{2,1,0:T(8,128)(2,1)} %records.1), channel_id=1, replica_groups=mesh['clus'=4,'trip'=32,'mode'=2] {'trip'}, dimensions={0} | all-to-all | bytes 276480 | tf_op jit(solution)/shard_map/records/all_to_all | solution.py:344
  30.9 0.7 collective-permute-start.10
  31.6 1.8 %collective-permute-start.11 = (bf16[23,2,8100]{2,1,0:T(2,128)(2,1)S(1)}, bf16[23,2,8100]{2,1,0:T(2,128)(2,1)S(1)}, u32[]{:S(2)}, u32[]{:S(2)}) collective-permute-start(bf16[23,2,8100]{2,1,0:T(2,128)(2,1)S(1)} %collective-permute-done.1.refs_2_), channel_id=1, source_target_pairs={{0,2},{2,4},{4,6},{6,8},{8,10},{10,12},{12,14},{14,0},{16,18},{18,... | collective-permute-start | bytes 2235608 | tf_op jit(solution)/shard_map/force_second/ppermute | solution.py:358
  33.3 1.1 slice.12
  34.4 1.0 slice.13
  35.5 1.5 %collective-permute-start.2 = (bf16[12,2,8100]{2,1,0:T(2,128)(2,1)}, bf16[12,2,8100]{2,1,0:T(2,128)(2,1)}, u32[]{:S(2)}, u32[]{:S(2)}) collective-permute-start(bf16[12,2,8100]{2,1,0:T(2,128)(2,1)} %slice.12), channel_id=1, source_target_pairs={{0,64},{64,128},{128,192},{192,0},{1,65},{65,129},{129,193},{193,1... | collective-permute-start | bytes 1166408 | tf_op jit(solution)/shard_map/force_second/ppermute | solution.py:359
  36.9 0.5 collective-permute-start.3
  37.5 0.1 copy.31
  37.7 0.6 pad.4.phase_ref
  38.3 1.7 %members.1 = bf16[8,4,16,180]{3,2,1,0:T(8,128)(2,1)} custom-call(s32[4,3]{1,0:T(4,128)} %table_ref.1, bf16[32,12,180]{2,1,0:T(8,128)(2,1)} %all_to_all.15.arrived_ref, bf16[4,16,180]{2,1,0:T(8,128)(2,1)} %pad.4.phase_ref), custom_call_target="tpu_custom_call" | custom-call | tf_op jit(solution)/shard_map/members/pallas_call | solution.py:363
  40.0 6.3 %all-to-all-start.1 = ((bf16[8,4,16,180]{3,2,1,0:T(8,128)(2,1)}), bf16[8,4,16,180]{3,2,1,0:T(8,128)(2,1)S(1)}, u32[]{:S(2)}, u32[]{:S(2)}) async-start(bf16[8,4,16,180]{3,2,1,0:T(8,128)(2,1)} %members.1), calls=%async_computation.1 | async-start | bytes 524288 | tf_op jit(solution)/shard_map/members/all_to_all | solution.py:370
  46.2 0.6 dynamic_slice.23
  46.8 1.2 %pad_add_fusion.where_ref = s32[4]{0:T(128)} fusion(s32[1]{0:T(128)} %bitcast.3, s32[1]{0:T(128)} %dynamic_slice.23, s32[1]{0:T(128)} %bitcast.2, s32[1]{0:T(128)} %bitcast.1), kind=kLoop, calls=%fused_computation.21 | loop fusion | flops 12 | bytes 32 | tf_op jit(solution)/shard_map/operands/stack | solution.py:379
  48.1 4.3 %all-to-all-done.1.members_ref = bf16[8,4,16,180]{3,2,1,0:T(8,128)(2,1)S(1)} async-done(((bf16[8,4,16,180]{3,2,1,0:T(8,128)(2,1)}), bf16[8,4,16,180]{3,2,1,0:T(8,128)(2,1)S(1)}, u32[]{:S(2)}, u32[]{:S(2)}) %all-to-all-start.1) | async-done | bytes 184352 | tf_op jit(solution)/shard_map/members/all_to_all | solution.py:370
  52.4 0.7 copy-done.2
  53.1 2.4 %operands.1 = (bf16[192,288]{1,0:T(8,128)(2,1)}, bf16[96,256]{1,0:T(8,128)(2,1)}, bf16[192,192]{1,0:T(8,128)(2,1)}, bf16[256,256]{1,0:T(8,128)(2,1)}, f32[4,96,128]{2,1,0:T(8,128)}, /*index=5*/f32[2,48,128]{2,1,0:T(8,128)}) custom-call(s32[4]{0:T(128)} %pad_add_fusion.where_ref, bf16[8,4,16,180]{3,2,1,0:T(8,128)(2,1)} %copy-done.2), custom_call_target="tpu_custom_call" | custom-call | tf_op jit(solution)/shard_map/operands/pallas_call | solution.py:380
  55.5 2.7 %collective-permute-start.4 = (bf16[12,2,8100]{2,1,0:T(2,128)(2,1)}, bf16[12,2,8100]{2,1,0:T(2,128)(2,1)}, u32[]{:S(2)}, u32[]{:S(2)}) collective-permute-start(bf16[12,2,8100]{2,1,0:T(2,128)(2,1)} %collective-permute-done.2.refs_5_), channel_id=1, source_target_pairs={{0,48},{2,50},{4,52},{6,54},{8,56},{10,58},{12,60},{14,62},{16,0},... | collective-permute-start | bytes 1166408 | tf_op jit(solution)/shard_map/force_shared/ppermute | solution.py:374
  58.2 0.9 copy-done.5
  59.1 0.3 copy-done.6
  59.4 5.8 %contract.1 = (bf16[96,8100]{1,0:T(8,128)(2,1)}, bf16[48,8100]{1,0:T(8,128)(2,1)}, bf16[48,8100]{1,0:T(8,128)(2,1)}) custom-call(bf16[192,288]{1,0:T(8,128)(2,1)} %get-tuple-element.24.lead_ref, bf16[45,2,8100]{2,1,0:T(2,128)(2,1)} %bitcast.27, bf16[23,2,8100]{2,1,0:T(2,128)(2,1)} %copy-done, bf16[23,2,8100]{2,1,0:T(2,128)(2,1)} %copy-done.5, ...), custom_call_target="tpu_custom_call" | custom-call | flops 895795200 | bytes 9720000 | tf_op jit(solution)/shard_map/contract/pallas_call | solution.py:398
  65.2 0.5 collective-permute-start.13
  65.7 1.5 %collective-permute-start.5 = (bf16[11,2,8100]{2,1,0:T(2,128)(2,1)}, bf16[11,2,8100]{2,1,0:T(2,128)(2,1)S(1)}, u32[]{:S(2)}, u32[]{:S(2)}) collective-permute-start(bf16[11,2,8100]{2,1,0:T(2,128)(2,1)} %collective-permute-done.3.refs_6_), channel_id=1, source_target_pairs={{0,14},{2,0},{4,2},{6,4},{8,6},{10,8},{12,10},{14,12},{16,30},{18,... | collective-permute-start | bytes 1069208 | tf_op jit(solution)/shard_map/force_shared/ppermute | solution.py:375
  67.2 2.1 %collective-permute-done.7.refs_10_ = bf16[11,2,8100]{2,1,0:T(2,128)(2,1)S(1)} collective-permute-done((bf16[11,2,8100]{2,1,0:T(2,128)(2,1)}, bf16[11,2,8100]{2,1,0:T(2,128)(2,1)S(1)}, u32[]{:S(2)}, u32[]{:S(2)}) %collective-permute-start.7) | collective-permute-done | bytes 356432 | tf_op jit(solution)/shard_map/contract/ppermute | solution.py:411
  69.3 0.1 collective-permute-start.6
  69.5 0.4 collective-permute-start.8
  69.8 6.9 %collective-permute-done.5.refs_8_ = bf16[11,2,8100]{2,1,0:T(2,128)(2,1)S(1)} collective-permute-done((bf16[11,2,8100]{2,1,0:T(2,128)(2,1)}, bf16[11,2,8100]{2,1,0:T(2,128)(2,1)S(1)}, u32[]{:S(2)}, u32[]{:S(2)}) %collective-permute-start.5) | collective-permute-done | bytes 356432 | tf_op jit(solution)/shard_map/force_shared/ppermute | solution.py:375
  76.7 0.6 fusion.9
  77.4 1.3 %iota_compare_fusion.2 = (pred[32]{0:T(512)(128)(4,1)S(1)}, pred[32]{0:T(512)(128)(4,1)S(1)}) fusion(s32[]{:T(128)} %bitcast.13, s32[]{:T(128)} %bitcast), kind=kLoop, calls=%fused_computation.26 | loop fusion | flops 64 | bytes 72 | tf_op jit(solution)/shard_map/collect/eq | solution.py:439
  78.8 0.6 copy-done.7
  79.4 0.1 copy-done.12
  79.6 0.1 copy-done.8
  79.7 0.2 copy-done.3
  79.9 0.3 copy-done.4
  80.2 10.9 %interaction.1 = f32[1,128]{1,0:T(1,128)} custom-call(f32[2,48,128]{2,1,0:T(8,128)} %get-tuple-element.15.refs_0_, bf16[192,192]{1,0:T(8,128)(2,1)} %get-tuple-element.16.refs_1_, bf16[256,256]{1,0:T(8,128)(2,1)} %get-tuple-element.17.refs_2_, f32[4,96,128]{2,1,0:T(8,128)} %get-tuple-element.18.refs_3_, bf16[96,256]{1,0:T(8,128)(2,1)} %get-tuple-element.19.refs_4_, ...), custom_call_target="tpu_custom_call" | custom-call | tf_op jit(solution)/shard_map/interaction/pallas_call | solution.py:415
  91.1 0.1 collective-permute-start.14
  91.2 3.5 %collective-permute-start.15 = (f32[1,128]{1,0:T(1,128)}, f32[1,128]{1,0:T(1,128)S(1)}, u32[]{:S(2)}, u32[]{:S(2)}) collective-permute-start(f32[1,128]{1,0:T(1,128)} %interaction.1), channel_id=1, source_target_pairs={{0,128},{64,192},{128,0},{192,64},{1,129},{65,193},{129,1},{193,65... | collective-permute-start | bytes 1544 | tf_op jit(solution)/shard_map/collect/ppermute | solution.py:434
  94.7 0.5 collective-permute-start.16
  95.3 1.1 iota_compare_fusion
  96.5 1.9 %collective-permute-done.16 = f32[1,128]{1,0:T(1,128)S(1)} collective-permute-done((f32[1,128]{1,0:T(1,128)}, f32[1,128]{1,0:T(1,128)S(1)}, u32[]{:S(2)}, u32[]{:S(2)}) %collective-permute-start.16) | collective-permute-done | bytes 544 | tf_op jit(solution)/shard_map/collect/ppermute | solution.py:434
  98.4 0.9 fusion.4
  99.3 14.0 %all_to_all.16 = f32[32,1,128]{2,1,0:T(1,128)S(1)} all-to-all(f32[32,1,128]{2,1,0:T(1,128)S(1)} %fusion.4), channel_id=1, replica_groups=mesh['clus'=4,'trip'=32,'mode'=2] {'trip'}, dimensions={0} | all-to-all | bytes 32768 | tf_op jit(solution)/shard_map/collect/all_to_all | solution.py:440
  113.3 0.6 add_divide_fusion
  (57 shorter events, 0.4 us)
Async XLA Ops:
  0.6 4.5 %copy-start.9 = (bf16[8,90,180]{2,0,1:T(8,128)(2,1)S(1)}, bf16[8,90,180]{2,0,1:T(8,128)(2,1)}, u32[]{:S(2)}) copy-start(bf16[8,90,180]{2,0,1:T(8,128)(2,1)} %param.13) | copy-start | bytes 777604
  0.6 4.5 %copy-start.15 = (bf16[8,90]{1,0:T(8,128)(2,1)S(1)}, bf16[8,90]{1,0:T(8,128)(2,1)}, u32[]{:S(2)}) copy-start(bf16[8,90]{1,0:T(8,128)(2,1)} %param.14) | copy-start | bytes 4324
  0.7 4.5 %copy-start.14 = (bf16[8,90]{1,0:T(8,128)(2,1)S(1)}, bf16[8,90]{1,0:T(8,128)(2,1)}, u32[]{:S(2)}) copy-start(bf16[8,90]{1,0:T(8,128)(2,1)} %param.15) | copy-start | bytes 4324
  2.7 28.2 %collective-permute-start = (bf16[23,2,8100]{2,1,0:T(2,128)(2,1)S(1)}, bf16[23,2,8100]{2,1,0:T(2,128)(2,1)S(1)}, u32[]{:S(2)}, u32[]{:S(2)}) collective-permute-start(bf16[23,2,8100]{2,1,0:T(2,128)(2,1)S(1)} %dynamic-slice_bitcast_fusion), channel_id=1, source_target_pairs={{0,64},{64,128},{128,192},{192,0},{1,65},{65,129},{129,193},{193,1... | collective-permute-start | bytes 2235608 | tf_op jit(solution)/shard_map/force/ppermute | solution.py:352
  4.2 26.6 %collective-permute-start.1 = (bf16[23,2,8100]{2,1,0:T(2,128)(2,1)S(1)}, bf16[23,2,8100]{2,1,0:T(2,128)(2,1)S(1)}, u32[]{:S(2)}, u32[]{:S(2)}) collective-permute-start(bf16[23,2,8100]{2,1,0:T(2,128)(2,1)S(1)} %dynamic-slice_bitcast_fusion), channel_id=1, source_target_pairs={{0,192},{64,0},{128,64},{192,128},{1,193},{65,1},{129,65},{193,129... | collective-permute-start | bytes 2235608 | tf_op jit(solution)/shard_map/force/ppermute | solution.py:353
  5.2 32.3 %copy-start.18 = (bf16[2,4]{1,0:T(2,128)(2,1)S(1)}, bf16[2,4]{1,0:T(2,128)(2,1)}, u32[]{:S(2)}) copy-start(bf16[2,4]{1,0:T(2,128)(2,1)} %param.12) | copy-start | bytes 52
  7.7 38.5 %copy-start.19 = (s32[4]{0:T(128)S(1)}, s32[4]{0:T(128)}, u32[]{:S(2)}) copy-start(s32[4]{0:T(128)} %param.19) | copy-start | bytes 52
  30.9 27.3 %copy-start = (bf16[23,2,8100]{2,1,0:T(2,128)(2,1)}, bf16[23,2,8100]{2,1,0:T(2,128)(2,1)S(1)}, u32[]{:S(2)}) copy-start(bf16[23,2,8100]{2,1,0:T(2,128)(2,1)S(1)} %collective-permute-done.refs_0_) | copy-start | bytes 2235604
  30.9 27.3 %copy-start.1 = (bf16[23,2,8100]{2,1,0:T(2,128)(2,1)}, bf16[23,2,8100]{2,1,0:T(2,128)(2,1)S(1)}, u32[]{:S(2)}) copy-start(bf16[23,2,8100]{2,1,0:T(2,128)(2,1)S(1)} %collective-permute-done.1.refs_2_) | copy-start | bytes 2235604
  30.9 27.3 %collective-permute-start.10 = (bf16[23,2,8100]{2,1,0:T(2,128)(2,1)S(1)}, bf16[23,2,8100]{2,1,0:T(2,128)(2,1)S(1)}, u32[]{:S(2)}, u32[]{:S(2)}) collective-permute-start(bf16[23,2,8100]{2,1,0:T(2,128)(2,1)S(1)} %collective-permute-done.refs_0_), channel_id=1, source_target_pairs={{0,16},{2,18},{4,20},{6,22},{8,24},{10,26},{12,28},{14,30},{16,32}... | collective-permute-start | bytes 2235608 | tf_op jit(solution)/shard_map/force_second/ppermute | solution.py:357
  31.6 26.6 %collective-permute-start.11 = (bf16[23,2,8100]{2,1,0:T(2,128)(2,1)S(1)}, bf16[23,2,8100]{2,1,0:T(2,128)(2,1)S(1)}, u32[]{:S(2)}, u32[]{:S(2)}) collective-permute-start(bf16[23,2,8100]{2,1,0:T(2,128)(2,1)S(1)} %collective-permute-done.1.refs_2_), channel_id=1, source_target_pairs={{0,2},{2,4},{4,6},{6,8},{8,10},{10,12},{12,14},{14,0},{16,18},{18,... | collective-permute-start | bytes 2235608 | tf_op jit(solution)/shard_map/force_second/ppermute | solution.py:358
  35.5 20.0 %collective-permute-start.2 = (bf16[12,2,8100]{2,1,0:T(2,128)(2,1)}, bf16[12,2,8100]{2,1,0:T(2,128)(2,1)}, u32[]{:S(2)}, u32[]{:S(2)}) collective-permute-start(bf16[12,2,8100]{2,1,0:T(2,128)(2,1)} %slice.12), channel_id=1, source_target_pairs={{0,64},{64,128},{128,192},{192,0},{1,65},{65,129},{129,193},{193,1... | collective-permute-start | bytes 1166408 | tf_op jit(solution)/shard_map/force_second/ppermute | solution.py:359
  36.9 18.5 %collective-permute-start.3 = (bf16[11,2,8100]{2,1,0:T(2,128)(2,1)}, bf16[11,2,8100]{2,1,0:T(2,128)(2,1)}, u32[]{:S(2)}, u32[]{:S(2)}) collective-permute-start(bf16[11,2,8100]{2,1,0:T(2,128)(2,1)} %slice.13), channel_id=1, source_target_pairs={{0,192},{64,0},{128,64},{192,128},{1,193},{65,1},{129,65},{193,129... | collective-permute-start | bytes 1069208 | tf_op jit(solution)/shard_map/force_second/ppermute | solution.py:360
  40.0 12.4 %all-to-all-start.1 = ((bf16[8,4,16,180]{3,2,1,0:T(8,128)(2,1)}), bf16[8,4,16,180]{3,2,1,0:T(8,128)(2,1)S(1)}, u32[]{:S(2)}, u32[]{:S(2)}) async-start(bf16[8,4,16,180]{3,2,1,0:T(8,128)(2,1)} %members.1), calls=%async_computation.1 | async-start | bytes 524288 | tf_op jit(solution)/shard_map/members/all_to_all | solution.py:370
  52.4 0.7 copy-start.2
  55.5 14.0 %collective-permute-start.4 = (bf16[12,2,8100]{2,1,0:T(2,128)(2,1)}, bf16[12,2,8100]{2,1,0:T(2,128)(2,1)}, u32[]{:S(2)}, u32[]{:S(2)}) collective-permute-start(bf16[12,2,8100]{2,1,0:T(2,128)(2,1)} %collective-permute-done.2.refs_5_), channel_id=1, source_target_pairs={{0,48},{2,50},{4,52},{6,54},{8,56},{10,58},{12,60},{14,62},{16,0},... | collective-permute-start | bytes 1166408 | tf_op jit(solution)/shard_map/force_shared/ppermute | solution.py:374
  58.2 0.9 copy-start.5
  58.2 1.2 %copy-start.6 = (bf16[23,2,8100]{2,1,0:T(2,128)(2,1)}, bf16[23,2,8100]{2,1,0:T(2,128)(2,1)S(1)}, u32[]{:S(2)}) copy-start(bf16[23,2,8100]{2,1,0:T(2,128)(2,1)S(1)} %collective-permute-done.11.refs_3_) | copy-start | bytes 2235604
  59.4 17.4 %copy-start.13 = (s32[4]{0:T(128)S(1)}, s32[4]{0:T(128)}, u32[]{:S(2)}) copy-start(s32[4]{0:T(128)} %param.18) | copy-start | bytes 52
  65.2 13.6 %collective-permute-start.12 = (bf16[48,8100]{1,0:T(8,128)(2,1)}, bf16[48,8100]{1,0:T(8,128)(2,1)S(1)}, u32[]{:S(2)}, u32[]{:S(2)}) collective-permute-start(bf16[48,8100]{1,0:T(8,128)(2,1)} %get-tuple-element.26), channel_id=1, source_target_pairs={{0,1},{1,0},{2,3},{3,2},{4,5},{5,4},{6,7},{7,6},{8,9},{9,8},{10,11... | collective-permute-start | bytes 2332808 | tf_op jit(solution)/shard_map/contract/ppermute | solution.py:409
  65.2 13.6 %collective-permute-start.13 = (bf16[48,8100]{1,0:T(8,128)(2,1)}, bf16[48,8100]{1,0:T(8,128)(2,1)S(1)}, u32[]{:S(2)}, u32[]{:S(2)}) collective-permute-start(bf16[48,8100]{1,0:T(8,128)(2,1)} %get-tuple-element.27), channel_id=1, source_target_pairs={{0,1},{1,0},{2,3},{3,2},{4,5},{5,4},{6,7},{7,6},{8,9},{9,8},{10,11... | collective-permute-start | bytes 2332808 | tf_op jit(solution)/shard_map/contract/ppermute | solution.py:409
  65.7 3.6 %collective-permute-start.7 = (bf16[11,2,8100]{2,1,0:T(2,128)(2,1)}, bf16[11,2,8100]{2,1,0:T(2,128)(2,1)S(1)}, u32[]{:S(2)}, u32[]{:S(2)}) collective-permute-start(bf16[11,2,8100]{2,1,0:T(2,128)(2,1)} %collective-permute-done.3.refs_6_), channel_id=1, source_target_pairs={{0,1},{1,0},{2,3},{3,2},{4,5},{5,4},{6,7},{7,6},{8,9},{9,8},{10,11... | collective-permute-start | bytes 1069208 | tf_op jit(solution)/shard_map/contract/ppermute | solution.py:411
  65.7 11.0 %collective-permute-start.5 = (bf16[11,2,8100]{2,1,0:T(2,128)(2,1)}, bf16[11,2,8100]{2,1,0:T(2,128)(2,1)S(1)}, u32[]{:S(2)}, u32[]{:S(2)}) collective-permute-start(bf16[11,2,8100]{2,1,0:T(2,128)(2,1)} %collective-permute-done.3.refs_6_), channel_id=1, source_target_pairs={{0,14},{2,0},{4,2},{6,4},{8,6},{10,8},{12,10},{14,12},{16,30},{18,... | collective-permute-start | bytes 1069208 | tf_op jit(solution)/shard_map/force_shared/ppermute | solution.py:375
  69.3 9.5 %copy-start.10 = (bf16[11,2,8100]{2,1,0:T(2,128)(2,1)}, bf16[11,2,8100]{2,1,0:T(2,128)(2,1)S(1)}, u32[]{:S(2)}) copy-start(bf16[11,2,8100]{2,1,0:T(2,128)(2,1)S(1)} %collective-permute-done.7.refs_10_) | copy-start | bytes 1069204
  69.3 9.4 %collective-permute-start.6 = (bf16[12,2,8100]{2,1,0:T(2,128)(2,1)}, bf16[12,2,8100]{2,1,0:T(2,128)(2,1)S(1)}, u32[]{:S(2)}, u32[]{:S(2)}) collective-permute-start(bf16[12,2,8100]{2,1,0:T(2,128)(2,1)} %collective-permute-done.2.refs_5_), channel_id=1, source_target_pairs={{0,1},{1,0},{2,3},{3,2},{4,5},{5,4},{6,7},{7,6},{8,9},{9,8},{10,11... | collective-permute-start | bytes 1166408 | tf_op jit(solution)/shard_map/contract/ppermute | solution.py:411
  69.5 9.3 %collective-permute-start.8 = (bf16[12,2,8100]{2,1,0:T(2,128)(2,1)}, bf16[12,2,8100]{2,1,0:T(2,128)(2,1)S(1)}, u32[]{:S(2)}, u32[]{:S(2)}) collective-permute-start(bf16[12,2,8100]{2,1,0:T(2,128)(2,1)} %collective-permute-done.4.refs_7_), channel_id=1, source_target_pairs={{0,1},{1,0},{2,3},{3,2},{4,5},{5,4},{6,7},{7,6},{8,9},{9,8},{10,11... | collective-permute-start | bytes 1166408 | tf_op jit(solution)/shard_map/contract/ppermute | solution.py:411
  76.7 2.1 %copy-start.11 = (bf16[11,2,8100]{2,1,0:T(2,128)(2,1)}, bf16[11,2,8100]{2,1,0:T(2,128)(2,1)S(1)}, u32[]{:S(2)}) copy-start(bf16[11,2,8100]{2,1,0:T(2,128)(2,1)S(1)} %collective-permute-done.5.refs_8_) | copy-start | bytes 1069204
  76.7 2.0 %collective-permute-start.9 = (bf16[11,2,8100]{2,1,0:T(2,128)(2,1)S(1)}, bf16[11,2,8100]{2,1,0:T(2,128)(2,1)S(1)}, u32[]{:S(2)}, u32[]{:S(2)}) collective-permute-start(bf16[11,2,8100]{2,1,0:T(2,128)(2,1)S(1)} %collective-permute-done.5.refs_8_), channel_id=1, source_target_pairs={{0,1},{1,0},{2,3},{3,2},{4,5},{5,4},{6,7},{7,6},{8,9},{9,8},{10,11... | collective-permute-start | bytes 1069208 | tf_op jit(solution)/shard_map/contract/ppermute | solution.py:411
  78.7 0.7 copy-start.7
  78.7 0.9 copy-start.12
  78.7 1.0 copy-start.8
  78.7 1.2 %copy-start.3 = (bf16[48,8100]{1,0:T(8,128)(2,1)}, bf16[48,8100]{1,0:T(8,128)(2,1)S(1)}, u32[]{:S(2)}) copy-start(bf16[48,8100]{1,0:T(8,128)(2,1)S(1)} %collective-permute-done.12.refs_14_) | copy-start | bytes 2332804
  78.8 1.4 %copy-start.4 = (bf16[48,8100]{1,0:T(8,128)(2,1)}, bf16[48,8100]{1,0:T(8,128)(2,1)S(1)}, u32[]{:S(2)}) copy-start(bf16[48,8100]{1,0:T(8,128)(2,1)S(1)} %collective-permute-done.13.refs_15_) | copy-start | bytes 2332804
  80.2 33.0 %copy-start.16 = (f32[1,45]{1,0:T(1,128)S(1)}, f32[1,45]{1,0:T(1,128)}, u32[]{:S(2)}) copy-start(f32[1,45]{1,0:T(1,128)} %param.20) | copy-start | bytes 544
  80.2 33.0 %copy-start.17 = (f32[1,45]{1,0:T(1,128)S(1)}, f32[1,45]{1,0:T(1,128)}, u32[]{:S(2)}) copy-start(f32[1,45]{1,0:T(1,128)} %param.21) | copy-start | bytes 544
  91.1 5.3 %collective-permute-start.14 = (f32[1,128]{1,0:T(1,128)}, f32[1,128]{1,0:T(1,128)S(1)}, u32[]{:S(2)}, u32[]{:S(2)}) collective-permute-start(f32[1,128]{1,0:T(1,128)} %interaction.1), channel_id=1, source_target_pairs={{0,64},{64,128},{128,192},{192,0},{1,65},{65,129},{129,193},{193,1... | collective-permute-start | bytes 1544 | tf_op jit(solution)/shard_map/collect/ppermute | solution.py:434
  91.2 5.3 %collective-permute-start.15 = (f32[1,128]{1,0:T(1,128)}, f32[1,128]{1,0:T(1,128)S(1)}, u32[]{:S(2)}, u32[]{:S(2)}) collective-permute-start(f32[1,128]{1,0:T(1,128)} %interaction.1), channel_id=1, source_target_pairs={{0,128},{64,192},{128,0},{192,64},{1,129},{65,193},{129,1},{193,65... | collective-permute-start | bytes 1544 | tf_op jit(solution)/shard_map/collect/ppermute | solution.py:434
  94.7 3.7 %collective-permute-start.16 = (f32[1,128]{1,0:T(1,128)}, f32[1,128]{1,0:T(1,128)S(1)}, u32[]{:S(2)}, u32[]{:S(2)}) collective-permute-start(f32[1,128]{1,0:T(1,128)} %interaction.1), channel_id=1, source_target_pairs={{0,192},{64,0},{128,64},{192,128},{1,193},{65,1},{129,65},{193,129... | collective-permute-start | bytes 1544 | tf_op jit(solution)/shard_map/collect/ppermute | solution.py:434

commit v8 on v7

--- a/solution.py
+++ b/solution.py
@@ -164,12 +164,12 @@
         )
         mine_ref[:, cols] = product[0:WIDE].astype(mine_ref.dtype)
         for i, far_ref in enumerate(far_refs):
-            rows = product[WIDE + 48 * i : WIDE + 48 * i + 48]
+            rows = product[WIDE + 32 * i : WIDE + 32 * i + 32]
             far_ref[:, cols] = rows.astype(far_ref.dtype)
 
 
 def interaction_kernel(*refs):
-    count = 16
+    count = 17
     operands, out_ref, buffers = refs[:count], refs[count], refs[count + 1 : 2 * count + 1]
     flat, windows, mid_real, mid_imag, rate_acc, couple_acc, done = refs[2 * count + 1 :]
     scalars_ref, middle_ref, last_ref, tables_ref, late_ref = buffers[:5]
@@ -398,9 +398,9 @@
         mine, *far = pl.pallas_call(
             early_kernel,
             out_shape=(jax.ShapeDtypeStruct((WIDE, total), b16),)
-            + (jax.ShapeDtypeStruct((WIDE // 2, total), b16),) * 2,
+            + (jax.ShapeDtypeStruct((WIDE // 3, total), b16),) * 3,
             in_specs=[VMEM] * 6,
-            out_specs=(VMEM,) * 3,
+            out_specs=(VMEM,) * 4,
             compiler_params=PARAMS,
             cost_estimate=pl.CostEstimate(
                 flops=2 * 192 * 288 * total, bytes_accessed=1200 * total, transcendentals=0

time: 114 us -> 107 us (0.939)
  waiting for transfers between devices: 15.3 us -> 9.29 us
    ppermute x1, waiting for transfers between devices: 6.9 us -> 0.01 us  [body(): bottom_other = lax.ppermute(sent_bottom, 'trip', grid_shift(0, -1))]
    all_to_all x1, waiting for transfers between devices: 4.29 us -> 5.95 us  [body(): members = lax.all_to_all(picks, group, 0, 0, tiled=True)]
    unnamed x41 -> x37, local copies, waits for them, and re-layouts: 3.4 us -> 2.31 us
  transfers between devices with their start and end apart: 18 -> 19, of which waited for: 5 -> 3; matrix products, arithmetic and copies ran while one was open for 8% -> 8% of each run, Pallas kernels for 10% -> 11%
where the time goes in v8:
time: 107 us; the launch traced here: 106 us
  blocking collectives  36.4 us (34%)
  starting transfers between devices  23 us (21%)
  Pallas kernels  22.3 us (21%)
  waiting for transfers between devices  9.29 us (9%)
  local copies, waits for them, and re-layouts  8.39 us (8%)
  other arithmetic  6.02 us (6%)
    all_to_all x1, blocking collectives, body(): arrived = lax.all_to_all(chosen, 'trip', 0, 0, tiled=True)  23.2 us
    all_to_all x1, blocking collectives, body(): received = lax.all_to_all(partial[:, None, :], 'trip', 0, 0, tiled=True)  13.3 us
    pallas_call x1, Pallas kernels, body(): pl.pallas_call(interaction_kernel, out_shape=jax.ShapeDtypeStruct((1, 128...  10.9 us
    all_to_all x1, starting transfers between devices, body(): members = lax.all_to_all(picks, group, 0, 0, tiled=True)  6.27 us
    all_to_all x1, waiting for transfers between devices, body(): members = lax.all_to_all(picks, group, 0, 0, tiled=True)  5.95 us
    pallas_call x1, Pallas kernels, body(): pl.pallas_call(early_kernel, out_shape=(jax.ShapeDtypeStruct((WIDE, total...  5.83 us
    ppermute x3, starting transfers between devices, body(): lax.ppermute(own_row, 'clus', ring(4, step))  4.15 us
    ppermute x1, starting transfers between devices, body(): top_other = lax.ppermute(sent_top, 'trip', grid_shift(-1, 0))  2.63 us
  transfers between devices with their start and end apart: 19, of which 3 were waited for; matrix products, arithmetic and copies ran while one was open for 8% of the time, Pallas kernels for 11%

profile of v8, /device:TPU:2, one launch (start us, length us, event | category | flops | bytes accessed | tf_op | source)
XLA Modules:
  0.0 106.4 jit_solution(7509244608331731024)
XLA Ops:
  0.7 1.8 %dynamic-slice_bitcast_fusion = bf16[23,2,8100]{2,1,0:T(2,128)(2,1)S(1)} fusion(bf16[2,45,8100]{2,0,1:T(2,128)(2,1)} %param.11, s32[]{:T(128)S(6)} %select_n.101), kind=kLoop, calls=%fused_computation | loop fusion | bytes 1490404 | tf_op jit(solution)/shard_map/force/dynamic_slice | solution.py:351
  2.5 1.6 %collective-permute-start = (bf16[23,2,8100]{2,1,0:T(2,128)(2,1)S(1)}, bf16[23,2,8100]{2,1,0:T(2,128)(2,1)S(1)}, u32[]{:S(2)}, u32[]{:S(2)}) collective-permute-start(bf16[23,2,8100]{2,1,0:T(2,128)(2,1)S(1)} %dynamic-slice_bitcast_fusion), channel_id=1, source_target_pairs={{0,64},{64,128},{128,192},{192,0},{1,65},{65,129},{129,193},{193,1... | collective-permute-start | bytes 2235608 | tf_op jit(solution)/shard_map/force/ppermute | solution.py:352
  4.1 0.9 collective-permute-start.1
  5.2 0.1 pad_dynamic-slice_fusion.2
  5.3 0.7 fusion.1.share_ref
  6.0 1.6 %records.1 = bf16[32,12,180]{2,1,0:T(8,128)(2,1)} custom-call(s32[1,32]{1,0:T(1,128)} %rows_ref.1, bf16[8,12,180]{2,1,0:T(8,128)(2,1)} %fusion.1.share_ref), custom_call_target="tpu_custom_call" | custom-call | tf_op jit(solution)/shard_map/records/pallas_call | solution.py:337
  7.6 23.2 %all_to_all.15.arrived_ref = bf16[32,12,180]{2,1,0:T(8,128)(2,1)} all-to-all(bf16[32,12,180]{2,1,0:T(8,128)(2,1)} %records.1), channel_id=1, replica_groups=mesh['clus'=4,'trip'=32,'mode'=2] {'trip'}, dimensions={0} | all-to-all | bytes 276480 | tf_op jit(solution)/shard_map/records/all_to_all | solution.py:344
  30.8 0.7 collective-permute-start.10
  31.4 1.1 %slice.12 = bf16[12,2,8100]{2,1,0:T(2,128)(2,1)} slice(bf16[23,2,8100]{2,1,0:T(2,128)(2,1)S(1)} %collective-permute-done.refs_0_), slice={[0:12], [0:2], [0:8100]} | slice | bytes 777600 | tf_op jit(solution)/shard_map/force_second/slice | solution.py:359
  32.5 1.8 %collective-permute-start.11 = (bf16[23,2,8100]{2,1,0:T(2,128)(2,1)S(1)}, bf16[23,2,8100]{2,1,0:T(2,128)(2,1)S(1)}, u32[]{:S(2)}, u32[]{:S(2)}) collective-permute-start(bf16[23,2,8100]{2,1,0:T(2,128)(2,1)S(1)} %collective-permute-done.1.refs_2_), channel_id=1, source_target_pairs={{0,2},{2,4},{4,6},{6,8},{8,10},{10,12},{12,14},{14,0},{16,18},{18,... | collective-permute-start | bytes 2235608 | tf_op jit(solution)/shard_map/force_second/ppermute | solution.py:358
  34.3 1.0 slice.13
  35.3 1.5 %collective-permute-start.2 = (bf16[12,2,8100]{2,1,0:T(2,128)(2,1)}, bf16[12,2,8100]{2,1,0:T(2,128)(2,1)}, u32[]{:S(2)}, u32[]{:S(2)}) collective-permute-start(bf16[12,2,8100]{2,1,0:T(2,128)(2,1)} %slice.12), channel_id=1, source_target_pairs={{0,64},{64,128},{128,192},{192,0},{1,65},{65,129},{129,193},{193,1... | collective-permute-start | bytes 1166408 | tf_op jit(solution)/shard_map/force_second/ppermute | solution.py:359
  36.8 0.5 collective-permute-start.3
  37.4 0.1 copy.31
  37.5 0.6 pad.4.phase_ref
  38.1 1.7 %members.1 = bf16[8,4,16,180]{3,2,1,0:T(8,128)(2,1)} custom-call(s32[4,3]{1,0:T(4,128)} %table_ref.1, bf16[32,12,180]{2,1,0:T(8,128)(2,1)} %all_to_all.15.arrived_ref, bf16[4,16,180]{2,1,0:T(8,128)(2,1)} %pad.4.phase_ref), custom_call_target="tpu_custom_call" | custom-call | tf_op jit(solution)/shard_map/members/pallas_call | solution.py:363
  39.8 6.3 %all-to-all-start.1 = ((bf16[8,4,16,180]{3,2,1,0:T(8,128)(2,1)}), bf16[8,4,16,180]{3,2,1,0:T(8,128)(2,1)S(1)}, u32[]{:S(2)}, u32[]{:S(2)}) async-start(bf16[8,4,16,180]{3,2,1,0:T(8,128)(2,1)} %members.1), calls=%async_computation.1 | async-start | bytes 524288 | tf_op jit(solution)/shard_map/members/all_to_all | solution.py:370
  46.1 0.1 collective-permute-start.7
  46.3 6.0 %all-to-all-done.1.members_ref = bf16[8,4,16,180]{3,2,1,0:T(8,128)(2,1)S(1)} async-done(((bf16[8,4,16,180]{3,2,1,0:T(8,128)(2,1)}), bf16[8,4,16,180]{3,2,1,0:T(8,128)(2,1)S(1)}, u32[]{:S(2)}, u32[]{:S(2)}) %all-to-all-start.1) | async-done | bytes 184352 | tf_op jit(solution)/shard_map/members/all_to_all | solution.py:370
  52.2 1.5 %collective-permute-start.5 = (bf16[11,2,8100]{2,1,0:T(2,128)(2,1)}, bf16[11,2,8100]{2,1,0:T(2,128)(2,1)}, u32[]{:S(2)}, u32[]{:S(2)}) collective-permute-start(bf16[11,2,8100]{2,1,0:T(2,128)(2,1)} %collective-permute-done.3.refs_6_), channel_id=1, source_target_pairs={{0,14},{2,0},{4,2},{6,4},{8,6},{10,8},{12,10},{14,12},{16,30},{18,... | collective-permute-start | bytes 1069208 | tf_op jit(solution)/shard_map/force_shared/ppermute | solution.py:375
  53.7 2.6 %collective-permute-start.4 = (bf16[12,2,8100]{2,1,0:T(2,128)(2,1)}, bf16[12,2,8100]{2,1,0:T(2,128)(2,1)}, u32[]{:S(2)}, u32[]{:S(2)}) collective-permute-start(bf16[12,2,8100]{2,1,0:T(2,128)(2,1)} %collective-permute-done.2.refs_5_), channel_id=1, source_target_pairs={{0,48},{2,50},{4,52},{6,54},{8,56},{10,58},{12,60},{14,62},{16,0},... | collective-permute-start | bytes 1166408 | tf_op jit(solution)/shard_map/force_shared/ppermute | solution.py:374
  56.4 0.7 dynamic_slice.23
  57.0 1.2 %pad_add_fusion.where_ref = s32[4]{0:T(128)} fusion(s32[1]{0:T(128)} %bitcast.3, s32[1]{0:T(128)} %dynamic_slice.23, s32[1]{0:T(128)} %bitcast.2, s32[1]{0:T(128)} %bitcast.1), kind=kLoop, calls=%fused_computation.21 | loop fusion | flops 12 | bytes 32 | tf_op jit(solution)/shard_map/operands/stack | solution.py:379
  58.3 2.4 %operands.1 = (bf16[192,288]{1,0:T(8,128)(2,1)}, bf16[96,256]{1,0:T(8,128)(2,1)}, bf16[192,192]{1,0:T(8,128)(2,1)}, bf16[256,256]{1,0:T(8,128)(2,1)}, f32[4,96,128]{2,1,0:T(8,128)}, /*index=5*/f32[2,48,128]{2,1,0:T(8,128)}) custom-call(s32[4]{0:T(128)} %pad_add_fusion.where_ref, bf16[8,4,16,180]{3,2,1,0:T(8,128)(2,1)} %copy-done.2), custom_call_target="tpu_custom_call" | custom-call | tf_op jit(solution)/shard_map/operands/pallas_call | solution.py:380
  60.7 0.9 copy-done.4
  61.6 5.8 %contract.1 = (bf16[96,8100]{1,0:T(8,128)(2,1)}, bf16[32,8100]{1,0:T(8,128)(2,1)}, bf16[32,8100]{1,0:T(8,128)(2,1)}, bf16[32,8100]{1,0:T(8,128)(2,1)}) custom-call(bf16[192,288]{1,0:T(8,128)(2,1)} %get-tuple-element.25.lead_ref, bf16[45,2,8100]{2,1,0:T(2,128)(2,1)} %bitcast.27, bf16[23,2,8100]{2,1,0:T(2,128)(2,1)} %copy-done, ...), custom_call_target="tpu_custom_call" | custom-call | flops 895795200 | bytes 9720000 | tf_op jit(solution)/shard_map/contract/pallas_call | solution.py:398
  67.4 0.4 collective-permute-start.12
  67.8 0.1 collective-permute-start.13
  67.9 0.4 collective-permute-start.14
  68.3 0.1 collective-permute-start.8
  68.4 0.4 collective-permute-start.9
  68.8 0.6 fusion.9
  69.4 1.3 %iota_compare_fusion.2 = (pred[32]{0:T(512)(128)(4,1)S(1)}, pred[32]{0:T(512)(128)(4,1)S(1)}) fusion(s32[]{:T(128)} %bitcast.13, s32[]{:T(128)} %bitcast), kind=kLoop, calls=%fused_computation.26 | loop fusion | flops 64 | bytes 72 | tf_op jit(solution)/shard_map/collect/eq | solution.py:439
  70.7 1.4 %collective-permute-done.9.refs_12_ = bf16[11,2,8100]{2,1,0:T(2,128)(2,1)S(1)} collective-permute-done((bf16[11,2,8100]{2,1,0:T(2,128)(2,1)}, bf16[11,2,8100]{2,1,0:T(2,128)(2,1)S(1)}, u32[]{:S(2)}, u32[]{:S(2)}) %collective-permute-start.9) | collective-permute-done | bytes 356432 | tf_op jit(solution)/shard_map/contract/ppermute | solution.py:411
  72.2 0.7 copy-done.10
  72.9 0.1 copy-done.8
  73.0 0.2 copy-done.5
  73.2 0.1 copy-done.6
  73.4 0.2 copy-done.7
  73.5 10.9 %interaction.1 = f32[1,128]{1,0:T(1,128)} custom-call(f32[2,48,128]{2,1,0:T(8,128)} %get-tuple-element.16.refs_0_, bf16[192,192]{1,0:T(8,128)(2,1)} %get-tuple-element.17.refs_1_, bf16[256,256]{1,0:T(8,128)(2,1)} %get-tuple-element.18.refs_2_, f32[4,96,128]{2,1,0:T(8,128)} %get-tuple-element.19.refs_3_, bf16[96,256]{1,0:T(8,128)(2,1)} %get-tuple-element.20.refs_4_, ...), custom_call_target="tpu_custom_call" | custom-call | tf_op jit(solution)/shard_map/interaction/pallas_call | solution.py:415
  84.4 0.1 collective-permute-start.15
  84.5 3.5 %collective-permute-start.16 = (f32[1,128]{1,0:T(1,128)}, f32[1,128]{1,0:T(1,128)S(1)}, u32[]{:S(2)}, u32[]{:S(2)}) collective-permute-start(f32[1,128]{1,0:T(1,128)} %interaction.1), channel_id=1, source_target_pairs={{0,128},{64,192},{128,0},{192,64},{1,129},{65,193},{129,1},{193,65... | collective-permute-start | bytes 1544 | tf_op jit(solution)/shard_map/collect/ppermute | solution.py:434
  88.0 0.5 collective-permute-start.17
  88.6 1.2 %iota_compare_fusion = (pred[32]{0:T(512)(128)(4,1)S(1)}, pred[32]{0:T(512)(128)(4,1)S(1)}) fusion(s32[]{:T(128)} %bitcast.17, s32[]{:T(128)} %bitcast.15), kind=kLoop, calls=%fused_computation.24 | loop fusion | flops 64 | bytes 72 | tf_op jit(solution)/shard_map/collect/eq | solution.py:439
  89.8 1.9 %collective-permute-done.17 = f32[1,128]{1,0:T(1,128)S(1)} collective-permute-done((f32[1,128]{1,0:T(1,128)}, f32[1,128]{1,0:T(1,128)S(1)}, u32[]{:S(2)}, u32[]{:S(2)}) %collective-permute-start.17) | collective-permute-done | bytes 544 | tf_op jit(solution)/shard_map/collect/ppermute | solution.py:434
  91.7 0.9 fusion.4
  92.5 13.3 %all_to_all.16 = f32[32,1,128]{2,1,0:T(1,128)S(1)} all-to-all(f32[32,1,128]{2,1,0:T(1,128)S(1)} %fusion.4), channel_id=1, replica_groups=mesh['clus'=4,'trip'=32,'mode'=2] {'trip'}, dimensions={0} | all-to-all | bytes 32768 | tf_op jit(solution)/shard_map/collect/all_to_all | solution.py:440
  105.8 0.6 add_divide_fusion
  (55 shorter events, 0.3 us)
Async XLA Ops:
  0.6 4.4 %copy-start.9 = (bf16[8,90,180]{2,0,1:T(8,128)(2,1)S(1)}, bf16[8,90,180]{2,0,1:T(8,128)(2,1)}, u32[]{:S(2)}) copy-start(bf16[8,90,180]{2,0,1:T(8,128)(2,1)} %param.13) | copy-start | bytes 777604
  0.6 4.4 %copy-start.13 = (bf16[8,90]{1,0:T(8,128)(2,1)S(1)}, bf16[8,90]{1,0:T(8,128)(2,1)}, u32[]{:S(2)}) copy-start(bf16[8,90]{1,0:T(8,128)(2,1)} %param.14) | copy-start | bytes 4324
  0.7 4.4 %copy-start.12 = (bf16[8,90]{1,0:T(8,128)(2,1)S(1)}, bf16[8,90]{1,0:T(8,128)(2,1)}, u32[]{:S(2)}) copy-start(bf16[8,90]{1,0:T(8,128)(2,1)} %param.15) | copy-start | bytes 4324
  2.5 28.2 %collective-permute-start = (bf16[23,2,8100]{2,1,0:T(2,128)(2,1)S(1)}, bf16[23,2,8100]{2,1,0:T(2,128)(2,1)S(1)}, u32[]{:S(2)}, u32[]{:S(2)}) collective-permute-start(bf16[23,2,8100]{2,1,0:T(2,128)(2,1)S(1)} %dynamic-slice_bitcast_fusion), channel_id=1, source_target_pairs={{0,64},{64,128},{128,192},{192,0},{1,65},{65,129},{129,193},{193,1... | collective-permute-start | bytes 2235608 | tf_op jit(solution)/shard_map/force/ppermute | solution.py:352
  4.1 26.6 %collective-permute-start.1 = (bf16[23,2,8100]{2,1,0:T(2,128)(2,1)S(1)}, bf16[23,2,8100]{2,1,0:T(2,128)(2,1)S(1)}, u32[]{:S(2)}, u32[]{:S(2)}) collective-permute-start(bf16[23,2,8100]{2,1,0:T(2,128)(2,1)S(1)} %dynamic-slice_bitcast_fusion), channel_id=1, source_target_pairs={{0,192},{64,0},{128,64},{192,128},{1,193},{65,1},{129,65},{193,129... | collective-permute-start | bytes 2235608 | tf_op jit(solution)/shard_map/force/ppermute | solution.py:353
  5.1 32.3 %copy-start.16 = (bf16[2,4]{1,0:T(2,128)(2,1)S(1)}, bf16[2,4]{1,0:T(2,128)(2,1)}, u32[]{:S(2)}) copy-start(bf16[2,4]{1,0:T(2,128)(2,1)} %param.12) | copy-start | bytes 52
  7.6 48.8 %copy-start.17 = (s32[4]{0:T(128)S(1)}, s32[4]{0:T(128)}, u32[]{:S(2)}) copy-start(s32[4]{0:T(128)} %param.19) | copy-start | bytes 52
  30.7 29.9 %copy-start = (bf16[23,2,8100]{2,1,0:T(2,128)(2,1)}, bf16[23,2,8100]{2,1,0:T(2,128)(2,1)S(1)}, u32[]{:S(2)}) copy-start(bf16[23,2,8100]{2,1,0:T(2,128)(2,1)S(1)} %collective-permute-done.refs_0_) | copy-start | bytes 2235604
  30.7 29.9 %copy-start.1 = (bf16[23,2,8100]{2,1,0:T(2,128)(2,1)}, bf16[23,2,8100]{2,1,0:T(2,128)(2,1)S(1)}, u32[]{:S(2)}) copy-start(bf16[23,2,8100]{2,1,0:T(2,128)(2,1)S(1)} %collective-permute-done.1.refs_2_) | copy-start | bytes 2235604
  30.8 25.6 %collective-permute-start.10 = (bf16[23,2,8100]{2,1,0:T(2,128)(2,1)S(1)}, bf16[23,2,8100]{2,1,0:T(2,128)(2,1)S(1)}, u32[]{:S(2)}, u32[]{:S(2)}) collective-permute-start(bf16[23,2,8100]{2,1,0:T(2,128)(2,1)S(1)} %collective-permute-done.refs_0_), channel_id=1, source_target_pairs={{0,16},{2,18},{4,20},{6,22},{8,24},{10,26},{12,28},{14,30},{16,32}... | collective-permute-start | bytes 2235608 | tf_op jit(solution)/shard_map/force_second/ppermute | solution.py:357
  32.5 28.2 %collective-permute-start.11 = (bf16[23,2,8100]{2,1,0:T(2,128)(2,1)S(1)}, bf16[23,2,8100]{2,1,0:T(2,128)(2,1)S(1)}, u32[]{:S(2)}, u32[]{:S(2)}) collective-permute-start(bf16[23,2,8100]{2,1,0:T(2,128)(2,1)S(1)} %collective-permute-done.1.refs_2_), channel_id=1, source_target_pairs={{0,2},{2,4},{4,6},{6,8},{8,10},{10,12},{12,14},{14,0},{16,18},{18,... | collective-permute-start | bytes 2235608 | tf_op jit(solution)/shard_map/force_second/ppermute | solution.py:358
  35.3 16.9 %collective-permute-start.2 = (bf16[12,2,8100]{2,1,0:T(2,128)(2,1)}, bf16[12,2,8100]{2,1,0:T(2,128)(2,1)}, u32[]{:S(2)}, u32[]{:S(2)}) collective-permute-start(bf16[12,2,8100]{2,1,0:T(2,128)(2,1)} %slice.12), channel_id=1, source_target_pairs={{0,64},{64,128},{128,192},{192,0},{1,65},{65,129},{129,193},{193,1... | collective-permute-start | bytes 1166408 | tf_op jit(solution)/shard_map/force_second/ppermute | solution.py:359
  36.8 9.3 %collective-permute-start.3 = (bf16[11,2,8100]{2,1,0:T(2,128)(2,1)}, bf16[11,2,8100]{2,1,0:T(2,128)(2,1)}, u32[]{:S(2)}, u32[]{:S(2)}) collective-permute-start(bf16[11,2,8100]{2,1,0:T(2,128)(2,1)} %slice.13), channel_id=1, source_target_pairs={{0,192},{64,0},{128,64},{192,128},{1,193},{65,1},{129,65},{193,129... | collective-permute-start | bytes 1069208 | tf_op jit(solution)/shard_map/force_second/ppermute | solution.py:360
  39.8 12.4 %all-to-all-start.1 = ((bf16[8,4,16,180]{3,2,1,0:T(8,128)(2,1)}), bf16[8,4,16,180]{3,2,1,0:T(8,128)(2,1)S(1)}, u32[]{:S(2)}, u32[]{:S(2)}) async-start(bf16[8,4,16,180]{3,2,1,0:T(8,128)(2,1)} %members.1), calls=%async_computation.1 | async-start | bytes 524288 | tf_op jit(solution)/shard_map/members/all_to_all | solution.py:370
  46.1 21.7 %collective-permute-start.7 = (bf16[11,2,8100]{2,1,0:T(2,128)(2,1)}, bf16[11,2,8100]{2,1,0:T(2,128)(2,1)}, u32[]{:S(2)}, u32[]{:S(2)}) collective-permute-start(bf16[11,2,8100]{2,1,0:T(2,128)(2,1)} %collective-permute-done.3.refs_6_), channel_id=1, source_target_pairs={{0,1},{1,0},{2,3},{3,2},{4,5},{5,4},{6,7},{7,6},{8,9},{9,8},{10,11... | collective-permute-start | bytes 1069208 | tf_op jit(solution)/shard_map/contract/ppermute | solution.py:411
  52.2 6.1 %copy-start.2 = (bf16[8,4,16,180]{3,2,1,0:T(8,128)(2,1)}, bf16[8,4,16,180]{3,2,1,0:T(8,128)(2,1)S(1)}, u32[]{:S(2)}) copy-start(bf16[8,4,16,180]{3,2,1,0:T(8,128)(2,1)S(1)} %all-to-all-done.1.members_ref) | copy-start | bytes 552964
  52.2 15.7 %collective-permute-start.5 = (bf16[11,2,8100]{2,1,0:T(2,128)(2,1)}, bf16[11,2,8100]{2,1,0:T(2,128)(2,1)}, u32[]{:S(2)}, u32[]{:S(2)}) collective-permute-start(bf16[11,2,8100]{2,1,0:T(2,128)(2,1)} %collective-permute-done.3.refs_6_), channel_id=1, source_target_pairs={{0,14},{2,0},{4,2},{6,4},{8,6},{10,8},{12,10},{14,12},{16,30},{18,... | collective-permute-start | bytes 1069208 | tf_op jit(solution)/shard_map/force_shared/ppermute | solution.py:375
  53.7 14.6 %collective-permute-start.4 = (bf16[12,2,8100]{2,1,0:T(2,128)(2,1)}, bf16[12,2,8100]{2,1,0:T(2,128)(2,1)}, u32[]{:S(2)}, u32[]{:S(2)}) collective-permute-start(bf16[12,2,8100]{2,1,0:T(2,128)(2,1)} %collective-permute-done.2.refs_5_), channel_id=1, source_target_pairs={{0,48},{2,50},{4,52},{6,54},{8,56},{10,58},{12,60},{14,62},{16,0},... | collective-permute-start | bytes 1166408 | tf_op jit(solution)/shard_map/force_shared/ppermute | solution.py:374
  56.3 4.3 %copy-start.3 = (bf16[23,2,8100]{2,1,0:T(2,128)(2,1)}, bf16[23,2,8100]{2,1,0:T(2,128)(2,1)S(1)}, u32[]{:S(2)}) copy-start(bf16[23,2,8100]{2,1,0:T(2,128)(2,1)S(1)} %collective-permute-done.10.refs_1_) | copy-start | bytes 2235604
  56.3 12.1 %collective-permute-start.6 = (bf16[12,2,8100]{2,1,0:T(2,128)(2,1)}, bf16[12,2,8100]{2,1,0:T(2,128)(2,1)}, u32[]{:S(2)}, u32[]{:S(2)}) collective-permute-start(bf16[12,2,8100]{2,1,0:T(2,128)(2,1)} %collective-permute-done.2.refs_5_), channel_id=1, source_target_pairs={{0,1},{1,0},{2,3},{3,2},{4,5},{5,4},{6,7},{7,6},{8,9},{9,8},{10,11... | collective-permute-start | bytes 1166408 | tf_op jit(solution)/shard_map/contract/ppermute | solution.py:411
  60.7 0.9 copy-start.4
  61.5 7.3 %copy-start.11 = (s32[4]{0:T(128)S(1)}, s32[4]{0:T(128)}, u32[]{:S(2)}) copy-start(s32[4]{0:T(128)} %param.18) | copy-start | bytes 52
  67.4 4.8 %collective-permute-start.12 = (bf16[32,8100]{1,0:T(8,128)(2,1)}, bf16[32,8100]{1,0:T(8,128)(2,1)S(1)}, u32[]{:S(2)}, u32[]{:S(2)}) collective-permute-start(bf16[32,8100]{1,0:T(8,128)(2,1)} %get-tuple-element.27), channel_id=1, source_target_pairs={{0,1},{1,0},{2,3},{3,2},{4,5},{5,4},{6,7},{7,6},{8,9},{9,8},{10,11... | collective-permute-start | bytes 1555208 | tf_op jit(solution)/shard_map/contract/ppermute | solution.py:409
  67.8 4.3 %collective-permute-start.13 = (bf16[32,8100]{1,0:T(8,128)(2,1)}, bf16[32,8100]{1,0:T(8,128)(2,1)S(1)}, u32[]{:S(2)}, u32[]{:S(2)}) collective-permute-start(bf16[32,8100]{1,0:T(8,128)(2,1)} %get-tuple-element.28), channel_id=1, source_target_pairs={{0,1},{1,0},{2,3},{3,2},{4,5},{5,4},{6,7},{7,6},{8,9},{9,8},{10,11... | collective-permute-start | bytes 1555208 | tf_op jit(solution)/shard_map/contract/ppermute | solution.py:409
  67.9 4.3 %collective-permute-start.14 = (bf16[32,8100]{1,0:T(8,128)(2,1)}, bf16[32,8100]{1,0:T(8,128)(2,1)S(1)}, u32[]{:S(2)}, u32[]{:S(2)}) collective-permute-start(bf16[32,8100]{1,0:T(8,128)(2,1)} %get-tuple-element.29), channel_id=1, source_target_pairs={{0,1},{1,0},{2,3},{3,2},{4,5},{5,4},{6,7},{7,6},{8,9},{9,8},{10,11... | collective-permute-start | bytes 1555208 | tf_op jit(solution)/shard_map/contract/ppermute | solution.py:409
  68.3 3.8 %collective-permute-start.8 = (bf16[12,2,8100]{2,1,0:T(2,128)(2,1)}, bf16[12,2,8100]{2,1,0:T(2,128)(2,1)S(1)}, u32[]{:S(2)}, u32[]{:S(2)}) collective-permute-start(bf16[12,2,8100]{2,1,0:T(2,128)(2,1)} %collective-permute-done.4.refs_7_), channel_id=1, source_target_pairs={{0,1},{1,0},{2,3},{3,2},{4,5},{5,4},{6,7},{7,6},{8,9},{9,8},{10,11... | collective-permute-start | bytes 1166408 | tf_op jit(solution)/shard_map/contract/ppermute | solution.py:411
  68.4 3.7 %collective-permute-start.9 = (bf16[11,2,8100]{2,1,0:T(2,128)(2,1)}, bf16[11,2,8100]{2,1,0:T(2,128)(2,1)S(1)}, u32[]{:S(2)}, u32[]{:S(2)}) collective-permute-start(bf16[11,2,8100]{2,1,0:T(2,128)(2,1)} %collective-permute-done.5.refs_8_), channel_id=1, source_target_pairs={{0,1},{1,0},{2,3},{3,2},{4,5},{5,4},{6,7},{7,6},{8,9},{9,8},{10,11... | collective-permute-start | bytes 1069208 | tf_op jit(solution)/shard_map/contract/ppermute | solution.py:411
  72.1 0.7 copy-start.10
  72.1 0.9 copy-start.8
  72.1 1.1 %copy-start.5 = (bf16[32,8100]{1,0:T(8,128)(2,1)}, bf16[32,8100]{1,0:T(8,128)(2,1)S(1)}, u32[]{:S(2)}) copy-start(bf16[32,8100]{1,0:T(8,128)(2,1)S(1)} %collective-permute-done.12.refs_14_) | copy-start | bytes 1555204
  72.2 1.2 %copy-start.6 = (bf16[32,8100]{1,0:T(8,128)(2,1)}, bf16[32,8100]{1,0:T(8,128)(2,1)S(1)}, u32[]{:S(2)}) copy-start(bf16[32,8100]{1,0:T(8,128)(2,1)S(1)} %collective-permute-done.13.refs_15_) | copy-start | bytes 1555204
  72.2 1.3 %copy-start.7 = (bf16[32,8100]{1,0:T(8,128)(2,1)}, bf16[32,8100]{1,0:T(8,128)(2,1)S(1)}, u32[]{:S(2)}) copy-start(bf16[32,8100]{1,0:T(8,128)(2,1)S(1)} %collective-permute-done.14.refs_16_) | copy-start | bytes 1555204
  73.5 32.3 %copy-start.14 = (f32[1,45]{1,0:T(1,128)S(1)}, f32[1,45]{1,0:T(1,128)}, u32[]{:S(2)}) copy-start(f32[1,45]{1,0:T(1,128)} %param.20) | copy-start | bytes 544
  73.5 32.3 %copy-start.15 = (f32[1,45]{1,0:T(1,128)S(1)}, f32[1,45]{1,0:T(1,128)}, u32[]{:S(2)}) copy-start(f32[1,45]{1,0:T(1,128)} %param.21) | copy-start | bytes 544
  84.4 5.4 %collective-permute-start.15 = (f32[1,128]{1,0:T(1,128)}, f32[1,128]{1,0:T(1,128)S(1)}, u32[]{:S(2)}, u32[]{:S(2)}) collective-permute-start(f32[1,128]{1,0:T(1,128)} %interaction.1), channel_id=1, source_target_pairs={{0,64},{64,128},{128,192},{192,0},{1,65},{65,129},{129,193},{193,1... | collective-permute-start | bytes 1544 | tf_op jit(solution)/shard_map/collect/ppermute | solution.py:434
  84.5 5.3 %collective-permute-start.16 = (f32[1,128]{1,0:T(1,128)}, f32[1,128]{1,0:T(1,128)S(1)}, u32[]{:S(2)}, u32[]{:S(2)}) collective-permute-start(f32[1,128]{1,0:T(1,128)} %interaction.1), channel_id=1, source_target_pairs={{0,128},{64,192},{128,0},{192,64},{1,129},{65,193},{129,1},{193,65... | collective-permute-start | bytes 1544 | tf_op jit(solution)/shard_map/collect/ppermute | solution.py:434
  88.0 3.7 %collective-permute-start.17 = (f32[1,128]{1,0:T(1,128)}, f32[1,128]{1,0:T(1,128)S(1)}, u32[]{:S(2)}, u32[]{:S(2)}) collective-permute-start(f32[1,128]{1,0:T(1,128)} %interaction.1), channel_id=1, source_target_pairs={{0,192},{64,0},{128,64},{192,128},{1,193},{65,1},{129,65},{193,129... | collective-permute-start | bytes 1544 | tf_op jit(solution)/shard_map/collect/ppermute | solution.py:434

commit v9 on v6

--- a/solution.py
+++ b/solution.py
@@ -70,14 +70,20 @@
     columns = []
     for array in (lead_r, lead_i):
         columns.append([halves(side) for side in sides(array)])
-    whole = [[spread(columns[i][0][h], 0, 45) for i in range(2)] for h in range(2)]
-    early_ref[...] = jnp.concatenate(
-        [
-            jnp.concatenate([turned(*whole[h], offset) for h in range(2)], axis=0)
-            for offset in (0, 3, 1)
-        ],
-        axis=1,
-    ).astype(early_ref.dtype)
+    blocks = []
+    for offset, start, count, width in (
+        (0, 0, 45, WIDE),
+        (3, 0, TOP, PAD),
+        (3, TOP, 45 - TOP, PAD),
+        (1, 0, TOP, PAD),
+        (1, TOP, 45 - TOP, PAD),
+    ):
+        rows = []
+        for h in range(2):
+            real, imag = (spread(columns[i][0][h], start, count)[:, 0:width] for i in range(2))
+            rows.append(turned(real, imag, offset))
+        blocks.append(jnp.concatenate(rows, axis=0))
+    early_ref[...] = jnp.concatenate(blocks, axis=1).astype(early_ref.dtype)
     parts = []
     for side in range(2):
         for start, count in ((0, TOP), (TOP, 45 - TOP)):
@@ -130,23 +136,26 @@
     return jnp.pad(values.reshape(rows, values.shape[2]), ((0, count - rows), (0, 0)))
 
 
-def early_kernel(lead_ref, own_ref, low_ref, high_ref, mine_ref, *far_refs):
+def early_kernel(lead_ref, own_ref, *refs):
+    halves, mine_ref, far_refs = refs[:4], refs[4], refs[5:]
     total = own_ref.shape[2]
     for start in range(0, total, CHUNK):
         cols = slice(start, min(start + CHUNK, total))
         product = jnp.dot(
             lead_ref[...],
-            jnp.concatenate([rows_of(ref, cols, WIDE) for ref in (own_ref, low_ref, high_ref)], axis=0),
+            jnp.concatenate(
+                [rows_of(own_ref, cols, WIDE)] + [rows_of(ref, cols, PAD) for ref in halves], axis=0
+            ),
             preferred_element_type=jnp.float32,
         )
         mine_ref[:, cols] = product[0:WIDE].astype(mine_ref.dtype)
         for i, far_ref in enumerate(far_refs):
-            rows = product[WIDE + 24 * i : WIDE + 24 * i + 24]
+            rows = product[WIDE + 48 * i : WIDE + 48 * i + 48]
             far_ref[:, cols] = rows.astype(far_ref.dtype)
 
 
 def interaction_kernel(*refs):
-    count = 14
+    count = 12
     operands, out_ref, buffers = refs[:count], refs[count], refs[count + 1 : 2 * count + 1]
     flat, windows, mid_real, mid_imag, rate_acc, couple_acc, done = refs[2 * count + 1 :]
     scalars_ref, middle_ref, last_ref, tables_ref, late_ref = buffers[:5]
@@ -224,8 +233,8 @@
 
     scaled = 0.5 / (smearing * smearing)
     def two_modes(s):
-        low = pl.ds(pl.multiple_of(s * WIDE, WIDE), WIDE)
-        high = pl.ds(pl.multiple_of(s * WIDE + WIDE, WIDE), WIDE)
+        low = pl.ds(s * WIDE, WIDE)
+        high = pl.ds(s * WIDE + WIDE, WIDE)
         operand = jnp.concatenate(
             [
                 jnp.concatenate([ref[low, :], ref[high, :]], axis=1).astype(jnp.bfloat16)
@@ -244,15 +253,13 @@
                 jnp.exp(-scaled * decays * decays) + jnp.exp(-scaled * merges * merges)
             )
             weight = weight * tables_ref[2] * scalars_ref[1, pl.ds(s + i, 1), :]
-            at = pl.ds(pl.multiple_of((s + i) * 8, 8), 8)
+            at = pl.ds((s + i) * 8, 8)
             rate_acc[at, :] = jnp.sum(weight.reshape(WIDE // 8, 8, 128), axis=0)
             weight = weight * tables_ref[3]
             couple_acc[at, :] = jnp.sum(weight.reshape(WIDE // 8, 8, 128), axis=0)
 
-    @pl.loop(0, 12)
-    def _(i):
-        two_modes(4 * i)
-        two_modes(4 * i + 2)
+    for i in range(24):
+        two_modes(2 * i)
 
     sums = jnp.concatenate(
         [
@@ -318,8 +325,17 @@
 
     with jax.named_scope("force"):
         own = jnp.transpose(force_third, (1, 0, 2))
-        low = lax.ppermute(own, "clus", ring(4, 1))
-        high = lax.ppermute(own, "clus", ring(4, 3))
+        own_top, own_bottom = own[:TOP], own[TOP:]
+        low_top = lax.ppermute(own_top, "clus", ring(4, 1))
+        high_bottom = lax.ppermute(own_bottom, "clus", ring(4, 3))
+        own_top, own_bottom, _ = lax.optimization_barrier((own_top, own_bottom, chosen))
+        low_bottom = lax.ppermute(own_bottom, "clus", ring(4, 1))
+        high_top = lax.ppermute(own_top, "clus", ring(4, 3))
+
+    with jax.named_scope("force_second"):
+        passed_top, passed_bottom, _ = lax.optimization_barrier((low_top, high_bottom, arrived))
+        top = lax.ppermute(passed_top, "clus", ring(4, 1))
+        bottom = lax.ppermute(passed_bottom, "clus", ring(4, 3))
 
     with jax.named_scope("members"):
         picks = pl.pallas_call(
@@ -330,11 +346,6 @@
             compiler_params=PARAMS,
         )(trip_table, arrived, phases)
         members = lax.all_to_all(picks, group, 0, 0, tiled=True)
-
-    with jax.named_scope("force_second"):
-        low_top, high_bottom, _ = lax.optimization_barrier((low[:TOP], high[TOP:], members))
-        top = lax.ppermute(low_top, "clus", ring(4, 1))
-        bottom = lax.ppermute(high_bottom, "clus", ring(4, 3))
 
     with jax.named_scope("operands"):
         mult = lax.dynamic_index_in_dim(multiplicity, clus, 0, keepdims=False)
@@ -360,14 +371,14 @@
         mine, *far = pl.pallas_call(
             early_kernel,
             out_shape=(jax.ShapeDtypeStruct((WIDE, total), b16),)
-            + (jax.ShapeDtypeStruct((WIDE // 4, total), b16),) * 4,
-            in_specs=[VMEM] * 4,
-            out_specs=(VMEM,) * 5,
+            + (jax.ShapeDtypeStruct((WIDE // 2, total), b16),) * 2,
+            in_specs=[VMEM] * 6,
+            out_specs=(VMEM,) * 3,
             compiler_params=PARAMS,
             cost_estimate=pl.CostEstimate(
                 flops=2 * 192 * 288 * total, bytes_accessed=1200 * total, transcendentals=0
             ),
-        )(early, own, low, high)
+        )(early, own, low_top, low_bottom, high_top, high_bottom)
         other = [lax.ppermute(rows, "mode", swap) for rows in far]
         far_top = lax.ppermute(top, "mode", swap)
         far_bottom = lax.ppermute(bottom, "mode", swap)

time: 107 us -> 117 us (1.093)
  waiting for transfers between devices: 24.1 us -> 28.7 us
  blocking collectives: 16.3 us -> 19.1 us
  starting transfers between devices: 27.3 us -> 29.5 us
  local copies, waits for them, and re-layouts: 8.01 us -> 9.35 us
    all_to_all x1, waiting for transfers between devices: 3.04 us -> 13.8 us  [body(): members = lax.all_to_all(picks, group, 0, 0, tiled=True)]
    ppermute x4 -> x6, waiting for transfers between devices: 6.37 us -> 0.02 us  [the longest x1 0.01 us: body(): high_bottom = lax.ppermute(own_bottom, 'clus', ring(4, 3))]
    all_to_all x1, blocking collectives: 16.3 us -> 19.1 us  [body(): received = lax.all_to_all(partial[:, None, :], 'trip', 0, 0, tiled=True)]
    ppermute x4 -> x6, starting transfers between devices: 4.47 us -> 6.57 us  [the longest x1 1.82 us: body(): high_top = lax.ppermute(own_top, 'clus', ring(4, 3))]
    ppermute x1, waiting for transfers between devices: 0.01 us -> 2.11 us  [body(): far_bottom = lax.ppermute(bottom, 'mode', swap)]
    slice x2, local copies, waits for them, and re-layouts: 3.04 us -> 4.54 us  [body(): own_top, own_bottom = (own[:TOP], own[TOP:])]
    ppermute x4 -> x2, waiting for transfers between devices: 2.02 us -> 0.66 us  [body(): other = [lax.ppermute(rows, 'mode', swap) for rows in far]]
    all_to_all x1, waiting for transfers between devices: 11 us -> 9.68 us  [body(): arrived = lax.all_to_all(chosen, 'trip', 0, 0, tiled=True)]
  transfers between devices with their start and end apart: 15 -> 15, of which waited for: 7 -> 6; matrix products, arithmetic and copies ran while one was open for 11% -> 8% of each run, Pallas kernels for 11% -> 10%
where the time goes in v9:
time: 117 us; the launch traced here: 116 us
  starting transfers between devices  29.5 us (25%)
  waiting for transfers between devices  28.7 us (25%)
  Pallas kernels  22.2 us (19%)
  blocking collectives  19.1 us (16%)
  local copies, waits for them, and re-layouts  9.35 us (8%)
  other arithmetic  6.02 us (5%)
    all_to_all x1, blocking collectives, body(): received = lax.all_to_all(partial[:, None, :], 'trip', 0, 0, tiled=True)  19.1 us
    all_to_all x1, waiting for transfers between devices, body(): members = lax.all_to_all(picks, group, 0, 0, tiled=True)  13.8 us
    all_to_all x1, starting transfers between devices, body(): arrived = lax.all_to_all(chosen, 'trip', 0, 0, tiled=True)  11.2 us
    pallas_call x1, Pallas kernels, body(): pl.pallas_call(interaction_kernel, out_shape=jax.ShapeDtypeStruct((1, 128...  10.8 us
    all_to_all x1, waiting for transfers between devices, body(): arrived = lax.all_to_all(chosen, 'trip', 0, 0, tiled=True)  9.68 us
    all_to_all x1, starting transfers between devices, body(): members = lax.all_to_all(picks, group, 0, 0, tiled=True)  6.27 us
    pallas_call x1, Pallas kernels, body(): pl.pallas_call(early_kernel, out_shape=(jax.ShapeDtypeStruct((WIDE, total...  5.76 us
    slice x2, local copies, waits for them, and re-layouts, body(): own_top, own_bottom = (own[:TOP], own[TOP:])  4.54 us
  transfers between devices with their start and end apart: 15, of which 6 were waited for; matrix products, arithmetic and copies ran while one was open for 8% of the time, Pallas kernels for 10%

profile of v9, /device:TPU:2, one launch (start us, length us, event | category | flops | bytes accessed | tf_op | source)
XLA Modules:
  0.0 115.7 jit_solution(1507429592034311427)
XLA Ops:
  0.7 1.8 %slice.16 = bf16[23,2,8100]{2,1,0:T(2,128)(2,1)S(1)} slice(bf16[45,2,8100]{2,1,0:T(2,128)(2,1)} %bitcast.24), slice={[0:23], [0:2], [0:8100]} | slice | bytes 1490400 | tf_op jit(solution)/shard_map/force/slice | solution.py:328
  2.5 0.0 copy-start.14
  2.5 1.6 %collective-permute-start = (bf16[23,2,8100]{2,1,0:T(2,128)(2,1)S(1)}, bf16[23,2,8100]{2,1,0:T(2,128)(2,1)S(1)}, u32[]{:S(2)}, u32[]{:S(2)}) collective-permute-start(bf16[23,2,8100]{2,1,0:T(2,128)(2,1)S(1)} %slice.16), channel_id=1, source_target_pairs={{0,64},{64,128},{128,192},{192,0},{1,65},{65,129},{129,193},{193,1... | collective-permute-start | bytes 2235608 | tf_op jit(solution)/shard_map/force/ppermute | solution.py:329
  4.1 2.7 %slice.17 = bf16[22,2,8100]{2,1,0:T(2,128)(2,1)} slice(bf16[45,2,8100]{2,1,0:T(2,128)(2,1)} %bitcast.25), slice={[23:45], [0:2], [0:8100]} | slice | bytes 1425600 | tf_op jit(solution)/shard_map/force/slice | solution.py:328
  6.8 0.8 collective-permute-start.1
  7.6 0.1 copy.27
  7.7 0.1 maximum_bitcast_fusion
  7.8 0.1 pad_dynamic-slice_fusion.2
  7.9 0.7 fusion.1.share_ref
  8.6 1.6 %records.1 = bf16[32,12,180]{2,1,0:T(8,128)(2,1)} custom-call(s32[1,32]{1,0:T(1,128)} %rows_ref.1, bf16[8,12,180]{2,1,0:T(8,128)(2,1)} %fusion.1.share_ref), custom_call_target="tpu_custom_call" | custom-call | tf_op jit(solution)/shard_map/records/pallas_call | solution.py:314
  10.2 11.2 %all-to-all-start = ((bf16[32,12,180]{2,1,0:T(8,128)(2,1)}), bf16[32,12,180]{2,1,0:T(8,128)(2,1)S(1)}, u32[]{:S(2)}, u32[]{:S(2)}) async-start(bf16[32,12,180]{2,1,0:T(8,128)(2,1)} %records.1), calls=%async_computation | async-start | bytes 524288 | tf_op jit(solution)/shard_map/records/all_to_all | solution.py:321
  21.4 1.8 %collective-permute-start.7 = (bf16[23,2,8100]{2,1,0:T(2,128)(2,1)S(1)}, bf16[23,2,8100]{2,1,0:T(2,128)(2,1)S(1)}, u32[]{:S(2)}, u32[]{:S(2)}) collective-permute-start(bf16[23,2,8100]{2,1,0:T(2,128)(2,1)S(1)} %slice.16), channel_id=1, source_target_pairs={{0,192},{64,0},{128,64},{192,128},{1,193},{65,1},{129,65},{193,129... | collective-permute-start | bytes 2235608 | tf_op jit(solution)/shard_map/force/ppermute | solution.py:333
  23.2 0.3 collective-permute-start.6
  23.5 9.7 %all-to-all-done.arrived_ref = bf16[32,12,180]{2,1,0:T(8,128)(2,1)S(1)} async-done(((bf16[32,12,180]{2,1,0:T(8,128)(2,1)}), bf16[32,12,180]{2,1,0:T(8,128)(2,1)S(1)}, u32[]{:S(2)}, u32[]{:S(2)}) %all-to-all-start) | async-done | bytes 138272 | tf_op jit(solution)/shard_map/records/all_to_all | solution.py:321
  33.2 0.0 collective-permute-done.1.refs_3_
  33.2 0.0 collective-permute-done.refs_0_
  33.2 1.6 %collective-permute-start.2 = (bf16[23,2,8100]{2,1,0:T(2,128)(2,1)S(1)}, bf16[23,2,8100]{2,1,0:T(2,128)(2,1)}, u32[]{:S(2)}, u32[]{:S(2)}) collective-permute-start(bf16[23,2,8100]{2,1,0:T(2,128)(2,1)S(1)} %collective-permute-done.refs_0_), channel_id=1, source_target_pairs={{0,64},{64,128},{128,192},{192,0},{1,65},{65,129},{129,193},{193,1... | collective-permute-start | bytes 2235608 | tf_op jit(solution)/shard_map/force_second/ppermute | solution.py:337
  34.8 0.5 collective-permute-start.3
  35.4 0.1 copy.31
  35.5 0.6 pad.4.phase_ref
  36.1 1.7 %members.1 = bf16[8,4,16,180]{3,2,1,0:T(8,128)(2,1)} custom-call(s32[4,3]{1,0:T(4,128)} %table_ref.1, bf16[32,12,180]{2,1,0:T(8,128)(2,1)} %copy-done, bf16[4,16,180]{2,1,0:T(8,128)(2,1)} %pad.4.phase_ref), custom_call_target="tpu_custom_call" | custom-call | tf_op jit(solution)/shard_map/members/pallas_call | solution.py:341
  37.8 6.3 %all-to-all-start.1 = ((bf16[8,4,16,180]{3,2,1,0:T(8,128)(2,1)}), bf16[8,4,16,180]{3,2,1,0:T(8,128)(2,1)S(1)}, u32[]{:S(2)}, u32[]{:S(2)}) async-start(bf16[8,4,16,180]{3,2,1,0:T(8,128)(2,1)} %members.1), calls=%async_computation.1 | async-start | bytes 524288 | tf_op jit(solution)/shard_map/members/all_to_all | solution.py:348
  44.1 0.6 dynamic_slice.20
  44.6 1.2 %pad_add_fusion.where_ref = s32[3]{0:T(128)} fusion(s32[1]{0:T(128)} %dynamic_slice.20, s32[1]{0:T(128)} %bitcast.2, s32[1]{0:T(128)} %bitcast.1), kind=kLoop, calls=%fused_computation.20 | loop fusion | flops 6 | bytes 24 | tf_op jit(solution)/shard_map/operands/stack | solution.py:352
  45.9 13.8 %all-to-all-done.1.members_ref = bf16[8,4,16,180]{3,2,1,0:T(8,128)(2,1)S(1)} async-done(((bf16[8,4,16,180]{3,2,1,0:T(8,128)(2,1)}), bf16[8,4,16,180]{3,2,1,0:T(8,128)(2,1)S(1)}, u32[]{:S(2)}, u32[]{:S(2)}) %all-to-all-start.1) | async-done | bytes 184352 | tf_op jit(solution)/shard_map/members/all_to_all | solution.py:348
  59.6 0.7 copy-done.1
  60.3 2.4 %operands.1 = (bf16[192,288]{1,0:T(8,128)(2,1)}, bf16[96,192]{1,0:T(8,128)(2,1)}, bf16[192,192]{1,0:T(8,128)(2,1)}, bf16[256,256]{1,0:T(8,128)(2,1)}, f32[4,96,128]{2,1,0:T(8,128)}, /*index=5*/f32[2,48,128]{2,1,0:T(8,128)}) custom-call(s32[3]{0:T(128)} %pad_add_fusion.where_ref, bf16[8,4,16,180]{3,2,1,0:T(8,128)(2,1)} %copy-done.1), custom_call_target="tpu_custom_call" | custom-call | tf_op jit(solution)/shard_map/operands/pallas_call | solution.py:353
  62.8 0.9 copy-done.5
  63.7 5.8 %contract.1 = (bf16[96,8100]{1,0:T(8,128)(2,1)}, bf16[48,8100]{1,0:T(8,128)(2,1)}, bf16[48,8100]{1,0:T(8,128)(2,1)}) custom-call(bf16[192,288]{1,0:T(8,128)(2,1)} %get-tuple-element.22.lead_ref, bf16[45,2,8100]{2,1,0:T(2,128)(2,1)} %bitcast.26, bf16[23,2,8100]{2,1,0:T(2,128)(2,1)} %copy-done.4, bf16[22,2,8100]{2,1,0:T(2,128)(2,1)} %collective-permute-done.6.refs_1_, ...), custom_call_target="tpu_custom_call" | custom-call | flops 895795200 | bytes 9720000 | tf_op jit(solution)/shard_map/contract/pallas_call | solution.py:371
  69.4 0.5 collective-permute-start.9
  69.9 0.0 collective-permute-done.2.refs_5_
  69.9 0.0 collective-permute-start.4
  69.9 0.5 collective-permute-start.5
  70.4 0.6 fusion.9
  71.1 1.3 %iota_compare_fusion.2 = (pred[32]{0:T(512)(128)(4,1)S(1)}, pred[32]{0:T(512)(128)(4,1)S(1)}) fusion(s32[]{:T(128)} %bitcast.11, s32[]{:T(128)} %bitcast), kind=kLoop, calls=%fused_computation.25 | loop fusion | flops 64 | bytes 72 | tf_op jit(solution)/shard_map/collect/eq | solution.py:412
  72.4 0.7 collective-permute-done.9.refs_11_
  73.0 2.1 %collective-permute-done.5.refs_8_ = bf16[22,2,8100]{2,1,0:T(2,128)(2,1)S(1)} collective-permute-done((bf16[22,2,8100]{2,1,0:T(2,128)(2,1)}, bf16[22,2,8100]{2,1,0:T(2,128)(2,1)S(1)}, u32[]{:S(2)}, u32[]{:S(2)}) %collective-permute-start.5) | collective-permute-done | bytes 712832 | tf_op jit(solution)/shard_map/contract/ppermute | solution.py:384
  75.2 0.9 copy-done.7
  76.0 0.2 copy-done.6
  76.3 10.8 %interaction.1 = f32[1,128]{1,0:T(1,128)} custom-call(f32[2,48,128]{2,1,0:T(8,128)} %get-tuple-element.15.refs_0_, bf16[192,192]{1,0:T(8,128)(2,1)} %get-tuple-element.16.refs_1_, bf16[256,256]{1,0:T(8,128)(2,1)} %get-tuple-element.17.refs_2_, f32[4,96,128]{2,1,0:T(8,128)} %get-tuple-element.18.refs_3_, bf16[96,192]{1,0:T(8,128)(2,1)} %get-tuple-element.19.refs_4_, ...), custom_call_target="tpu_custom_call" | custom-call | tf_op jit(solution)/shard_map/interaction/pallas_call | solution.py:388
  87.1 1.0 collective-permute-start.10
  88.1 3.4 %collective-permute-start.11 = (f32[1,128]{1,0:T(1,128)}, f32[1,128]{1,0:T(1,128)S(1)}, u32[]{:S(2)}, u32[]{:S(2)}) collective-permute-start(f32[1,128]{1,0:T(1,128)} %interaction.1), channel_id=1, source_target_pairs={{0,128},{64,192},{128,0},{192,64},{1,129},{65,193},{129,1},{193,65... | collective-permute-start | bytes 1544 | tf_op jit(solution)/shard_map/collect/ppermute | solution.py:407
  91.5 1.2 %iota_compare_fusion = (pred[32]{0:T(512)(128)(4,1)S(1)}, pred[32]{0:T(512)(128)(4,1)S(1)}) fusion(s32[]{:T(128)} %bitcast.15, s32[]{:T(128)} %bitcast.13), kind=kLoop, calls=%fused_computation.23 | loop fusion | flops 64 | bytes 72 | tf_op jit(solution)/shard_map/collect/eq | solution.py:412
  92.7 0.6 collective-permute-done.11
  93.3 1.9 %collective-permute-done.12 = f32[1,128]{1,0:T(1,128)S(1)} collective-permute-done((f32[1,128]{1,0:T(1,128)}, f32[1,128]{1,0:T(1,128)S(1)}, u32[]{:S(2)}, u32[]{:S(2)}) %collective-permute-start.12) | collective-permute-done | bytes 544 | tf_op jit(solution)/shard_map/collect/ppermute | solution.py:407
  95.1 0.9 fusion.4
  96.0 19.1 %all_to_all.15 = f32[32,1,128]{2,1,0:T(1,128)S(1)} all-to-all(f32[32,1,128]{2,1,0:T(1,128)S(1)} %fusion.4), channel_id=1, replica_groups=mesh['clus'=4,'trip'=32,'mode'=2] {'trip'}, dimensions={0} | all-to-all | bytes 32768 | tf_op jit(solution)/shard_map/collect/all_to_all | solution.py:413
  115.1 0.6 add_divide_fusion
  (41 shorter events, 0.2 us)
Async XLA Ops:
  0.6 7.0 %copy-start.8 = (bf16[8,90,180]{2,0,1:T(8,128)(2,1)S(1)}, bf16[8,90,180]{2,0,1:T(8,128)(2,1)}, u32[]{:S(2)}) copy-start(bf16[8,90,180]{2,0,1:T(8,128)(2,1)} %param.13) | copy-start | bytes 777604
  0.6 7.0 %copy-start.10 = (bf16[8,90]{1,0:T(8,128)(2,1)S(1)}, bf16[8,90]{1,0:T(8,128)(2,1)}, u32[]{:S(2)}) copy-start(bf16[8,90]{1,0:T(8,128)(2,1)} %param.15) | copy-start | bytes 4324
  0.7 7.0 %copy-start.11 = (bf16[8,90]{1,0:T(8,128)(2,1)S(1)}, bf16[8,90]{1,0:T(8,128)(2,1)}, u32[]{:S(2)}) copy-start(bf16[8,90]{1,0:T(8,128)(2,1)} %param.14) | copy-start | bytes 4324
  2.5 32.8 %copy-start.14 = (bf16[2,4]{1,0:T(2,128)(2,1)S(1)}, bf16[2,4]{1,0:T(2,128)(2,1)}, u32[]{:S(2)}) copy-start(bf16[2,4]{1,0:T(2,128)(2,1)} %param.12) | copy-start | bytes 52
  2.5 30.7 %collective-permute-start = (bf16[23,2,8100]{2,1,0:T(2,128)(2,1)S(1)}, bf16[23,2,8100]{2,1,0:T(2,128)(2,1)S(1)}, u32[]{:S(2)}, u32[]{:S(2)}) collective-permute-start(bf16[23,2,8100]{2,1,0:T(2,128)(2,1)S(1)} %slice.16), channel_id=1, source_target_pairs={{0,64},{64,128},{128,192},{192,0},{1,65},{65,129},{129,193},{193,1... | collective-permute-start | bytes 2235608 | tf_op jit(solution)/shard_map/force/ppermute | solution.py:329
  6.8 26.4 %collective-permute-start.1 = (bf16[22,2,8100]{2,1,0:T(2,128)(2,1)}, bf16[22,2,8100]{2,1,0:T(2,128)(2,1)}, u32[]{:S(2)}, u32[]{:S(2)}) collective-permute-start(bf16[22,2,8100]{2,1,0:T(2,128)(2,1)} %slice.17), channel_id=1, source_target_pairs={{0,192},{64,0},{128,64},{192,128},{1,193},{65,1},{129,65},{193,129... | collective-permute-start | bytes 2138408 | tf_op jit(solution)/shard_map/force/ppermute | solution.py:330
  7.6 36.5 %copy-start.15 = (s32[4]{0:T(128)S(1)}, s32[4]{0:T(128)}, u32[]{:S(2)}) copy-start(s32[4]{0:T(128)} %param.19) | copy-start | bytes 52
  10.2 23.0 %all-to-all-start = ((bf16[32,12,180]{2,1,0:T(8,128)(2,1)}), bf16[32,12,180]{2,1,0:T(8,128)(2,1)S(1)}, u32[]{:S(2)}, u32[]{:S(2)}) async-start(bf16[32,12,180]{2,1,0:T(8,128)(2,1)} %records.1), calls=%async_computation | async-start | bytes 524288 | tf_op jit(solution)/shard_map/records/all_to_all | solution.py:321
  21.4 41.4 %collective-permute-start.7 = (bf16[23,2,8100]{2,1,0:T(2,128)(2,1)S(1)}, bf16[23,2,8100]{2,1,0:T(2,128)(2,1)S(1)}, u32[]{:S(2)}, u32[]{:S(2)}) collective-permute-start(bf16[23,2,8100]{2,1,0:T(2,128)(2,1)S(1)} %slice.16), channel_id=1, source_target_pairs={{0,192},{64,0},{128,64},{192,128},{1,193},{65,1},{129,65},{193,129... | collective-permute-start | bytes 2235608 | tf_op jit(solution)/shard_map/force/ppermute | solution.py:333
  23.2 39.5 %collective-permute-start.6 = (bf16[22,2,8100]{2,1,0:T(2,128)(2,1)}, bf16[22,2,8100]{2,1,0:T(2,128)(2,1)}, u32[]{:S(2)}, u32[]{:S(2)}) collective-permute-start(bf16[22,2,8100]{2,1,0:T(2,128)(2,1)} %slice.17), channel_id=1, source_target_pairs={{0,64},{64,128},{128,192},{192,0},{1,65},{65,129},{129,193},{193,1... | collective-permute-start | bytes 2138408 | tf_op jit(solution)/shard_map/force/ppermute | solution.py:332
  33.2 2.9 %copy-start = (bf16[32,12,180]{2,1,0:T(8,128)(2,1)}, bf16[32,12,180]{2,1,0:T(8,128)(2,1)S(1)}, u32[]{:S(2)}) copy-start(bf16[32,12,180]{2,1,0:T(8,128)(2,1)S(1)} %all-to-all-done.arrived_ref) | copy-start | bytes 414724
  33.2 29.6 %copy-start.4 = (bf16[23,2,8100]{2,1,0:T(2,128)(2,1)}, bf16[23,2,8100]{2,1,0:T(2,128)(2,1)S(1)}, u32[]{:S(2)}) copy-start(bf16[23,2,8100]{2,1,0:T(2,128)(2,1)S(1)} %collective-permute-done.refs_0_) | copy-start | bytes 2235604
  33.2 36.7 %collective-permute-start.2 = (bf16[23,2,8100]{2,1,0:T(2,128)(2,1)S(1)}, bf16[23,2,8100]{2,1,0:T(2,128)(2,1)}, u32[]{:S(2)}, u32[]{:S(2)}) collective-permute-start(bf16[23,2,8100]{2,1,0:T(2,128)(2,1)S(1)} %collective-permute-done.refs_0_), channel_id=1, source_target_pairs={{0,64},{64,128},{128,192},{192,0},{1,65},{65,129},{129,193},{193,1... | collective-permute-start | bytes 2235608 | tf_op jit(solution)/shard_map/force_second/ppermute | solution.py:337
  34.8 35.2 %collective-permute-start.3 = (bf16[22,2,8100]{2,1,0:T(2,128)(2,1)}, bf16[22,2,8100]{2,1,0:T(2,128)(2,1)}, u32[]{:S(2)}, u32[]{:S(2)}) collective-permute-start(bf16[22,2,8100]{2,1,0:T(2,128)(2,1)} %collective-permute-done.1.refs_3_), channel_id=1, source_target_pairs={{0,192},{64,0},{128,64},{192,128},{1,193},{65,1},{129,65},{193,129... | collective-permute-start | bytes 2138408 | tf_op jit(solution)/shard_map/force_second/ppermute | solution.py:338
  37.8 21.9 %all-to-all-start.1 = ((bf16[8,4,16,180]{3,2,1,0:T(8,128)(2,1)}), bf16[8,4,16,180]{3,2,1,0:T(8,128)(2,1)S(1)}, u32[]{:S(2)}, u32[]{:S(2)}) async-start(bf16[8,4,16,180]{3,2,1,0:T(8,128)(2,1)} %members.1), calls=%async_computation.1 | async-start | bytes 524288 | tf_op jit(solution)/shard_map/members/all_to_all | solution.py:348
  59.6 0.7 copy-start.1
  62.7 0.9 copy-start.5
  63.6 6.8 %copy-start.9 = (s32[4]{0:T(128)S(1)}, s32[4]{0:T(128)}, u32[]{:S(2)}) copy-start(s32[4]{0:T(128)} %param.18) | copy-start | bytes 52
  69.4 2.9 %collective-permute-start.8 = (bf16[48,8100]{1,0:T(8,128)(2,1)}, bf16[48,8100]{1,0:T(8,128)(2,1)S(1)}, u32[]{:S(2)}, u32[]{:S(2)}) collective-permute-start(bf16[48,8100]{1,0:T(8,128)(2,1)} %get-tuple-element.26), channel_id=1, source_target_pairs={{0,1},{1,0},{2,3},{3,2},{4,5},{5,4},{6,7},{7,6},{8,9},{9,8},{10,11... | collective-permute-start | bytes 2332808 | tf_op jit(solution)/shard_map/contract/ppermute | solution.py:382
  69.4 3.6 %collective-permute-start.9 = (bf16[48,8100]{1,0:T(8,128)(2,1)}, bf16[48,8100]{1,0:T(8,128)(2,1)S(1)}, u32[]{:S(2)}, u32[]{:S(2)}) collective-permute-start(bf16[48,8100]{1,0:T(8,128)(2,1)} %get-tuple-element.27), channel_id=1, source_target_pairs={{0,1},{1,0},{2,3},{3,2},{4,5},{5,4},{6,7},{7,6},{8,9},{9,8},{10,11... | collective-permute-start | bytes 2332808 | tf_op jit(solution)/shard_map/contract/ppermute | solution.py:382
  69.9 5.2 %collective-permute-start.4 = (bf16[23,2,8100]{2,1,0:T(2,128)(2,1)}, bf16[23,2,8100]{2,1,0:T(2,128)(2,1)S(1)}, u32[]{:S(2)}, u32[]{:S(2)}) collective-permute-start(bf16[23,2,8100]{2,1,0:T(2,128)(2,1)} %collective-permute-done.2.refs_5_), channel_id=1, source_target_pairs={{0,1},{1,0},{2,3},{3,2},{4,5},{5,4},{6,7},{7,6},{8,9},{9,8},{10,11... | collective-permute-start | bytes 2235608 | tf_op jit(solution)/shard_map/contract/ppermute | solution.py:383
  69.9 5.2 %collective-permute-start.5 = (bf16[22,2,8100]{2,1,0:T(2,128)(2,1)}, bf16[22,2,8100]{2,1,0:T(2,128)(2,1)S(1)}, u32[]{:S(2)}, u32[]{:S(2)}) collective-permute-start(bf16[22,2,8100]{2,1,0:T(2,128)(2,1)} %collective-permute-done.3.refs_6_), channel_id=1, source_target_pairs={{0,1},{1,0},{2,3},{3,2},{4,5},{5,4},{6,7},{7,6},{8,9},{9,8},{10,11... | collective-permute-start | bytes 2138408 | tf_op jit(solution)/shard_map/contract/ppermute | solution.py:384
  72.4 2.8 %copy-start.2 = (bf16[48,8100]{1,0:T(8,128)(2,1)}, bf16[48,8100]{1,0:T(8,128)(2,1)S(1)}, u32[]{:S(2)}) copy-start(bf16[48,8100]{1,0:T(8,128)(2,1)S(1)} %collective-permute-done.8.refs_10_) | copy-start | bytes 2332804
  73.0 2.1 %copy-start.3 = (bf16[48,8100]{1,0:T(8,128)(2,1)}, bf16[48,8100]{1,0:T(8,128)(2,1)S(1)}, u32[]{:S(2)}) copy-start(bf16[48,8100]{1,0:T(8,128)(2,1)S(1)} %collective-permute-done.9.refs_11_) | copy-start | bytes 2332804
  75.1 0.9 copy-start.7
  75.2 1.1 copy-start.6
  76.3 38.8 %copy-start.12 = (f32[1,45]{1,0:T(1,128)S(1)}, f32[1,45]{1,0:T(1,128)}, u32[]{:S(2)}) copy-start(f32[1,45]{1,0:T(1,128)} %param.20) | copy-start | bytes 544
  76.3 38.8 %copy-start.13 = (f32[1,45]{1,0:T(1,128)S(1)}, f32[1,45]{1,0:T(1,128)}, u32[]{:S(2)}) copy-start(f32[1,45]{1,0:T(1,128)} %param.21) | copy-start | bytes 544
  87.1 5.6 %collective-permute-start.10 = (f32[1,128]{1,0:T(1,128)}, f32[1,128]{1,0:T(1,128)S(1)}, u32[]{:S(2)}, u32[]{:S(2)}) collective-permute-start(f32[1,128]{1,0:T(1,128)} %interaction.1), channel_id=1, source_target_pairs={{0,64},{64,128},{128,192},{192,0},{1,65},{65,129},{129,193},{193,1... | collective-permute-start | bytes 1544 | tf_op jit(solution)/shard_map/collect/ppermute | solution.py:407
  88.1 5.2 %collective-permute-start.11 = (f32[1,128]{1,0:T(1,128)}, f32[1,128]{1,0:T(1,128)S(1)}, u32[]{:S(2)}, u32[]{:S(2)}) collective-permute-start(f32[1,128]{1,0:T(1,128)} %interaction.1), channel_id=1, source_target_pairs={{0,128},{64,192},{128,0},{192,64},{1,129},{65,193},{129,1},{193,65... | collective-permute-start | bytes 1544 | tf_op jit(solution)/shard_map/collect/ppermute | solution.py:407
  91.5 3.7 %collective-permute-start.12 = (f32[1,128]{1,0:T(1,128)}, f32[1,128]{1,0:T(1,128)S(1)}, u32[]{:S(2)}, u32[]{:S(2)}) collective-permute-start(f32[1,128]{1,0:T(1,128)} %interaction.1), channel_id=1, source_target_pairs={{0,192},{64,0},{128,64},{192,128},{1,193},{65,1},{129,65},{193,129... | collective-permute-start | bytes 1544 | tf_op jit(solution)/shard_map/collect/ppermute | solution.py:407

commit v10 on v8

--- a/solution.py
+++ b/solution.py
@@ -18,19 +18,18 @@
 
 
 def send_kernel(rows_ref, share_ref, out_ref):
-    for target in range(out_ref.shape[0]):
-        out_ref[target] = share_ref[rows_ref[0, target]]
+    for z in range(RING_Z):
+        for y in range(RING_Y):
+            out_ref[z, y] = share_ref[rows_ref[0, y * RING_Z + z]]
 
 
 def pick_kernel(table_ref, arrived_ref, phase_ref, out_ref):
     for triplet in range(4):
         for member in range(3):
-            block = arrived_ref[table_ref[triplet, member]]
-            out_ref[2 * triplet, member, 0:12] = block
-            out_ref[2 * triplet + 1, member, 0:12] = block
-            fill = jnp.zeros((4, block.shape[1]), block.dtype)
-            out_ref[2 * triplet, member, 12:16] = fill
-            out_ref[2 * triplet + 1, member, 12:16] = fill
+            source = table_ref[triplet, member]
+            block = arrived_ref[source & (RING_Z - 1), source >> 3]
+            out_ref[2 * triplet, member] = block
+            out_ref[2 * triplet + 1, member] = block
         out_ref[2 * triplet, 3] = phase_ref[triplet]
         out_ref[2 * triplet + 1, 3] = phase_ref[triplet]
 
@@ -324,8 +323,8 @@
     f32, b16 = jnp.float32, jnp.bfloat16
     clus = lax.axis_index("clus")
     mode = lax.axis_index("mode")
-    trip = lax.axis_index("trip")
-    color = (trip // RING_Z + trip % RING_Z) % 2
+    color = (lax.axis_index("trip_y") + lax.axis_index("trip_z")) % 2
+    trip = ("trip_y", "trip_z")
     group = ("clus", "mode")
 
     with jax.named_scope("records"):
@@ -334,14 +333,16 @@
             [eigenvectors, extra, jnp.zeros((extra.shape[0], 5, 180), b16)], axis=1
         )
         share = lax.dynamic_slice_in_dim(record, 12 * (2 * clus + mode), 12, 1)
+        share = jnp.pad(share, ((0, 0), (0, 4), (0, 0)))
         chosen = pl.pallas_call(
             send_kernel,
-            out_shape=jax.ShapeDtypeStruct((send_rows.shape[1],) + share.shape[1:], b16),
+            out_shape=jax.ShapeDtypeStruct((RING_Z, RING_Y) + share.shape[1:], b16),
             in_specs=[SMEM, VMEM],
             out_specs=VMEM,
             compiler_params=PARAMS,
         )(send_rows, share)
-        arrived = lax.all_to_all(chosen, "trip", 0, 0, tiled=True)
+        halfway = lax.all_to_all(chosen, "trip_z", 0, 0, tiled=True)
+        arrived = lax.all_to_all(halfway, "trip_y", 1, 1, tiled=True)
         angles = phase_angle.astype(f32)
         trig = jnp.stack([jnp.cos(angles), jnp.sin(angles)], axis=1).astype(b16)
         phases = jnp.pad(trig.reshape(4, 4).T[:, None, :], ((0, 0), (0, 15), (0, 176)))
@@ -351,13 +352,6 @@
         half = lax.dynamic_slice_in_dim(own, SHARED * color, HALF, 0)
         low = lax.ppermute(half, "clus", ring(4, 1))
         high = lax.ppermute(half, "clus", ring(4, 3))
-
-    with jax.named_scope("force_second"):
-        low, high, _ = lax.optimization_barrier((low, high, arrived))
-        low_other = lax.ppermute(low, "trip", grid_shift(1, 0))
-        high_other = lax.ppermute(high, "trip", grid_shift(0, 1))
-        top = lax.ppermute(low[:TOP], "clus", ring(4, 1))
-        bottom = lax.ppermute(high[TOP:], "clus", ring(4, 3))
 
     with jax.named_scope("members"):
         picks = pl.pallas_call(
@@ -369,10 +363,16 @@
         )(trip_table, arrived, phases)
         members = lax.all_to_all(picks, group, 0, 0, tiled=True)
 
-    with jax.named_scope("force_shared"):
-        sent_top, sent_bottom, _ = lax.optimization_barrier((top, bottom, members))
-        top_other = lax.ppermute(sent_top, "trip", grid_shift(-1, 0))
-        bottom_other = lax.ppermute(sent_bottom, "trip", grid_shift(0, -1))
+    with jax.named_scope("force_second"):
+        low, high, low_top, high_rest, _ = lax.optimization_barrier(
+            (low, high, low[:TOP], high[TOP:], members)
+        )
+        top = lax.ppermute(low_top, "clus", ring(4, 1))
+        bottom = lax.ppermute(high_rest, "clus", ring(4, 3))
+        low_other = lax.ppermute(low, trip, grid_shift(1, 0))
+        high_other = lax.ppermute(high, trip, grid_shift(0, 1))
+        top_other = lax.ppermute(top, trip, grid_shift(-1, 0))
+        bottom_other = lax.ppermute(bottom, trip, grid_shift(0, -1))
 
     with jax.named_scope("operands"):
         mult = lax.dynamic_index_in_dim(multiplicity, clus, 0, keepdims=False)
@@ -437,29 +437,32 @@
         for step in range(4):
             point = lax.dynamic_index_in_dim(irreducible, (clus - step) % 4, 0, keepdims=False)
             partial = partial + jnp.where((points == point)[:, None], rows[step], 0.0)
-        received = lax.all_to_all(partial[:, None, :], "trip", 0, 0, tiled=True)
+        received = lax.all_to_all(partial[:, None, :], trip, 0, 0, tiled=True)
         final = jnp.sum(received[:, 0, :], axis=0)[None, :]
         gamma_total = final[:, 0:45] + boundary
         return gamma_total, (drive_term + final[:, PAD : PAD + 45]) / gamma_total
 
 
 def solution(mesh):
+    devices = mesh.devices.reshape(4, RING_Y, RING_Z, 2)
+    mesh = jax.sharding.Mesh(devices, ("clus", "trip_y", "trip_z", "mode"))
+    trip = ("trip_y", "trip_z")
     return jax.shard_map(
         body,
         mesh=mesh,
         in_specs=(
             P("clus", "mode", None),
-            P("clus", "trip"),
-            P("trip", None, None),
-            P("trip", None),
-            P("trip", None),
-            P("trip", None),
-            P("trip", None),
-            P("trip"),
-            P("trip"),
-            P("trip", "mode"),
-            P("trip", "mode"),
+            P("clus", trip),
+            P(trip, None, None),
+            P(trip, None),
+            P(trip, None),
+            P(trip, None),
+            P(trip, None),
+            P(trip),
+            P(trip),
+            P(trip, "mode"),
+            P(trip, "mode"),
         ),
-        out_specs=(P("trip", "mode"), P("trip", "mode")),
+        out_specs=(P(trip, "mode"), P(trip, "mode")),
         check_vma=False,
     )

time: 107 us -> 120 us (1.12)
  blocking collectives: 36.4 us -> 12.8 us
  waiting for transfers between devices: 9.29 us -> 32.8 us
  starting transfers between devices: 23 us -> 34.1 us
  local copies, waits for them, and re-layouts: 8.39 us -> 10.6 us
    all_to_all x2 -> x1, blocking collectives: 36.4 us -> 12.8 us  [body(): received = lax.all_to_all(partial[:, None, :], trip, 0, 0, tiled=True)]
    all_to_all x0 -> x2, waiting for transfers between devices: none -> 14.9 us  [the longest x1 8.99 us: body(): halfway = lax.all_to_all(chosen, 'trip_z', 0, 0, tiled=True)]
    all_to_all x0 -> x2, starting transfers between devices: none -> 13.1 us  [the longest x1 8.6 us: body(): halfway = lax.all_to_all(chosen, 'trip_z', 0, 0, tiled=True)]
    ppermute x6, waiting for transfers between devices: 0.02 us -> 10.9 us  [the longest x1 7.52 us: body(): bottom = lax.ppermute(high_rest, 'clus', ring(4, 3))]
    all_to_all x1, waiting for transfers between devices: 5.95 us -> 3.96 us  [body(): members = lax.all_to_all(picks, group, 0, 0, tiled=True)]
    all_to_all x1, starting transfers between devices: 6.27 us -> 4.83 us  [body(): members = lax.all_to_all(picks, group, 0, 0, tiled=True)]
    all_to_all x0 -> x2, local copies, waits for them, and re-layouts: none -> 1.43 us  [the longest x1 0.72 us: body(): arrived = lax.all_to_all(halfway, 'trip_y', 1, 1, tiled=True)]
    unnamed x37 -> x33, local copies, waits for them, and re-layouts: 2.31 us -> 3.39 us
  transfers between devices with their start and end apart: 19 -> 21, of which waited for: 3 -> 7; matrix products, arithmetic and copies ran while one was open for 8% -> 9% of each run, Pallas kernels for 11% -> 8%
where the time goes in v10:
time: 120 us
  starting transfers between devices  34.1 us (28%)
  waiting for transfers between devices  32.8 us (27%)
  Pallas kernels  22.3 us (19%)
  blocking collectives  12.8 us (11%)
  local copies, waits for them, and re-layouts  10.6 us (9%)
  other arithmetic  6.27 us (5%)
    all_to_all x1, blocking collectives, body(): received = lax.all_to_all(partial[:, None, :], trip, 0, 0, tiled=True)  12.8 us
    pallas_call x1, Pallas kernels, body(): pl.pallas_call(interaction_kernel, out_shape=jax.ShapeDtypeStruct((1, 128...  10.9 us
    all_to_all x1, waiting for transfers between devices, body(): halfway = lax.all_to_all(chosen, 'trip_z', 0, 0, tiled=True)  8.99 us
    all_to_all x1, starting transfers between devices, body(): halfway = lax.all_to_all(chosen, 'trip_z', 0, 0, tiled=True)  8.6 us
    ppermute x1, waiting for transfers between devices, body(): bottom = lax.ppermute(high_rest, 'clus', ring(4, 3))  7.52 us
    all_to_all x1, waiting for transfers between devices, body(): arrived = lax.all_to_all(halfway, 'trip_y', 1, 1, tiled=True)  5.87 us
    pallas_call x1, Pallas kernels, body(): pl.pallas_call(early_kernel, out_shape=(jax.ShapeDtypeStruct((WIDE, total...  5.84 us
    all_to_all x1, starting transfers between devices, body(): members = lax.all_to_all(picks, group, 0, 0, tiled=True)  4.83 us
  transfers between devices with their start and end apart: 21, of which 7 were waited for; matrix products, arithmetic and copies ran while one was open for 9% of the time, Pallas kernels for 8%

profile of v10, /device:TPU:2, one launch (start us, length us, event | category | flops | bytes accessed | tf_op | source)
XLA Modules:
  0.0 119.8 jit_solution(6282433207475466717)
XLA Ops:
  0.6 1.2 copy.36
  1.8 0.8 maximum_bitcast_fusion
  2.8 0.6 pad.8.share_ref
  3.4 1.6 %records.1 = bf16[8,4,16,180]{3,2,1,0:T(8,128)(2,1)} custom-call(s32[1,32]{1,0:T(1,128)} %rows_ref.1, bf16[8,16,180]{2,1,0:T(8,128)(2,1)} %pad.8.share_ref), custom_call_target="tpu_custom_call" | custom-call | tf_op jit(solution)/shard_map/records/pallas_call | solution.py:337
  5.0 8.6 %all-to-all-start = ((bf16[8,4,16,180]{3,2,1,0:T(8,128)(2,1)}), bf16[8,4,16,180]{3,2,1,0:T(8,128)(2,1)S(1)}, u32[]{:S(2)}, u32[]{:S(2)}) async-start(bf16[8,4,16,180]{3,2,1,0:T(8,128)(2,1)} %records.1), calls=%async_computation | async-start | bytes 524288 | tf_op jit(solution)/shard_map/records/all_to_all | solution.py:344
  13.6 0.8 dynamic-slice_bitcast_fusion
  14.4 1.6 %collective-permute-start = (bf16[23,2,8100]{2,1,0:T(2,128)(2,1)S(1)}, bf16[23,2,8100]{2,1,0:T(2,128)(2,1)S(1)}, u32[]{:S(2)}, u32[]{:S(2)}) collective-permute-start(bf16[23,2,8100]{2,1,0:T(2,128)(2,1)S(1)} %dynamic-slice_bitcast_fusion), channel_id=1, source_target_pairs={{0,64},{64,128},{128,192},{192,0},{1,65},{65,129},{129,193},{193,1... | collective-permute-start | bytes 2235608 | tf_op jit(solution)/shard_map/force/ppermute | solution.py:353
  16.0 0.5 collective-permute-start.1
  16.5 9.0 %all-to-all-done = bf16[8,4,16,180]{3,2,1,0:T(8,128)(2,1)S(1)} async-done(((bf16[8,4,16,180]{3,2,1,0:T(8,128)(2,1)}), bf16[8,4,16,180]{3,2,1,0:T(8,128)(2,1)S(1)}, u32[]{:S(2)}, u32[]{:S(2)}) %all-to-all-start) | async-done | bytes 184352 | tf_op jit(solution)/shard_map/records/all_to_all | solution.py:344
  25.5 0.7 copy.38
  26.2 4.5 %all-to-all-start.1 = ((bf16[8,4,16,180]{3,2,0,1:T(8,128)(2,1)}), bf16[8,4,16,180]{3,2,0,1:T(8,128)(2,1)S(1)}, u32[]{:S(2)}, u32[]{:S(2)}) async-start(bf16[8,4,16,180]{3,2,0,1:T(8,128)(2,1)} %copy.38), calls=%async_computation.1 | async-start | bytes 524288 | tf_op jit(solution)/shard_map/records/all_to_all | solution.py:345
  30.9 0.6 pad.9.phase_ref
  31.5 5.9 %all-to-all-done.1 = bf16[8,4,16,180]{3,2,0,1:T(8,128)(2,1)S(1)} async-done(((bf16[8,4,16,180]{3,2,0,1:T(8,128)(2,1)}), bf16[8,4,16,180]{3,2,0,1:T(8,128)(2,1)S(1)}, u32[]{:S(2)}, u32[]{:S(2)}) %all-to-all-start.1) | async-done | bytes 184352 | tf_op jit(solution)/shard_map/records/all_to_all | solution.py:345
  37.3 0.7 copy.42.arrived_ref
  38.1 1.7 %members.1 = bf16[8,4,16,180]{3,2,1,0:T(8,128)(2,1)} custom-call(s32[4,3]{1,0:T(4,128)} %table_ref.1, bf16[8,4,16,180]{3,2,1,0:T(8,128)(2,1)} %copy.42.arrived_ref, bf16[4,16,180]{2,1,0:T(8,128)(2,1)} %pad.9.phase_ref), custom_call_target="tpu_custom_call" | custom-call | tf_op jit(solution)/shard_map/members/pallas_call | solution.py:357
  39.8 4.8 %all-to-all-start.2 = ((bf16[8,4,16,180]{3,2,1,0:T(8,128)(2,1)}), bf16[8,4,16,180]{3,2,1,0:T(8,128)(2,1)S(1)}, u32[]{:S(2)}, u32[]{:S(2)}) async-start(bf16[8,4,16,180]{3,2,1,0:T(8,128)(2,1)} %members.1), calls=%async_computation.2 | async-start | bytes 524288 | tf_op jit(solution)/shard_map/members/all_to_all | solution.py:364
  44.6 1.1 slice.16
  45.7 1.0 slice.17
  46.7 4.0 %all-to-all-done.2.members_ref = bf16[8,4,16,180]{3,2,1,0:T(8,128)(2,1)S(1)} async-done(((bf16[8,4,16,180]{3,2,1,0:T(8,128)(2,1)}), bf16[8,4,16,180]{3,2,1,0:T(8,128)(2,1)S(1)}, u32[]{:S(2)}, u32[]{:S(2)}) %all-to-all-start.2) | async-done | bytes 184352 | tf_op jit(solution)/shard_map/members/all_to_all | solution.py:364
  50.7 0.6 collective-permute-start.10
  51.2 0.6 collective-permute-start.11
  51.8 1.5 %collective-permute-start.3 = (bf16[11,2,8100]{2,1,0:T(2,128)(2,1)}, bf16[11,2,8100]{2,1,0:T(2,128)(2,1)}, u32[]{:S(2)}, u32[]{:S(2)}) collective-permute-start(bf16[11,2,8100]{2,1,0:T(2,128)(2,1)} %slice.17), channel_id=1, source_target_pairs={{0,192},{64,0},{128,64},{192,128},{1,193},{65,1},{129,65},{193,129... | collective-permute-start | bytes 1069208 | tf_op jit(solution)/shard_map/force_second/ppermute | solution.py:371
  53.3 0.6 collective-permute-start.2
  53.8 7.5 %collective-permute-done.3.refs_6_ = bf16[11,2,8100]{2,1,0:T(2,128)(2,1)} collective-permute-done((bf16[11,2,8100]{2,1,0:T(2,128)(2,1)}, bf16[11,2,8100]{2,1,0:T(2,128)(2,1)}, u32[]{:S(2)}, u32[]{:S(2)}) %collective-permute-start.3) | collective-permute-done | bytes 356432 | tf_op jit(solution)/shard_map/force_second/ppermute | solution.py:371
  61.3 2.7 %collective-permute-start.5 = (bf16[11,2,8100]{2,1,0:T(2,128)(2,1)}, bf16[11,2,8100]{2,1,0:T(2,128)(2,1)}, u32[]{:S(2)}, u32[]{:S(2)}) collective-permute-start(bf16[11,2,8100]{2,1,0:T(2,128)(2,1)} %collective-permute-done.3.refs_6_), channel_id=1, source_target_pairs={{0,14},{2,0},{4,2},{6,4},{8,6},{10,8},{12,10},{14,12},{16,30},{18,... | collective-permute-start | bytes 1069208 | tf_op jit(solution)/shard_map/force_second/ppermute | solution.py:375
  64.0 2.7 %collective-permute-start.4 = (bf16[12,2,8100]{2,1,0:T(2,128)(2,1)}, bf16[12,2,8100]{2,1,0:T(2,128)(2,1)}, u32[]{:S(2)}, u32[]{:S(2)}) collective-permute-start(bf16[12,2,8100]{2,1,0:T(2,128)(2,1)} %collective-permute-done.2.refs_5_), channel_id=1, source_target_pairs={{0,48},{2,50},{4,52},{6,54},{8,56},{10,58},{12,60},{14,62},{16,0},... | collective-permute-start | bytes 1166408 | tf_op jit(solution)/shard_map/force_second/ppermute | solution.py:374
  66.7 3.4 %collective-permute-done.10.refs_1_ = bf16[23,2,8100]{2,1,0:T(2,128)(2,1)S(1)} collective-permute-done((bf16[23,2,8100]{2,1,0:T(2,128)(2,1)S(1)}, bf16[23,2,8100]{2,1,0:T(2,128)(2,1)S(1)}, u32[]{:S(2)}, u32[]{:S(2)}) %collective-permute-start.10) | collective-permute-done | bytes 745232 | tf_op jit(solution)/shard_map/force_second/ppermute | solution.py:372
  70.1 0.7 dynamic_slice.23
  70.8 1.3 %pad_add_fusion.where_ref = s32[4]{0:T(128)} fusion(s32[1]{0:T(128)} %bitcast.3, s32[1]{0:T(128)} %dynamic_slice.23, s32[1]{0:T(128)} %bitcast.2, s32[1]{0:T(128)} %bitcast.1), kind=kLoop, calls=%fused_computation.21 | loop fusion | flops 12 | bytes 32 | tf_op jit(solution)/shard_map/operands/stack | solution.py:379
  72.1 2.4 %operands.1 = (bf16[192,288]{1,0:T(8,128)(2,1)}, bf16[96,256]{1,0:T(8,128)(2,1)}, bf16[192,192]{1,0:T(8,128)(2,1)}, bf16[256,256]{1,0:T(8,128)(2,1)}, f32[4,96,128]{2,1,0:T(8,128)}, /*index=5*/f32[2,48,128]{2,1,0:T(8,128)}) custom-call(s32[4]{0:T(128)} %pad_add_fusion.where_ref, bf16[8,4,16,180]{3,2,1,0:T(8,128)(2,1)} %copy-done.3), custom_call_target="tpu_custom_call" | custom-call | tf_op jit(solution)/shard_map/operands/pallas_call | solution.py:380
  74.5 0.8 copy-done.5
  75.4 5.8 %contract.1 = (bf16[96,8100]{1,0:T(8,128)(2,1)}, bf16[32,8100]{1,0:T(8,128)(2,1)}, bf16[32,8100]{1,0:T(8,128)(2,1)}, bf16[32,8100]{1,0:T(8,128)(2,1)}) custom-call(bf16[192,288]{1,0:T(8,128)(2,1)} %get-tuple-element.23.lead_ref, bf16[45,2,8100]{2,1,0:T(2,128)(2,1)} %bitcast.27, bf16[23,2,8100]{2,1,0:T(2,128)(2,1)} %copy-done.1, ...), custom_call_target="tpu_custom_call" | custom-call | flops 895795200 | bytes 9720000 | tf_op jit(solution)/shard_map/contract/pallas_call | solution.py:398
  81.2 0.4 collective-permute-start.12
  81.7 0.4 collective-permute-start.14
  82.3 0.4 collective-permute-start.9
  82.7 0.7 fusion.9
  83.4 1.3 %iota_compare_fusion.2 = (pred[32]{0:T(512)(128)(4,1)S(1)}, pred[32]{0:T(512)(128)(4,1)S(1)}) fusion(s32[]{:T(128)} %bitcast.13, s32[]{:T(128)} %bitcast), kind=kLoop, calls=%fused_computation.26 | loop fusion | flops 64 | bytes 72 | tf_op jit(solution)/shard_map/collect/eq | solution.py:439
  84.7 1.3 %collective-permute-done.9.refs_12_ = bf16[11,2,8100]{2,1,0:T(2,128)(2,1)S(1)} collective-permute-done((bf16[11,2,8100]{2,1,0:T(2,128)(2,1)}, bf16[11,2,8100]{2,1,0:T(2,128)(2,1)S(1)}, u32[]{:S(2)}, u32[]{:S(2)}) %collective-permute-start.9) | collective-permute-done | bytes 356432 | tf_op jit(solution)/shard_map/contract/ppermute | solution.py:411
  86.0 0.7 copy-done.10
  87.4 10.9 %interaction.1 = f32[1,128]{1,0:T(1,128)} custom-call(f32[2,48,128]{2,1,0:T(8,128)} %get-tuple-element.16.refs_0_, bf16[192,192]{1,0:T(8,128)(2,1)} %get-tuple-element.17.refs_1_, bf16[256,256]{1,0:T(8,128)(2,1)} %get-tuple-element.18.refs_2_, f32[4,96,128]{2,1,0:T(8,128)} %get-tuple-element.19.refs_3_, bf16[96,256]{1,0:T(8,128)(2,1)} %get-tuple-element.20.refs_4_, ...), custom_call_target="tpu_custom_call" | custom-call | tf_op jit(solution)/shard_map/interaction/pallas_call | solution.py:415
  98.2 0.3 collective-permute-start.15
  98.5 3.3 %collective-permute-start.16 = (f32[1,128]{1,0:T(1,128)}, f32[1,128]{1,0:T(1,128)S(1)}, u32[]{:S(2)}, u32[]{:S(2)}) collective-permute-start(f32[1,128]{1,0:T(1,128)} %interaction.1), channel_id=1, source_target_pairs={{0,128},{64,192},{128,0},{192,64},{1,129},{65,193},{129,1},{193,65... | collective-permute-start | bytes 1544 | tf_op jit(solution)/shard_map/collect/ppermute | solution.py:434
  101.9 0.6 collective-permute-start.17
  102.4 1.3 %iota_compare_fusion = (pred[32]{0:T(512)(128)(4,1)S(1)}, pred[32]{0:T(512)(128)(4,1)S(1)}) fusion(s32[]{:T(128)} %bitcast.17, s32[]{:T(128)} %bitcast.15), kind=kLoop, calls=%fused_computation.24 | loop fusion | flops 64 | bytes 72 | tf_op jit(solution)/shard_map/collect/eq | solution.py:439
  103.8 1.8 %collective-permute-done.17 = f32[1,128]{1,0:T(1,128)S(1)} collective-permute-done((f32[1,128]{1,0:T(1,128)}, f32[1,128]{1,0:T(1,128)S(1)}, u32[]{:S(2)}, u32[]{:S(2)}) %collective-permute-start.17) | collective-permute-done | bytes 544 | tf_op jit(solution)/shard_map/collect/ppermute | solution.py:434
  105.5 0.9 fusion.4
  106.4 12.8 %all_to_all.20 = f32[32,1,128]{2,1,0:T(1,128)S(1)} all-to-all(f32[32,1,128]{2,1,0:T(1,128)S(1)} %fusion.4), channel_id=1, replica_groups=mesh['clus'=4,'trip_y'=4,'trip_z'=8,'mode'=2] {'trip_y','trip_z'}, dimensions={0} | all-to-all | bytes 32768 | tf_op jit(solution)/shard_map/collect/all_to_all | solution.py:440
  119.2 0.6 add_divide_fusion
  (57 shorter events, 1.3 us)
Async XLA Ops:
  0.6 13.0 %copy-start = (bf16[2,45,8100]{2,0,1:T(2,128)(2,1)S(1)}, bf16[2,45,8100]{2,0,1:T(2,128)(2,1)}, u32[]{:S(2)}) copy-start(bf16[2,45,8100]{2,0,1:T(2,128)(2,1)} %param.11) | copy-start | bytes 4374004
  5.0 25.7 %copy-start.14 = (bf16[2,4]{1,0:T(2,128)(2,1)S(1)}, bf16[2,4]{1,0:T(2,128)(2,1)}, u32[]{:S(2)}) copy-start(bf16[2,4]{1,0:T(2,128)(2,1)} %param.12) | copy-start | bytes 52
  5.0 20.5 %all-to-all-start = ((bf16[8,4,16,180]{3,2,1,0:T(8,128)(2,1)}), bf16[8,4,16,180]{3,2,1,0:T(8,128)(2,1)S(1)}, u32[]{:S(2)}, u32[]{:S(2)}) async-start(bf16[8,4,16,180]{3,2,1,0:T(8,128)(2,1)} %records.1), calls=%async_computation | async-start | bytes 524288 | tf_op jit(solution)/shard_map/records/all_to_all | solution.py:344
  14.4 30.2 %collective-permute-start = (bf16[23,2,8100]{2,1,0:T(2,128)(2,1)S(1)}, bf16[23,2,8100]{2,1,0:T(2,128)(2,1)S(1)}, u32[]{:S(2)}, u32[]{:S(2)}) collective-permute-start(bf16[23,2,8100]{2,1,0:T(2,128)(2,1)S(1)} %dynamic-slice_bitcast_fusion), channel_id=1, source_target_pairs={{0,64},{64,128},{128,192},{192,0},{1,65},{65,129},{129,193},{193,1... | collective-permute-start | bytes 2235608 | tf_op jit(solution)/shard_map/force/ppermute | solution.py:353
  16.0 29.7 %collective-permute-start.1 = (bf16[23,2,8100]{2,1,0:T(2,128)(2,1)S(1)}, bf16[23,2,8100]{2,1,0:T(2,128)(2,1)S(1)}, u32[]{:S(2)}, u32[]{:S(2)}) collective-permute-start(bf16[23,2,8100]{2,1,0:T(2,128)(2,1)S(1)} %dynamic-slice_bitcast_fusion), channel_id=1, source_target_pairs={{0,192},{64,0},{128,64},{192,128},{1,193},{65,1},{129,65},{193,129... | collective-permute-start | bytes 2235608 | tf_op jit(solution)/shard_map/force/ppermute | solution.py:354
  26.2 11.1 %all-to-all-start.1 = ((bf16[8,4,16,180]{3,2,0,1:T(8,128)(2,1)}), bf16[8,4,16,180]{3,2,0,1:T(8,128)(2,1)S(1)}, u32[]{:S(2)}, u32[]{:S(2)}) async-start(bf16[8,4,16,180]{3,2,0,1:T(8,128)(2,1)} %copy.38), calls=%async_computation.1 | async-start | bytes 524288 | tf_op jit(solution)/shard_map/records/all_to_all | solution.py:345
  31.5 38.6 %copy-start.15 = (s32[4]{0:T(128)S(1)}, s32[4]{0:T(128)}, u32[]{:S(2)}) copy-start(s32[4]{0:T(128)} %param.19) | copy-start | bytes 52
  39.8 10.9 %all-to-all-start.2 = ((bf16[8,4,16,180]{3,2,1,0:T(8,128)(2,1)}), bf16[8,4,16,180]{3,2,1,0:T(8,128)(2,1)S(1)}, u32[]{:S(2)}, u32[]{:S(2)}) async-start(bf16[8,4,16,180]{3,2,1,0:T(8,128)(2,1)} %members.1), calls=%async_computation.2 | async-start | bytes 524288 | tf_op jit(solution)/shard_map/members/all_to_all | solution.py:364
  44.6 29.9 %copy-start.1 = (bf16[23,2,8100]{2,1,0:T(2,128)(2,1)}, bf16[23,2,8100]{2,1,0:T(2,128)(2,1)S(1)}, u32[]{:S(2)}) copy-start(bf16[23,2,8100]{2,1,0:T(2,128)(2,1)S(1)} %collective-permute-done.refs_0_) | copy-start | bytes 2235604
  45.7 28.9 %copy-start.2 = (bf16[23,2,8100]{2,1,0:T(2,128)(2,1)}, bf16[23,2,8100]{2,1,0:T(2,128)(2,1)S(1)}, u32[]{:S(2)}) copy-start(bf16[23,2,8100]{2,1,0:T(2,128)(2,1)S(1)} %collective-permute-done.1.refs_2_) | copy-start | bytes 2235604
  50.7 21.4 %copy-start.3 = (bf16[8,4,16,180]{3,2,1,0:T(8,128)(2,1)}, bf16[8,4,16,180]{3,2,1,0:T(8,128)(2,1)S(1)}, u32[]{:S(2)}) copy-start(bf16[8,4,16,180]{3,2,1,0:T(8,128)(2,1)S(1)} %all-to-all-done.2.members_ref) | copy-start | bytes 552964
  50.7 19.4 %collective-permute-start.10 = (bf16[23,2,8100]{2,1,0:T(2,128)(2,1)S(1)}, bf16[23,2,8100]{2,1,0:T(2,128)(2,1)S(1)}, u32[]{:S(2)}, u32[]{:S(2)}) collective-permute-start(bf16[23,2,8100]{2,1,0:T(2,128)(2,1)S(1)} %collective-permute-done.refs_0_), channel_id=1, source_target_pairs={{0,16},{2,18},{4,20},{6,22},{8,24},{10,26},{12,28},{14,30},{16,32}... | collective-permute-start | bytes 2235608 | tf_op jit(solution)/shard_map/force_second/ppermute | solution.py:372
  51.2 23.3 %collective-permute-start.11 = (bf16[23,2,8100]{2,1,0:T(2,128)(2,1)S(1)}, bf16[23,2,8100]{2,1,0:T(2,128)(2,1)S(1)}, u32[]{:S(2)}, u32[]{:S(2)}) collective-permute-start(bf16[23,2,8100]{2,1,0:T(2,128)(2,1)S(1)} %collective-permute-done.1.refs_2_), channel_id=1, source_target_pairs={{0,2},{2,4},{4,6},{6,8},{8,10},{10,12},{12,14},{14,0},{16,18},{18,... | collective-permute-start | bytes 2235608 | tf_op jit(solution)/shard_map/force_second/ppermute | solution.py:373
  51.8 9.5 %collective-permute-start.3 = (bf16[11,2,8100]{2,1,0:T(2,128)(2,1)}, bf16[11,2,8100]{2,1,0:T(2,128)(2,1)}, u32[]{:S(2)}, u32[]{:S(2)}) collective-permute-start(bf16[11,2,8100]{2,1,0:T(2,128)(2,1)} %slice.17), channel_id=1, source_target_pairs={{0,192},{64,0},{128,64},{192,128},{1,193},{65,1},{129,65},{193,129... | collective-permute-start | bytes 1069208 | tf_op jit(solution)/shard_map/force_second/ppermute | solution.py:371
  53.3 10.8 %collective-permute-start.2 = (bf16[12,2,8100]{2,1,0:T(2,128)(2,1)}, bf16[12,2,8100]{2,1,0:T(2,128)(2,1)}, u32[]{:S(2)}, u32[]{:S(2)}) collective-permute-start(bf16[12,2,8100]{2,1,0:T(2,128)(2,1)} %slice.16), channel_id=1, source_target_pairs={{0,64},{64,128},{128,192},{192,0},{1,65},{65,129},{129,193},{193,1... | collective-permute-start | bytes 1166408 | tf_op jit(solution)/shard_map/force_second/ppermute | solution.py:370
  61.3 20.3 %collective-permute-start.5 = (bf16[11,2,8100]{2,1,0:T(2,128)(2,1)}, bf16[11,2,8100]{2,1,0:T(2,128)(2,1)}, u32[]{:S(2)}, u32[]{:S(2)}) collective-permute-start(bf16[11,2,8100]{2,1,0:T(2,128)(2,1)} %collective-permute-done.3.refs_6_), channel_id=1, source_target_pairs={{0,14},{2,0},{4,2},{6,4},{8,6},{10,8},{12,10},{14,12},{16,30},{18,... | collective-permute-start | bytes 1069208 | tf_op jit(solution)/shard_map/force_second/ppermute | solution.py:375
  64.0 17.7 %collective-permute-start.7 = (bf16[11,2,8100]{2,1,0:T(2,128)(2,1)}, bf16[11,2,8100]{2,1,0:T(2,128)(2,1)}, u32[]{:S(2)}, u32[]{:S(2)}) collective-permute-start(bf16[11,2,8100]{2,1,0:T(2,128)(2,1)} %collective-permute-done.3.refs_6_), channel_id=1, source_target_pairs={{0,1},{1,0},{2,3},{3,2},{4,5},{5,4},{6,7},{7,6},{8,9},{9,8},{10,11... | collective-permute-start | bytes 1069208 | tf_op jit(solution)/shard_map/contract/ppermute | solution.py:411
  64.0 18.1 %collective-permute-start.4 = (bf16[12,2,8100]{2,1,0:T(2,128)(2,1)}, bf16[12,2,8100]{2,1,0:T(2,128)(2,1)}, u32[]{:S(2)}, u32[]{:S(2)}) collective-permute-start(bf16[12,2,8100]{2,1,0:T(2,128)(2,1)} %collective-permute-done.2.refs_5_), channel_id=1, source_target_pairs={{0,48},{2,50},{4,52},{6,54},{8,56},{10,58},{12,60},{14,62},{16,0},... | collective-permute-start | bytes 1166408 | tf_op jit(solution)/shard_map/force_second/ppermute | solution.py:374
  70.1 4.4 %copy-start.4 = (bf16[23,2,8100]{2,1,0:T(2,128)(2,1)}, bf16[23,2,8100]{2,1,0:T(2,128)(2,1)S(1)}, u32[]{:S(2)}) copy-start(bf16[23,2,8100]{2,1,0:T(2,128)(2,1)S(1)} %collective-permute-done.10.refs_1_) | copy-start | bytes 2235604
  70.1 12.2 %collective-permute-start.6 = (bf16[12,2,8100]{2,1,0:T(2,128)(2,1)}, bf16[12,2,8100]{2,1,0:T(2,128)(2,1)}, u32[]{:S(2)}, u32[]{:S(2)}) collective-permute-start(bf16[12,2,8100]{2,1,0:T(2,128)(2,1)} %collective-permute-done.2.refs_5_), channel_id=1, source_target_pairs={{0,1},{1,0},{2,3},{3,2},{4,5},{5,4},{6,7},{7,6},{8,9},{9,8},{10,11... | collective-permute-start | bytes 1166408 | tf_op jit(solution)/shard_map/contract/ppermute | solution.py:411
  74.5 0.9 copy-start.5
  75.4 7.3 %copy-start.11 = (s32[4]{0:T(128)S(1)}, s32[4]{0:T(128)}, u32[]{:S(2)}) copy-start(s32[4]{0:T(128)} %param.18) | copy-start | bytes 52
  81.2 4.8 %collective-permute-start.12 = (bf16[32,8100]{1,0:T(8,128)(2,1)}, bf16[32,8100]{1,0:T(8,128)(2,1)S(1)}, u32[]{:S(2)}, u32[]{:S(2)}) collective-permute-start(bf16[32,8100]{1,0:T(8,128)(2,1)} %get-tuple-element.27), channel_id=1, source_target_pairs={{0,1},{1,0},{2,3},{3,2},{4,5},{5,4},{6,7},{7,6},{8,9},{9,8},{10,11... | collective-permute-start | bytes 1555208 | tf_op jit(solution)/shard_map/contract/ppermute | solution.py:409
  81.6 4.3 %collective-permute-start.13 = (bf16[32,8100]{1,0:T(8,128)(2,1)}, bf16[32,8100]{1,0:T(8,128)(2,1)S(1)}, u32[]{:S(2)}, u32[]{:S(2)}) collective-permute-start(bf16[32,8100]{1,0:T(8,128)(2,1)} %get-tuple-element.28), channel_id=1, source_target_pairs={{0,1},{1,0},{2,3},{3,2},{4,5},{5,4},{6,7},{7,6},{8,9},{9,8},{10,11... | collective-permute-start | bytes 1555208 | tf_op jit(solution)/shard_map/contract/ppermute | solution.py:409
  81.7 4.3 %collective-permute-start.14 = (bf16[32,8100]{1,0:T(8,128)(2,1)}, bf16[32,8100]{1,0:T(8,128)(2,1)S(1)}, u32[]{:S(2)}, u32[]{:S(2)}) collective-permute-start(bf16[32,8100]{1,0:T(8,128)(2,1)} %get-tuple-element.29), channel_id=1, source_target_pairs={{0,1},{1,0},{2,3},{3,2},{4,5},{5,4},{6,7},{7,6},{8,9},{9,8},{10,11... | collective-permute-start | bytes 1555208 | tf_op jit(solution)/shard_map/contract/ppermute | solution.py:409
  82.2 3.8 %collective-permute-start.8 = (bf16[12,2,8100]{2,1,0:T(2,128)(2,1)}, bf16[12,2,8100]{2,1,0:T(2,128)(2,1)S(1)}, u32[]{:S(2)}, u32[]{:S(2)}) collective-permute-start(bf16[12,2,8100]{2,1,0:T(2,128)(2,1)} %collective-permute-done.4.refs_7_), channel_id=1, source_target_pairs={{0,1},{1,0},{2,3},{3,2},{4,5},{5,4},{6,7},{7,6},{8,9},{9,8},{10,11... | collective-permute-start | bytes 1166408 | tf_op jit(solution)/shard_map/contract/ppermute | solution.py:411
  82.3 3.7 %collective-permute-start.9 = (bf16[11,2,8100]{2,1,0:T(2,128)(2,1)}, bf16[11,2,8100]{2,1,0:T(2,128)(2,1)S(1)}, u32[]{:S(2)}, u32[]{:S(2)}) collective-permute-start(bf16[11,2,8100]{2,1,0:T(2,128)(2,1)} %collective-permute-done.5.refs_8_), channel_id=1, source_target_pairs={{0,1},{1,0},{2,3},{3,2},{4,5},{5,4},{6,7},{7,6},{8,9},{9,8},{10,11... | collective-permute-start | bytes 1069208 | tf_op jit(solution)/shard_map/contract/ppermute | solution.py:411
  86.0 0.7 copy-start.10
  86.0 0.9 copy-start.9
  86.0 1.0 copy-start.6
  86.0 1.2 copy-start.7
  86.0 1.3 %copy-start.8 = (bf16[32,8100]{1,0:T(8,128)(2,1)}, bf16[32,8100]{1,0:T(8,128)(2,1)S(1)}, u32[]{:S(2)}) copy-start(bf16[32,8100]{1,0:T(8,128)(2,1)S(1)} %collective-permute-done.14.refs_16_) | copy-start | bytes 1555204
  87.4 31.8 %copy-start.12 = (f32[1,45]{1,0:T(1,128)S(1)}, f32[1,45]{1,0:T(1,128)}, u32[]{:S(2)}) copy-start(f32[1,45]{1,0:T(1,128)} %param.20) | copy-start | bytes 544
  87.4 31.8 %copy-start.13 = (f32[1,45]{1,0:T(1,128)S(1)}, f32[1,45]{1,0:T(1,128)}, u32[]{:S(2)}) copy-start(f32[1,45]{1,0:T(1,128)} %param.21) | copy-start | bytes 544
  98.2 5.5 %collective-permute-start.15 = (f32[1,128]{1,0:T(1,128)}, f32[1,128]{1,0:T(1,128)S(1)}, u32[]{:S(2)}, u32[]{:S(2)}) collective-permute-start(f32[1,128]{1,0:T(1,128)} %interaction.1), channel_id=1, source_target_pairs={{0,64},{64,128},{128,192},{192,0},{1,65},{65,129},{129,193},{193,1... | collective-permute-start | bytes 1544 | tf_op jit(solution)/shard_map/collect/ppermute | solution.py:434
  98.5 5.2 %collective-permute-start.16 = (f32[1,128]{1,0:T(1,128)}, f32[1,128]{1,0:T(1,128)S(1)}, u32[]{:S(2)}, u32[]{:S(2)}) collective-permute-start(f32[1,128]{1,0:T(1,128)} %interaction.1), channel_id=1, source_target_pairs={{0,128},{64,192},{128,0},{192,64},{1,129},{65,193},{129,1},{193,65... | collective-permute-start | bytes 1544 | tf_op jit(solution)/shard_map/collect/ppermute | solution.py:434
  101.9 3.7 %collective-permute-start.17 = (f32[1,128]{1,0:T(1,128)}, f32[1,128]{1,0:T(1,128)S(1)}, u32[]{:S(2)}, u32[]{:S(2)}) collective-permute-start(f32[1,128]{1,0:T(1,128)} %interaction.1), channel_id=1, source_target_pairs={{0,192},{64,0},{128,64},{192,128},{1,193},{65,1},{129,65},{193,129... | collective-permute-start | bytes 1544 | tf_op jit(solution)/shard_map/collect/ppermute | solution.py:434

commit v11 on v6

--- a/solution.py
+++ b/solution.py
@@ -141,12 +141,12 @@
         )
         mine_ref[:, cols] = product[0:WIDE].astype(mine_ref.dtype)
         for i, far_ref in enumerate(far_refs):
-            rows = product[WIDE + 24 * i : WIDE + 24 * i + 24]
+            rows = product[WIDE + 48 * i : WIDE + 48 * i + 48]
             far_ref[:, cols] = rows.astype(far_ref.dtype)
 
 
 def interaction_kernel(*refs):
-    count = 14
+    count = 12
     operands, out_ref, buffers = refs[:count], refs[count], refs[count + 1 : 2 * count + 1]
     flat, windows, mid_real, mid_imag, rate_acc, couple_acc, done = refs[2 * count + 1 :]
     scalars_ref, middle_ref, last_ref, tables_ref, late_ref = buffers[:5]
@@ -224,8 +224,8 @@
 
     scaled = 0.5 / (smearing * smearing)
     def two_modes(s):
-        low = pl.ds(pl.multiple_of(s * WIDE, WIDE), WIDE)
-        high = pl.ds(pl.multiple_of(s * WIDE + WIDE, WIDE), WIDE)
+        low = pl.ds(s * WIDE, WIDE)
+        high = pl.ds(s * WIDE + WIDE, WIDE)
         operand = jnp.concatenate(
             [
                 jnp.concatenate([ref[low, :], ref[high, :]], axis=1).astype(jnp.bfloat16)
@@ -244,15 +244,13 @@
                 jnp.exp(-scaled * decays * decays) + jnp.exp(-scaled * merges * merges)
             )
             weight = weight * tables_ref[2] * scalars_ref[1, pl.ds(s + i, 1), :]
-            at = pl.ds(pl.multiple_of((s + i) * 8, 8), 8)
+            at = pl.ds((s + i) * 8, 8)
             rate_acc[at, :] = jnp.sum(weight.reshape(WIDE // 8, 8, 128), axis=0)
             weight = weight * tables_ref[3]
             couple_acc[at, :] = jnp.sum(weight.reshape(WIDE // 8, 8, 128), axis=0)
 
-    @pl.loop(0, 12)
-    def _(i):
-        two_modes(4 * i)
-        two_modes(4 * i + 2)
+    for i in range(24):
+        two_modes(2 * i)
 
     sums = jnp.concatenate(
         [
@@ -360,9 +358,9 @@
         mine, *far = pl.pallas_call(
             early_kernel,
             out_shape=(jax.ShapeDtypeStruct((WIDE, total), b16),)
-            + (jax.ShapeDtypeStruct((WIDE // 4, total), b16),) * 4,
+            + (jax.ShapeDtypeStruct((WIDE // 2, total), b16),) * 2,
             in_specs=[VMEM] * 4,
-            out_specs=(VMEM,) * 5,
+            out_specs=(VMEM,) * 3,
             compiler_params=PARAMS,
             cost_estimate=pl.CostEstimate(
                 flops=2 * 192 * 288 * total, bytes_accessed=1200 * total, transcendentals=0

time: 107 us -> 104 us (0.972)
  waiting for transfers between devices: 24.1 us -> 22.7 us
  Pallas kernels: 23.3 us -> 22.2 us
    ppermute x4 -> x2, waiting for transfers between devices: 2.02 us -> 0.01 us  [body(): other = [lax.ppermute(rows, 'mode', swap) for rows in far]]
    ppermute x1, waiting for transfers between devices: 0.01 us -> 1.12 us  [body(): far_bottom = lax.ppermute(bottom, 'mode', swap)]
    pallas_call x1, Pallas kernels: 11.9 us -> 10.8 us  [body(): pl.pallas_call(interaction_kernel, out_shape=jax.ShapeDtypeStruct((1, 128...]
    unnamed x29 -> x27, local copies, waits for them, and re-layouts: 2.88 us -> 2.65 us
  transfers between devices with their start and end apart: 15 -> 13, of which waited for: 7 -> 5; matrix products, arithmetic and copies ran while one was open for 11% -> 11% of each run, Pallas kernels for 11% -> 11%
where the time goes in v11:
time: 104 us
  starting transfers between devices  27.2 us (26%)
  waiting for transfers between devices  22.7 us (22%)
  Pallas kernels  22.2 us (21%)
  blocking collectives  16.3 us (16%)
  local copies, waits for them, and re-layouts  7.83 us (8%)
  other arithmetic  6.69 us (6%)
    all_to_all x1, blocking collectives, body(): received = lax.all_to_all(partial[:, None, :], 'trip', 0, 0, tiled=True)  16.3 us
    all_to_all x1, starting transfers between devices, body(): arrived = lax.all_to_all(chosen, 'trip', 0, 0, tiled=True)  11.1 us
    all_to_all x1, waiting for transfers between devices, body(): arrived = lax.all_to_all(chosen, 'trip', 0, 0, tiled=True)  11 us
    pallas_call x1, Pallas kernels, body(): pl.pallas_call(interaction_kernel, out_shape=jax.ShapeDtypeStruct((1, 128...  10.8 us
    ppermute x1, waiting for transfers between devices, body(): top = lax.ppermute(low_top, 'clus', ring(4, 1))  5.89 us
    pallas_call x1, Pallas kernels, body(): pl.pallas_call(early_kernel, out_shape=(jax.ShapeDtypeStruct((WIDE, total...  5.8 us
    ppermute x3, starting transfers between devices, body(): lax.ppermute(own_row, 'clus', ring(4, step))  5.48 us
    all_to_all x1, starting transfers between devices, body(): members = lax.all_to_all(picks, group, 0, 0, tiled=True)  5.06 us
  transfers between devices with their start and end apart: 13, of which 5 were waited for; matrix products, arithmetic and copies ran while one was open for 11% of the time, Pallas kernels for 11%

profile of v11, /device:TPU:2, one launch (start us, length us, event | category | flops | bytes accessed | tf_op | source)
XLA Modules:
  0.0 103.8 jit_solution(535302992758746871)
XLA Ops:
  0.6 1.6 %collective-permute-start = (bf16[45,2,8100]{2,1,0:T(2,128)(2,1)}, bf16[45,2,8100]{2,1,0:T(2,128)(2,1)S(1)}, u32[]{:S(2)}, u32[]{:S(2)}) collective-permute-start(bf16[45,2,8100]{2,1,0:T(2,128)(2,1)} %bitcast.24), channel_id=1, source_target_pairs={{0,64},{64,128},{128,192},{192,0},{1,65},{65,129},{129,193},{193,1... | collective-permute-start | bytes 4374008 | tf_op jit(solution)/shard_map/force/ppermute | solution.py:319
  2.2 0.9 collective-permute-start.1
  3.1 1.1 %copy.27 = bf16[8,90,180]{2,1,0:T(8,128)(2,1)S(1)} copy(bf16[8,90,180]{2,0,1:T(8,128)(2,1)} %param.13) | data formatting | bytes 518400 | tf_op args[2]
  4.1 0.8 maximum_bitcast_fusion
  4.9 0.1 pad_dynamic-slice_fusion.2
  5.0 0.7 fusion.1.share_ref
  5.7 1.6 %records.1 = bf16[32,12,180]{2,1,0:T(8,128)(2,1)} custom-call(s32[1,32]{1,0:T(1,128)} %rows_ref.1, bf16[8,12,180]{2,1,0:T(8,128)(2,1)} %fusion.1.share_ref), custom_call_target="tpu_custom_call" | custom-call | tf_op jit(solution)/shard_map/records/pallas_call | solution.py:305
  7.3 11.1 %all-to-all-start = ((bf16[32,12,180]{2,1,0:T(8,128)(2,1)}), bf16[32,12,180]{2,1,0:T(8,128)(2,1)S(1)}, u32[]{:S(2)}, u32[]{:S(2)}) async-start(bf16[32,12,180]{2,1,0:T(8,128)(2,1)} %records.1), calls=%async_computation | async-start | bytes 524288 | tf_op jit(solution)/shard_map/records/all_to_all | solution.py:312
  18.6 0.1 copy.31
  18.7 0.6 pad.4.phase_ref
  19.3 11.0 %all-to-all-done.arrived_ref = bf16[32,12,180]{2,1,0:T(8,128)(2,1)S(1)} async-done(((bf16[32,12,180]{2,1,0:T(8,128)(2,1)}), bf16[32,12,180]{2,1,0:T(8,128)(2,1)S(1)}, u32[]{:S(2)}, u32[]{:S(2)}) %all-to-all-start) | async-done | bytes 138272 | tf_op jit(solution)/shard_map/records/all_to_all | solution.py:312
  30.3 0.7 copy-done.3
  30.9 1.7 %members.1 = bf16[8,4,16,180]{3,2,1,0:T(8,128)(2,1)} custom-call(s32[4,3]{1,0:T(4,128)} %table_ref.1, bf16[32,12,180]{2,1,0:T(8,128)(2,1)} %copy-done.3, bf16[4,16,180]{2,1,0:T(8,128)(2,1)} %pad.4.phase_ref), custom_call_target="tpu_custom_call" | custom-call | tf_op jit(solution)/shard_map/members/pallas_call | solution.py:323
  32.6 5.1 %all-to-all-start.1 = ((bf16[8,4,16,180]{3,2,1,0:T(8,128)(2,1)}), bf16[8,4,16,180]{3,2,1,0:T(8,128)(2,1)S(1)}, u32[]{:S(2)}, u32[]{:S(2)}) async-start(bf16[8,4,16,180]{3,2,1,0:T(8,128)(2,1)} %members.1), calls=%async_computation.1 | async-start | bytes 524288 | tf_op jit(solution)/shard_map/members/all_to_all | solution.py:330
  37.7 0.0 collective-permute-done.low_ref
  37.7 1.6 %slice.16 = bf16[23,2,8100]{2,1,0:T(2,128)(2,1)} slice(bf16[45,2,8100]{2,1,0:T(2,128)(2,1)S(1)} %collective-permute-done.low_ref), slice={[0:23], [0:2], [0:8100]} | slice | bytes 1490400 | tf_op jit(solution)/shard_map/force_second/slice | solution.py:333
  39.3 0.0 collective-permute-done.1.high_ref
  39.3 1.6 %slice.17 = bf16[22,2,8100]{2,1,0:T(2,128)(2,1)} slice(bf16[45,2,8100]{2,1,0:T(2,128)(2,1)S(1)} %collective-permute-done.1.high_ref), slice={[23:45], [0:2], [0:8100]} | slice | bytes 1425600 | tf_op jit(solution)/shard_map/force_second/slice | solution.py:333
  40.9 3.0 %all-to-all-done.1.members_ref = bf16[8,4,16,180]{3,2,1,0:T(8,128)(2,1)S(1)} async-done(((bf16[8,4,16,180]{3,2,1,0:T(8,128)(2,1)}), bf16[8,4,16,180]{3,2,1,0:T(8,128)(2,1)S(1)}, u32[]{:S(2)}, u32[]{:S(2)}) %all-to-all-start.1) | async-done | bytes 184352 | tf_op jit(solution)/shard_map/members/all_to_all | solution.py:330
  43.8 0.0 collective-permute-start.2
  43.8 2.0 %collective-permute-start.3 = (bf16[22,2,8100]{2,1,0:T(2,128)(2,1)}, bf16[22,2,8100]{2,1,0:T(2,128)(2,1)}, u32[]{:S(2)}, u32[]{:S(2)}) collective-permute-start(bf16[22,2,8100]{2,1,0:T(2,128)(2,1)} %slice.17), channel_id=1, source_target_pairs={{0,192},{64,0},{128,64},{192,128},{1,193},{65,1},{129,65},{193,129... | collective-permute-start | bytes 2138408 | tf_op jit(solution)/shard_map/force_second/ppermute | solution.py:335
  45.8 0.6 dynamic_slice.20
  46.4 1.2 %pad_add_fusion.where_ref = s32[3]{0:T(128)} fusion(s32[1]{0:T(128)} %dynamic_slice.20, s32[1]{0:T(128)} %bitcast.2, s32[1]{0:T(128)} %bitcast.1), kind=kLoop, calls=%fused_computation.20 | loop fusion | flops 6 | bytes 24 | tf_op jit(solution)/shard_map/operands/stack | solution.py:339
  47.6 2.4 %operands.1 = (bf16[192,288]{1,0:T(8,128)(2,1)}, bf16[96,192]{1,0:T(8,128)(2,1)}, bf16[192,192]{1,0:T(8,128)(2,1)}, bf16[256,256]{1,0:T(8,128)(2,1)}, f32[4,96,128]{2,1,0:T(8,128)}, /*index=5*/f32[2,48,128]{2,1,0:T(8,128)}) custom-call(s32[3]{0:T(128)} %pad_add_fusion.where_ref, bf16[8,4,16,180]{3,2,1,0:T(8,128)(2,1)} %copy-done.2), custom_call_target="tpu_custom_call" | custom-call | tf_op jit(solution)/shard_map/operands/pallas_call | solution.py:340
  50.0 5.8 %contract.1 = (bf16[96,8100]{1,0:T(8,128)(2,1)}, bf16[48,8100]{1,0:T(8,128)(2,1)}, bf16[48,8100]{1,0:T(8,128)(2,1)}) custom-call(bf16[192,288]{1,0:T(8,128)(2,1)} %get-tuple-element.20.lead_ref, bf16[45,2,8100]{2,1,0:T(2,128)(2,1)} %bitcast.26, bf16[45,2,8100]{2,1,0:T(2,128)(2,1)} %copy-done, bf16[45,2,8100]{2,1,0:T(2,128)(2,1)} %copy-done.1), custom_call_target="tpu_custom_call" | custom-call | flops 895795200 | bytes 9720000 | tf_op jit(solution)/shard_map/contract/pallas_call | solution.py:358
  55.8 0.0 collective-permute-start.6
  55.8 0.5 collective-permute-start.7
  56.3 5.9 %collective-permute-done.2.refs_5_ = bf16[23,2,8100]{2,1,0:T(2,128)(2,1)S(1)} collective-permute-done((bf16[23,2,8100]{2,1,0:T(2,128)(2,1)}, bf16[23,2,8100]{2,1,0:T(2,128)(2,1)S(1)}, u32[]{:S(2)}, u32[]{:S(2)}) %collective-permute-start.2) | collective-permute-done | bytes 745232 | tf_op jit(solution)/shard_map/force_second/ppermute | solution.py:334
  62.2 0.0 collective-permute-start.4
  62.2 0.0 collective-permute-done.3.refs_6_
  62.2 0.5 collective-permute-start.5
  62.8 0.6 fusion.9
  63.4 1.3 %iota_compare_fusion.2 = (pred[32]{0:T(512)(128)(4,1)S(1)}, pred[32]{0:T(512)(128)(4,1)S(1)}) fusion(s32[]{:T(128)} %bitcast.11, s32[]{:T(128)} %bitcast), kind=kLoop, calls=%fused_computation.25 | loop fusion | flops 64 | bytes 72 | tf_op jit(solution)/shard_map/collect/eq | solution.py:399
  64.7 0.0 collective-permute-done.6.refs_10_
  64.7 1.1 %collective-permute-done.5.refs_8_ = bf16[22,2,8100]{2,1,0:T(2,128)(2,1)} collective-permute-done((bf16[22,2,8100]{2,1,0:T(2,128)(2,1)}, bf16[22,2,8100]{2,1,0:T(2,128)(2,1)}, u32[]{:S(2)}, u32[]{:S(2)}) %collective-permute-start.5) | collective-permute-done | bytes 712832 | tf_op jit(solution)/shard_map/contract/ppermute | solution.py:371
  65.8 0.0 collective-permute-done.4.refs_7_
  65.9 0.9 copy-done.7
  66.7 10.8 %interaction.1 = f32[1,128]{1,0:T(1,128)} custom-call(f32[2,48,128]{2,1,0:T(8,128)} %get-tuple-element.13.refs_0_, bf16[192,192]{1,0:T(8,128)(2,1)} %get-tuple-element.14.refs_1_, bf16[256,256]{1,0:T(8,128)(2,1)} %get-tuple-element.15.refs_2_, f32[4,96,128]{2,1,0:T(8,128)} %get-tuple-element.16.refs_3_, bf16[96,192]{1,0:T(8,128)(2,1)} %get-tuple-element.17.refs_4_, ...), custom_call_target="tpu_custom_call" | custom-call | tf_op jit(solution)/shard_map/interaction/pallas_call | solution.py:375
  77.5 0.5 collective-permute-start.8
  78.0 4.3 %collective-permute-start.9 = (f32[1,128]{1,0:T(1,128)}, f32[1,128]{1,0:T(1,128)S(1)}, u32[]{:S(2)}, u32[]{:S(2)}) collective-permute-start(f32[1,128]{1,0:T(1,128)} %interaction.1), channel_id=1, source_target_pairs={{0,128},{64,192},{128,0},{192,64},{1,129},{65,193},{129,1},{193,65... | collective-permute-start | bytes 1544 | tf_op jit(solution)/shard_map/collect/ppermute | solution.py:394
  82.3 0.7 collective-permute-start.10
  83.0 1.2 %iota_compare_fusion = (pred[32]{0:T(512)(128)(4,1)S(1)}, pred[32]{0:T(512)(128)(4,1)S(1)}) fusion(s32[]{:T(128)} %bitcast.15, s32[]{:T(128)} %bitcast.13), kind=kLoop, calls=%fused_computation.23 | loop fusion | flops 64 | bytes 72 | tf_op jit(solution)/shard_map/collect/eq | solution.py:399
  84.2 0.0 collective-permute-done.8
  84.2 0.0 collective-permute-done.9
  84.2 1.8 %collective-permute-done.10 = f32[1,128]{1,0:T(1,128)S(1)} collective-permute-done((f32[1,128]{1,0:T(1,128)}, f32[1,128]{1,0:T(1,128)S(1)}, u32[]{:S(2)}, u32[]{:S(2)}) %collective-permute-start.10) | collective-permute-done | bytes 544 | tf_op jit(solution)/shard_map/collect/ppermute | solution.py:394
  86.0 0.9 fusion.4
  86.9 16.3 %all_to_all.15 = f32[32,1,128]{2,1,0:T(1,128)S(1)} all-to-all(f32[32,1,128]{2,1,0:T(1,128)S(1)} %fusion.4), channel_id=1, replica_groups=mesh['clus'=4,'trip'=32,'mode'=2] {'trip'}, dimensions={0} | all-to-all | bytes 32768 | tf_op jit(solution)/shard_map/collect/all_to_all | solution.py:400
  103.2 0.6 add_divide_fusion
  (31 shorter events, 0.1 us)
Async XLA Ops:
  0.6 17.8 %copy-start.11 = (bf16[2,4]{1,0:T(2,128)(2,1)S(1)}, bf16[2,4]{1,0:T(2,128)(2,1)}, u32[]{:S(2)}) copy-start(bf16[2,4]{1,0:T(2,128)(2,1)} %param.12) | copy-start | bytes 52
  0.6 37.1 %collective-permute-start = (bf16[45,2,8100]{2,1,0:T(2,128)(2,1)}, bf16[45,2,8100]{2,1,0:T(2,128)(2,1)S(1)}, u32[]{:S(2)}, u32[]{:S(2)}) collective-permute-start(bf16[45,2,8100]{2,1,0:T(2,128)(2,1)} %bitcast.24), channel_id=1, source_target_pairs={{0,64},{64,128},{128,192},{192,0},{1,65},{65,129},{129,193},{193,1... | collective-permute-start | bytes 4374008 | tf_op jit(solution)/shard_map/force/ppermute | solution.py:319
  2.2 37.1 %collective-permute-start.1 = (bf16[45,2,8100]{2,1,0:T(2,128)(2,1)}, bf16[45,2,8100]{2,1,0:T(2,128)(2,1)S(1)}, u32[]{:S(2)}, u32[]{:S(2)}) collective-permute-start(bf16[45,2,8100]{2,1,0:T(2,128)(2,1)} %bitcast.25), channel_id=1, source_target_pairs={{0,192},{64,0},{128,64},{192,128},{1,193},{65,1},{129,65},{193,129... | collective-permute-start | bytes 4374008 | tf_op jit(solution)/shard_map/force/ppermute | solution.py:320
  7.3 22.9 %all-to-all-start = ((bf16[32,12,180]{2,1,0:T(8,128)(2,1)}), bf16[32,12,180]{2,1,0:T(8,128)(2,1)S(1)}, u32[]{:S(2)}, u32[]{:S(2)}) async-start(bf16[32,12,180]{2,1,0:T(8,128)(2,1)} %records.1), calls=%async_computation | async-start | bytes 524288 | tf_op jit(solution)/shard_map/records/all_to_all | solution.py:312
  30.2 0.7 copy-start.3
  32.6 11.2 %all-to-all-start.1 = ((bf16[8,4,16,180]{3,2,1,0:T(8,128)(2,1)}), bf16[8,4,16,180]{3,2,1,0:T(8,128)(2,1)S(1)}, u32[]{:S(2)}, u32[]{:S(2)}) async-start(bf16[8,4,16,180]{3,2,1,0:T(8,128)(2,1)} %members.1), calls=%async_computation.1 | async-start | bytes 524288 | tf_op jit(solution)/shard_map/members/all_to_all | solution.py:330
  37.7 8.1 %copy-start.12 = (s32[4]{0:T(128)S(1)}, s32[4]{0:T(128)}, u32[]{:S(2)}) copy-start(s32[4]{0:T(128)} %param.19) | copy-start | bytes 52
  37.7 3.1 %copy-start = (bf16[45,2,8100]{2,1,0:T(2,128)(2,1)}, bf16[45,2,8100]{2,1,0:T(2,128)(2,1)S(1)}, u32[]{:S(2)}) copy-start(bf16[45,2,8100]{2,1,0:T(2,128)(2,1)S(1)} %collective-permute-done.low_ref) | copy-start | bytes 4374004
  39.3 10.7 %copy-start.1 = (bf16[45,2,8100]{2,1,0:T(2,128)(2,1)}, bf16[45,2,8100]{2,1,0:T(2,128)(2,1)S(1)}, u32[]{:S(2)}) copy-start(bf16[45,2,8100]{2,1,0:T(2,128)(2,1)S(1)} %collective-permute-done.1.high_ref) | copy-start | bytes 4374004
  43.8 3.8 %copy-start.2 = (bf16[8,4,16,180]{3,2,1,0:T(8,128)(2,1)}, bf16[8,4,16,180]{3,2,1,0:T(8,128)(2,1)S(1)}, u32[]{:S(2)}) copy-start(bf16[8,4,16,180]{3,2,1,0:T(8,128)(2,1)S(1)} %all-to-all-done.1.members_ref) | copy-start | bytes 552964
  43.8 18.4 %collective-permute-start.2 = (bf16[23,2,8100]{2,1,0:T(2,128)(2,1)}, bf16[23,2,8100]{2,1,0:T(2,128)(2,1)S(1)}, u32[]{:S(2)}, u32[]{:S(2)}) collective-permute-start(bf16[23,2,8100]{2,1,0:T(2,128)(2,1)} %slice.16), channel_id=1, source_target_pairs={{0,64},{64,128},{128,192},{192,0},{1,65},{65,129},{129,193},{193,1... | collective-permute-start | bytes 2235608 | tf_op jit(solution)/shard_map/force_second/ppermute | solution.py:334
  43.8 18.4 %collective-permute-start.3 = (bf16[22,2,8100]{2,1,0:T(2,128)(2,1)}, bf16[22,2,8100]{2,1,0:T(2,128)(2,1)}, u32[]{:S(2)}, u32[]{:S(2)}) collective-permute-start(bf16[22,2,8100]{2,1,0:T(2,128)(2,1)} %slice.17), channel_id=1, source_target_pairs={{0,192},{64,0},{128,64},{192,128},{1,193},{65,1},{129,65},{193,129... | collective-permute-start | bytes 2138408 | tf_op jit(solution)/shard_map/force_second/ppermute | solution.py:335
  50.0 12.7 %copy-start.8 = (s32[4]{0:T(128)S(1)}, s32[4]{0:T(128)}, u32[]{:S(2)}) copy-start(s32[4]{0:T(128)} %param.18) | copy-start | bytes 52
  55.8 8.9 %collective-permute-start.6 = (bf16[48,8100]{1,0:T(8,128)(2,1)}, bf16[48,8100]{1,0:T(8,128)(2,1)S(1)}, u32[]{:S(2)}, u32[]{:S(2)}) collective-permute-start(bf16[48,8100]{1,0:T(8,128)(2,1)} %get-tuple-element.22), channel_id=1, source_target_pairs={{0,1},{1,0},{2,3},{3,2},{4,5},{5,4},{6,7},{7,6},{8,9},{9,8},{10,11... | collective-permute-start | bytes 2332808 | tf_op jit(solution)/shard_map/contract/ppermute | solution.py:369
  55.8 8.9 %collective-permute-start.7 = (bf16[48,8100]{1,0:T(8,128)(2,1)}, bf16[48,8100]{1,0:T(8,128)(2,1)S(1)}, u32[]{:S(2)}, u32[]{:S(2)}) collective-permute-start(bf16[48,8100]{1,0:T(8,128)(2,1)} %get-tuple-element.23), channel_id=1, source_target_pairs={{0,1},{1,0},{2,3},{3,2},{4,5},{5,4},{6,7},{7,6},{8,9},{9,8},{10,11... | collective-permute-start | bytes 2332808 | tf_op jit(solution)/shard_map/contract/ppermute | solution.py:369
  62.2 3.6 %copy-start.6 = (bf16[23,2,8100]{2,1,0:T(2,128)(2,1)}, bf16[23,2,8100]{2,1,0:T(2,128)(2,1)S(1)}, u32[]{:S(2)}) copy-start(bf16[23,2,8100]{2,1,0:T(2,128)(2,1)S(1)} %collective-permute-done.2.refs_5_) | copy-start | bytes 2235604
  62.2 3.6 %collective-permute-start.4 = (bf16[23,2,8100]{2,1,0:T(2,128)(2,1)S(1)}, bf16[23,2,8100]{2,1,0:T(2,128)(2,1)S(1)}, u32[]{:S(2)}, u32[]{:S(2)}) collective-permute-start(bf16[23,2,8100]{2,1,0:T(2,128)(2,1)S(1)} %collective-permute-done.2.refs_5_), channel_id=1, source_target_pairs={{0,1},{1,0},{2,3},{3,2},{4,5},{5,4},{6,7},{7,6},{8,9},{9,8},{10,11... | collective-permute-start | bytes 2235608 | tf_op jit(solution)/shard_map/contract/ppermute | solution.py:370
  62.2 3.6 %collective-permute-start.5 = (bf16[22,2,8100]{2,1,0:T(2,128)(2,1)}, bf16[22,2,8100]{2,1,0:T(2,128)(2,1)}, u32[]{:S(2)}, u32[]{:S(2)}) collective-permute-start(bf16[22,2,8100]{2,1,0:T(2,128)(2,1)} %collective-permute-done.3.refs_6_), channel_id=1, source_target_pairs={{0,1},{1,0},{2,3},{3,2},{4,5},{5,4},{6,7},{7,6},{8,9},{9,8},{10,11... | collective-permute-start | bytes 2138408 | tf_op jit(solution)/shard_map/contract/ppermute | solution.py:371
  64.7 1.2 %copy-start.4 = (bf16[48,8100]{1,0:T(8,128)(2,1)}, bf16[48,8100]{1,0:T(8,128)(2,1)S(1)}, u32[]{:S(2)}) copy-start(bf16[48,8100]{1,0:T(8,128)(2,1)S(1)} %collective-permute-done.6.refs_10_) | copy-start | bytes 2332804
  64.7 1.2 %copy-start.5 = (bf16[48,8100]{1,0:T(8,128)(2,1)}, bf16[48,8100]{1,0:T(8,128)(2,1)S(1)}, u32[]{:S(2)}) copy-start(bf16[48,8100]{1,0:T(8,128)(2,1)S(1)} %collective-permute-done.7.refs_11_) | copy-start | bytes 2332804
  65.8 0.9 copy-start.7
  66.7 36.5 %copy-start.9 = (f32[1,45]{1,0:T(1,128)S(1)}, f32[1,45]{1,0:T(1,128)}, u32[]{:S(2)}) copy-start(f32[1,45]{1,0:T(1,128)} %param.20) | copy-start | bytes 544
  66.7 36.5 %copy-start.10 = (f32[1,45]{1,0:T(1,128)S(1)}, f32[1,45]{1,0:T(1,128)}, u32[]{:S(2)}) copy-start(f32[1,45]{1,0:T(1,128)} %param.21) | copy-start | bytes 544
  77.5 6.7 %collective-permute-start.8 = (f32[1,128]{1,0:T(1,128)}, f32[1,128]{1,0:T(1,128)S(1)}, u32[]{:S(2)}, u32[]{:S(2)}) collective-permute-start(f32[1,128]{1,0:T(1,128)} %interaction.1), channel_id=1, source_target_pairs={{0,64},{64,128},{128,192},{192,0},{1,65},{65,129},{129,193},{193,1... | collective-permute-start | bytes 1544 | tf_op jit(solution)/shard_map/collect/ppermute | solution.py:394
  78.0 6.2 %collective-permute-start.9 = (f32[1,128]{1,0:T(1,128)}, f32[1,128]{1,0:T(1,128)S(1)}, u32[]{:S(2)}, u32[]{:S(2)}) collective-permute-start(f32[1,128]{1,0:T(1,128)} %interaction.1), channel_id=1, source_target_pairs={{0,128},{64,192},{128,0},{192,64},{1,129},{65,193},{129,1},{193,65... | collective-permute-start | bytes 1544 | tf_op jit(solution)/shard_map/collect/ppermute | solution.py:394
  82.3 3.7 %collective-permute-start.10 = (f32[1,128]{1,0:T(1,128)}, f32[1,128]{1,0:T(1,128)S(1)}, u32[]{:S(2)}, u32[]{:S(2)}) collective-permute-start(f32[1,128]{1,0:T(1,128)} %interaction.1), channel_id=1, source_target_pairs={{0,192},{64,0},{128,64},{192,128},{1,193},{65,1},{129,65},{193,129... | collective-permute-start | bytes 1544 | tf_op jit(solution)/shard_map/collect/ppermute | solution.py:394

commit v12 on v11

--- a/solution.py
+++ b/solution.py
@@ -128,6 +128,15 @@
     values = ref[:, :, cols]
     rows = values.shape[0] * values.shape[1]
     return jnp.pad(values.reshape(rows, values.shape[2]), ((0, count - rows), (0, 0)))
+
+
+def halves_kernel(low_ref, high_ref, top_ref, bottom_ref, done):
+    top = pltpu.make_async_copy(low_ref.at[0:TOP], top_ref, done.at[0])
+    bottom = pltpu.make_async_copy(high_ref.at[TOP:45], bottom_ref, done.at[1])
+    top.start()
+    bottom.start()
+    top.wait()
+    bottom.wait()
 
 
 def early_kernel(lead_ref, own_ref, low_ref, high_ref, mine_ref, *far_refs):
@@ -330,7 +339,19 @@
         members = lax.all_to_all(picks, group, 0, 0, tiled=True)
 
     with jax.named_scope("force_second"):
-        low_top, high_bottom, _ = lax.optimization_barrier((low[:TOP], high[TOP:], members))
+        any_space = pl.BlockSpec(memory_space=pl.ANY)
+        low_top, high_bottom = pl.pallas_call(
+            halves_kernel,
+            out_shape=(
+                jax.ShapeDtypeStruct((TOP,) + low.shape[1:], b16),
+                jax.ShapeDtypeStruct((45 - TOP,) + high.shape[1:], b16),
+            ),
+            in_specs=[any_space] * 2,
+            out_specs=(any_space,) * 2,
+            scratch_shapes=[pltpu.SemaphoreType.DMA((2,))],
+            compiler_params=pltpu.CompilerParams(vmem_limit_bytes=4 << 20),
+        )(low, high)
+        low_top, high_bottom, _ = lax.optimization_barrier((low_top, high_bottom, members))
         top = lax.ppermute(low_top, "clus", ring(4, 1))
         bottom = lax.ppermute(high_bottom, "clus", ring(4, 3))
 
@@ -369,6 +390,14 @@
         other = [lax.ppermute(rows, "mode", swap) for rows in far]
         far_top = lax.ppermute(top, "mode", swap)
         far_bottom = lax.ppermute(bottom, "mode", swap)
+
+    with jax.named_scope("masks"):
+        points = jnp.arange(32, dtype=jnp.int32)
+        masks = [
+            points == lax.dynamic_index_in_dim(irreducible, (clus - step) % 4, 0, keepdims=False)
+            for step in range(4)
+        ]
+        mine, *masks = lax.optimization_barrier((mine, *masks))
 
     with jax.named_scope("interaction"):
         inputs = (scalars, mid, last_all, tables, late, top, bottom, far_top, far_bottom, mine, *other)
@@ -392,11 +421,9 @@
     with jax.named_scope("collect"):
         own_row = sums
         rows = [own_row] + [lax.ppermute(own_row, "clus", ring(4, step)) for step in (1, 2, 3)]
-        points = jnp.arange(32, dtype=jnp.int32)
         partial = jnp.zeros((32, 128), f32)
-        for step in range(4):
-            point = lax.dynamic_index_in_dim(irreducible, (clus - step) % 4, 0, keepdims=False)
-            partial = partial + jnp.where((points == point)[:, None], rows[step], 0.0)
+        for mask, row in zip(masks, rows):
+            partial = partial + jnp.where(mask[:, None], row, 0.0)
         received = lax.all_to_all(partial[:, None, :], "trip", 0, 0, tiled=True)
         final = jnp.sum(received[:, 0, :], axis=0)[None, :]
         gamma_total = final[:, 0:45] + boundary

time: 104 us -> 106 us (1.019)
  starting transfers between devices: 27.2 us -> 28.5 us
  waiting for transfers between devices: 22.7 us -> 21.4 us
    unnamed x27 -> x31, local copies, waits for them, and re-layouts: 2.65 us -> 5.82 us
    slice x2 -> x0, local copies, waits for them, and re-layouts: 3.13 us -> none  [the longest x1 1.57 us: body(): high[TOP:]]
    ppermute x1, starting transfers between devices: 1.57 us -> 0.01 us  [body(): low = lax.ppermute(own, 'clus', ring(4, 1))]
    ppermute x1, starting transfers between devices: 0.87 us -> 2.35 us  [body(): high = lax.ppermute(own, 'clus', ring(4, 3))]
    ppermute x1, waiting for transfers between devices: 1.12 us -> 0.01 us  [body(): far_bottom = lax.ppermute(bottom, 'mode', swap)]
  transfers between devices with their start and end apart: 13 -> 13, of which waited for: 5 -> 4; matrix products, arithmetic and copies ran while one was open for 11% -> 8% of each run, Pallas kernels for 11% -> 11%
where the time goes in v12:
time: 106 us; the launch traced here: 105 us
  starting transfers between devices  28.5 us (27%)
  Pallas kernels  22.9 us (22%)
  waiting for transfers between devices  21.4 us (20%)
  blocking collectives  17.1 us (16%)
  local copies, waits for them, and re-layouts  7.89 us (7%)
  other arithmetic  6.81 us (6%)
    all_to_all x1, blocking collectives, body(): received = lax.all_to_all(partial[:, None, :], 'trip', 0, 0, tiled=True)  17.1 us
    all_to_all x1, starting transfers between devices, body(): arrived = lax.all_to_all(chosen, 'trip', 0, 0, tiled=True)  11.2 us
    all_to_all x1, waiting for transfers between devices, body(): arrived = lax.all_to_all(chosen, 'trip', 0, 0, tiled=True)  11 us
    pallas_call x1, Pallas kernels, body(): pl.pallas_call(interaction_kernel, out_shape=jax.ShapeDtypeStruct((1, 128...  10.8 us
    ppermute x3, starting transfers between devices, body(): lax.ppermute(own_row, 'clus', ring(4, step))  6.06 us
    pallas_call x1, Pallas kernels, body(): pl.pallas_call(early_kernel, out_shape=(jax.ShapeDtypeStruct((WIDE, total...  5.83 us
    unnamed x31, local copies, waits for them, and re-layouts  5.82 us
    ppermute x1, waiting for transfers between devices, body(): top = lax.ppermute(low_top, 'clus', ring(4, 1))  5.82 us
  transfers between devices with their start and end apart: 13, of which 4 were waited for; matrix products, arithmetic and copies ran while one was open for 8% of the time, Pallas kernels for 11%

profile of v12, /device:TPU:2, one launch (start us, length us, event | category | flops | bytes accessed | tf_op | source)
XLA Modules:
  0.0 105.4 jit_solution(6419159680274462620)
XLA Ops:
  0.6 2.3 %collective-permute-start.1 = (bf16[45,2,8100]{2,1,0:T(2,128)(2,1)}, bf16[45,2,8100]{2,1,0:T(2,128)(2,1)S(1)}, u32[]{:S(2)}, u32[]{:S(2)}) collective-permute-start(bf16[45,2,8100]{2,1,0:T(2,128)(2,1)} %bitcast.24), channel_id=1, source_target_pairs={{0,192},{64,0},{128,64},{192,128},{1,193},{65,1},{129,65},{193,129... | collective-permute-start | bytes 4374008 | tf_op jit(solution)/shard_map/force/ppermute | solution.py:329
  3.0 0.0 collective-permute-start
  3.0 0.8 maximum_bitcast_fusion
  3.8 1.1 %copy.27 = bf16[8,90,180]{2,1,0:T(8,128)(2,1)S(1)} copy(bf16[8,90,180]{2,0,1:T(8,128)(2,1)} %param.13) | data formatting | bytes 518400 | tf_op args[2]
  4.9 0.1 pad_dynamic-slice_fusion.2
  4.9 0.7 fusion.1.share_ref
  5.6 1.6 %records.1 = bf16[32,12,180]{2,1,0:T(8,128)(2,1)} custom-call(s32[1,32]{1,0:T(1,128)} %rows_ref.1, bf16[8,12,180]{2,1,0:T(8,128)(2,1)} %fusion.1.share_ref), custom_call_target="tpu_custom_call" | custom-call | tf_op jit(solution)/shard_map/records/pallas_call | solution.py:314
  7.2 11.2 %all-to-all-start = ((bf16[32,12,180]{2,1,0:T(8,128)(2,1)}), bf16[32,12,180]{2,1,0:T(8,128)(2,1)S(1)}, u32[]{:S(2)}, u32[]{:S(2)}) async-start(bf16[32,12,180]{2,1,0:T(8,128)(2,1)} %records.1), calls=%async_computation | async-start | bytes 524288 | tf_op jit(solution)/shard_map/records/all_to_all | solution.py:321
  18.5 0.1 copy.31
  18.6 0.6 pad.4.phase_ref
  19.3 11.0 %all-to-all-done.arrived_ref = bf16[32,12,180]{2,1,0:T(8,128)(2,1)S(1)} async-done(((bf16[32,12,180]{2,1,0:T(8,128)(2,1)}), bf16[32,12,180]{2,1,0:T(8,128)(2,1)S(1)}, u32[]{:S(2)}, u32[]{:S(2)}) %all-to-all-start) | async-done | bytes 138272 | tf_op jit(solution)/shard_map/records/all_to_all | solution.py:321
  30.2 0.7 copy-done.5
  30.9 1.7 %members.1 = bf16[8,4,16,180]{3,2,1,0:T(8,128)(2,1)} custom-call(s32[4,3]{1,0:T(4,128)} %table_ref.1, bf16[32,12,180]{2,1,0:T(8,128)(2,1)} %copy-done.5, bf16[4,16,180]{2,1,0:T(8,128)(2,1)} %pad.4.phase_ref), custom_call_target="tpu_custom_call" | custom-call | tf_op jit(solution)/shard_map/members/pallas_call | solution.py:332
  32.6 5.8 %all-to-all-start.1 = ((bf16[8,4,16,180]{3,2,1,0:T(8,128)(2,1)}), bf16[8,4,16,180]{3,2,1,0:T(8,128)(2,1)S(1)}, u32[]{:S(2)}, u32[]{:S(2)}) async-start(bf16[8,4,16,180]{3,2,1,0:T(8,128)(2,1)} %members.1), calls=%async_computation.1 | async-start | bytes 524288 | tf_op jit(solution)/shard_map/members/all_to_all | solution.py:339
  38.4 0.0 collective-permute-done.1.high_ref
  38.4 0.0 collective-permute-done.low_ref
  38.4 0.6 force_second.1
  39.1 0.5 copy-done
  39.5 0.4 copy-done.1
  40.0 0.9 copy-done.2
  40.9 0.9 copy-done.3
  41.8 2.7 %all-to-all-done.1.members_ref = bf16[8,4,16,180]{3,2,1,0:T(8,128)(2,1)S(1)} async-done(((bf16[8,4,16,180]{3,2,1,0:T(8,128)(2,1)}), bf16[8,4,16,180]{3,2,1,0:T(8,128)(2,1)S(1)}, u32[]{:S(2)}, u32[]{:S(2)}) %all-to-all-start.1) | async-done | bytes 184352 | tf_op jit(solution)/shard_map/members/all_to_all | solution.py:339
  44.5 2.0 %collective-permute-start.3 = (bf16[22,2,8100]{2,1,0:T(2,128)(2,1)}, bf16[22,2,8100]{2,1,0:T(2,128)(2,1)}, u32[]{:S(2)}, u32[]{:S(2)}) collective-permute-start(bf16[22,2,8100]{2,1,0:T(2,128)(2,1)} %copy-done.3), channel_id=1, source_target_pairs={{0,192},{64,0},{128,64},{192,128},{1,193},{65,1},{129,65},{193,129... | collective-permute-start | bytes 2138408 | tf_op jit(solution)/shard_map/force_second/ppermute | solution.py:356
  46.5 0.6 dynamic_slice.19
  47.1 1.3 %pad_add_fusion.where_ref = s32[3]{0:T(128)} fusion(s32[1]{0:T(128)} %dynamic_slice.19, s32[1]{0:T(128)} %bitcast.1, s32[1]{0:T(128)} %bitcast), kind=kLoop, calls=%fused_computation.20 | loop fusion | flops 6 | bytes 24 | tf_op jit(solution)/shard_map/operands/stack | solution.py:360
  48.3 2.4 %operands.1 = (bf16[192,288]{1,0:T(8,128)(2,1)}, bf16[96,192]{1,0:T(8,128)(2,1)}, bf16[192,192]{1,0:T(8,128)(2,1)}, bf16[256,256]{1,0:T(8,128)(2,1)}, f32[4,96,128]{2,1,0:T(8,128)}, /*index=5*/f32[2,48,128]{2,1,0:T(8,128)}) custom-call(s32[3]{0:T(128)} %pad_add_fusion.where_ref, bf16[8,4,16,180]{3,2,1,0:T(8,128)(2,1)} %copy-done.4), custom_call_target="tpu_custom_call" | custom-call | tf_op jit(solution)/shard_map/operands/pallas_call | solution.py:361
  50.7 5.8 %contract.1 = (bf16[96,8100]{1,0:T(8,128)(2,1)}, bf16[48,8100]{1,0:T(8,128)(2,1)}, bf16[48,8100]{1,0:T(8,128)(2,1)}) custom-call(bf16[192,288]{1,0:T(8,128)(2,1)} %get-tuple-element.20.lead_ref, bf16[45,2,8100]{2,1,0:T(2,128)(2,1)} %bitcast.26, bf16[45,2,8100]{2,1,0:T(2,128)(2,1)} %copy-done.1, bf16[45,2,8100]{2,1,0:T(2,128)(2,1)} %copy-done), custom_call_target="tpu_custom_call" | custom-call | flops 895795200 | bytes 9720000 | tf_op jit(solution)/shard_map/contract/pallas_call | solution.py:379
  56.6 0.5 collective-permute-start.7
  57.1 5.8 %collective-permute-done.2.refs_5_ = bf16[23,2,8100]{2,1,0:T(2,128)(2,1)S(1)} collective-permute-done((bf16[23,2,8100]{2,1,0:T(2,128)(2,1)}, bf16[23,2,8100]{2,1,0:T(2,128)(2,1)S(1)}, u32[]{:S(2)}, u32[]{:S(2)}) %collective-permute-start.2) | collective-permute-done | bytes 745232 | tf_op jit(solution)/shard_map/force_second/ppermute | solution.py:355
  62.9 0.5 collective-permute-start.5
  63.4 0.7 fusion.9
  64.1 1.3 %iota_compare_fusion = (pred[32]{0:T(512)(128)(4,1)S(1)}, pred[32]{0:T(512)(128)(4,1)S(1)}) fusion(s32[]{:T(128)} %bitcast.12, s32[]{:T(128)} %bitcast.11), kind=kLoop, calls=%fused_computation.23 | loop fusion | flops 64 | bytes 72 | tf_op jit(solution)/shard_map/masks/eq | solution.py:397
  65.4 1.3 %iota_compare_fusion.2 = (pred[32]{0:T(512)(128)(4,1)S(1)}, pred[32]{0:T(512)(128)(4,1)S(1)}) fusion(s32[]{:T(128)} %bitcast.10, s32[]{:T(128)} %bitcast.9), kind=kLoop, calls=%fused_computation.25 | loop fusion | flops 64 | bytes 72 | tf_op jit(solution)/shard_map/masks/eq | solution.py:397
  66.7 0.0 collective-permute-done.6.refs_10_
  66.7 0.0 collective-permute-done.7.refs_11_
  66.7 0.0 collective-permute-done.4.refs_7_
  66.7 0.8 copy-done.6
  67.6 0.2 copy-done.7
  67.8 0.2 copy-done.9
  68.1 10.8 %interaction.1 = f32[1,128]{1,0:T(1,128)} custom-call(f32[2,48,128]{2,1,0:T(8,128)} %get-tuple-element.23.refs_0_, bf16[192,192]{1,0:T(8,128)(2,1)} %get-tuple-element.24.refs_1_, bf16[256,256]{1,0:T(8,128)(2,1)} %get-tuple-element.25.refs_2_, f32[4,96,128]{2,1,0:T(8,128)} %get-tuple-element.26.refs_3_, bf16[96,192]{1,0:T(8,128)(2,1)} %get-tuple-element.27.refs_4_, ...), custom_call_target="tpu_custom_call" | custom-call | tf_op jit(solution)/shard_map/interaction/pallas_call | solution.py:404
  78.9 2.7 %collective-permute-start.10 = (f32[1,128]{1,0:T(1,128)}, f32[1,128]{1,0:T(1,128)S(1)}, u32[]{:S(2)}, u32[]{:S(2)}) collective-permute-start(f32[1,128]{1,0:T(1,128)} %interaction.1), channel_id=1, source_target_pairs={{0,192},{64,0},{128,64},{192,128},{1,193},{65,1},{129,65},{193,129... | collective-permute-start | bytes 1544 | tf_op jit(solution)/shard_map/collect/ppermute | solution.py:423
  81.6 0.8 collective-permute-start.9
  82.4 2.5 %collective-permute-start.8 = (f32[1,128]{1,0:T(1,128)}, f32[1,128]{1,0:T(1,128)S(1)}, u32[]{:S(2)}, u32[]{:S(2)}) collective-permute-start(f32[1,128]{1,0:T(1,128)} %interaction.1), channel_id=1, source_target_pairs={{0,64},{64,128},{128,192},{192,0},{1,65},{65,129},{129,193},{193,1... | collective-permute-start | bytes 1544 | tf_op jit(solution)/shard_map/collect/ppermute | solution.py:423
  84.9 0.0 collective-permute-done.10
  84.9 1.9 %collective-permute-done.9 = f32[1,128]{1,0:T(1,128)S(1)} collective-permute-done((f32[1,128]{1,0:T(1,128)}, f32[1,128]{1,0:T(1,128)S(1)}, u32[]{:S(2)}, u32[]{:S(2)}) %collective-permute-start.9) | collective-permute-done | bytes 544 | tf_op jit(solution)/shard_map/collect/ppermute | solution.py:423
  86.8 0.9 fusion.4
  87.7 17.1 %all_to_all.15 = f32[32,1,128]{2,1,0:T(1,128)S(1)} all-to-all(f32[32,1,128]{2,1,0:T(1,128)S(1)} %fusion.4), channel_id=1, replica_groups=mesh['clus'=4,'trip'=32,'mode'=2] {'trip'}, dimensions={0} | all-to-all | bytes 32768 | tf_op jit(solution)/shard_map/collect/all_to_all | solution.py:427
  104.8 0.6 add_divide_fusion
  (34 shorter events, 0.1 us)
Async XLA Ops:
  0.6 17.8 %copy-start.13 = (bf16[2,4]{1,0:T(2,128)(2,1)S(1)}, bf16[2,4]{1,0:T(2,128)(2,1)}, u32[]{:S(2)}) copy-start(bf16[2,4]{1,0:T(2,128)(2,1)} %param.12) | copy-start | bytes 52
  0.6 37.8 %collective-permute-start.1 = (bf16[45,2,8100]{2,1,0:T(2,128)(2,1)}, bf16[45,2,8100]{2,1,0:T(2,128)(2,1)S(1)}, u32[]{:S(2)}, u32[]{:S(2)}) collective-permute-start(bf16[45,2,8100]{2,1,0:T(2,128)(2,1)} %bitcast.24), channel_id=1, source_target_pairs={{0,192},{64,0},{128,64},{192,128},{1,193},{65,1},{129,65},{193,129... | collective-permute-start | bytes 4374008 | tf_op jit(solution)/shard_map/force/ppermute | solution.py:329
  3.0 35.4 %collective-permute-start = (bf16[45,2,8100]{2,1,0:T(2,128)(2,1)}, bf16[45,2,8100]{2,1,0:T(2,128)(2,1)S(1)}, u32[]{:S(2)}, u32[]{:S(2)}) collective-permute-start(bf16[45,2,8100]{2,1,0:T(2,128)(2,1)} %bitcast.25), channel_id=1, source_target_pairs={{0,64},{64,128},{128,192},{192,0},{1,65},{65,129},{129,193},{193,1... | collective-permute-start | bytes 4374008 | tf_op jit(solution)/shard_map/force/ppermute | solution.py:328
  7.2 23.0 %all-to-all-start = ((bf16[32,12,180]{2,1,0:T(8,128)(2,1)}), bf16[32,12,180]{2,1,0:T(8,128)(2,1)S(1)}, u32[]{:S(2)}, u32[]{:S(2)}) async-start(bf16[32,12,180]{2,1,0:T(8,128)(2,1)} %records.1), calls=%async_computation | async-start | bytes 524288 | tf_op jit(solution)/shard_map/records/all_to_all | solution.py:321
  30.2 0.7 copy-start.5
  32.6 11.9 %all-to-all-start.1 = ((bf16[8,4,16,180]{3,2,1,0:T(8,128)(2,1)}), bf16[8,4,16,180]{3,2,1,0:T(8,128)(2,1)S(1)}, u32[]{:S(2)}, u32[]{:S(2)}) async-start(bf16[8,4,16,180]{3,2,1,0:T(8,128)(2,1)} %members.1), calls=%async_computation.1 | async-start | bytes 524288 | tf_op jit(solution)/shard_map/members/all_to_all | solution.py:339
  38.4 8.1 %copy-start.14 = (s32[4]{0:T(128)S(1)}, s32[4]{0:T(128)}, u32[]{:S(2)}) copy-start(s32[4]{0:T(128)} %param.19) | copy-start | bytes 52
  38.4 1.1 %copy-start = (bf16[45,2,8100]{2,1,0:T(2,128)(2,1)}, bf16[45,2,8100]{2,1,0:T(2,128)(2,1)S(1)}, u32[]{:S(2)}) copy-start(bf16[45,2,8100]{2,1,0:T(2,128)(2,1)S(1)} %collective-permute-done.1.high_ref) | copy-start | bytes 4374004
  38.4 1.5 %copy-start.1 = (bf16[45,2,8100]{2,1,0:T(2,128)(2,1)}, bf16[45,2,8100]{2,1,0:T(2,128)(2,1)S(1)}, u32[]{:S(2)}) copy-start(bf16[45,2,8100]{2,1,0:T(2,128)(2,1)S(1)} %collective-permute-done.low_ref) | copy-start | bytes 4374004
  40.0 0.9 copy-start.2
  40.9 0.9 copy-start.3
  44.5 3.9 %copy-start.4 = (bf16[8,4,16,180]{3,2,1,0:T(8,128)(2,1)}, bf16[8,4,16,180]{3,2,1,0:T(8,128)(2,1)S(1)}, u32[]{:S(2)}) copy-start(bf16[8,4,16,180]{3,2,1,0:T(8,128)(2,1)S(1)} %all-to-all-done.1.members_ref) | copy-start | bytes 552964
  44.5 18.4 %collective-permute-start.2 = (bf16[23,2,8100]{2,1,0:T(2,128)(2,1)}, bf16[23,2,8100]{2,1,0:T(2,128)(2,1)S(1)}, u32[]{:S(2)}, u32[]{:S(2)}) collective-permute-start(bf16[23,2,8100]{2,1,0:T(2,128)(2,1)} %copy-done.2), channel_id=1, source_target_pairs={{0,64},{64,128},{128,192},{192,0},{1,65},{65,129},{129,193},{193,1... | collective-permute-start | bytes 2235608 | tf_op jit(solution)/shard_map/force_second/ppermute | solution.py:355
  44.5 18.4 %collective-permute-start.3 = (bf16[22,2,8100]{2,1,0:T(2,128)(2,1)}, bf16[22,2,8100]{2,1,0:T(2,128)(2,1)}, u32[]{:S(2)}, u32[]{:S(2)}) collective-permute-start(bf16[22,2,8100]{2,1,0:T(2,128)(2,1)} %copy-done.3), channel_id=1, source_target_pairs={{0,192},{64,0},{128,64},{192,128},{1,193},{65,1},{129,65},{193,129... | collective-permute-start | bytes 2138408 | tf_op jit(solution)/shard_map/force_second/ppermute | solution.py:356
  50.7 12.7 %copy-start.10 = (s32[4]{0:T(128)S(1)}, s32[4]{0:T(128)}, u32[]{:S(2)}) copy-start(s32[4]{0:T(128)} %param.18) | copy-start | bytes 52
  56.6 10.1 %collective-permute-start.6 = (bf16[48,8100]{1,0:T(8,128)(2,1)}, bf16[48,8100]{1,0:T(8,128)(2,1)S(1)}, u32[]{:S(2)}, u32[]{:S(2)}) collective-permute-start(bf16[48,8100]{1,0:T(8,128)(2,1)} %get-tuple-element.33), channel_id=1, source_target_pairs={{0,1},{1,0},{2,3},{3,2},{4,5},{5,4},{6,7},{7,6},{8,9},{9,8},{10,11... | collective-permute-start | bytes 2332808 | tf_op jit(solution)/shard_map/contract/ppermute | solution.py:390
  56.6 10.1 %collective-permute-start.7 = (bf16[48,8100]{1,0:T(8,128)(2,1)}, bf16[48,8100]{1,0:T(8,128)(2,1)S(1)}, u32[]{:S(2)}, u32[]{:S(2)}) collective-permute-start(bf16[48,8100]{1,0:T(8,128)(2,1)} %get-tuple-element.34), channel_id=1, source_target_pairs={{0,1},{1,0},{2,3},{3,2},{4,5},{5,4},{6,7},{7,6},{8,9},{9,8},{10,11... | collective-permute-start | bytes 2332808 | tf_op jit(solution)/shard_map/contract/ppermute | solution.py:390
  62.9 3.8 %copy-start.8 = (bf16[23,2,8100]{2,1,0:T(2,128)(2,1)}, bf16[23,2,8100]{2,1,0:T(2,128)(2,1)S(1)}, u32[]{:S(2)}) copy-start(bf16[23,2,8100]{2,1,0:T(2,128)(2,1)S(1)} %collective-permute-done.2.refs_5_) | copy-start | bytes 2235604
  62.9 3.8 %collective-permute-start.4 = (bf16[23,2,8100]{2,1,0:T(2,128)(2,1)S(1)}, bf16[23,2,8100]{2,1,0:T(2,128)(2,1)S(1)}, u32[]{:S(2)}, u32[]{:S(2)}) collective-permute-start(bf16[23,2,8100]{2,1,0:T(2,128)(2,1)S(1)} %collective-permute-done.2.refs_5_), channel_id=1, source_target_pairs={{0,1},{1,0},{2,3},{3,2},{4,5},{5,4},{6,7},{7,6},{8,9},{9,8},{10,11... | collective-permute-start | bytes 2235608 | tf_op jit(solution)/shard_map/contract/ppermute | solution.py:391
  62.9 3.8 %collective-permute-start.5 = (bf16[22,2,8100]{2,1,0:T(2,128)(2,1)}, bf16[22,2,8100]{2,1,0:T(2,128)(2,1)}, u32[]{:S(2)}, u32[]{:S(2)}) collective-permute-start(bf16[22,2,8100]{2,1,0:T(2,128)(2,1)} %collective-permute-done.3.refs_6_), channel_id=1, source_target_pairs={{0,1},{1,0},{2,3},{3,2},{4,5},{5,4},{6,7},{7,6},{8,9},{9,8},{10,11... | collective-permute-start | bytes 2138408 | tf_op jit(solution)/shard_map/contract/ppermute | solution.py:392
  66.7 0.9 copy-start.6
  66.7 1.1 %copy-start.7 = (bf16[48,8100]{1,0:T(8,128)(2,1)}, bf16[48,8100]{1,0:T(8,128)(2,1)S(1)}, u32[]{:S(2)}) copy-start(bf16[48,8100]{1,0:T(8,128)(2,1)S(1)} %collective-permute-done.7.refs_11_) | copy-start | bytes 2332804
  66.7 1.3 %copy-start.9 = (bf16[23,2,8100]{2,1,0:T(2,128)(2,1)}, bf16[23,2,8100]{2,1,0:T(2,128)(2,1)S(1)}, u32[]{:S(2)}) copy-start(bf16[23,2,8100]{2,1,0:T(2,128)(2,1)S(1)} %collective-permute-done.4.refs_7_) | copy-start | bytes 2235604
  68.1 36.7 %copy-start.11 = (f32[1,45]{1,0:T(1,128)S(1)}, f32[1,45]{1,0:T(1,128)}, u32[]{:S(2)}) copy-start(f32[1,45]{1,0:T(1,128)} %param.20) | copy-start | bytes 544
  68.1 36.7 %copy-start.12 = (f32[1,45]{1,0:T(1,128)S(1)}, f32[1,45]{1,0:T(1,128)}, u32[]{:S(2)}) copy-start(f32[1,45]{1,0:T(1,128)} %param.21) | copy-start | bytes 544
  78.9 6.1 %collective-permute-start.10 = (f32[1,128]{1,0:T(1,128)}, f32[1,128]{1,0:T(1,128)S(1)}, u32[]{:S(2)}, u32[]{:S(2)}) collective-permute-start(f32[1,128]{1,0:T(1,128)} %interaction.1), channel_id=1, source_target_pairs={{0,192},{64,0},{128,64},{192,128},{1,193},{65,1},{129,65},{193,129... | collective-permute-start | bytes 1544 | tf_op jit(solution)/shard_map/collect/ppermute | solution.py:423
  81.6 5.2 %collective-permute-start.9 = (f32[1,128]{1,0:T(1,128)}, f32[1,128]{1,0:T(1,128)S(1)}, u32[]{:S(2)}, u32[]{:S(2)}) collective-permute-start(f32[1,128]{1,0:T(1,128)} %interaction.1), channel_id=1, source_target_pairs={{0,128},{64,192},{128,0},{192,64},{1,129},{65,193},{129,1},{193,65... | collective-permute-start | bytes 1544 | tf_op jit(solution)/shard_map/collect/ppermute | solution.py:423
  82.4 4.4 %collective-permute-start.8 = (f32[1,128]{1,0:T(1,128)}, f32[1,128]{1,0:T(1,128)S(1)}, u32[]{:S(2)}, u32[]{:S(2)}) collective-permute-start(f32[1,128]{1,0:T(1,128)} %interaction.1), channel_id=1, source_target_pairs={{0,64},{64,128},{128,192},{192,0},{1,65},{65,129},{129,193},{193,1... | collective-permute-start | bytes 1544 | tf_op jit(solution)/shard_map/collect/ppermute | solution.py:423

commit v13 on v11

--- a/solution.py
+++ b/solution.py
@@ -390,14 +390,11 @@
             compiler_params=PARAMS,
         )(*inputs)
     with jax.named_scope("collect"):
-        own_row = sums
-        rows = [own_row] + [lax.ppermute(own_row, "clus", ring(4, step)) for step in (1, 2, 3)]
         points = jnp.arange(32, dtype=jnp.int32)
-        partial = jnp.zeros((32, 128), f32)
-        for step in range(4):
-            point = lax.dynamic_index_in_dim(irreducible, (clus - step) % 4, 0, keepdims=False)
-            partial = partial + jnp.where((points == point)[:, None], rows[step], 0.0)
-        received = lax.all_to_all(partial[:, None, :], "trip", 0, 0, tiled=True)
+        mine_is = points == lax.dynamic_index_in_dim(irreducible, clus, 0, keepdims=False)
+        partial = jnp.where(mine_is[None, :, None], sums[None], 0.0)
+        partial = jnp.broadcast_to(partial, (4, 32, 128)).reshape(128, 1, 128)
+        received = lax.all_to_all(partial, ("clus", "trip"), 0, 0, tiled=True)
         final = jnp.sum(received[:, 0, :], axis=0)[None, :]
         gamma_total = final[:, 0:45] + boundary
         return gamma_total, (drive_term + final[:, PAD : PAD + 45]) / gamma_total

time: 104 us -> 102 us (0.981); the launches traced: 104 us -> 101 us
  starting transfers between devices: 27.2 us -> 21.7 us
  blocking collectives: 16.3 us -> 21.7 us
  other arithmetic: 6.69 us -> 4.89 us
  waiting for transfers between devices: 22.7 us -> 21.2 us
    ppermute x3 -> x0, starting transfers between devices: 5.48 us -> none  [body(): lax.ppermute(own_row, 'clus', ring(4, step))]
    all_to_all x1, blocking collectives: 16.3 us -> 21.7 us  [body(): received = lax.all_to_all(partial, ('clus', 'trip'), 0, 0, tiled=True)]
    eq x2 -> x1, other arithmetic: 2.48 us -> 0.65 us  [body(): points == lax.dynamic_index_in_dim(irreducible, clus, 0, keepdims=False)]
    ppermute x3 -> x0, waiting for transfers between devices: 1.79 us -> none  [body(): lax.ppermute(own_row, 'clus', ring(4, step))]
    unnamed x27 -> x31, local copies, waits for them, and re-layouts: 2.65 us -> 2.87 us
  transfers between devices with their start and end apart: 13 -> 10, of which waited for: 5 -> 4; matrix products, arithmetic and copies ran while one was open for 11% -> 10% of each run, Pallas kernels for 11% -> 11%
where the time goes in v13:
time: 102 us; the launch traced here: 101 us
  Pallas kernels  22.3 us (22%)
  starting transfers between devices  21.7 us (21%)
  blocking collectives  21.7 us (21%)
  waiting for transfers between devices  21.2 us (21%)
  local copies, waits for them, and re-layouts  8.03 us (8%)
  other arithmetic  4.89 us (5%)
    all_to_all x1, blocking collectives, body(): received = lax.all_to_all(partial, ('clus', 'trip'), 0, 0, tiled=True)  21.7 us
    all_to_all x1, starting transfers between devices, body(): arrived = lax.all_to_all(chosen, 'trip', 0, 0, tiled=True)  11.1 us
    all_to_all x1, waiting for transfers between devices, body(): arrived = lax.all_to_all(chosen, 'trip', 0, 0, tiled=True)  11 us
    pallas_call x1, Pallas kernels, body(): pl.pallas_call(interaction_kernel, out_shape=jax.ShapeDtypeStruct((1, 128...  10.8 us
    ppermute x1, waiting for transfers between devices, body(): top = lax.ppermute(low_top, 'clus', ring(4, 1))  5.83 us
    pallas_call x1, Pallas kernels, body(): pl.pallas_call(early_kernel, out_shape=(jax.ShapeDtypeStruct((WIDE, total...  5.81 us
    all_to_all x1, starting transfers between devices, body(): members = lax.all_to_all(picks, group, 0, 0, tiled=True)  5.06 us
    all_to_all x1, waiting for transfers between devices, body(): members = lax.all_to_all(picks, group, 0, 0, tiled=True)  2.93 us
  transfers between devices with their start and end apart: 10, of which 4 were waited for; matrix products, arithmetic and copies ran while one was open for 10% of the time, Pallas kernels for 11%

profile of v13, /device:TPU:2, one launch (start us, length us, event | category | flops | bytes accessed | tf_op | source)
XLA Modules:
  0.0 100.6 jit_solution(12352103159410724754)
XLA Ops:
  0.6 1.6 %collective-permute-start = (bf16[45,2,8100]{2,1,0:T(2,128)(2,1)}, bf16[45,2,8100]{2,1,0:T(2,128)(2,1)S(1)}, u32[]{:S(2)}, u32[]{:S(2)}) collective-permute-start(bf16[45,2,8100]{2,1,0:T(2,128)(2,1)} %bitcast.18), channel_id=1, source_target_pairs={{0,64},{64,128},{128,192},{192,0},{1,65},{65,129},{129,193},{193,1... | collective-permute-start | bytes 4374008 | tf_op jit(solution)/shard_map/force/ppermute | solution.py:319
  2.2 0.9 collective-permute-start.1
  3.1 1.1 %copy.22 = bf16[8,90,180]{2,1,0:T(8,128)(2,1)S(1)} copy(bf16[8,90,180]{2,0,1:T(8,128)(2,1)} %param.13) | data formatting | bytes 518400 | tf_op args[2]
  4.1 0.8 maximum_bitcast_fusion
  4.9 0.1 pad_dynamic-slice_fusion.2
  5.0 0.7 fusion.1.share_ref
  5.7 1.6 %records.1 = bf16[32,12,180]{2,1,0:T(8,128)(2,1)} custom-call(s32[1,32]{1,0:T(1,128)} %rows_ref.1, bf16[8,12,180]{2,1,0:T(8,128)(2,1)} %fusion.1.share_ref), custom_call_target="tpu_custom_call" | custom-call | tf_op jit(solution)/shard_map/records/pallas_call | solution.py:305
  7.3 11.1 %all-to-all-start = ((bf16[32,12,180]{2,1,0:T(8,128)(2,1)}), bf16[32,12,180]{2,1,0:T(8,128)(2,1)S(1)}, u32[]{:S(2)}, u32[]{:S(2)}) async-start(bf16[32,12,180]{2,1,0:T(8,128)(2,1)} %records.1), calls=%async_computation | async-start | bytes 524288 | tf_op jit(solution)/shard_map/records/all_to_all | solution.py:312
  18.6 0.1 copy.26
  18.7 0.6 pad.4.phase_ref
  19.3 11.0 %all-to-all-done.arrived_ref = bf16[32,12,180]{2,1,0:T(8,128)(2,1)S(1)} async-done(((bf16[32,12,180]{2,1,0:T(8,128)(2,1)}), bf16[32,12,180]{2,1,0:T(8,128)(2,1)S(1)}, u32[]{:S(2)}, u32[]{:S(2)}) %all-to-all-start) | async-done | bytes 138272 | tf_op jit(solution)/shard_map/records/all_to_all | solution.py:312
  30.3 0.7 copy-done.3
  31.0 1.7 %members.1 = bf16[8,4,16,180]{3,2,1,0:T(8,128)(2,1)} custom-call(s32[4,3]{1,0:T(4,128)} %table_ref.1, bf16[32,12,180]{2,1,0:T(8,128)(2,1)} %copy-done.3, bf16[4,16,180]{2,1,0:T(8,128)(2,1)} %pad.4.phase_ref), custom_call_target="tpu_custom_call" | custom-call | tf_op jit(solution)/shard_map/members/pallas_call | solution.py:323
  32.7 5.1 %all-to-all-start.1 = ((bf16[8,4,16,180]{3,2,1,0:T(8,128)(2,1)}), bf16[8,4,16,180]{3,2,1,0:T(8,128)(2,1)S(1)}, u32[]{:S(2)}, u32[]{:S(2)}) async-start(bf16[8,4,16,180]{3,2,1,0:T(8,128)(2,1)} %members.1), calls=%async_computation.1 | async-start | bytes 524288 | tf_op jit(solution)/shard_map/members/all_to_all | solution.py:330
  37.7 0.0 collective-permute-done.low_ref
  37.7 1.6 %slice.16 = bf16[23,2,8100]{2,1,0:T(2,128)(2,1)} slice(bf16[45,2,8100]{2,1,0:T(2,128)(2,1)S(1)} %collective-permute-done.low_ref), slice={[0:23], [0:2], [0:8100]} | slice | bytes 1490400 | tf_op jit(solution)/shard_map/force_second/slice | solution.py:333
  39.3 0.0 collective-permute-done.1.high_ref
  39.3 1.6 %slice.17 = bf16[22,2,8100]{2,1,0:T(2,128)(2,1)} slice(bf16[45,2,8100]{2,1,0:T(2,128)(2,1)S(1)} %collective-permute-done.1.high_ref), slice={[23:45], [0:2], [0:8100]} | slice | bytes 1425600 | tf_op jit(solution)/shard_map/force_second/slice | solution.py:333
  40.9 0.0 copy-done
  40.9 2.9 %all-to-all-done.1.members_ref = bf16[8,4,16,180]{3,2,1,0:T(8,128)(2,1)S(1)} async-done(((bf16[8,4,16,180]{3,2,1,0:T(8,128)(2,1)}), bf16[8,4,16,180]{3,2,1,0:T(8,128)(2,1)S(1)}, u32[]{:S(2)}, u32[]{:S(2)}) %all-to-all-start.1) | async-done | bytes 184352 | tf_op jit(solution)/shard_map/members/all_to_all | solution.py:330
  43.8 0.0 collective-permute-start.2
  43.8 2.0 %collective-permute-start.3 = (bf16[22,2,8100]{2,1,0:T(2,128)(2,1)}, bf16[22,2,8100]{2,1,0:T(2,128)(2,1)S(1)}, u32[]{:S(2)}, u32[]{:S(2)}) collective-permute-start(bf16[22,2,8100]{2,1,0:T(2,128)(2,1)} %slice.17), channel_id=1, source_target_pairs={{0,192},{64,0},{128,64},{192,128},{1,193},{65,1},{129,65},{193,129... | collective-permute-start | bytes 2138408 | tf_op jit(solution)/shard_map/force_second/ppermute | solution.py:335
  45.9 0.6 dynamic_slice.11
  46.4 1.2 %pad_add_fusion.where_ref = s32[3]{0:T(128)} fusion(s32[1]{0:T(128)} %dynamic_slice.11, s32[1]{0:T(128)} %bitcast.2, s32[1]{0:T(128)} %bitcast.1), kind=kLoop, calls=%fused_computation.14 | loop fusion | flops 6 | bytes 24 | tf_op jit(solution)/shard_map/operands/stack | solution.py:339
  47.7 2.4 %operands.1 = (bf16[192,288]{1,0:T(8,128)(2,1)}, bf16[96,192]{1,0:T(8,128)(2,1)}, bf16[192,192]{1,0:T(8,128)(2,1)}, bf16[256,256]{1,0:T(8,128)(2,1)}, f32[4,96,128]{2,1,0:T(8,128)}, /*index=5*/f32[2,48,128]{2,1,0:T(8,128)}) custom-call(s32[3]{0:T(128)} %pad_add_fusion.where_ref, bf16[8,4,16,180]{3,2,1,0:T(8,128)(2,1)} %copy-done.2), custom_call_target="tpu_custom_call" | custom-call | tf_op jit(solution)/shard_map/operands/pallas_call | solution.py:340
  50.1 0.0 copy-done.1
  50.1 5.8 %contract.1 = (bf16[96,8100]{1,0:T(8,128)(2,1)}, bf16[48,8100]{1,0:T(8,128)(2,1)}, bf16[48,8100]{1,0:T(8,128)(2,1)}) custom-call(bf16[192,288]{1,0:T(8,128)(2,1)} %get-tuple-element.20.lead_ref, bf16[45,2,8100]{2,1,0:T(2,128)(2,1)} %bitcast.20, bf16[45,2,8100]{2,1,0:T(2,128)(2,1)} %copy-done, bf16[45,2,8100]{2,1,0:T(2,128)(2,1)} %copy-done.1), custom_call_target="tpu_custom_call" | custom-call | flops 895795200 | bytes 9720000 | tf_op jit(solution)/shard_map/contract/pallas_call | solution.py:358
  55.9 0.0 collective-permute-start.6
  55.9 0.5 collective-permute-start.7
  56.4 5.8 %collective-permute-done.2.refs_5_ = bf16[23,2,8100]{2,1,0:T(2,128)(2,1)S(1)} collective-permute-done((bf16[23,2,8100]{2,1,0:T(2,128)(2,1)}, bf16[23,2,8100]{2,1,0:T(2,128)(2,1)S(1)}, u32[]{:S(2)}, u32[]{:S(2)}) %collective-permute-start.2) | collective-permute-done | bytes 745232 | tf_op jit(solution)/shard_map/force_second/ppermute | solution.py:334
  62.3 0.0 collective-permute-start.4
  62.3 0.0 collective-permute-done.3.refs_6_
  62.3 0.5 collective-permute-start.5
  62.8 0.6 dynamic_slice.10
  63.4 0.6 iota_compare_fusion
  64.0 0.0 collective-permute-done.6.refs_10_
  64.0 0.0 collective-permute-done.7.refs_11_
  64.1 1.5 %collective-permute-done.5.refs_8_ = bf16[22,2,8100]{2,1,0:T(2,128)(2,1)S(1)} collective-permute-done((bf16[22,2,8100]{2,1,0:T(2,128)(2,1)S(1)}, bf16[22,2,8100]{2,1,0:T(2,128)(2,1)S(1)}, u32[]{:S(2)}, u32[]{:S(2)}) %collective-permute-start.5) | collective-permute-done | bytes 712832 | tf_op jit(solution)/shard_map/contract/ppermute | solution.py:371
  65.5 0.0 collective-permute-done.4.refs_7_
  65.5 0.0 copy-done.8
  65.6 0.0 copy-done.4
  65.6 0.8 copy-done.9
  66.4 0.2 copy-done.7
  66.6 10.8 %interaction.1 = f32[1,128]{1,0:T(1,128)} custom-call(f32[2,48,128]{2,1,0:T(8,128)} %get-tuple-element.13.refs_0_, bf16[192,192]{1,0:T(8,128)(2,1)} %get-tuple-element.14.refs_1_, bf16[256,256]{1,0:T(8,128)(2,1)} %get-tuple-element.15.refs_2_, f32[4,96,128]{2,1,0:T(8,128)} %get-tuple-element.16.refs_3_, bf16[96,192]{1,0:T(8,128)(2,1)} %get-tuple-element.17.refs_4_, ...), custom_call_target="tpu_custom_call" | custom-call | tf_op jit(solution)/shard_map/interaction/pallas_call | solution.py:375
  77.4 0.7 broadcast_select_fusion
  78.2 21.7 %all_to_all.15 = f32[128,1,128]{2,1,0:T(1,128)S(1)} all-to-all(f32[128,1,128]{2,1,0:T(1,128)S(1)} %bitcast.21), channel_id=1, replica_groups=mesh['clus'=4,'trip'=32,'mode'=2] {'clus','trip'}, dimensions={0} | all-to-all | bytes 131072 | tf_op jit(solution)/shard_map/collect/all_to_all | solution.py:397
  99.9 0.2 reduce_sum.9
  100.0 0.6 add_divide_fusion
  (29 shorter events, 0.1 us)
Async XLA Ops:
  0.6 17.9 %copy-start.12 = (bf16[2,4]{1,0:T(2,128)(2,1)S(1)}, bf16[2,4]{1,0:T(2,128)(2,1)}, u32[]{:S(2)}) copy-start(bf16[2,4]{1,0:T(2,128)(2,1)} %param.12) | copy-start | bytes 52
  0.6 37.1 %collective-permute-start = (bf16[45,2,8100]{2,1,0:T(2,128)(2,1)}, bf16[45,2,8100]{2,1,0:T(2,128)(2,1)S(1)}, u32[]{:S(2)}, u32[]{:S(2)}) collective-permute-start(bf16[45,2,8100]{2,1,0:T(2,128)(2,1)} %bitcast.18), channel_id=1, source_target_pairs={{0,64},{64,128},{128,192},{192,0},{1,65},{65,129},{129,193},{193,1... | collective-permute-start | bytes 4374008 | tf_op jit(solution)/shard_map/force/ppermute | solution.py:319
  2.2 37.1 %collective-permute-start.1 = (bf16[45,2,8100]{2,1,0:T(2,128)(2,1)}, bf16[45,2,8100]{2,1,0:T(2,128)(2,1)S(1)}, u32[]{:S(2)}, u32[]{:S(2)}) collective-permute-start(bf16[45,2,8100]{2,1,0:T(2,128)(2,1)} %bitcast.19), channel_id=1, source_target_pairs={{0,192},{64,0},{128,64},{192,128},{1,193},{65,1},{129,65},{193,129... | collective-permute-start | bytes 4374008 | tf_op jit(solution)/shard_map/force/ppermute | solution.py:320
  7.3 22.9 %all-to-all-start = ((bf16[32,12,180]{2,1,0:T(8,128)(2,1)}), bf16[32,12,180]{2,1,0:T(8,128)(2,1)S(1)}, u32[]{:S(2)}, u32[]{:S(2)}) async-start(bf16[32,12,180]{2,1,0:T(8,128)(2,1)} %records.1), calls=%async_computation | async-start | bytes 524288 | tf_op jit(solution)/shard_map/records/all_to_all | solution.py:312
  30.3 0.7 copy-start.3
  32.7 11.2 %all-to-all-start.1 = ((bf16[8,4,16,180]{3,2,1,0:T(8,128)(2,1)}), bf16[8,4,16,180]{3,2,1,0:T(8,128)(2,1)S(1)}, u32[]{:S(2)}, u32[]{:S(2)}) async-start(bf16[8,4,16,180]{3,2,1,0:T(8,128)(2,1)} %members.1), calls=%async_computation.1 | async-start | bytes 524288 | tf_op jit(solution)/shard_map/members/all_to_all | solution.py:330
  37.7 8.1 %copy-start.13 = (s32[4]{0:T(128)S(1)}, s32[4]{0:T(128)}, u32[]{:S(2)}) copy-start(s32[4]{0:T(128)} %param.19) | copy-start | bytes 52
  37.7 3.2 %copy-start = (bf16[45,2,8100]{2,1,0:T(2,128)(2,1)}, bf16[45,2,8100]{2,1,0:T(2,128)(2,1)S(1)}, u32[]{:S(2)}) copy-start(bf16[45,2,8100]{2,1,0:T(2,128)(2,1)S(1)} %collective-permute-done.low_ref) | copy-start | bytes 4374004
  39.3 10.8 %copy-start.1 = (bf16[45,2,8100]{2,1,0:T(2,128)(2,1)}, bf16[45,2,8100]{2,1,0:T(2,128)(2,1)S(1)}, u32[]{:S(2)}) copy-start(bf16[45,2,8100]{2,1,0:T(2,128)(2,1)S(1)} %collective-permute-done.1.high_ref) | copy-start | bytes 4374004
  43.8 3.9 %copy-start.2 = (bf16[8,4,16,180]{3,2,1,0:T(8,128)(2,1)}, bf16[8,4,16,180]{3,2,1,0:T(8,128)(2,1)S(1)}, u32[]{:S(2)}) copy-start(bf16[8,4,16,180]{3,2,1,0:T(8,128)(2,1)S(1)} %all-to-all-done.1.members_ref) | copy-start | bytes 552964
  43.8 18.4 %collective-permute-start.2 = (bf16[23,2,8100]{2,1,0:T(2,128)(2,1)}, bf16[23,2,8100]{2,1,0:T(2,128)(2,1)S(1)}, u32[]{:S(2)}, u32[]{:S(2)}) collective-permute-start(bf16[23,2,8100]{2,1,0:T(2,128)(2,1)} %slice.16), channel_id=1, source_target_pairs={{0,64},{64,128},{128,192},{192,0},{1,65},{65,129},{129,193},{193,1... | collective-permute-start | bytes 2235608 | tf_op jit(solution)/shard_map/force_second/ppermute | solution.py:334
  43.8 18.4 %collective-permute-start.3 = (bf16[22,2,8100]{2,1,0:T(2,128)(2,1)}, bf16[22,2,8100]{2,1,0:T(2,128)(2,1)S(1)}, u32[]{:S(2)}, u32[]{:S(2)}) collective-permute-start(bf16[22,2,8100]{2,1,0:T(2,128)(2,1)} %slice.17), channel_id=1, source_target_pairs={{0,192},{64,0},{128,64},{192,128},{1,193},{65,1},{129,65},{193,129... | collective-permute-start | bytes 2138408 | tf_op jit(solution)/shard_map/force_second/ppermute | solution.py:335
  50.1 12.7 %copy-start.14 = (s32[4]{0:T(128)S(1)}, s32[4]{0:T(128)}, u32[]{:S(2)}) copy-start(s32[4]{0:T(128)} %param.18) | copy-start | bytes 52
  55.9 8.1 %collective-permute-start.6 = (bf16[48,8100]{1,0:T(8,128)(2,1)}, bf16[48,8100]{1,0:T(8,128)(2,1)S(1)}, u32[]{:S(2)}, u32[]{:S(2)}) collective-permute-start(bf16[48,8100]{1,0:T(8,128)(2,1)} %get-tuple-element.22), channel_id=1, source_target_pairs={{0,1},{1,0},{2,3},{3,2},{4,5},{5,4},{6,7},{7,6},{8,9},{9,8},{10,11... | collective-permute-start | bytes 2332808 | tf_op jit(solution)/shard_map/contract/ppermute | solution.py:369
  55.9 8.1 %collective-permute-start.7 = (bf16[48,8100]{1,0:T(8,128)(2,1)}, bf16[48,8100]{1,0:T(8,128)(2,1)S(1)}, u32[]{:S(2)}, u32[]{:S(2)}) collective-permute-start(bf16[48,8100]{1,0:T(8,128)(2,1)} %get-tuple-element.23), channel_id=1, source_target_pairs={{0,1},{1,0},{2,3},{3,2},{4,5},{5,4},{6,7},{7,6},{8,9},{9,8},{10,11... | collective-permute-start | bytes 2332808 | tf_op jit(solution)/shard_map/contract/ppermute | solution.py:369
  62.3 3.3 %copy-start.6 = (bf16[23,2,8100]{2,1,0:T(2,128)(2,1)}, bf16[23,2,8100]{2,1,0:T(2,128)(2,1)S(1)}, u32[]{:S(2)}) copy-start(bf16[23,2,8100]{2,1,0:T(2,128)(2,1)S(1)} %collective-permute-done.2.refs_5_) | copy-start | bytes 2235604
  62.3 3.3 %collective-permute-start.4 = (bf16[23,2,8100]{2,1,0:T(2,128)(2,1)S(1)}, bf16[23,2,8100]{2,1,0:T(2,128)(2,1)S(1)}, u32[]{:S(2)}, u32[]{:S(2)}) collective-permute-start(bf16[23,2,8100]{2,1,0:T(2,128)(2,1)S(1)} %collective-permute-done.2.refs_5_), channel_id=1, source_target_pairs={{0,1},{1,0},{2,3},{3,2},{4,5},{5,4},{6,7},{7,6},{8,9},{9,8},{10,11... | collective-permute-start | bytes 2235608 | tf_op jit(solution)/shard_map/contract/ppermute | solution.py:370
  62.3 3.3 %copy-start.8 = (bf16[22,2,8100]{2,1,0:T(2,128)(2,1)}, bf16[22,2,8100]{2,1,0:T(2,128)(2,1)S(1)}, u32[]{:S(2)}) copy-start(bf16[22,2,8100]{2,1,0:T(2,128)(2,1)S(1)} %collective-permute-done.3.refs_6_) | copy-start | bytes 2138404
  62.3 3.3 %collective-permute-start.5 = (bf16[22,2,8100]{2,1,0:T(2,128)(2,1)S(1)}, bf16[22,2,8100]{2,1,0:T(2,128)(2,1)S(1)}, u32[]{:S(2)}, u32[]{:S(2)}) collective-permute-start(bf16[22,2,8100]{2,1,0:T(2,128)(2,1)S(1)} %collective-permute-done.3.refs_6_), channel_id=1, source_target_pairs={{0,1},{1,0},{2,3},{3,2},{4,5},{5,4},{6,7},{7,6},{8,9},{9,8},{10,11... | collective-permute-start | bytes 2138408 | tf_op jit(solution)/shard_map/contract/ppermute | solution.py:371
  64.0 1.5 %copy-start.4 = (bf16[48,8100]{1,0:T(8,128)(2,1)}, bf16[48,8100]{1,0:T(8,128)(2,1)S(1)}, u32[]{:S(2)}) copy-start(bf16[48,8100]{1,0:T(8,128)(2,1)S(1)} %collective-permute-done.6.refs_10_) | copy-start | bytes 2332804
  64.0 1.5 %copy-start.5 = (bf16[48,8100]{1,0:T(8,128)(2,1)}, bf16[48,8100]{1,0:T(8,128)(2,1)S(1)}, u32[]{:S(2)}) copy-start(bf16[48,8100]{1,0:T(8,128)(2,1)S(1)} %collective-permute-done.7.refs_11_) | copy-start | bytes 2332804
  65.5 0.9 copy-start.9
  65.5 1.1 %copy-start.7 = (bf16[23,2,8100]{2,1,0:T(2,128)(2,1)}, bf16[23,2,8100]{2,1,0:T(2,128)(2,1)S(1)}, u32[]{:S(2)}) copy-start(bf16[23,2,8100]{2,1,0:T(2,128)(2,1)S(1)} %collective-permute-done.4.refs_7_) | copy-start | bytes 2235604
  66.6 33.4 %copy-start.10 = (f32[1,45]{1,0:T(1,128)S(1)}, f32[1,45]{1,0:T(1,128)}, u32[]{:S(2)}) copy-start(f32[1,45]{1,0:T(1,128)} %param.20) | copy-start | bytes 544
  66.6 33.4 %copy-start.11 = (f32[1,45]{1,0:T(1,128)S(1)}, f32[1,45]{1,0:T(1,128)}, u32[]{:S(2)}) copy-start(f32[1,45]{1,0:T(1,128)} %param.21) | copy-start | bytes 544
